TPU v7x, 32 devices: a whole 2x2x4 slice. The times are simulated.
32 devices in a mesh: sp: 8 (over y, x, core), fs: 4 (over z).
Axes of the slice: x: 2, y: 2, z: 4, core: 2. Of those that a mesh axis runs over, the one named last changes fastest.
Arguments:
- tokens: bfloat16 [2, 4, 16, 192, 256], P(None, 'fs', 'sp'), may hold values from -6 to 6
- cotangent: float32 [2, 4, 16, 192, 256], P(None, 'fs', 'sp'), may hold values from -6 to 6
- image_sizes: int32 [2, 4, 2], P(None, 'fs'), may hold values from 8 to 192, as said below
- first_gain: bfloat16 [256], P('fs'), may hold values from 0.25 to 1.75
- first_bias: bfloat16 [256], P('fs'), may hold values from -0.109375 to 0.109375
- query_weight: bfloat16 [256, 256], P('fs'), may hold values from -0.375 to 0.375
- query_bias: bfloat16 [256], P('fs'), may hold values from -1.75 to 1.75
- reduce_weight: bfloat16 [1024, 256], P('fs'), may hold values from -0.1875 to 0.1875
- reduce_bias: bfloat16 [256], P('fs'), may hold values from -0.109375 to 0.109375
- keys_gain: bfloat16 [256], P('fs'), may hold values from 0.25 to 1.75
- keys_bias: bfloat16 [256], P('fs'), may hold values from -0.109375 to 0.109375
- keyval_weight: bfloat16 [256, 512], P('fs'), may hold values from -0.375 to 0.375
- value_bias: bfloat16 [256], P('fs'), may hold values from -0.109375 to 0.109375
- output_weight: bfloat16 [256, 256], P('fs'), may hold values from -6 to 6
- output_bias: bfloat16 [256], P('fs'), may hold values from -1.75 to 1.75
- second_gain: bfloat16 [256], P('fs'), may hold values from 0.25 to 1.75
- second_bias: bfloat16 [256], P('fs'), may hold values from -1.75 to 1.75
- hidden_weight: bfloat16 [256, 1024], P('fs'), may hold values from -0.375 to 0.375
- hidden_bias: bfloat16 [1024], P('fs'), may hold values from -1.75 to 1.75
- return_weight: bfloat16 [1024, 256], P('fs'), may hold values from -0.1875 to 0.1875
- return_bias: bfloat16 [256], P('fs'), may hold values from -1.75 to 1.75
Outputs:
- activations: float32 [2, 4, 16, 192, 256], P(None, 'fs', 'sp')
- input_grad: float32 [2, 4, 16, 192, 256], P(None, 'fs', 'sp')
- grad_first_gain: float32 [256], P('fs')
- grad_first_bias: float32 [256], P('fs')
- grad_query_weight: float32 [256, 256], P('fs')
- grad_query_bias: float32 [256], P('fs')
- grad_reduce_weight: float32 [1024, 256], P('fs')
- grad_reduce_bias: float32 [256], P('fs')
- grad_keys_gain: float32 [256], P('fs')
- grad_keys_bias: float32 [256], P('fs')
- grad_keyval_weight: float32 [256, 512], P('fs')
- grad_value_bias: float32 [256], P('fs')
- grad_output_weight: float32 [256, 256], P('fs')
- grad_output_bias: float32 [256], P('fs')
- grad_second_gain: float32 [256], P('fs')
- grad_second_bias: float32 [256], P('fs')
- grad_hidden_weight: float32 [256, 1024], P('fs')
- grad_hidden_bias: float32 [1024], P('fs')
- grad_return_weight: float32 [1024, 256], P('fs')
- grad_return_bias: float32 [256], P('fs')
Inputs may be any that keep to these rules, and one draw needn't show every extreme that they name: image_sizes[b, i] = (height, width) in patches of image i of micro-batch b; heights from 8 to 16, widths from 96 to 192; for every i one micro-batch's image fills the whole 16 x 192 grid.
All inputs are finite; a program needn't handle non-finite values.
Results may differ from a plain program's by a relative error of at most 0.019.
Values may be sent and summed in bfloat16 or wider, within the bound.
No kernel may reach another device: no remote copies, remote signals or barrier semaphores. Data moves between devices by JAX's collectives and lax.ppermute only.
A program may use at most 128 MiB of HBM per device.

v0:
```python
import jax
import jax.numpy as jnp
from jax import lax
from jax.sharding import PartitionSpec as P

HEADS = 8
HDIM = 32


norm_eps = 1e-06
neg_large = -1e30


def matmul(left, right):
    return jnp.dot(left, right, preferred_element_type=jnp.float32)


def left_contract(left, right):
    return lax.dot_general(
        left, right, (((0,), (0,)), ((), ())), preferred_element_type=jnp.float32
    )


def right_contract(left, right):
    return lax.dot_general(
        left, right, (((1,), (1,)), ((), ())), preferred_element_type=jnp.float32
    )


def layer_norm(tensor, norm_gain, norm_shift):
    row_mean = jnp.mean(tensor, axis=-1, keepdims=True)
    centered = tensor - row_mean
    variance = jnp.mean(centered * centered, axis=-1, keepdims=True)
    return centered * lax.rsqrt(variance + norm_eps) * norm_gain + norm_shift


def gelu_exact(tensor):
    return jax.nn.gelu(tensor, approximate=False)


def block_size(piece_rows):
    block_rows = piece_rows
    while block_rows > 512 and block_rows % 2 == 0:
        block_rows = block_rows // 2
    return block_rows


def key_valid(key_start, piece_rows, half_cols, height, image_width):
    key_ids = key_start + jnp.arange(piece_rows, dtype=jnp.int32)
    return (2 * (key_ids // half_cols) < height) & (2 * (key_ids % half_cols) < image_width)


def attend_block(carried, key_heads, value_heads, is_valid, query_heads):
    running_max, running_sum, running_out = carried
    scores = jnp.einsum(
        "qhd,khd->hqk", query_heads, key_heads, preferred_element_type=jnp.float32
    ) * HDIM ** (-0.5)
    scores = jnp.where(is_valid[None, None, :], scores, neg_large)
    new_max = jnp.maximum(running_max, jnp.max(scores, axis=-1))
    weights = jnp.where(is_valid[None, None, :], jnp.exp(scores - new_max[:, :, None]), 0.0)
    factor = jnp.exp(running_max - new_max)
    running_sum = running_sum * factor + jnp.sum(weights, axis=-1)
    update = jnp.einsum(
        "hqk,khd->qhd",
        weights.astype(jnp.bfloat16),
        value_heads,
        preferred_element_type=jnp.float32,
    )
    running_out = running_out * factor.T[:, :, None] + update
    return (new_max, running_sum, running_out)


def fold_keys(carried, key_piece, query_heads, half_cols, height, image_width):
    piece_rows = key_piece.shape[0]
    model_dim = key_piece.shape[1] // 2
    block_rows = block_size(piece_rows)
    turns = piece_rows // block_rows

    def one_block(state, block_index):
        offset = block_index * block_rows
        key_rows = lax.dynamic_slice_in_dim(key_piece, offset, block_rows, 0)
        key_heads = key_rows[:, :model_dim].reshape(block_rows, HEADS, HDIM)
        value_heads = key_rows[:, model_dim:].reshape(block_rows, HEADS, HDIM)
        is_valid = key_valid(offset, block_rows, half_cols, height, image_width)
        return (attend_block(state, key_heads, value_heads, is_valid, query_heads), None)

    carried, _ = lax.scan(one_block, carried, jnp.arange(turns, dtype=jnp.int32))
    return carried


def gather_weights(shards):
    return (
        lax.all_gather(shards[0], "fs", axis=0, tiled=True),
        lax.all_gather(shards[1], "fs", axis=0, tiled=True),
        lax.all_gather(shards[2], "fs", axis=0, tiled=True),
        lax.all_gather(shards[3], "fs", axis=0, tiled=True),
        lax.all_gather(shards[4], "fs", axis=0, tiled=True),
        lax.all_gather(shards[5], "fs", axis=0, tiled=True),
        lax.all_gather(shards[6], "fs", axis=0, tiled=True),
        lax.all_gather(shards[7], "fs", axis=0, tiled=True),
        lax.all_gather(shards[8], "fs", axis=0, tiled=True),
        lax.all_gather(shards[9], "fs", axis=0, tiled=True),
        lax.all_gather(shards[10], "fs", axis=0, tiled=True),
        lax.all_gather(shards[11], "fs", axis=0, tiled=True),
        lax.all_gather(shards[12], "fs", axis=0, tiled=True),
        lax.all_gather(shards[13], "fs", axis=0, tiled=True),
        lax.all_gather(shards[14], "fs", axis=0, tiled=True),
        lax.all_gather(shards[15], "fs", axis=0, tiled=True),
        lax.all_gather(shards[16], "fs", axis=0, tiled=True),
        lax.all_gather(shards[17], "fs", axis=0, tiled=True),
    )


def reduce_grads(grads):
    shares = (
        lax.psum_scatter(
            grads[0].astype(jnp.bfloat16), "fs", scatter_dimension=0, tiled=True
        ).astype(jnp.float32),
        lax.psum_scatter(
            grads[1].astype(jnp.bfloat16), "fs", scatter_dimension=0, tiled=True
        ).astype(jnp.float32),
        lax.psum_scatter(
            grads[2].astype(jnp.bfloat16), "fs", scatter_dimension=0, tiled=True
        ).astype(jnp.float32),
        lax.psum_scatter(
            grads[3].astype(jnp.bfloat16), "fs", scatter_dimension=0, tiled=True
        ).astype(jnp.float32),
        lax.psum_scatter(
            grads[4].astype(jnp.bfloat16), "fs", scatter_dimension=0, tiled=True
        ).astype(jnp.float32),
        lax.psum_scatter(
            grads[5].astype(jnp.bfloat16), "fs", scatter_dimension=0, tiled=True
        ).astype(jnp.float32),
        lax.psum_scatter(
            grads[6].astype(jnp.bfloat16), "fs", scatter_dimension=0, tiled=True
        ).astype(jnp.float32),
        lax.psum_scatter(
            grads[7].astype(jnp.bfloat16), "fs", scatter_dimension=0, tiled=True
        ).astype(jnp.float32),
        lax.psum_scatter(
            grads[8].astype(jnp.bfloat16), "fs", scatter_dimension=0, tiled=True
        ).astype(jnp.float32),
        lax.psum_scatter(
            grads[9].astype(jnp.bfloat16), "fs", scatter_dimension=0, tiled=True
        ).astype(jnp.float32),
        lax.psum_scatter(
            grads[10].astype(jnp.bfloat16), "fs", scatter_dimension=0, tiled=True
        ).astype(jnp.float32),
        lax.psum_scatter(
            grads[11].astype(jnp.bfloat16), "fs", scatter_dimension=0, tiled=True
        ).astype(jnp.float32),
        lax.psum_scatter(
            grads[12].astype(jnp.bfloat16), "fs", scatter_dimension=0, tiled=True
        ).astype(jnp.float32),
        lax.psum_scatter(
            grads[13].astype(jnp.bfloat16), "fs", scatter_dimension=0, tiled=True
        ).astype(jnp.float32),
        lax.psum_scatter(
            grads[14].astype(jnp.bfloat16), "fs", scatter_dimension=0, tiled=True
        ).astype(jnp.float32),
        lax.psum_scatter(
            grads[15].astype(jnp.bfloat16), "fs", scatter_dimension=0, tiled=True
        ).astype(jnp.float32),
        lax.psum_scatter(
            grads[16].astype(jnp.bfloat16), "fs", scatter_dimension=0, tiled=True
        ).astype(jnp.float32),
        lax.psum_scatter(
            grads[17].astype(jnp.bfloat16), "fs", scatter_dimension=0, tiled=True
        ).astype(jnp.float32),
    )
    return lax.psum(
        (
            shares[0],
            shares[1],
            shares[2],
            shares[3],
            shares[4],
            shares[5],
            shares[6],
            shares[7],
            shares[8],
            shares[9],
            shares[10],
            shares[11],
            shares[12],
            shares[13],
            shares[14],
            shares[15],
            shares[16],
            shares[17],
        ),
        "sp",
    )


def on_device(
    tokens,
    cotangent,
    image_sizes,
    first_gain,
    first_bias,
    query_weight,
    query_bias,
    reduce_weight,
    reduce_bias,
    keys_gain,
    keys_bias,
    keyval_weight,
    value_bias,
    output_weight,
    output_bias,
    second_gain,
    second_bias,
    hidden_weight,
    hidden_bias,
    return_weight,
    return_bias,
):
    shards = (
        first_gain,
        first_bias,
        query_weight,
        query_bias,
        reduce_weight,
        reduce_bias,
        keys_gain,
        keys_bias,
        keyval_weight,
        value_bias,
        output_weight,
        output_bias,
        second_gain,
        second_bias,
        hidden_weight,
        hidden_bias,
        return_weight,
        return_bias,
    )
    batches = tokens.shape[0]
    row_dev = tokens.shape[2]
    cols_all = tokens.shape[3]
    model_dim = tokens.shape[4]
    half_cols = cols_all // 2
    tok_dev = row_dev * cols_all
    key_dev = tok_dev // 4
    score_scale = HDIM ** (-0.5)
    row_ids = lax.axis_index("sp") * row_dev + jnp.arange(row_dev, dtype=jnp.int32)
    col_ids = jnp.arange(cols_all, dtype=jnp.int32)
    collected = None
    acts_list = []
    input_list = []
    for microbatch in range(batches):
        full = gather_weights(shards)
        wide = tuple(
            (weight.astype(jnp.float32) if weight.ndim == 1 else weight for weight in full)
        )
        height = image_sizes[microbatch, 0, 0]
        image_width = image_sizes[microbatch, 0, 1]
        tok_mask = (
            ((row_ids[:, None] < height) & (col_ids[None, :] < image_width))
            .astype(jnp.float32)
            .reshape(tok_dev)
        )
        inputs = tokens[microbatch, 0].reshape(tok_dev, model_dim).astype(jnp.float32)
        normed, first_back = jax.vjp(layer_norm, inputs, wide[0], wide[1])
        normed_low = normed.astype(jnp.bfloat16)
        queries = (matmul(normed_low, wide[2]) + wide[3]).astype(jnp.bfloat16)
        masked = normed_low * tok_mask[:, None].astype(jnp.bfloat16)
        patches = (
            masked.reshape(row_dev // 2, 2, half_cols, 2, model_dim)
            .transpose(0, 2, 1, 3, 4)
            .reshape(key_dev, 4 * model_dim)
        )
        reduced = matmul(patches, wide[4]) + wide[5]
        key_normed, keys_back = jax.vjp(layer_norm, reduced, wide[6], wide[7])
        key_low = key_normed.astype(jnp.bfloat16)
        shift_row = jnp.concatenate([jnp.zeros((model_dim,), jnp.float32), wide[9]])
        keyval = (matmul(key_low, wide[8]) + shift_row).astype(jnp.bfloat16)
        query_heads = queries.reshape(tok_dev, HEADS, HDIM)
        start_state = (
            jnp.full((HEADS, tok_dev), neg_large, jnp.float32),
            jnp.zeros((HEADS, tok_dev), jnp.float32),
            jnp.zeros((tok_dev, HEADS, HDIM), jnp.float32),
        )
        running_max, running_sum, running_out = fold_keys(
            start_state,
            lax.all_gather(keyval, "sp", axis=0, tiled=True),
            query_heads,
            half_cols,
            height,
            image_width,
        )
        attended = running_out / running_sum.T[:, :, None]
        log_total = running_max + jnp.log(running_sum)
        attended_low = attended.reshape(tok_dev, model_dim).astype(jnp.bfloat16)
        middle = inputs + matmul(attended_low, wide[10]) + wide[11]
        second, second_back = jax.vjp(layer_norm, middle, wide[12], wide[13])
        second_low = second.astype(jnp.bfloat16)
        hidden = matmul(second_low, wide[14]) + wide[15]
        activated, gelu_back = jax.vjp(gelu_exact, hidden)
        activated_low = activated.astype(jnp.bfloat16)
        outputs = (middle + matmul(activated_low, wide[16]) + wide[17]) * tok_mask[:, None]
        grad_out = cotangent[microbatch, 0].reshape(tok_dev, model_dim) * tok_mask[:, None]
        grad_mlp = grad_out.astype(jnp.bfloat16)
        grad_return_w = left_contract(activated_low, grad_mlp)
        grad_return_b = jnp.sum(grad_mlp.astype(jnp.float32), axis=0)
        grad_hidden = gelu_back(right_contract(grad_mlp, wide[16]))[0].astype(jnp.bfloat16)
        grad_hidden_w = left_contract(second_low, grad_hidden)
        grad_hidden_b = jnp.sum(grad_hidden.astype(jnp.float32), axis=0)
        middle_part, grad_second_g, grad_second_b = second_back(
            right_contract(grad_hidden, wide[14])
        )
        grad_middle = grad_out + middle_part
        grad_branch = grad_middle.astype(jnp.bfloat16)
        grad_output_w = left_contract(attended_low, grad_branch)
        grad_output_b = jnp.sum(grad_branch.astype(jnp.float32), axis=0)
        grad_attended = (
            right_contract(grad_branch, wide[10]).astype(jnp.bfloat16).reshape(tok_dev, HEADS, HDIM)
        )
        row_delta = jnp.einsum("qhd,qhd->hq", grad_attended.astype(jnp.float32), attended)
        keyval_all = lax.all_gather(keyval, "sp", axis=0, tiled=True)
        key_total = keyval_all.shape[0]
        block_rows = block_size(key_total)
        turns = key_total // block_rows

        def key_grad_block(grad_query, block_index):
            offset = block_index * block_rows
            key_rows = lax.dynamic_slice_in_dim(keyval_all, offset, block_rows, 0)
            key_heads = key_rows[:, :model_dim].reshape(block_rows, HEADS, HDIM)
            value_heads = key_rows[:, model_dim:].reshape(block_rows, HEADS, HDIM)
            is_valid = key_valid(offset, block_rows, half_cols, height, image_width)
            scores = (
                jnp.einsum(
                    "qhd,khd->hqk", query_heads, key_heads, preferred_element_type=jnp.float32
                )
                * score_scale
            )
            weights = jnp.where(
                is_valid[None, None, :], jnp.exp(scores - log_total[:, :, None]), 0.0
            )
            grad_probs = jnp.einsum(
                "qhd,khd->hqk", grad_attended, value_heads, preferred_element_type=jnp.float32
            )
            grad_scores = (weights * (grad_probs - row_delta[:, :, None])).astype(jnp.bfloat16)
            grad_query = (
                grad_query
                + jnp.einsum(
                    "hqk,khd->qhd", grad_scores, key_heads, preferred_element_type=jnp.float32
                )
                * score_scale
            )
            grad_keys = (
                jnp.einsum(
                    "hqk,qhd->khd", grad_scores, query_heads, preferred_element_type=jnp.float32
                )
                * score_scale
            )
            grad_values = jnp.einsum(
                "hqk,qhd->khd",
                weights.astype(jnp.bfloat16),
                grad_attended,
                preferred_element_type=jnp.float32,
            )
            joined = jnp.concatenate(
                [
                    grad_keys.reshape(block_rows, model_dim),
                    grad_values.reshape(block_rows, model_dim),
                ],
                axis=1,
            )
            return (grad_query, joined)

        grad_query, key_terms = lax.scan(
            key_grad_block,
            jnp.zeros((tok_dev, HEADS, HDIM), jnp.float32),
            jnp.arange(turns, dtype=jnp.int32),
        )
        key_terms = key_terms.reshape(key_total, 2 * model_dim)
        grad_keyval = lax.psum_scatter(key_terms, "sp", scatter_dimension=0, tiled=True)
        grad_query_low = grad_query.reshape(tok_dev, model_dim).astype(jnp.bfloat16)
        grad_query_w = left_contract(normed_low, grad_query_low)
        grad_query_b = jnp.sum(grad_query_low.astype(jnp.float32), axis=0)
        grad_normed = right_contract(grad_query_low, wide[2])
        grad_kv_low = grad_keyval.astype(jnp.bfloat16)
        grad_keyval_w = left_contract(key_low, grad_kv_low)
        grad_value_b = jnp.sum(grad_kv_low[:, model_dim:].astype(jnp.float32), axis=0)
        grad_reduced, grad_keys_g, grad_keys_b = keys_back(right_contract(grad_kv_low, wide[8]))
        grad_reduced_low = grad_reduced.astype(jnp.bfloat16)
        grad_reduce_w = left_contract(patches, grad_reduced_low)
        grad_reduce_b = jnp.sum(grad_reduced_low.astype(jnp.float32), axis=0)
        grad_patches = right_contract(grad_reduced_low, wide[4])
        grad_patches = (
            grad_patches.reshape(row_dev // 2, half_cols, 2, 2, model_dim)
            .transpose(0, 2, 1, 3, 4)
            .reshape(tok_dev, model_dim)
        )
        grad_normed = grad_normed + grad_patches * tok_mask[:, None]
        inputs_part, grad_first_g, grad_first_b = first_back(grad_normed)
        grad_inputs = grad_middle + inputs_part
        local_grads = (
            grad_first_g,
            grad_first_b,
            grad_query_w,
            grad_query_b,
            grad_reduce_w,
            grad_reduce_b,
            grad_keys_g,
            grad_keys_b,
            grad_keyval_w,
            grad_value_b,
            grad_output_w,
            grad_output_b,
            grad_second_g,
            grad_second_b,
            grad_hidden_w,
            grad_hidden_b,
            grad_return_w,
            grad_return_b,
        )
        portion = reduce_grads(local_grads)
        collected = (
            portion
            if collected is None
            else tuple((left + right for left, right in zip(collected, portion)))
        )
        acts_list.append(outputs.reshape(1, 1, row_dev, cols_all, model_dim))
        input_list.append(grad_inputs.reshape(1, 1, row_dev, cols_all, model_dim))
    acts_out = jnp.concatenate(acts_list, axis=0)
    input_out = jnp.concatenate(input_list, axis=0)
    return (acts_out, input_out) + tuple(collected)


def solution(mesh):
    return jax.shard_map(
        on_device,
        mesh=mesh,
        in_specs=(
            P(None, "fs", "sp", None, None),
            P(None, "fs", "sp", None, None),
            P(None, "fs", None),
            P("fs"),
            P("fs"),
            P("fs", None),
            P("fs"),
            P("fs", None),
            P("fs"),
            P("fs"),
            P("fs"),
            P("fs", None),
            P("fs"),
            P("fs", None),
            P("fs"),
            P("fs"),
            P("fs"),
            P("fs", None),
            P("fs"),
            P("fs", None),
            P("fs"),
        ),
        out_specs=(
            P(None, "fs", "sp", None, None),
            P(None, "fs", "sp", None, None),
            P("fs"),
            P("fs"),
            P("fs", None),
            P("fs"),
            P("fs", None),
            P("fs"),
            P("fs"),
            P("fs"),
            P("fs", None),
            P("fs"),
            P("fs", None),
            P("fs"),
            P("fs"),
            P("fs"),
            P("fs", None),
            P("fs"),
            P("fs", None),
            P("fs"),
        ),
        check_vma=False,
    )
```

profile of v0, /device:TPU:9, one launch (start us, length us, event | category | flops | bytes accessed | tf_op | source)
XLA Modules:
  0.0 673.6 jit_solution(17936575861978214735)
XLA Ops:
  19.6 7.8 %all-reduce.39 = (bf16[256]{0:T(256)(128)(2,1)S(1)}, bf16[256]{0:T(256)(128)(2,1)S(1)}, bf16[256]{0:T(256)(128)(2,1)S(1)}, bf16[256]{0:T(256)(128)(2,1)S(1)}, bf...) all-reduce(bf16[256]{0:T(256)(128)(2,1)S(1)} %dynamic-update-slice., ...), channel_id=1, replica_groups=mesh['sp'=8,'fs'=4] {'fs'}, use_global_device_ids=true, to_apply=%add.6 | all-reduce | flops 2560 | bytes 10240
  31.0 11.8 %all_gather.82 = bf16[1024,256]{1,0:T(8,128)(2,1)S(1)} all-gather(bf16[256,256]{1,0:T(8,128)(2,1)S(1)} %copy-done.67), channel_id=1, replica_groups=mesh['sp'=8,'fs'=4] {'fs'}, dimensions={0}, use_global_device_ids=true | all-gather | bytes 655360 | tf_op jit(solution)/shard_map/all_gather | solution.py:97
  43.4 12.2 %all_gather.86 = bf16[256,512]{1,0:T(8,128)(2,1)S(1)} all-gather(bf16[64,512]{1,0:T(8,128)(2,1)S(1)} %copy-done.69), channel_id=1, replica_groups=mesh['sp'=8,'fs'=4] {'fs'}, dimensions={0}, use_global_device_ids=true | all-gather | bytes 327680 | tf_op jit(solution)/shard_map/all_gather | solution.py:101
  55.8 19.3 %all_gather.88 = bf16[768,512]{1,0:T(8,128)(2,1)} all-gather(bf16[96,512]{1,0:T(8,128)(2,1)S(1)} %fusion.106), channel_id=1, replica_groups=mesh['sp'=8,'fs'=4] {'sp'}, dimensions={0}, use_global_device_ids=true | all-gather | bytes 884736 | tf_op jit(solution)/shard_map/all_gather | solution.py:287
  75.2 2.4 copy.104
  78.4 11.0 %all_gather.89 = bf16[256,256]{1,0:T(8,128)(2,1)S(1)} all-gather(bf16[64,256]{1,0:T(8,128)(2,1)S(1)} %copy-done.89), channel_id=1, replica_groups=mesh['sp'=8,'fs'=4] {'fs'}, dimensions={0}, use_global_device_ids=true | all-gather | bytes 163840 | tf_op jit(solution)/shard_map/all_gather | solution.py:95
  90.7 24.4 %while.64 = (s32[]{:T(128)}, f32[8,384]{1,0:T(8,128)S(1)}, f32[8,384]{1,0:T(8,128)S(1)}, f32[384,8,32]{0,2,1:T(8,128)S(1)}, s32[2]{0:T(128)S(1)}, /*index=5*/s32...) while((s32[]{:T(128)}, f32[8,384]{1,0:T(8,128)S(1)}, ...), condition=%wide.region_7.8_spmd.clone, body=%wide.region_4.7_spmd.clone.sunk | while | flops 166650624 | bytes 35391236 | solution.py:87
  94.4 3.4 bitcast_reduce_fusion.4
  97.8 3.7 fusion.329
  106.5 3.4 bitcast_reduce_fusion.4
  110.0 3.7 fusion.329
  115.2 11.0 %all_gather.91 = bf16[256,256]{1,0:T(8,128)(2,1)S(1)} all-gather(bf16[64,256]{1,0:T(8,128)(2,1)S(1)} %copy-done.90), channel_id=1, replica_groups=mesh['sp'=8,'fs'=4] {'fs'}, dimensions={0}, use_global_device_ids=true | all-gather | bytes 163840 | tf_op jit(solution)/shard_map/all_gather | solution.py:103
  129.6 13.7 %all_gather.95 = bf16[256,1024]{1,0:T(8,128)(2,1)} all-gather(bf16[64,1024]{1,0:T(8,128)(2,1)S(1)} %copy-done.68), channel_id=1, replica_groups=mesh['sp'=8,'fs'=4] {'fs'}, dimensions={0}, use_global_device_ids=true | all-gather | bytes 655360 | tf_op jit(solution)/shard_map/all_gather | solution.py:107
  143.3 8.6 %all-gather = bf16[4,1,256]{2,1,0:T(2,128)(2,1)S(1)} all-gather(bf16[1,1,256]{2,1,0:T(2,128)(2,1)S(1)} %reshape.865), channel_id=1, replica_groups=mesh['sp'=8,'fs'=4] {'fs'}, dimensions={0}, use_global_device_ids=true | all-gather | bytes 2560 | tf_op jit(solution)/shard_map/all_gather | solution.py:108
  154.7 10.6 %all_gather.97 = bf16[1024,256]{1,0:T(8,128)(2,1)S(1)} all-gather(bf16[256,256]{1,0:T(8,128)(2,1)} %param.48), channel_id=1, replica_groups=mesh['sp'=8,'fs'=4] {'fs'}, dimensions={0}, use_global_device_ids=true | all-gather | bytes 655360 | tf_op jit(solution)/shard_map/all_gather | solution.py:109
  166.5 24.1 %all_gather.99 = bf16[768,512]{1,0:T(8,128)(2,1)} all-gather(bf16[96,512]{1,0:T(8,128)(2,1)S(1)} %fusion.107), channel_id=1, replica_groups=mesh['sp'=8,'fs'=4] {'sp'}, dimensions={0}, use_global_device_ids=true | all-gather | bytes 884736 | tf_op jit(solution)/shard_map/all_gather | solution.py:287
  190.6 2.3 copy.110
  193.3 25.9 %while.65 = (s32[]{:T(128)}, f32[8,384]{1,0:T(8,128)S(1)}, f32[8,384]{1,0:T(8,128)S(1)}, f32[384,8,32]{0,2,1:T(8,128)}, s32[2]{0:T(128)S(1)}, /*index=5*/s32[]{:...) while((s32[]{:T(128)}, f32[8,384]{1,0:T(8,128)S(1)}, ...), condition=%wide.region_17.18_spmd.clone, body=%wide.region_14.17_spmd.clone.sunk | while | flops 166650624 | bytes 35391236 | solution.py:87
  196.9 3.4 bitcast_reduce_fusion.5
  200.4 4.5 fusion.339
  209.8 3.4 bitcast_reduce_fusion.5
  213.3 4.6 fusion.339
  221.0 5.1 multiply_convert_fusion.3
  226.1 5.6 multiply_convert_fusion.2
  232.0 3.5 fusion.178
  249.0 29.1 %while.66 = (s32[]{:T(128)}, f32[384,8,32]{0,2,1:T(8,128)}, f32[2,384,512]{2,1,0:T(8,128)}, s32[2]{0:T(128)S(1)}, bf16[768,512]{0,1:T(8,128)(2,1)}, /*index=5*/s...) while((s32[]{:T(128)}, f32[384,8,32]{0,2,1:T(8,128)}, ...), condition=%wide.region_23.24_spmd.clone, body=%wide.region_22.23_spmd.clone.sunk | while | flops 389880576 | bytes 34642128 | solution.py:373
  253.4 2.7 multiply_convert_fusion.8
  260.1 2.1 constant_dynamic-update-slice_fusion.4
  267.9 2.7 multiply_convert_fusion.8
  274.7 2.1 constant_dynamic-update-slice_fusion.4
  282.4 2.7 fusion.108
  287.1 29.3 %while.67 = (s32[]{:T(128)}, f32[384,8,32]{0,2,1:T(8,128)}, f32[2,384,512]{2,1,0:T(8,128)}, s32[2]{0:T(128)S(1)}, bf16[768,512]{0,1:T(8,128)(2,1)}, /*index=5*/s...) while((s32[]{:T(128)}, f32[384,8,32]{0,2,1:T(8,128)}, ...), condition=%wide.region_32.33_spmd.clone, body=%wide.region_31.32_spmd.clone.sunk | while | flops 389880576 | bytes 32872488 | solution.py:373
  291.7 2.7 multiply_convert_fusion.9
  306.3 2.7 multiply_convert_fusion.9
  313.0 2.1 constant_dynamic-update-slice_fusion.5
  319.6 2.7 convolution_convert_fusion.3
  335.4 21.2 %reduce-scatter.35.cloned.1.call-done = bf16[64,1024]{1,0:T(8,128)(2,1)} async-done(((bf16[256,1024]{1,0:T(8,128)(2,1)}), bf16[64,1024]{1,0:T(8,128)(2,1)}) %reduce-scatter.35.cloned.1.call-update) | async-done | bytes 131088 | tf_op jit(solution)/shard_map/reduce_scatter | solution.py:158
  356.6 22.6 %reduce-scatter.37.cloned.1.call-done = bf16[64,1024]{1,0:T(8,128)(2,1)} async-done(((bf16[256,1024]{1,0:T(8,128)(2,1)}), bf16[64,1024]{1,0:T(8,128)(2,1)}) %reduce-scatter.37.cloned.1.call-update) | async-done | bytes 131088 | tf_op jit(solution)/shard_map/reduce_scatter | solution.py:158
  380.9 20.6 %reduce-scatter.39.cloned.1.call-done = bf16[256,256]{1,0:T(8,128)(2,1)} async-done(((bf16[1024,256]{1,0:T(8,128)(2,1)}), bf16[256,256]{1,0:T(8,128)(2,1)}) %reduce-scatter.39.cloned.1.call-update) | async-done | bytes 131088 | tf_op jit(solution)/shard_map/reduce_scatter | solution.py:164
  401.5 22.3 %reduce-scatter.41.cloned.1.call-done = bf16[256,256]{1,0:T(8,128)(2,1)} async-done(((bf16[1024,256]{1,0:T(8,128)(2,1)}), bf16[256,256]{1,0:T(8,128)(2,1)}) %reduce-scatter.41.cloned.1.call-update) | async-done | bytes 131088 | tf_op jit(solution)/shard_map/reduce_scatter | solution.py:164
  425.5 42.2 %reduce-scatter.15.cloned.1.call-done = f32[96,512]{1,0:T(8,128)} async-done(((f32[768,512]{1,0:T(8,128)}), f32[96,512]{1,0:T(8,128)}) %reduce-scatter.15.cloned.1.call-update) | async-done | bytes 196624 | tf_op jit(solution)/shard_map/reduce_scatter | solution.py:379
  469.8 39.5 %reduce-scatter.17.cloned.1.call-done = f32[96,512]{1,0:T(8,128)} async-done(((f32[768,512]{1,0:T(8,128)}), f32[96,512]{1,0:T(8,128)}) %reduce-scatter.17.cloned.1.call-update) | async-done | bytes 196624 | tf_op jit(solution)/shard_map/reduce_scatter | solution.py:379
  522.5 12.7 %all-reduce.38 = (bf16[256]{0:T(256)(128)(2,1)S(1)}, bf16[256]{0:T(256)(128)(2,1)S(1)}, bf16[256]{0:T(256)(128)(2,1)S(1)}, bf16[256]{0:T(256)(128)(2,1)S(1)}, bf...) all-reduce(bf16[256]{0:T(256)(128)(2,1)} %copy-done.148, ...), channel_id=1, replica_groups=mesh['sp'=8,'fs'=4] {'fs'}, use_global_device_ids=true, to_apply=%add.11 | all-reduce | flops 7936 | bytes 31744
  536.1 16.1 %all-reduce.36 = (f32[64]{0:T(128)}, f32[64]{0:T(128)}, f32[64]{0:T(128)}, f32[64]{0:T(128)}, f32[64]{0:T(128)}, /*index=5*/f32[64]{0:T(128)}, f32[64]{0:T(128)}...) all-reduce(f32[64]{0:T(128)S(1)} %fusion.144, ...), channel_id=1, replica_groups=mesh['sp'=8,'fs'=4] {'sp'}, use_global_device_ids=true, to_apply=%region_40.41 | all-reduce | flops 960 | bytes 7680 | tf_op jit(solution)/shard_map/psum | solution.py:171
  552.2 2.3 fusion.100
  557.3 13.7 %reduce-scatter.23.cloned.1.call-done = bf16[256,256]{1,0:T(8,128)(2,1)} async-done(((bf16[1024,256]{1,0:T(8,128)(2,1)}), bf16[256,256]{1,0:T(8,128)(2,1)}) %reduce-scatter.23.cloned.1.call-update) | async-done | bytes 131088 | tf_op jit(solution)/shard_map/reduce_scatter | solution.py:128
  571.0 22.7 %reduce-scatter.25.cloned.1.call-done = bf16[256,256]{1,0:T(8,128)(2,1)} async-done(((bf16[1024,256]{1,0:T(8,128)(2,1)}), bf16[256,256]{1,0:T(8,128)(2,1)}) %reduce-scatter.25.cloned.1.call-update) | async-done | bytes 131088 | tf_op jit(solution)/shard_map/reduce_scatter | solution.py:128
  598.8 59.4 %all-reduce.42.cloned.1.call-done = (f32[64,256]{1,0:T(8,128)}, f32[256,256]{1,0:T(8,128)}, f32[64,512]{1,0:T(8,128)}, f32[64,256]{1,0:T(8,128)}, f32[64,1024]{1,0:T(8,128)}, /*index=5*/f32[256,256]{1,0:T(8,128)}) async-done(((f32[64,256]{1,0:T(8,128)}, f32[256,256]{1,0:T(8,128)}, f32[64,512]{1,0:T(8,128)}, f32[64,256]{1,0:T(8,128)}, f32[64,1024]{1,0:T(8,128)}, /*index=5*/f32[256,256]{1,0:T(8,128)}), ...) | async-done | bytes 1048592 | tf_op jit(solution)/shard_map/psum | solution.py:171
  (677 shorter events, 152.2 us)
Async XLA Ops:
  7.3 324.2 %reduce-scatter.31.cloned.1.call-start = ((), (), s32[]{:S(2)}) async-start(), calls=%async_computation.22 | async-start | bytes 163840 | tf_op jit(solution)/shard_map/reduce_scatter | solution.py:146
  11.6 77.8 %copy-start.70 = (f32[384]{0:T(512)}, f32[384]{0:T(512)S(1)}, u32[]{:S(2)}) copy-start(f32[384]{0:T(512)S(1)} %div.183) | copy-start | bytes 4612
  11.6 77.7 %copy-start.72 = (f32[384]{0:T(512)}, f32[384]{0:T(512)S(1)}, u32[]{:S(2)}) copy-start(f32[384]{0:T(512)S(1)} %div.193) | copy-start | bytes 4612
  27.4 62.0 %copy-start.80 = (f32[256]{0:T(256)}, f32[256]{0:T(256)S(1)}, u32[]{:S(2)}) copy-start(f32[256]{0:T(256)S(1)} %convert_element_type.527) | copy-start | bytes 3076
  27.4 62.0 %copy-start.121 = (f32[256]{0:T(256)}, f32[256]{0:T(256)S(1)}, u32[]{:S(2)}) copy-start(f32[256]{0:T(256)S(1)} %convert_element_type.528) | copy-start | bytes 3076
  42.8 122.8 %copy-start.10 = (bf16[1024,256]{1,0:T(8,128)(2,1)}, bf16[1024,256]{1,0:T(8,128)(2,1)S(1)}, u32[]{:S(2)}) copy-start(bf16[1024,256]{1,0:T(8,128)(2,1)S(1)} %all_gather.82) | copy-start | bytes 1572868
  43.1 34.4 %copy-start.24 = (f32[96,256]{1,0:T(8,128)}, f32[96,256]{1,0:T(8,128)S(1)}, u32[]{:S(2)}) copy-start(f32[96,256]{1,0:T(8,128)S(1)} %get-tuple-element.1119) | copy-start | bytes 294916
  43.1 34.4 %copy-start.113 = (f32[96]{0:T(128)}, f32[96]{0:T(128)S(1)}, u32[]{:S(2)}) copy-start(f32[96]{0:T(128)S(1)} %broadcast_multiply_fusion.5) | copy-start | bytes 1156
  43.3 34.2 %copy-start.144 = (f32[96]{0:T(128)}, f32[96]{0:T(128)S(1)}, u32[]{:S(2)}) copy-start(f32[96]{0:T(128)S(1)} %multiply_reduce_fusion.17) | copy-start | bytes 1156
  43.3 34.2 %copy-start.125 = (f32[96]{0:T(128)}, f32[96]{0:T(128)S(1)}, u32[]{:S(2)}) copy-start(f32[96]{0:T(128)S(1)} %fusion.147) | copy-start | bytes 1156
  43.4 122.9 %copy-start.83 = (f32[256]{0:T(256)}, f32[256]{0:T(256)S(1)}, u32[]{:S(2)}) copy-start(f32[256]{0:T(256)S(1)} %convert_element_type.533) | copy-start | bytes 3076
  43.4 122.9 %copy-start.111 = (f32[256]{0:T(256)}, f32[256]{0:T(256)S(1)}, u32[]{:S(2)}) copy-start(f32[256]{0:T(256)S(1)} %convert_element_type.534) | copy-start | bytes 3076
  43.4 34.9 %copy-start.89 = (bf16[64,256]{1,0:T(8,128)(2,1)S(1)}, bf16[64,256]{1,0:T(8,128)(2,1)}, u32[]{:S(2)}) copy-start(bf16[64,256]{1,0:T(8,128)(2,1)} %param.34) | copy-start | bytes 98308
  55.6 110.6 %copy-start.16 = (bf16[256,512]{1,0:T(8,128)(2,1)}, bf16[256,512]{1,0:T(8,128)(2,1)S(1)}, u32[]{:S(2)}) copy-start(bf16[256,512]{1,0:T(8,128)(2,1)S(1)} %all_gather.86) | copy-start | bytes 786436
  55.6 33.8 %copy-start.4 = (bf16[2,1,2,192,256]{4,3,2,1,0:T(8,128)(2,1)S(1)}, bf16[2,1,2,192,256]{4,3,2,1,0:T(8,128)(2,1)}, u32[]{:S(2)}) copy-start(bf16[2,1,2,192,256]{4,3,2,1,0:T(8,128)(2,1)} %param.29) | copy-start | bytes 1179652
  115.1 37.6 %copy-start.58 = (f32[8,384]{1,0:T(8,128)}, f32[8,384]{1,0:T(8,128)S(1)}, u32[]{:S(2)}) copy-start(f32[8,384]{1,0:T(8,128)S(1)} %get-tuple-element.539) | copy-start | bytes 36868
  115.2 37.4 %copy-start.150 = (pred[192]{0:T(512)(128)(4,1)S(1)}, pred[192]{0:T(512)(128)(4,1)}, u32[]{:S(2)}) copy-start(pred[192]{0:T(512)(128)(4,1)} %iota_compare_fusion.1) | copy-start | bytes 580
  127.6 112.3 %copy-start.12 = (f32[384,256]{1,0:T(8,128)}, f32[384,256]{1,0:T(8,128)S(1)}, u32[]{:S(2)}) copy-start(f32[384,256]{1,0:T(8,128)S(1)} %get-tuple-element.1121) | copy-start | bytes 1179652
  127.6 112.3 %copy-start.91 = (f32[384]{0:T(512)}, f32[384]{0:T(512)S(1)}, u32[]{:S(2)}) copy-start(f32[384]{0:T(512)S(1)} %broadcast_multiply_fusion.1) | copy-start | bytes 4612
  165.3 71.7 %copy-start.22 = (bf16[1024,256]{1,0:T(8,128)(2,1)}, bf16[1024,256]{1,0:T(8,128)(2,1)S(1)}, u32[]{:S(2)}) copy-start(bf16[1024,256]{1,0:T(8,128)(2,1)S(1)} %all_gather.97) | copy-start | bytes 1572868
  242.8 88.7 %reduce-scatter.33.cloned.1.call-start = ((), (), s32[]{:S(2)}) async-start(), calls=%async_computation.23 | async-start | bytes 163840 | tf_op jit(solution)/shard_map/reduce_scatter | solution.py:146
  245.5 87.4 %reduce-scatter.19.cloned.1.call-start = ((), (), s32[]{:S(2)}) async-start(), calls=%async_computation.16 | async-start | bytes 163840 | tf_op jit(solution)/shard_map/reduce_scatter | solution.py:122
  282.3 51.6 %reduce-scatter.21.cloned.1.call-start = ((), (), s32[]{:S(2)}) async-start(), calls=%async_computation.17 | async-start | bytes 163840 | tf_op jit(solution)/shard_map/reduce_scatter | solution.py:122
  319.5 37.1 %reduce-scatter.35.cloned.1.call-start = ((), (), s32[]{:S(2)}) async-start(), calls=%async_computation.24 | async-start | bytes 655360 | tf_op jit(solution)/shard_map/reduce_scatter | solution.py:158
  322.3 56.9 %reduce-scatter.37.cloned.1.call-start = ((), (), s32[]{:S(2)}) async-start(), calls=%async_computation.25 | async-start | bytes 655360 | tf_op jit(solution)/shard_map/reduce_scatter | solution.py:158
  323.8 77.7 %reduce-scatter.39.cloned.1.call-start = ((), (), s32[]{:S(2)}) async-start(), calls=%async_computation.26 | async-start | bytes 655360 | tf_op jit(solution)/shard_map/reduce_scatter | solution.py:164
  325.2 98.6 %reduce-scatter.41.cloned.1.call-start = ((), (), s32[]{:S(2)}) async-start(), calls=%async_computation.27 | async-start | bytes 655360 | tf_op jit(solution)/shard_map/reduce_scatter | solution.py:164
  326.5 141.2 %reduce-scatter.15.cloned.1.call-start = ((), (), s32[]{:S(2)}) async-start(), calls=%async_computation.14 | async-start | bytes 1769472 | tf_op jit(solution)/shard_map/reduce_scatter | solution.py:379
  327.3 182.1 %reduce-scatter.17.cloned.1.call-start = ((), (), s32[]{:S(2)}) async-start(), calls=%async_computation.15 | async-start | bytes 1769472 | tf_op jit(solution)/shard_map/reduce_scatter | solution.py:379
  327.9 140.8 %copy-start.25 = (f32[96,256]{1,0:T(8,128)S(1)}, f32[96,256]{1,0:T(8,128)}, u32[]{:S(2)}) copy-start(f32[96,256]{1,0:T(8,128)} %copy-done.24) | copy-start | bytes 294916
  327.9 140.8 %copy-start.84 = (f32[256]{0:T(256)S(1)}, f32[256]{0:T(256)}, u32[]{:S(2)}) copy-start(f32[256]{0:T(256)} %copy-done.83) | copy-start | bytes 3076
  327.9 140.8 %copy-start.112 = (f32[256]{0:T(256)S(1)}, f32[256]{0:T(256)}, u32[]{:S(2)}) copy-start(f32[256]{0:T(256)} %copy-done.111) | copy-start | bytes 3076
  327.9 140.8 %copy-start.114 = (f32[96]{0:T(128)S(1)}, f32[96]{0:T(128)}, u32[]{:S(2)}) copy-start(f32[96]{0:T(128)} %copy-done.113) | copy-start | bytes 1156
  327.9 140.8 %copy-start.126 = (f32[96]{0:T(128)S(1)}, f32[96]{0:T(128)}, u32[]{:S(2)}) copy-start(f32[96]{0:T(128)} %copy-done.125) | copy-start | bytes 1156
  327.9 227.8 %reduce-scatter.27.cloned.1.call-start = ((), (), s32[]{:S(2)}) async-start(), calls=%async_computation.20 | async-start | bytes 327680 | tf_op jit(solution)/shard_map/reduce_scatter | solution.py:140
  330.7 48.5 %copy-start.148 = (bf16[256]{0:T(256)(128)(2,1)}, bf16[256]{0:T(256)(128)(2,1)S(1)}, u32[]{:S(2)}) copy-start(bf16[256]{0:T(256)(128)(2,1)S(1)} %dynamic-update-slice.10) | copy-start | bytes 1540
  330.7 179.6 %copy-start.17 = (bf16[256,512]{1,0:T(8,128)(2,1)S(1)}, bf16[256,512]{1,0:T(8,128)(2,1)}, u32[]{:S(2)}) copy-start(bf16[256,512]{1,0:T(8,128)(2,1)} %copy-done.16) | copy-start | bytes 786436
  331.5 179.0 %copy-start.27 = (f32[96,256]{1,0:T(8,128)S(1)}, f32[96,256]{1,0:T(8,128)}, u32[]{:S(2)}) copy-start(f32[96,256]{1,0:T(8,128)} %copy-done.26) | copy-start | bytes 294916
  331.5 179.0 %copy-start.116 = (f32[96]{0:T(128)S(1)}, f32[96]{0:T(128)}, u32[]{:S(2)}) copy-start(f32[96]{0:T(128)} %copy-done.115) | copy-start | bytes 1156
  331.5 179.0 %copy-start.128 = (f32[96]{0:T(128)S(1)}, f32[96]{0:T(128)}, u32[]{:S(2)}) copy-start(f32[96]{0:T(128)} %copy-done.127) | copy-start | bytes 1156
  380.9 130.4 %copy-start.147 = (f32[96]{0:T(128)S(1)}, f32[96]{0:T(128)}, u32[]{:S(2)}) copy-start(f32[96]{0:T(128)} %copy-done.146) | copy-start | bytes 1156
  380.9 130.4 %copy-start.145 = (f32[96]{0:T(128)S(1)}, f32[96]{0:T(128)}, u32[]{:S(2)}) copy-start(f32[96]{0:T(128)} %copy-done.144) | copy-start | bytes 1156
  468.7 43.5 %copy-start.11 = (bf16[1024,256]{1,0:T(8,128)(2,1)S(1)}, bf16[1024,256]{1,0:T(8,128)(2,1)}, u32[]{:S(2)}) copy-start(bf16[1024,256]{1,0:T(8,128)(2,1)} %copy-done.10) | copy-start | bytes 1572868
  469.8 85.9 %reduce-scatter.29.cloned.1.call-start = ((), (), s32[]{:S(2)}) async-start(), calls=%async_computation.21 | async-start | bytes 327680 | tf_op jit(solution)/shard_map/reduce_scatter | solution.py:140
  516.5 54.5 %reduce-scatter.23.cloned.1.call-start = ((), (), s32[]{:S(2)}) async-start(), calls=%async_computation.18 | async-start | bytes 655360 | tf_op jit(solution)/shard_map/reduce_scatter | solution.py:128
  519.8 74.0 %reduce-scatter.25.cloned.1.call-start = ((), (), s32[]{:S(2)}) async-start(), calls=%async_computation.19 | async-start | bytes 655360 | tf_op jit(solution)/shard_map/reduce_scatter | solution.py:128
  522.4 135.9 %all-reduce.42.cloned.1.call-start = ((), (), s32[]{:S(2)}) async-start(), calls=%async_computation.28 | async-start | bytes 2097152 | tf_op jit(solution)/shard_map/psum | solution.py:171
  555.7 39.7 %copy-start.52 = (f32[384,256]{1,0:T(8,128)S(1)}, f32[384,256]{1,0:T(8,128)}, u32[]{:S(2)}) copy-start(f32[384,256]{1,0:T(8,128)} %get-tuple-element.1088) | copy-start | bytes 1179652
  (154 other events, 1300.8 us)
Sparse Core Ops, SparseCore 0:
  242.9 14.2 reduce-scatter.30
  259.6 17.3 reduce-scatter.32
  282.4 14.2 reduce-scatter.18
  319.6 14.2 reduce-scatter.20
  336.1 20.4 reduce-scatter.34
  359.3 19.8 reduce-scatter.36
  381.5 19.9 reduce-scatter.38
  403.8 19.9 reduce-scatter.40
  427.1 40.6 reduce-scatter.14
  470.8 38.4 reduce-scatter.16
  512.2 15.3 reduce-scatter.26
  530.4 17.8 reduce-scatter.28
  550.6 20.4 reduce-scatter.22
  573.7 19.9 reduce-scatter.24
  599.1 59.1 all-reduce.41
where the time goes:
time: 686 us; the launch traced here: 674 us
  waiting for transfers between devices  267 us (39%)
  blocking collectives  159 us (23%)
  matrix products  104 us (15%)
  local copies, waits for them, and re-layouts  60.6 us (9%)
  other arithmetic  58.4 us (9%)
  between operations  18.3 us (3%)
    reduce_scatter x2, waiting for transfers between devices, on_device(): lax.psum_scatter(key_terms, 'sp', scatter_dimension=0, tiled=True)  81.7 us
    psum x1, waiting for transfers between devices, reduce_grads(): lax.psum((shares[0], shares[1], shares[2], shares[3], shares[4], shares[5...  59.4 us
    reduce_scatter x2, waiting for transfers between devices, reduce_grads(): lax.psum_scatter(grads[14].astype(jnp.bfloat16), 'fs', scatter_dimension=...  43.8 us
    all_gather x2, blocking collectives, on_device(): lax.all_gather(keyval, 'sp', axis=0, tiled=True)  43.4 us
    reduce_scatter x2, waiting for transfers between devices, reduce_grads(): lax.psum_scatter(grads[16].astype(jnp.bfloat16), 'fs', scatter_dimension=...  42.8 us
    reduce_scatter x2, waiting for transfers between devices, reduce_grads(): lax.psum_scatter(grads[4].astype(jnp.bfloat16), 'fs', scatter_dimension=0...  36.4 us
    unnamed x2, blocking collectives  20.5 us
    unnamed x342, local copies, waits for them, and re-layouts  19.7 us
  transfers between devices with their start and end apart: 15, of which 10 were waited for; matrix products, arithmetic and copies ran while one was open for 16% of the time, Pallas kernels for 0%

commit v1 on v0

v1 whole, which is shorter than its diff:
```python
import functools

import jax
import jax.numpy as jnp
from jax import lax
from jax.experimental import pallas as pl
from jax.experimental.pallas import tpu as pltpu
from jax.sharding import PartitionSpec as P

HEADS = 8
HDIM = 32
PAIRS = HEADS // 2
SCALE = HDIM ** (-0.5)
EXP_SCALE = SCALE * 1.4426950408889634
EPS = 1e-06
NEG = -1e30
KEY_BLOCK = 768
VMEM_LIMIT = 58 * 2**20

bf16 = jnp.bfloat16
f32 = jnp.float32

(
    FIRST_G,
    FIRST_B,
    QUERY_B,
    REDUCE_B,
    KEYS_G,
    KEYS_B,
    VALUE_B,
    OUTPUT_B,
    SECOND_G,
    SECOND_B,
    RETURN_B,
    HIDDEN_B,
) = range(12)
VECS = 16


def mm(left, right):
    return jnp.dot(left, right, preferred_element_type=f32)


def mm_tn(left, right):
    return lax.dot_general(left, right, (((0,), (0,)), ((), ())), preferred_element_type=f32)


def mm_nt(left, right):
    return lax.dot_general(left, right, (((1,), (1,)), ((), ())), preferred_element_type=f32)


def normalize(rows):
    mean = jnp.mean(rows, axis=-1, keepdims=True)
    centered = rows - mean
    var = jnp.mean(centered * centered, axis=-1, keepdims=True)
    rstd = lax.rsqrt(var + EPS)
    return centered * rstd, rstd


def normalize_back(grad, normal, rstd, gain):
    scaled = grad * gain
    mean_a = jnp.mean(scaled, axis=-1, keepdims=True)
    mean_b = jnp.mean(scaled * normal, axis=-1, keepdims=True)
    return (scaled - mean_a - normal * mean_b) * rstd


def token_mask(first_row, rows, cols, width, height, image_width):
    row_ids = lax.broadcasted_iota(jnp.int32, (rows, cols, width), 0) + first_row
    col_ids = lax.broadcasted_iota(jnp.int32, (rows, cols, width), 1)
    valid = (row_ids < height) & (col_ids < image_width)
    return jnp.where(valid, 1.0, 0.0).astype(f32).reshape(rows * cols, width)


def key_bias(rows, cols, width, height, image_width):
    row_ids = lax.broadcasted_iota(jnp.int32, (rows, cols, width), 0)
    col_ids = lax.broadcasted_iota(jnp.int32, (rows, cols, width), 1)
    valid = (2 * row_ids < height) & (2 * col_ids < image_width)
    return jnp.where(valid, 0.0, NEG).astype(f32).reshape(rows * cols, width)


def reduce_kernel(dims, sizes, tokens, own_w, own_v, *refs):
    n_fs, batches, row_dev, cols, dim = dims
    mine, other = refs[: n_fs - 1], refs[n_fs - 1 : 2 * n_fs - 2]
    normed_ref, patch_ref, reduced_ref, key_ref, weight_ref, vec_ref, wide = refs[2 * n_fs - 2 :]
    half = dim // 2
    tok = row_dev * cols
    half_cols = cols // 2
    key_dev = tok // 4
    fs = lax.axis_index("fs")
    sp = lax.axis_index("sp")
    is_low = sp % 2 == 0
    weight_ref[fs] = own_w[...]
    vec = own_v[...].astype(f32)
    for step in range(1, n_fs):
        a, b = mine[step - 1][...], other[step - 1][...]
        place = lax.rem(fs + n_fs - step, n_fs)
        weight_ref[place, :half] = jnp.where(is_low, a[:half], b[:half])
        weight_ref[place, half:] = jnp.where(is_low, b[:half], a[:half])
        vec = vec + a[half:].astype(f32)
    vec_ref[...] = vec
    for batch in range(batches):
        x = tokens[batch, 0].reshape(tok, dim).astype(f32)
        normal, _ = normalize(x)
        low = (normal * vec[FIRST_G : FIRST_G + 1] + vec[FIRST_B : FIRST_B + 1]).astype(bf16)
        normed_ref[batch * tok : (batch + 1) * tok] = low
        mask = token_mask(sp * row_dev, row_dev, cols, dim, sizes[batch, 0, 0], sizes[batch, 0, 1])
        masked = low.astype(f32) * mask
        for part in range(dim // 128):
            wide[part] = masked[:, part * 128 : (part + 1) * 128]
        for row in range(row_dev // 2):
            start = batch * key_dev + row * half_cols
            for offset in range(4):
                dr, dc = offset // 2, offset % 2
                for part in range(dim // 128):
                    piece = wide[part, pl.ds((2 * row + dr) * cols + dc, half_cols, stride=2), :]
                    lanes = slice(offset * dim + part * 128, offset * dim + (part + 1) * 128)
                    patch_ref[start : start + half_cols, lanes] = piece.astype(bf16)
    reduced = mm(patch_ref[...], weight_ref[...].reshape(4 * dim, dim)) + vec[REDUCE_B : REDUCE_B + 1]
    reduced_ref[...] = reduced
    normal, _ = normalize(reduced)
    key_ref[...] = (normal * vec[KEYS_G : KEYS_G + 1] + vec[KEYS_B : KEYS_B + 1]).astype(bf16)


def place_weights(place, lows, highs, wq, wkv, wo, wh, wr, shard):
    rows = pl.ds(pl.multiple_of(place * shard, shard), shard)
    dim = wq.shape[1]
    wq[rows, :] = lows[:shard]
    wkv[rows, :dim] = lows[shard : 2 * shard]
    wkv[rows, dim:] = lows[2 * shard : 3 * shard]
    wo[rows, :] = lows[3 * shard : 4 * shard]
    wh[rows, :dim] = lows[4 * shard : 5 * shard]
    wh[rows, dim : 2 * dim] = lows[5 * shard :]
    wh[rows, 2 * dim : 3 * dim] = highs[:shard]
    wh[rows, 3 * dim :] = highs[shard : 2 * shard]
    wr[pl.ds(pl.multiple_of(place * dim, dim), dim), :] = highs[2 * shard :]


def head_stack_t(values_t, pair, tok):
    both = jnp.concatenate([values_t, values_t], axis=1)
    head = lax.broadcasted_iota(jnp.int32, both.shape, 0) // HDIM
    want = 2 * pair + jnp.where(lax.broadcasted_iota(jnp.int32, both.shape, 1) >= tok, 1, 0)
    return jnp.where(head == want, both, jnp.zeros_like(both))


def head_stack(values, pair):
    head = lax.broadcasted_iota(jnp.int32, values.shape, 1) // HDIM
    zero = jnp.zeros_like(values)
    return jnp.concatenate(
        [jnp.where(head == 2 * pair, values, zero), jnp.where(head == 2 * pair + 1, values, zero)],
        axis=0,
    )


def split_pair(both, tok):
    return jnp.concatenate([both[:HDIM, :tok], both[HDIM:, tok:]], axis=0)


def main_kernel(dims, sizes, tokens, normed, keys_in, cotangent, vec_ref, own, mine, other, outs, scratch):
    n_fs, n_sp, batches, row_dev, cols, dim, hid = dims
    acts_ref, middle_ref, gnormed_ref, gkey_a, gkey_b, grad_a, grad_b, gvec_ref = outs
    (wq, wkv, wo, wh, wr, qs, kvs, attended, n2s, rstds, gmid, probs, stats, gatt, attf, gqs, dks, dvs) = (
        scratch
    )
    tok = row_dev * cols
    half_cols = cols // 2
    key_dev = tok // 4
    keys = n_sp * key_dev
    blocks = keys // KEY_BLOCK if keys > KEY_BLOCK else 1
    block = keys // blocks
    fs = lax.axis_index("fs")
    sp = lax.axis_index("sp")
    is_low = sp % 2 == 0
    shard = dim // n_fs

    own_q, own_kv, own_o, own_h, own_r = own
    first = pl.ds(pl.multiple_of(fs * shard, shard), shard)
    wq[first, :] = own_q[...]
    wkv[first, :] = own_kv[...]
    wo[first, :] = own_o[...]
    wh[first, :] = own_h[...]
    wr[pl.ds(pl.multiple_of(fs * dim, dim), dim), :] = own_r[...]
    for step in range(1, n_fs):
        a, b = mine[step - 1][...], other[step - 1][...]
        place = lax.rem(fs + n_fs - step, n_fs)
        place_weights(place, jnp.where(is_low, a, b), jnp.where(is_low, b, a), wq, wkv, wo, wh, wr, shard)

    def vec(index):
        return vec_ref[index : index + 1, :]

    masks = [
        token_mask(sp * row_dev, row_dev, cols, dim, sizes[b, 0, 0], sizes[b, 0, 1]) for b in range(batches)
    ]
    zero_row = jnp.zeros((1, dim), f32)
    lane = lax.broadcasted_iota(jnp.int32, (block, dim), 1)

    per_block = block // key_dev

    def key_piece(batch, piece):
        devices = slice(piece * per_block, (piece + 1) * per_block)
        return keys_in[devices, batch * key_dev : (batch + 1) * key_dev, :].reshape(block, dim)

    for batch in range(batches):
        rows = slice(batch * tok, (batch + 1) * tok)
        queries = (mm(normed[rows], wq[...]) + vec(QUERY_B)).astype(bf16)
        qs[rows] = queries
        queries_t = queries.T
        for piece in range(blocks):
            key_rows = key_piece(batch, piece)
            here = slice(piece * block, (piece + 1) * block)
            kvs[batch, here, :dim] = mm(key_rows, wkv[:, :dim]).astype(bf16)
            kvs[batch, here, dim:] = (mm(key_rows, wkv[:, dim:]) + vec(VALUE_B)).astype(bf16)
        height, image_width = sizes[batch, 0, 0], sizes[batch, 0, 1]

        def biased(index, lane_id, batch=batch, height=height, image_width=image_width):
            rows_in = block // half_cols
            row_ids = lax.broadcasted_iota(jnp.int32, (rows_in, half_cols, dim), 0) + index * rows_in
            col_ids = lax.broadcasted_iota(jnp.int32, (rows_in, half_cols, dim), 1)
            valid = (2 * row_ids < height) & (2 * col_ids < image_width)
            bias = jnp.where(valid, 0.0, NEG).astype(f32).reshape(block, dim)
            key_block = kvs[batch, pl.ds(index * block, block), :dim]
            return jnp.where(lane == lane_id, bias, key_block.astype(f32)).astype(bf16)

        def query_pair(pair, lane_id, queries_t=queries_t):
            stacked = head_stack_t(queries_t, pair, tok)
            row = lax.broadcasted_iota(jnp.int32, stacked.shape, 0)
            return jnp.where(row == lane_id, jnp.ones_like(stacked), stacked)

        if blocks == 1:
            key_high, key_low = biased(0, dim - 1), biased(0, 0)
            values_t = kvs[batch, :, dim:].T
            for pair in range(PAIRS):
                last = pair == PAIRS - 1
                scores = mm(key_low if last else key_high, query_pair(pair, 0 if last else dim - 1))
                top = jnp.max(scores, axis=0, keepdims=True)
                weights = jnp.exp2((scores - top) * EXP_SCALE)
                inverse = 1.0 / jnp.sum(weights, axis=0, keepdims=True)
                low = weights.astype(bf16)
                probs[batch, pair] = low
                stats[batch, pair, 0:1] = inverse
                mixed = mm(values_t[2 * HDIM * pair : 2 * HDIM * (pair + 1)], low) * inverse
                attf[batch, 2 * HDIM * pair : 2 * HDIM * (pair + 1)] = split_pair(mixed, tok)
        else:
            for pair in range(PAIRS):
                last = pair == PAIRS - 1
                lane_id = 0 if last else dim - 1
                stacked = query_pair(pair, lane_id)

                def find_top(index, top, stacked=stacked, lane_id=lane_id, biased=biased):
                    scores = mm(biased(index, lane_id), stacked)
                    return jnp.maximum(top, jnp.max(scores, axis=0, keepdims=True))

                top = lax.fori_loop(0, blocks, find_top, jnp.full((1, 2 * tok), NEG, f32))

                def add_block(index, carry, stacked=stacked, lane_id=lane_id, biased=biased, top=top, pair=pair, batch=batch):
                    total, mixed = carry
                    scores = mm(biased(index, lane_id), stacked)
                    weights = jnp.exp2((scores - top) * EXP_SCALE)
                    values = kvs[batch, pl.ds(index * block, block), dim:].T
                    mixed = mixed + mm(values[2 * HDIM * pair : 2 * HDIM * (pair + 1)], weights.astype(bf16))
                    return total + jnp.sum(weights, axis=0, keepdims=True), mixed

                total, mixed = lax.fori_loop(
                    0,
                    blocks,
                    add_block,
                    (jnp.zeros((1, 2 * tok), f32), jnp.zeros((2 * HDIM, 2 * tok), f32)),
                )
                inverse = 1.0 / total
                stats[batch, pair, 0:1] = inverse
                stats[batch, pair, 1:2] = top
                attf[batch, 2 * HDIM * pair : 2 * HDIM * (pair + 1)] = split_pair(mixed * inverse, tok)
        attended[rows] = attf[batch].T.astype(bf16)

    x = jnp.concatenate([tokens[b, 0].reshape(tok, dim).astype(f32) for b in range(batches)], axis=0)
    mask = jnp.concatenate(masks, axis=0)
    middle = x + mm(attended[...], wo[...]) + vec(OUTPUT_B)
    normal, rstd = normalize(middle)
    second = (normal * vec(SECOND_G) + vec(SECOND_B)).astype(bf16)
    grad_out = (
        jnp.concatenate([cotangent[b, 0].reshape(tok, dim) for b in range(batches)], axis=0) * mask
    )
    grad_mlp = grad_out.astype(bf16)
    total = middle + vec(RETURN_B)
    grad_second = jnp.zeros((batches * tok, dim), f32)
    low_rows = is_low

    def store(index, start, value):
        value = value.astype(bf16)
        rows = value.shape[0]
        half = 3 * dim // 2
        begin = start % half
        in_low = start < half
        keep = low_rows if in_low else jnp.logical_not(low_rows)

        @pl.when(keep)
        def _():
            grad_a[index, begin : begin + rows, :] = value

        @pl.when(jnp.logical_not(keep))
        def _():
            grad_b[index, begin : begin + rows, :] = value

    hidden_rows = []
    chunks = hid // dim
    for chunk in range(chunks):
        lanes = slice(chunk * dim, (chunk + 1) * dim)
        hidden = mm(second, wh[:, lanes]) + vec(HIDDEN_B + chunk)
        phi = 0.5 + 0.5 * lax.erf(hidden * 0.7071067811865476)
        density = 0.3989422804014327 * jnp.exp2(hidden * hidden * (-0.5 * 1.4426950408889634))
        activated = (hidden * phi).astype(bf16)
        total = total + mm(activated, wr[lanes, :])
        grad_activated = mm_nt(grad_mlp, wr[lanes, :])
        grad_hidden_wide = (phi + hidden * density) * grad_activated
        grad_hidden = grad_hidden_wide.astype(bf16)
        hidden_rows.append(jnp.sum(grad_hidden.astype(f32), axis=0, keepdims=True))
        grad_second = grad_second + mm_nt(grad_hidden, wh[:, lanes])
        grad_wr = mm_tn(activated, grad_mlp)
        store(chunk, 2 * dim, grad_wr[: dim])
        grad_wh = mm_tn(second, grad_hidden)
        for owner in range(n_fs):
            store(owner, 4 * shard + chunk * shard, grad_wh[owner * shard : (owner + 1) * shard])
    total = total * mask
    for batch in range(batches):
        acts_ref[batch, 0] = total[batch * tok : (batch + 1) * tok].reshape(row_dev, cols, dim)
    grad_middle = grad_out + normalize_back(grad_second, normal, rstd, vec(SECOND_G))
    middle_ref[...] = grad_middle
    grad_branch = grad_middle.astype(bf16)
    grad_wo = mm_tn(attended[...], grad_branch)
    for owner in range(n_fs):
        store(owner, 3 * shard, grad_wo[owner * shard : (owner + 1) * shard])
    gatt[...] = mm_nt(grad_branch, wo[...]).astype(bf16)
    bias_output = jnp.sum(grad_branch.astype(f32), axis=0, keepdims=True)
    gain_second = jnp.sum(grad_second * normal, axis=0, keepdims=True)
    bias_second = jnp.sum(grad_second, axis=0, keepdims=True)
    bias_return = jnp.sum(grad_mlp.astype(f32), axis=0, keepdims=True)

    bias_value = zero_row
    grad_wkv = [jnp.zeros((dim, dim), f32), jnp.zeros((dim, dim), f32)]
    for batch in range(batches):
        rows = slice(batch * tok, (batch + 1) * tok)
        queries = qs[rows]
        grad_att_t = gatt[rows].astype(f32).T
        product = grad_att_t * attf[batch]

        def pair_terms(pair, batch=batch, grad_att_t=grad_att_t, product=product):
            inverse = stats[batch, pair, 0:1]
            piece = product[2 * HDIM * pair : 2 * HDIM * (pair + 1)]
            delta = jnp.concatenate(
                [
                    jnp.sum(piece[:HDIM], axis=0, keepdims=True),
                    jnp.sum(piece[HDIM:], axis=0, keepdims=True),
                ],
                axis=1,
            )
            stacked = head_stack_t(grad_att_t, pair, tok) * inverse
            return delta * inverse, stacked.astype(bf16)

        if blocks == 1:
            keys_t = kvs[batch, :, :dim].T
            values = kvs[batch, :, dim:]
            grad_k = jnp.zeros((keys, dim), f32)
            grad_v = jnp.zeros((keys, dim), f32)
            for pair in range(PAIRS):
                delta, stacked = pair_terms(pair)
                low = probs[batch, pair]
                grad_probs = mm(values, stacked)
                grad_scores = (low.astype(f32) * (grad_probs - delta)).astype(bf16)
                gq = mm(keys_t[2 * HDIM * pair : 2 * HDIM * (pair + 1)], grad_scores)
                gqs[2 * HDIM * pair : 2 * HDIM * (pair + 1)] = split_pair(gq, tok)
                grad_k = grad_k + mm(grad_scores, head_stack(queries, pair))
                grad_v = grad_v + mm(low, stacked.T)
        else:
            dks[...] = jnp.zeros_like(dks)
            dvs[...] = jnp.zeros_like(dvs)
            queries_t = queries.T
            height, image_width = sizes[batch, 0, 0], sizes[batch, 0, 1]
            for pair in range(PAIRS):
                last = pair == PAIRS - 1
                lane_id = 0 if last else dim - 1
                delta, stacked = pair_terms(pair)
                stacked_n = stacked.T
                query_t = head_stack_t(queries_t, pair, tok)
                row = lax.broadcasted_iota(jnp.int32, query_t.shape, 0)
                query_t = jnp.where(row == lane_id, jnp.ones_like(query_t), query_t)
                query_n = head_stack(queries, pair)
                top = stats[batch, pair, 1:2]

                def back_block(index, gq, pair=pair, lane_id=lane_id, delta=delta, stacked=stacked, stacked_n=stacked_n, query_t=query_t, query_n=query_n, top=top, batch=batch, height=height, image_width=image_width):
                    here = pl.ds(index * block, block)
                    rows_in = block // half_cols
                    row_ids = lax.broadcasted_iota(jnp.int32, (rows_in, half_cols, dim), 0) + index * rows_in
                    col_ids = lax.broadcasted_iota(jnp.int32, (rows_in, half_cols, dim), 1)
                    valid = (2 * row_ids < height) & (2 * col_ids < image_width)
                    bias = jnp.where(valid, 0.0, NEG).astype(f32).reshape(block, dim)
                    key_block = kvs[batch, here, :dim]
                    masked = jnp.where(lane == lane_id, bias, key_block.astype(f32)).astype(bf16)
                    weights = jnp.exp2((mm(masked, query_t) - top) * EXP_SCALE)
                    grad_probs = mm(kvs[batch, here, dim:], stacked)
                    grad_scores = (weights * (grad_probs - delta)).astype(bf16)
                    keys_t = key_block.T[2 * HDIM * pair : 2 * HDIM * (pair + 1)]
                    dks[here, :] += mm(grad_scores, query_n)
                    dvs[here, :] += mm(weights.astype(bf16), stacked_n)
                    return gq + mm(keys_t, grad_scores)

                gq = lax.fori_loop(0, blocks, back_block, jnp.zeros((2 * HDIM, 2 * tok), f32))
                gqs[2 * HDIM * pair : 2 * HDIM * (pair + 1)] = split_pair(gq, tok)
        qs[rows] = (gqs[...].T * SCALE).astype(bf16)
        for piece in range(blocks):
            if blocks > 1:
                here = slice(piece * block, (piece + 1) * block)
                grad_k, grad_v = dks[here], dvs[here]
            grad_k = (grad_k * SCALE).astype(bf16)
            bias_value = bias_value + jnp.sum(grad_v, axis=0, keepdims=True)
            grad_v = grad_v.astype(bf16)
            key_rows = key_piece(batch, piece)
            grad_wkv[0] = grad_wkv[0] + mm_tn(key_rows, grad_k)
            grad_wkv[1] = grad_wkv[1] + mm_tn(key_rows, grad_v)
            grad_key = (mm_nt(grad_k, wkv[:, :dim]) + mm_nt(grad_v, wkv[:, dim:])).astype(bf16)
            here = slice(batch * key_dev, (batch + 1) * key_dev)
            if n_sp == 8:
                pairs = grad_key.reshape(n_sp // 2, 2, key_dev, dim)
                even, odd = pairs[:, 0], pairs[:, 1]
                gkey_a[:, here, :] = jnp.where(is_low, even, odd)
                gkey_b[:, here, :] = jnp.where(is_low, odd, even)
            else:
                devices = slice(piece * per_block, (piece + 1) * per_block)
                gkey_a[devices, here, :] = grad_key.reshape(per_block, key_dev, dim)
    grad_queries = qs[...]
    gnormed_ref[...] = mm_nt(grad_queries, wq[...])
    grad_wq = mm_tn(normed[...], grad_queries)
    for owner in range(n_fs):
        part = slice(owner * shard, (owner + 1) * shard)
        store(owner, 0, grad_wq[part])
        store(owner, shard, grad_wkv[0][part])
        store(owner, 2 * shard, grad_wkv[1][part])
    bias_query = jnp.sum(grad_queries.astype(f32), axis=0, keepdims=True)
    gvec_ref[...] = jnp.zeros_like(gvec_ref)
    for index, value in (
        (QUERY_B, bias_query),
        (VALUE_B, bias_value),
        (OUTPUT_B, bias_output),
        (SECOND_G, gain_second),
        (SECOND_B, bias_second),
        (RETURN_B, bias_return),
    ):
        gvec_ref[index : index + 1, :] = value
    for chunk in range(chunks):
        gvec_ref[HIDDEN_B + chunk : HIDDEN_B + chunk + 1, :] = hidden_rows[chunk]


def main_entry(dims, n_outs, n_scratch, *refs):
    n_fs = dims[0]
    sizes, tokens, normed, keys_in, cotangent, vec_ref = refs[:6]
    own = refs[6:11]
    mine = refs[11 : 11 + n_fs - 1]
    other = refs[11 + n_fs - 1 : 11 + 2 * n_fs - 2]
    outs = refs[11 + 2 * n_fs - 2 : 11 + 2 * n_fs - 2 + n_outs]
    scratch = refs[11 + 2 * n_fs - 2 + n_outs :]
    main_kernel(dims, sizes, tokens, normed, keys_in, cotangent, vec_ref, own, mine, other, outs, scratch)


def input_kernel(dims, sizes, tokens, middle, gnormed, patches, reduced, weight, vec_ref, gvec, *refs):
    n_fs, batches, row_dev, cols, dim, n_parts = dims
    parts = refs[:n_parts]
    grad_ref, keep_ref, send_ref, wide = refs[n_parts:]
    tok = row_dev * cols
    half_cols = cols // 2
    key_dev = tok // 4
    sp = lax.axis_index("sp")
    is_low = sp % 2 == 0
    half = dim // 2

    def vec(index):
        return vec_ref[index : index + 1, :]

    def part_sum():
        if n_parts == 1:
            total = parts[0][0].astype(f32)
            for index in range(1, parts[0].shape[0]):
                total = total + parts[0][index].astype(f32)
            return total
        total = parts[0][...].astype(f32)
        for part in parts[1:]:
            total = total + part[...].astype(f32)
        return total

    grad_key = part_sum()
    normal, rstd = normalize(reduced[...])
    grad_reduced = normalize_back(grad_key, normal, rstd, vec(KEYS_G))
    gain_keys = jnp.sum(grad_key * normal, axis=0, keepdims=True)
    bias_keys = jnp.sum(grad_key, axis=0, keepdims=True)
    grad_low = grad_reduced.astype(bf16)
    bias_reduce = jnp.sum(grad_low.astype(f32), axis=0, keepdims=True)
    gain_first = jnp.zeros((1, dim), f32)
    bias_first = jnp.zeros((1, dim), f32)
    for offset in range(4):
        grad_w = mm_tn(patches[:, offset * dim : (offset + 1) * dim], grad_low).astype(bf16)
        low, high = grad_w[:half], grad_w[half:]
        keep_ref[offset, :half] = jnp.where(is_low, low, high)
        send_ref[offset, :half] = jnp.where(is_low, high, low)
    for batch in range(batches):
        for offset in range(4):
            dr, dc = offset // 2, offset % 2
            back = mm_nt(grad_low[batch * key_dev : (batch + 1) * key_dev], weight[offset])
            for row in range(row_dev // 2):
                for part in range(dim // 128):
                    wide[part, pl.ds((2 * row + dr) * cols + dc, half_cols, stride=2), :] = back[
                        row * half_cols : (row + 1) * half_cols, part * 128 : (part + 1) * 128
                    ]
        mask = token_mask(sp * row_dev, row_dev, cols, dim, sizes[batch, 0, 0], sizes[batch, 0, 1])
        rows = slice(batch * tok, (batch + 1) * tok)
        spread = jnp.concatenate([wide[part] for part in range(dim // 128)], axis=1)
        grad_normed = gnormed[rows] + spread * mask
        x = tokens[batch, 0].reshape(tok, dim).astype(f32)
        normal, rstd = normalize(x)
        grad_x = middle[rows] + normalize_back(grad_normed, normal, rstd, vec(FIRST_G))
        grad_ref[batch, 0] = grad_x.reshape(row_dev, cols, dim)
        gain_first = gain_first + jnp.sum(grad_normed * normal, axis=0, keepdims=True)
        bias_first = bias_first + jnp.sum(grad_normed, axis=0, keepdims=True)
    index = lax.broadcasted_iota(jnp.int32, (VECS, dim), 0)
    vectors = gvec[...]
    for place, value in (
        (FIRST_G, gain_first),
        (FIRST_B, bias_first),
        (REDUCE_B, bias_reduce),
        (KEYS_G, gain_keys),
        (KEYS_B, bias_keys),
    ):
        vectors = jnp.where(index == place, value, vectors)
    vectors = vectors.astype(bf16)
    for owner in range(n_fs):
        keep_ref[owner, half:] = vectors
        send_ref[owner, half:] = vectors


def add_kernel(axis, n, keep, arrived, *outs):
    if axis == "fs":
        me = lax.axis_index("fs")
        places = [lax.rem(me + step, n) for step in range(n)]
    else:
        me = lax.axis_index("sp") // 2
        places = [me ^ step for step in range(n)]
    for place, out in zip(places, outs):
        out[...] = (keep[place].astype(f32) + arrived[place].astype(f32)).astype(out.dtype)


def add_chunks(axis, keep, arrived):
    n = keep.shape[0]
    shape = jax.ShapeDtypeStruct(keep.shape[1:], keep.dtype)
    return pl.pallas_call(
        functools.partial(add_kernel, axis, n),
        out_shape=[shape] * n,
        compiler_params=pltpu.CompilerParams(vmem_limit_bytes=VMEM_LIMIT),
    )(keep, arrived)


def final_kernel(dims, lo_a, hi_a, lo_b, hi_b, *outs):
    n_fs, dim = dims
    shard = dim // n_fs
    is_low = lax.axis_index("sp") % 2 == 0
    fs = lax.axis_index("fs")
    a, b = lo_a[...], hi_a[...]
    low = jnp.where(is_low, a, b).astype(f32)
    high = jnp.where(is_low, b, a).astype(f32)
    query_w, keyval_w, output_w, hidden_w, return_w, reduce_w, vectors = outs
    query_w[...] = low[:shard]
    keyval_w[:, :dim] = low[shard : 2 * shard]
    keyval_w[:, dim:] = low[2 * shard : 3 * shard]
    output_w[...] = low[3 * shard : 4 * shard]
    hidden_w[:, :dim] = low[4 * shard : 5 * shard]
    hidden_w[:, dim : 2 * dim] = low[5 * shard :]
    hidden_w[:, 2 * dim : 3 * dim] = high[:shard]
    hidden_w[:, 3 * dim :] = high[shard : 2 * shard]
    return_w[...] = high[2 * shard :]
    a, b = lo_b[...], hi_b[...]
    low = jnp.where(is_low, a, b).astype(f32)
    high = jnp.where(is_low, b, a).astype(f32)
    half = dim // 2
    reduce_w[:half] = low[:half]
    reduce_w[half:] = high[:half]
    vecs = low[half:]
    lane = lax.broadcasted_iota(jnp.int32, vecs.shape, 1)
    chosen = jnp.where(lane // shard == fs, vecs, 0.0)
    folded = chosen[:, :shard]
    for index in range(1, n_fs):
        folded = folded + chosen[:, index * shard : (index + 1) * shard]
    vectors[:, :shard] = folded
    row = lax.broadcasted_iota(jnp.int32, vecs.shape, 0)
    vectors[0:1, dim:] = jnp.sum(jnp.where(row == HIDDEN_B + fs, vecs, 0.0), axis=0, keepdims=True)


def rotate(value, n, step):
    return lax.ppermute(value, "fs", [(i, (i + step) % n) for i in range(n)])


def flip(value, n, bits):
    return lax.ppermute(value, "sp", [(i, i ^ bits) for i in range(n)])


def sum_over_rows(value, n_sp):
    bit = 2
    while bit < n_sp:
        if 2 * bit < n_sp:
            a, b, c = flip(value, n_sp, bit), flip(value, n_sp, 2 * bit), flip(value, n_sp, 3 * bit)
            value = (
                (value.astype(f32) + a.astype(f32)) + (b.astype(f32) + c.astype(f32))
            ).astype(value.dtype)
            bit = 4 * bit
        else:
            a = flip(value, n_sp, bit)
            value = (value.astype(f32) + a.astype(f32)).astype(value.dtype)
            bit = 2 * bit
    return value


def reduce_shards(keep, send, n_fs, n_sp):
    parts = add_chunks("fs", keep, flip(send, n_sp, 1))
    arrived = [rotate(parts[step], n_fs, step) for step in range(1, n_fs)]
    total = parts[0].astype(f32)
    for piece in arrived:
        total = total + piece.astype(f32)
    mine = sum_over_rows(total.astype(bf16), n_sp)
    return mine, flip(mine, n_sp, 1)


def on_device(
    n_fs,
    n_sp,
    tokens,
    cotangent,
    image_sizes,
    first_gain,
    first_bias,
    query_weight,
    query_bias,
    reduce_weight,
    reduce_bias,
    keys_gain,
    keys_bias,
    keyval_weight,
    value_bias,
    output_weight,
    output_bias,
    second_gain,
    second_bias,
    hidden_weight,
    hidden_bias,
    return_weight,
    return_bias,
):
    batches, _, row_dev, cols, dim = tokens.shape
    hid = hidden_weight.shape[1]
    tok = row_dev * cols
    key_dev = tok // 4
    keys = n_sp * key_dev
    shard = dim // n_fs
    half = dim // 2
    fs = lax.axis_index("fs")
    core = lax.axis_index("sp") % 2
    vmem = pl.BlockSpec(memory_space=pltpu.VMEM)
    smem = pl.BlockSpec(memory_space=pltpu.SMEM)
    params = pltpu.CompilerParams(vmem_limit_bytes=VMEM_LIMIT)

    def shape(*dims, dtype=bf16):
        return jax.ShapeDtypeStruct(dims, dtype)

    small = jnp.stack(
        [
            first_gain,
            first_bias,
            query_bias,
            reduce_bias,
            keys_gain,
            keys_bias,
            value_bias,
            output_bias,
            second_gain,
            second_bias,
            return_bias,
        ]
    )
    lane = jnp.arange(dim, dtype=jnp.int32)[None, :]
    small = jnp.where(lane // shard == fs, jnp.tile(small, (1, n_fs)), jnp.zeros((), bf16))
    row = jnp.arange(VECS - HIDDEN_B, dtype=jnp.int32)[:, None]
    wide = jnp.where(row == fs, hidden_bias[None, :], jnp.zeros((), bf16))
    own_vec = jnp.concatenate([small, wide], axis=0)

    first_half = jnp.concatenate(
        [lax.dynamic_slice_in_dim(reduce_weight, core * half, half, 0), own_vec], axis=0
    )
    mine_first = [rotate(first_half, n_fs, step) for step in range(1, n_fs)]
    other_first = [flip(piece, n_sp, 1) for piece in mine_first]

    packed = jnp.concatenate(
        [query_weight]
        + [keyval_weight[:, j * dim : (j + 1) * dim] for j in range(2)]
        + [output_weight]
        + [hidden_weight[:, j * dim : (j + 1) * dim] for j in range(hid // dim)]
        + [return_weight],
        axis=0,
    )
    second_half = lax.dynamic_slice_in_dim(packed, core * (3 * half), 3 * half, 0)
    mine_second = [rotate(second_half, n_fs, step) for step in range(1, n_fs)]
    other_second = [flip(piece, n_sp, 1) for piece in mine_second]

    normed, patches, reduced, key_low, whole_reduce, vec = pl.pallas_call(
        functools.partial(reduce_kernel, (n_fs, batches, row_dev, cols, dim)),
        out_shape=[
            shape(batches * tok, dim),
            shape(batches * key_dev, 4 * dim),
            shape(batches * key_dev, dim, dtype=f32),
            shape(batches * key_dev, dim),
            shape(n_fs, dim, dim),
            shape(VECS, dim, dtype=f32),
        ],
        in_specs=[smem] + [vmem] * (3 + 2 * (n_fs - 1)),
        out_specs=[vmem] * 6,
        scratch_shapes=[pltpu.VMEM((dim // 128, tok, 128), f32)],
        compiler_params=params,
    )(image_sizes, tokens, reduce_weight, own_vec, *mine_first, *other_first)

    keys_all = lax.all_gather(key_low, "sp")

    single = keys <= KEY_BLOCK
    split = n_sp == 8
    tiny = (8, 128)
    gkey_shapes = (
        [shape(n_sp // 2, batches * key_dev, dim)] * 2
        if split
        else [shape(n_sp, batches * key_dev, dim), shape(16, 128)]
    )
    out_shapes = (
        [
            shape(batches, 1, row_dev, cols, dim, dtype=f32),
            shape(batches * tok, dim, dtype=f32),
            shape(batches * tok, dim, dtype=f32),
        ]
        + gkey_shapes
        + [shape(n_fs, 3 * half, dim)] * 2
        + [shape(VECS, dim, dtype=f32)]
    )
    scratch = [
        pltpu.VMEM((dim, dim), bf16),
        pltpu.VMEM((dim, 2 * dim), bf16),
        pltpu.VMEM((dim, dim), bf16),
        pltpu.VMEM((dim, hid), bf16),
        pltpu.VMEM((hid, dim), bf16),
        pltpu.VMEM((batches * tok, dim), bf16),
        pltpu.VMEM((batches, keys, 2 * dim), bf16),
        pltpu.VMEM((batches * tok, dim), bf16),
        pltpu.VMEM(tiny, f32),
        pltpu.VMEM(tiny, f32),
        pltpu.VMEM(tiny, f32),
        pltpu.VMEM((batches, PAIRS, keys, 2 * tok) if single else (16, 128), bf16),
        pltpu.VMEM((batches, PAIRS, 8, 2 * tok), f32),
        pltpu.VMEM((batches * tok, dim), bf16),
        pltpu.VMEM((batches, dim, tok), f32),
        pltpu.VMEM((dim, tok), f32),
        pltpu.VMEM(tiny if single else (keys, dim), f32),
        pltpu.VMEM(tiny if single else (keys, dim), f32),
    ]
    n_in = 5 + 5 + 2 * (n_fs - 1)
    acts, middle, gnormed, gkey_keep, gkey_send, keep, send, gvec = pl.pallas_call(
        functools.partial(
            main_entry, (n_fs, n_sp, batches, row_dev, cols, dim, hid), len(out_shapes), len(scratch)
        ),
        out_shape=out_shapes,
        in_specs=[smem] + [vmem] * n_in,
        out_specs=[vmem] * len(out_shapes),
        scratch_shapes=scratch,
        compiler_params=params,
    )(
        image_sizes,
        tokens,
        normed,
        keys_all,
        cotangent,
        vec,
        query_weight,
        keyval_weight,
        output_weight,
        hidden_weight,
        return_weight,
        *mine_second,
        *other_second,
    )

    if split:
        pieces = add_chunks("sp", gkey_keep, flip(gkey_send, n_sp, 1))
        parts = [pieces[0]] + [flip(pieces[step], n_sp, 2 * step) for step in range(1, n_sp // 2)]
    else:
        parts = [lax.all_to_all(gkey_keep, "sp", 0, 0)]

    mine_a, other_a = reduce_shards(keep, send, n_fs, n_sp)

    grads, keep, send = pl.pallas_call(
        functools.partial(input_kernel, (n_fs, batches, row_dev, cols, dim, len(parts))),
        out_shape=[
            shape(batches, 1, row_dev, cols, dim, dtype=f32),
            shape(n_fs, half + VECS, dim),
            shape(n_fs, half + VECS, dim),
        ],
        in_specs=[smem] + [vmem] * (8 + len(parts)),
        out_specs=[vmem] * 3,
        scratch_shapes=[pltpu.VMEM((dim // 128, tok, 128), f32)],
        compiler_params=params,
    )(image_sizes, tokens, middle, gnormed, patches, reduced, whole_reduce, vec, gvec, *parts)

    mine_b, other_b = reduce_shards(keep, send, n_fs, n_sp)

    gquery, gkeyval, goutput, ghidden, greturn, greduce, gvecs = pl.pallas_call(
        functools.partial(final_kernel, (n_fs, dim)),
        out_shape=[
            shape(shard, dim, dtype=f32),
            shape(shard, 2 * dim, dtype=f32),
            shape(shard, dim, dtype=f32),
            shape(shard, hid, dtype=f32),
            shape(dim, dim, dtype=f32),
            shape(dim, dim, dtype=f32),
            shape(VECS, 2 * dim, dtype=f32),
        ],
        in_specs=[vmem] * 4,
        out_specs=[vmem] * 7,
        compiler_params=params,
    )(mine_a, other_a, mine_b, other_b)
    vectors = [gvecs[index, :shard] for index in range(HIDDEN_B)]
    return (
        acts,
        grads,
        vectors[FIRST_G],
        vectors[FIRST_B],
        gquery,
        vectors[QUERY_B],
        greduce,
        vectors[REDUCE_B],
        vectors[KEYS_G],
        vectors[KEYS_B],
        gkeyval,
        vectors[VALUE_B],
        goutput,
        vectors[OUTPUT_B],
        vectors[SECOND_G],
        vectors[SECOND_B],
        ghidden,
        gvecs[0, dim:],
        greturn,
        vectors[RETURN_B],
    )


def solution(mesh):
    vec, mat = P("fs"), P("fs", None)
    image = P(None, "fs", "sp", None, None)
    weights = (vec, vec, mat, vec, mat, vec, vec, vec, mat, vec, mat, vec, vec, vec, mat, vec, mat, vec)
    return jax.shard_map(
        functools.partial(on_device, mesh.shape["fs"], mesh.shape["sp"]),
        mesh=mesh,
        in_specs=(image, image, P(None, "fs", None)) + weights,
        out_specs=(image, image) + weights,
        check_vma=False,
    )
```

time: 686 us -> 151 us (0.22); the launches traced: 674 us -> 151 us
  waiting for transfers between devices: 267 us -> 45.9 us
  blocking collectives: 159 us -> 12.9 us
  matrix products: 104 us -> 0 us
  other arithmetic: 58.4 us -> 1 us
  local copies, waits for them, and re-layouts: 60.6 us -> 13.2 us
  Pallas kernels: 0 us -> 45.5 us
  starting transfers between devices: 0.83 us -> 31.2 us
  between operations: 18.3 us -> 1.26 us
    reduce_scatter x14 -> x0, waiting for transfers between devices: 206 us -> none  [the longest x2 81.7 us: on_device(): lax.psum_scatter(key_terms, 'sp', scatter_dimension=0, tiled=True)]
    all_gather x9 -> x1, blocking collectives: 122 us -> 12.9 us  [on_device(): keys_all = lax.all_gather(key_low, 'sp')]
    dot_general x64 -> x0, matrix products: 104 us -> none  [the longest x12 16.7 us: matmul(): return jnp.dot(left, right, preferred_element_type=jnp.float32)]
    psum x1 -> x0, waiting for transfers between devices: 59.4 us -> none  [reduce_grads(): lax.psum((shares[0], shares[1], shares[2], shares[3], shares[4], shares[5...]
    ppermute x0 -> x32, waiting for transfers between devices: none -> 45.9 us  [the longest x12 31.1 us: rotate(): return lax.ppermute(value, 'fs', [(i, (i + step) % n) for i in range(n)])]
    pallas_call x0 -> x7, Pallas kernels: none -> 45.5 us  [the longest x1 30.1 us: on_device(): pl.pallas_call(functools.partial(main_entry, (n_fs, n_sp, batches, row_de...]
    ppermute x0 -> x32, starting transfers between devices: none -> 31.2 us  [the longest x20 19.6 us: flip(): return lax.ppermute(value, 'sp', [(i, i ^ bits) for i in range(n)])]
    unnamed x2 -> x0, blocking collectives: 20.5 us -> none
  transfers between devices with their start and end apart: 15 -> 32, of which waited for: 10 -> 12; matrix products, arithmetic and copies ran while one was open for 16% -> 1% of each run, Pallas kernels for 0% -> 9%
where the time goes in v1:
time: 151 us
  waiting for transfers between devices  45.9 us (30%)
  Pallas kernels  45.5 us (30%)
  starting transfers between devices  31.2 us (21%)
  local copies, waits for them, and re-layouts  13.2 us (9%)
  blocking collectives  12.9 us (9%)
    ppermute x12, waiting for transfers between devices, rotate(): return lax.ppermute(value, 'fs', [(i, (i + step) % n) for i in range(n)])  31.1 us
    pallas_call x1, Pallas kernels, on_device(): pl.pallas_call(functools.partial(main_entry, (n_fs, n_sp, batches, row_de...  30.1 us
    ppermute x20, starting transfers between devices, flip(): return lax.ppermute(value, 'sp', [(i, i ^ bits) for i in range(n)])  19.6 us
    ppermute x20, waiting for transfers between devices, flip(): return lax.ppermute(value, 'sp', [(i, i ^ bits) for i in range(n)])  14.7 us
    all_gather x1, blocking collectives, on_device(): keys_all = lax.all_gather(key_low, 'sp')  12.9 us
    ppermute x12, starting transfers between devices, rotate(): return lax.ppermute(value, 'fs', [(i, (i + step) % n) for i in range(n)])  11.6 us
    unnamed x92, local copies, waits for them, and re-layouts  10.2 us
    pallas_call x3, Pallas kernels, add_chunks(): pl.pallas_call(functools.partial(add_kernel, axis, n), out_shape=[shape]...  6.06 us
  transfers between devices with their start and end apart: 32, of which 12 were waited for; matrix products, arithmetic and copies ran while one was open for 1% of the time, Pallas kernels for 9%

profile of v1, /device:TPU:9, one launch (start us, length us, event | category | flops | bytes accessed | tf_op | source)
XLA Modules:
  0.0 150.9 jit_solution(5872615424015840796)
XLA Ops:
  0.7 0.7 copy-done.17
  1.5 0.8 copy-done.2
  2.4 0.9 copy-done.3
  3.4 2.5 %collective-permute-start.7 = (bf16[384,256]{1,0:T(8,128)(2,1)S(1)}, bf16[384,256]{1,0:T(8,128)(2,1)S(1)}, u32[]{:S(2)}, u32[]{:S(2)}) collective-permute-start(bf16[384,256]{1,0:T(8,128)(2,1)S(1)} %constant_dynamic-slice_fusion), channel_id=1, source_target_pairs={{0,2},{1,3},{2,0},{3,1},{4,6},{5,7},{6,4},{7,5},{8,10},{9,11},{10,... | collective-permute-start | bytes 589832 | tf_op jit(solution)/shard_map/ppermute | solution.py:593
  5.8 2.2 %collective-permute-start.6 = (bf16[384,256]{1,0:T(8,128)(2,1)S(1)}, bf16[384,256]{1,0:T(8,128)(2,1)S(1)}, u32[]{:S(2)}, u32[]{:S(2)}) collective-permute-start(bf16[384,256]{1,0:T(8,128)(2,1)S(1)} %constant_dynamic-slice_fusion), channel_id=1, source_target_pairs={{0,1},{1,2},{2,3},{3,0},{4,5},{5,6},{6,7},{7,4},{8,9},{9,10},{10,1... | collective-permute-start | bytes 589832 | tf_op jit(solution)/shard_map/ppermute | solution.py:593
  9.0 0.7 copy-done.41
  9.9 1.2 collective-permute-start.1
  11.0 14.6 %collective-permute-done.2.refs_2_ = bf16[144,256]{1,0:T(8,128)(2,1)S(1)} collective-permute-done((bf16[144,256]{1,0:T(8,128)(2,1)S(1)}, bf16[144,256]{1,0:T(8,128)(2,1)S(1)}, u32[]{:S(2)}, u32[]{:S(2)}) %collective-permute-start.2) | collective-permute-done | bytes 73760 | tf_op jit(solution)/shard_map/ppermute | solution.py:593
  25.6 1.5 collective-permute-done.1.refs_1_
  27.1 2.1 %collective-permute-start.5 = (bf16[144,256]{1,0:T(8,128)(2,1)S(1)}, bf16[144,256]{1,0:T(8,128)(2,1)S(1)}, u32[]{:S(2)}, u32[]{:S(2)}) collective-permute-start(bf16[144,256]{1,0:T(8,128)(2,1)S(1)} %collective-permute-done.2.refs_2_), channel_id=1, source_target_pairs={{0,4},{4,0},{8,12},{12,8},{16,20},{20,16},{24,28},{28,24},{1,5},{5... | collective-permute-start | bytes 221192 | tf_op jit(solution)/shard_map/ppermute | solution.py:597
  29.2 4.0 %collective-permute-start.4 = (bf16[144,256]{1,0:T(8,128)(2,1)S(1)}, bf16[144,256]{1,0:T(8,128)(2,1)S(1)}, u32[]{:S(2)}, u32[]{:S(2)}) collective-permute-start(bf16[144,256]{1,0:T(8,128)(2,1)S(1)} %collective-permute-done.1.refs_1_), channel_id=1, source_target_pairs={{0,4},{4,0},{8,12},{12,8},{16,20},{20,16},{24,28},{28,24},{1,5},{5... | collective-permute-start | bytes 221192 | tf_op jit(solution)/shard_map/ppermute | solution.py:597
  35.5 0.6 copy-done.27
  36.1 3.0 %shard_map.356 = (bf16[768,256]{1,0:T(8,128)(2,1)}, bf16[192,1024]{1,0:T(8,128)(2,1)}, f32[192,256]{1,0:T(8,128)}, bf16[192,256]{1,0:T(8,128)(2,1)}, bf16[4,256,256]{2,1,0:T(8,128)(2,1)}, /*index=5*/f32[16,256]{1,0:T(8,128)}) custom-call(s32[2,1,2]{2,1,0:T(1,128)} %sizes.3, bf16[2,1,2,192,256]{4,3,2,1,0:T(8,128)(2,1)} %tokens.3, bf16[256,256]{1,0:T(8,128)(2,1)} %own_w.1, ...), custom_call_target="tpu_custom_call" | custom-call | tf_op jit(solution)/shard_map/pallas_call | solution.py:706
  39.1 12.9 %all-gather = bf16[1536,256]{1,0:T(8,128)(2,1)} all-gather(bf16[192,256]{1,0:T(8,128)(2,1)} %get-tuple-element.57), channel_id=2, replica_groups=mesh['sp'=8,'fs'=4] {'sp'}, dimensions={0}, use_global_device_ids=true | all-gather | bytes 884736 | tf_op jit(solution)/shard_map/all_gather | solution.py:722
  52.1 0.6 copy-done.12
  52.9 30.1 %shard_map.357 = (f32[2,1,2,192,256]{4,3,2,1,0:T(8,128)}, f32[768,256]{1,0:T(8,128)}, f32[768,256]{1,0:T(8,128)}, bf16[4,192,256]{2,1,0:T(8,128)(2,1)}, bf16[4,1...) custom-call(s32[2,1,2]{2,1,0:T(1,128)} %sizes.3, ...), custom_call_target="tpu_custom_call" | custom-call | tf_op jit(solution)/shard_map/pallas_call | solution.py:763
  83.6 2.5 %collective-permute-done.12.arrived = bf16[4,192,256]{2,1,0:T(8,128)(2,1)S(1)} collective-permute-done((bf16[4,192,256]{2,1,0:T(8,128)(2,1)}, bf16[4,192,256]{2,1,0:T(8,128)(2,1)S(1)}, u32[]{:S(2)}, u32[]{:S(2)}) %collective-permute-start.12) | collective-permute-done | bytes 393248 | tf_op jit(solution)/shard_map/ppermute | solution.py:597
  86.1 0.7 copy-done.4
  86.9 1.9 %shard_map.358 = (bf16[192,256]{1,0:T(8,128)(2,1)}, bf16[192,256]{1,0:T(8,128)(2,1)}, bf16[192,256]{1,0:T(8,128)(2,1)}, bf16[192,256]{1,0:T(8,128)(2,1)}) custom-call(bf16[4,192,256]{2,1,0:T(8,128)(2,1)} %get-tuple-element.66.keep, bf16[4,192,256]{2,1,0:T(8,128)(2,1)} %copy-done.4), custom_call_target="tpu_custom_call" | custom-call | tf_op jit(solution)/shard_map/pallas_call | solution.py:550
  89.0 1.2 collective-permute-start.14
  90.2 1.2 collective-permute-start.15
  91.4 1.8 %collective-permute-done.13.refs_1_ = bf16[192,256]{1,0:T(8,128)(2,1)S(1)} collective-permute-done((bf16[192,256]{1,0:T(8,128)(2,1)}, bf16[192,256]{1,0:T(8,128)(2,1)S(1)}, u32[]{:S(2)}, u32[]{:S(2)}) %collective-permute-start.13) | collective-permute-done | bytes 98336 | tf_op jit(solution)/shard_map/ppermute | solution.py:597
  93.2 1.6 %collective-permute-done.15.refs_3_ = bf16[192,256]{1,0:T(8,128)(2,1)S(1)} collective-permute-done((bf16[192,256]{1,0:T(8,128)(2,1)}, bf16[192,256]{1,0:T(8,128)(2,1)S(1)}, u32[]{:S(2)}, u32[]{:S(2)}) %collective-permute-start.15) | collective-permute-done | bytes 98336 | tf_op jit(solution)/shard_map/ppermute | solution.py:597
  95.4 4.2 %shard_map.359 = (f32[2,1,2,192,256]{4,3,2,1,0:T(8,128)}, bf16[4,144,256]{2,1,0:T(8,128)(2,1)}, bf16[4,144,256]{2,1,0:T(8,128)(2,1)}) custom-call(s32[2,1,2]{2,1,0:T(1,128)} %sizes.3, bf16[2,1,2,192,256]{4,3,2,1,0:T(8,128)(2,1)} %tokens.3, f32[768,256]{1,0:T(8,128)} %get-tuple-element.60.middle, f32[768,256]{1,0:T(8,128)} %get-tuple-element.61.gnormed, ...), custom_call_target="tpu_custom_call" | custom-call | tf_op jit(solution)/shard_map/pallas_call | solution.py:796
  99.6 1.9 %collective-permute-start.24 = (bf16[4,144,256]{2,1,0:T(8,128)(2,1)}, bf16[4,144,256]{2,1,0:T(8,128)(2,1)S(1)}, u32[]{:S(2)}, u32[]{:S(2)}) collective-permute-start(bf16[4,144,256]{2,1,0:T(8,128)(2,1)} %get-tuple-element.80), channel_id=1, source_target_pairs={{0,4},{4,0},{8,12},{12,8},{16,20},{20,16},{24,28},{28,24},{1,5},{5... | collective-permute-start | bytes 884744 | tf_op jit(solution)/shard_map/ppermute | solution.py:597
  101.5 0.9 copy-done
  102.5 2.4 %shard_map.360 = (bf16[384,256]{1,0:T(8,128)(2,1)}, bf16[384,256]{1,0:T(8,128)(2,1)}, bf16[384,256]{1,0:T(8,128)(2,1)}, bf16[384,256]{1,0:T(8,128)(2,1)}) custom-call(bf16[4,384,256]{2,1,0:T(8,128)(2,1)} %get-tuple-element.73.keep, bf16[4,384,256]{2,1,0:T(8,128)(2,1)} %copy-done), custom_call_target="tpu_custom_call" | custom-call | tf_op jit(solution)/shard_map/pallas_call | solution.py:550
  104.8 1.4 collective-permute-start.18
  106.3 0.7 copy-done.6
  107.0 1.8 %shard_map.361 = (bf16[144,256]{1,0:T(8,128)(2,1)}, bf16[144,256]{1,0:T(8,128)(2,1)}, bf16[144,256]{1,0:T(8,128)(2,1)}, bf16[144,256]{1,0:T(8,128)(2,1)}) custom-call(bf16[4,144,256]{2,1,0:T(8,128)(2,1)} %get-tuple-element.79.keep, bf16[4,144,256]{2,1,0:T(8,128)(2,1)} %copy-done.6), custom_call_target="tpu_custom_call" | custom-call | tf_op jit(solution)/shard_map/pallas_call | solution.py:550
  108.8 1.4 collective-permute-start.25
  110.3 2.7 %collective-permute-start.26 = (bf16[144,256]{1,0:T(8,128)(2,1)}, bf16[144,256]{1,0:T(8,128)(2,1)S(1)}, u32[]{:S(2)}, u32[]{:S(2)}) collective-permute-start(bf16[144,256]{1,0:T(8,128)(2,1)} %get-tuple-element.83), channel_id=1, source_target_pairs={{0,2},{1,3},{2,0},{3,1},{4,6},{5,7},{6,4},{7,5},{8,10},{9,11},{10,... | collective-permute-start | bytes 221192 | tf_op jit(solution)/shard_map/ppermute | solution.py:593
  113.0 12.4 %collective-permute-done.18 = bf16[384,256]{1,0:T(8,128)(2,1)S(1)} collective-permute-done((bf16[384,256]{1,0:T(8,128)(2,1)}, bf16[384,256]{1,0:T(8,128)(2,1)S(1)}, u32[]{:S(2)}, u32[]{:S(2)}) %collective-permute-start.18) | collective-permute-done | bytes 196640 | tf_op jit(solution)/shard_map/ppermute | solution.py:593
  125.5 2.3 %collective-permute-done.19 = bf16[384,256]{1,0:T(8,128)(2,1)S(1)} collective-permute-done((bf16[384,256]{1,0:T(8,128)(2,1)}, bf16[384,256]{1,0:T(8,128)(2,1)S(1)}, u32[]{:S(2)}, u32[]{:S(2)}) %collective-permute-start.19) | collective-permute-done | bytes 196640 | tf_op jit(solution)/shard_map/ppermute | solution.py:593
  127.8 1.3 collective-permute-start.22
  129.1 1.1 collective-permute-start.21
  130.9 1.3 collective-permute-start.30
  132.2 1.1 collective-permute-start.29
  133.3 1.5 %collective-permute-done.22 = bf16[384,256]{1,0:T(8,128)(2,1)S(1)} collective-permute-done((bf16[384,256]{1,0:T(8,128)(2,1)S(1)}, bf16[384,256]{1,0:T(8,128)(2,1)S(1)}, u32[]{:S(2)}, u32[]{:S(2)}) %collective-permute-start.22) | collective-permute-done | bytes 196640 | tf_op jit(solution)/shard_map/ppermute | solution.py:597
  134.8 1.1 collective-permute-start.28
  135.9 4.8 %collective-permute-done.21 = bf16[384,256]{1,0:T(8,128)(2,1)S(1)} collective-permute-done((bf16[384,256]{1,0:T(8,128)(2,1)S(1)}, bf16[384,256]{1,0:T(8,128)(2,1)S(1)}, u32[]{:S(2)}, u32[]{:S(2)}) %collective-permute-start.21) | collective-permute-done | bytes 196640 | tf_op jit(solution)/shard_map/ppermute | solution.py:597
  140.8 0.7 collective-permute-start.23
  141.4 1.6 %collective-permute-done.29 = bf16[144,256]{1,0:T(8,128)(2,1)S(1)} collective-permute-done((bf16[144,256]{1,0:T(8,128)(2,1)S(1)}, bf16[144,256]{1,0:T(8,128)(2,1)S(1)}, u32[]{:S(2)}, u32[]{:S(2)}) %collective-permute-start.29) | collective-permute-done | bytes 73760 | tf_op jit(solution)/shard_map/ppermute | solution.py:597
  143.6 0.9 collective-permute-done.31.hi_b
  145.2 0.7 copy-done.15
  145.8 2.1 %shard_map.362 = (f32[64,256]{1,0:T(8,128)}, f32[64,512]{1,0:T(8,128)}, f32[64,256]{1,0:T(8,128)}, f32[64,1024]{1,0:T(8,128)}, f32[256,256]{1,0:T(8,128)}, /*index=5*/f32[256,256]{1,0:T(8,128)}, f32[16,512]{1,0:T(8,128)}) custom-call(bf16[384,256]{1,0:T(8,128)(2,1)} %copy-done.1, bf16[384,256]{1,0:T(8,128)(2,1)} %copy-done.15, bf16[144,256]{1,0:T(8,128)(2,1)} %copy-done.7, ...), custom_call_target="tpu_custom_call" | custom-call | tf_op jit(solution)/shard_map/pallas_call | solution.py:811
  147.9 1.3 slice.70
  149.2 1.5 %slice_bitcast_fusion = (f32[64]{0:T(128)}, f32[64]{0:T(128)}, f32[64]{0:T(128)}, f32[64]{0:T(128)}, f32[64]{0:T(128)}, /*index=5*/f32[64]{0:T(128)}, f32[64]{0:...) fusion(f32[16,512]{1,0:T(8,128)} %get-tuple-element.85), kind=kLoop, calls=%fused_computation.22 | loop fusion | bytes 5632 | tf_op jit(solution)/shard_map/squeeze | solution.py:826
  (134 shorter events, 7.5 us)
Async XLA Ops:
  1.4 0.9 copy-start.2
  3.2 6.5 %copy-start.5 = (bf16[256,256]{1,0:T(8,128)(2,1)S(1)}, bf16[256,256]{1,0:T(8,128)(2,1)}, u32[]{:S(2)}) copy-start(bf16[256,256]{1,0:T(8,128)(2,1)} %own_w.1) | copy-start | bytes 393220
  3.3 30.0 %collective-permute-start.8 = (bf16[384,256]{1,0:T(8,128)(2,1)S(1)}, bf16[384,256]{1,0:T(8,128)(2,1)S(1)}, u32[]{:S(2)}, u32[]{:S(2)}) collective-permute-start(bf16[384,256]{1,0:T(8,128)(2,1)S(1)} %constant_dynamic-slice_fusion), channel_id=1, source_target_pairs={{0,3},{1,0},{2,1},{3,2},{4,7},{5,4},{6,5},{7,6},{8,11},{9,8},{10,9... | collective-permute-start | bytes 589832 | tf_op jit(solution)/shard_map/ppermute | solution.py:593
  3.4 30.4 %collective-permute-start.7 = (bf16[384,256]{1,0:T(8,128)(2,1)S(1)}, bf16[384,256]{1,0:T(8,128)(2,1)S(1)}, u32[]{:S(2)}, u32[]{:S(2)}) collective-permute-start(bf16[384,256]{1,0:T(8,128)(2,1)S(1)} %constant_dynamic-slice_fusion), channel_id=1, source_target_pairs={{0,2},{1,3},{2,0},{3,1},{4,6},{5,7},{6,4},{7,5},{8,10},{9,11},{10,... | collective-permute-start | bytes 589832 | tf_op jit(solution)/shard_map/ppermute | solution.py:593
  5.8 28.0 %collective-permute-start.6 = (bf16[384,256]{1,0:T(8,128)(2,1)S(1)}, bf16[384,256]{1,0:T(8,128)(2,1)S(1)}, u32[]{:S(2)}, u32[]{:S(2)}) collective-permute-start(bf16[384,256]{1,0:T(8,128)(2,1)S(1)} %constant_dynamic-slice_fusion), channel_id=1, source_target_pairs={{0,1},{1,2},{2,3},{3,0},{4,5},{5,6},{6,7},{7,4},{8,9},{9,10},{10,1... | collective-permute-start | bytes 589832 | tf_op jit(solution)/shard_map/ppermute | solution.py:593
  9.8 15.8 %collective-permute-start.2 = (bf16[144,256]{1,0:T(8,128)(2,1)S(1)}, bf16[144,256]{1,0:T(8,128)(2,1)S(1)}, u32[]{:S(2)}, u32[]{:S(2)}) collective-permute-start(bf16[144,256]{1,0:T(8,128)(2,1)S(1)} %pad_maximum_fusion), channel_id=1, source_target_pairs={{0,3},{1,0},{2,1},{3,2},{4,7},{5,4},{6,5},{7,6},{8,11},{9,8},{10,9... | collective-permute-start | bytes 221192 | tf_op jit(solution)/shard_map/ppermute | solution.py:593
  9.9 17.2 %collective-permute-start.1 = (bf16[144,256]{1,0:T(8,128)(2,1)S(1)}, bf16[144,256]{1,0:T(8,128)(2,1)S(1)}, u32[]{:S(2)}, u32[]{:S(2)}) collective-permute-start(bf16[144,256]{1,0:T(8,128)(2,1)S(1)} %pad_maximum_fusion), channel_id=1, source_target_pairs={{0,2},{1,3},{2,0},{3,1},{4,6},{5,7},{6,4},{7,5},{8,10},{9,11},{10,... | collective-permute-start | bytes 221192 | tf_op jit(solution)/shard_map/ppermute | solution.py:593
  25.6 9.2 %copy-start.22 = (bf16[144,256]{1,0:T(8,128)(2,1)}, bf16[144,256]{1,0:T(8,128)(2,1)S(1)}, u32[]{:S(2)}) copy-start(bf16[144,256]{1,0:T(8,128)(2,1)S(1)} %collective-permute-done.2.refs_2_) | copy-start | bytes 221188
  25.6 3.5 %collective-permute-start = (bf16[144,256]{1,0:T(8,128)(2,1)S(1)}, bf16[144,256]{1,0:T(8,128)(2,1)S(1)}, u32[]{:S(2)}, u32[]{:S(2)}) collective-permute-start(bf16[144,256]{1,0:T(8,128)(2,1)S(1)} %pad_maximum_fusion), channel_id=1, source_target_pairs={{0,1},{1,2},{2,3},{3,0},{4,5},{5,6},{6,7},{7,4},{8,9},{9,10},{10,1... | collective-permute-start | bytes 221192 | tf_op jit(solution)/shard_map/ppermute | solution.py:593
  27.1 7.8 %copy-start.23 = (bf16[144,256]{1,0:T(8,128)(2,1)}, bf16[144,256]{1,0:T(8,128)(2,1)S(1)}, u32[]{:S(2)}) copy-start(bf16[144,256]{1,0:T(8,128)(2,1)S(1)} %collective-permute-done.1.refs_1_) | copy-start | bytes 221188
  27.1 6.1 %collective-permute-start.5 = (bf16[144,256]{1,0:T(8,128)(2,1)S(1)}, bf16[144,256]{1,0:T(8,128)(2,1)S(1)}, u32[]{:S(2)}, u32[]{:S(2)}) collective-permute-start(bf16[144,256]{1,0:T(8,128)(2,1)S(1)} %collective-permute-done.2.refs_2_), channel_id=1, source_target_pairs={{0,4},{4,0},{8,12},{12,8},{16,20},{20,16},{24,28},{28,24},{1,5},{5... | collective-permute-start | bytes 221192 | tf_op jit(solution)/shard_map/ppermute | solution.py:597
  29.2 5.7 %copy-start.24 = (bf16[144,256]{1,0:T(8,128)(2,1)}, bf16[144,256]{1,0:T(8,128)(2,1)S(1)}, u32[]{:S(2)}) copy-start(bf16[144,256]{1,0:T(8,128)(2,1)S(1)} %collective-permute-done.refs_0_) | copy-start | bytes 221188
  29.2 5.7 %collective-permute-start.4 = (bf16[144,256]{1,0:T(8,128)(2,1)S(1)}, bf16[144,256]{1,0:T(8,128)(2,1)S(1)}, u32[]{:S(2)}, u32[]{:S(2)}) collective-permute-start(bf16[144,256]{1,0:T(8,128)(2,1)S(1)} %collective-permute-done.1.refs_1_), channel_id=1, source_target_pairs={{0,4},{4,0},{8,12},{12,8},{16,20},{20,16},{24,28},{28,24},{1,5},{5... | collective-permute-start | bytes 221192 | tf_op jit(solution)/shard_map/ppermute | solution.py:597
  33.2 1.7 %copy-start.25 = (bf16[144,256]{1,0:T(8,128)(2,1)}, bf16[144,256]{1,0:T(8,128)(2,1)S(1)}, u32[]{:S(2)}) copy-start(bf16[144,256]{1,0:T(8,128)(2,1)S(1)} %collective-permute-done.5.refs_5_) | copy-start | bytes 221188
  33.2 1.7 %collective-permute-start.3 = (bf16[144,256]{1,0:T(8,128)(2,1)S(1)}, bf16[144,256]{1,0:T(8,128)(2,1)S(1)}, u32[]{:S(2)}, u32[]{:S(2)}) collective-permute-start(bf16[144,256]{1,0:T(8,128)(2,1)S(1)} %collective-permute-done.refs_0_), channel_id=1, source_target_pairs={{0,4},{4,0},{8,12},{12,8},{16,20},{20,16},{24,28},{28,24},{1,5},{5... | collective-permute-start | bytes 221192 | tf_op jit(solution)/shard_map/ppermute | solution.py:597
  33.3 5.8 %copy-start.9 = (bf16[384,256]{1,0:T(8,128)(2,1)}, bf16[384,256]{1,0:T(8,128)(2,1)S(1)}, u32[]{:S(2)}) copy-start(bf16[384,256]{1,0:T(8,128)(2,1)S(1)} %collective-permute-done.8.refs_13_) | copy-start | bytes 589828
  33.3 18.8 %collective-permute-start.11 = (bf16[384,256]{1,0:T(8,128)(2,1)S(1)}, bf16[384,256]{1,0:T(8,128)(2,1)S(1)}, u32[]{:S(2)}, u32[]{:S(2)}) collective-permute-start(bf16[384,256]{1,0:T(8,128)(2,1)S(1)} %collective-permute-done.8.refs_13_), channel_id=1, source_target_pairs={{0,4},{4,0},{8,12},{12,8},{16,20},{20,16},{24,28},{28,24},{1,5},{5... | collective-permute-start | bytes 589832 | tf_op jit(solution)/shard_map/ppermute | solution.py:597
  33.7 5.4 %copy-start.10 = (bf16[384,256]{1,0:T(8,128)(2,1)}, bf16[384,256]{1,0:T(8,128)(2,1)S(1)}, u32[]{:S(2)}) copy-start(bf16[384,256]{1,0:T(8,128)(2,1)S(1)} %collective-permute-done.7.refs_12_) | copy-start | bytes 589828
  33.7 18.4 %collective-permute-start.10 = (bf16[384,256]{1,0:T(8,128)(2,1)S(1)}, bf16[384,256]{1,0:T(8,128)(2,1)S(1)}, u32[]{:S(2)}, u32[]{:S(2)}) collective-permute-start(bf16[384,256]{1,0:T(8,128)(2,1)S(1)} %collective-permute-done.7.refs_12_), channel_id=1, source_target_pairs={{0,4},{4,0},{8,12},{12,8},{16,20},{20,16},{24,28},{28,24},{1,5},{5... | collective-permute-start | bytes 589832 | tf_op jit(solution)/shard_map/ppermute | solution.py:597
  33.8 5.3 %copy-start.11 = (bf16[384,256]{1,0:T(8,128)(2,1)}, bf16[384,256]{1,0:T(8,128)(2,1)S(1)}, u32[]{:S(2)}) copy-start(bf16[384,256]{1,0:T(8,128)(2,1)S(1)} %collective-permute-done.6.refs_11_) | copy-start | bytes 589828
  33.8 18.3 %collective-permute-start.9 = (bf16[384,256]{1,0:T(8,128)(2,1)S(1)}, bf16[384,256]{1,0:T(8,128)(2,1)S(1)}, u32[]{:S(2)}, u32[]{:S(2)}) collective-permute-start(bf16[384,256]{1,0:T(8,128)(2,1)S(1)} %collective-permute-done.6.refs_11_), channel_id=1, source_target_pairs={{0,4},{4,0},{8,12},{12,8},{16,20},{20,16},{24,28},{28,24},{1,5},{5... | collective-permute-start | bytes 589832 | tf_op jit(solution)/shard_map/ppermute | solution.py:597
  83.0 18.6 %collective-permute-start.16 = (bf16[4,384,256]{2,1,0:T(8,128)(2,1)}, bf16[4,384,256]{2,1,0:T(8,128)(2,1)S(1)}, u32[]{:S(2)}, u32[]{:S(2)}) collective-permute-start(bf16[4,384,256]{2,1,0:T(8,128)(2,1)} %get-tuple-element.74), channel_id=1, source_target_pairs={{0,4},{4,0},{8,12},{12,8},{16,20},{20,16},{24,28},{28,24},{1,5},{5... | collective-permute-start | bytes 2359304 | tf_op jit(solution)/shard_map/ppermute | solution.py:597
  83.2 2.9 %collective-permute-start.12 = (bf16[4,192,256]{2,1,0:T(8,128)(2,1)}, bf16[4,192,256]{2,1,0:T(8,128)(2,1)S(1)}, u32[]{:S(2)}, u32[]{:S(2)}) collective-permute-start(bf16[4,192,256]{2,1,0:T(8,128)(2,1)} %get-tuple-element.67), channel_id=1, source_target_pairs={{0,4},{4,0},{8,12},{12,8},{16,20},{20,16},{24,28},{28,24},{1,5},{5... | collective-permute-start | bytes 1179656 | tf_op jit(solution)/shard_map/ppermute | solution.py:597
  88.7 4.4 %collective-permute-start.13 = (bf16[192,256]{1,0:T(8,128)(2,1)}, bf16[192,256]{1,0:T(8,128)(2,1)S(1)}, u32[]{:S(2)}, u32[]{:S(2)}) collective-permute-start(bf16[192,256]{1,0:T(8,128)(2,1)} %get-tuple-element.69), channel_id=1, source_target_pairs={{0,8},{4,12},{8,0},{12,4},{16,24},{20,28},{24,16},{28,20},{1,9},{5... | collective-permute-start | bytes 294920 | tf_op jit(solution)/shard_map/ppermute | solution.py:597
  89.0 4.2 %collective-permute-start.14 = (bf16[192,256]{1,0:T(8,128)(2,1)}, bf16[192,256]{1,0:T(8,128)(2,1)S(1)}, u32[]{:S(2)}, u32[]{:S(2)}) collective-permute-start(bf16[192,256]{1,0:T(8,128)(2,1)} %get-tuple-element.70), channel_id=1, source_target_pairs={{0,16},{4,20},{8,24},{12,28},{16,0},{20,4},{24,8},{28,12},{1,17},{... | collective-permute-start | bytes 294920 | tf_op jit(solution)/shard_map/ppermute | solution.py:597
  90.2 4.6 %collective-permute-start.15 = (bf16[192,256]{1,0:T(8,128)(2,1)}, bf16[192,256]{1,0:T(8,128)(2,1)S(1)}, u32[]{:S(2)}, u32[]{:S(2)}) collective-permute-start(bf16[192,256]{1,0:T(8,128)(2,1)} %get-tuple-element.71), channel_id=1, source_target_pairs={{0,24},{4,28},{8,16},{12,20},{16,8},{20,12},{24,0},{28,4},{1,25},{... | collective-permute-start | bytes 294920 | tf_op jit(solution)/shard_map/ppermute | solution.py:597
  93.2 1.6 %copy-start.19 = (bf16[192,256]{1,0:T(8,128)(2,1)}, bf16[192,256]{1,0:T(8,128)(2,1)S(1)}, u32[]{:S(2)}) copy-start(bf16[192,256]{1,0:T(8,128)(2,1)S(1)} %collective-permute-done.13.refs_1_) | copy-start | bytes 294916
  93.2 1.6 %copy-start.20 = (bf16[192,256]{1,0:T(8,128)(2,1)}, bf16[192,256]{1,0:T(8,128)(2,1)S(1)}, u32[]{:S(2)}) copy-start(bf16[192,256]{1,0:T(8,128)(2,1)S(1)} %collective-permute-done.14.refs_2_) | copy-start | bytes 294916
  99.6 6.7 %collective-permute-start.24 = (bf16[4,144,256]{2,1,0:T(8,128)(2,1)}, bf16[4,144,256]{2,1,0:T(8,128)(2,1)S(1)}, u32[]{:S(2)}, u32[]{:S(2)}) collective-permute-start(bf16[4,144,256]{2,1,0:T(8,128)(2,1)} %get-tuple-element.80), channel_id=1, source_target_pairs={{0,4},{4,0},{8,12},{12,8},{16,20},{20,16},{24,28},{28,24},{1,5},{5... | collective-permute-start | bytes 884744 | tf_op jit(solution)/shard_map/ppermute | solution.py:597
  101.5 0.9 copy-start
  104.8 8.2 %collective-permute-start.17 = (bf16[384,256]{1,0:T(8,128)(2,1)}, bf16[384,256]{1,0:T(8,128)(2,1)S(1)}, u32[]{:S(2)}, u32[]{:S(2)}) collective-permute-start(bf16[384,256]{1,0:T(8,128)(2,1)} %get-tuple-element.76), channel_id=1, source_target_pairs={{0,1},{1,2},{2,3},{3,0},{4,5},{5,6},{6,7},{7,4},{8,9},{9,10},{10,1... | collective-permute-start | bytes 589832 | tf_op jit(solution)/shard_map/ppermute | solution.py:593
  104.8 20.6 %collective-permute-start.18 = (bf16[384,256]{1,0:T(8,128)(2,1)}, bf16[384,256]{1,0:T(8,128)(2,1)S(1)}, u32[]{:S(2)}, u32[]{:S(2)}) collective-permute-start(bf16[384,256]{1,0:T(8,128)(2,1)} %get-tuple-element.77), channel_id=1, source_target_pairs={{0,2},{1,3},{2,0},{3,1},{4,6},{5,7},{6,4},{7,5},{8,10},{9,11},{10,... | collective-permute-start | bytes 589832 | tf_op jit(solution)/shard_map/ppermute | solution.py:593
  106.3 21.5 %collective-permute-start.19 = (bf16[384,256]{1,0:T(8,128)(2,1)}, bf16[384,256]{1,0:T(8,128)(2,1)S(1)}, u32[]{:S(2)}, u32[]{:S(2)}) collective-permute-start(bf16[384,256]{1,0:T(8,128)(2,1)} %get-tuple-element.78), channel_id=1, source_target_pairs={{0,3},{1,0},{2,1},{3,2},{4,7},{5,4},{6,5},{7,6},{8,11},{9,8},{10,9... | collective-permute-start | bytes 589832 | tf_op jit(solution)/shard_map/ppermute | solution.py:593
  107.0 20.7 %copy-start.16 = (bf16[384,256]{1,0:T(8,128)(2,1)S(1)}, bf16[384,256]{1,0:T(8,128)(2,1)}, u32[]{:S(2)}) copy-start(bf16[384,256]{1,0:T(8,128)(2,1)} %get-tuple-element.75) | copy-start | bytes 589828
  108.8 21.3 %collective-permute-start.25 = (bf16[144,256]{1,0:T(8,128)(2,1)}, bf16[144,256]{1,0:T(8,128)(2,1)S(1)}, u32[]{:S(2)}, u32[]{:S(2)}) collective-permute-start(bf16[144,256]{1,0:T(8,128)(2,1)} %get-tuple-element.82), channel_id=1, source_target_pairs={{0,1},{1,2},{2,3},{3,0},{4,5},{5,6},{6,7},{7,4},{8,9},{9,10},{10,1... | collective-permute-start | bytes 221192 | tf_op jit(solution)/shard_map/ppermute | solution.py:593
  110.3 20.3 %collective-permute-start.26 = (bf16[144,256]{1,0:T(8,128)(2,1)}, bf16[144,256]{1,0:T(8,128)(2,1)S(1)}, u32[]{:S(2)}, u32[]{:S(2)}) collective-permute-start(bf16[144,256]{1,0:T(8,128)(2,1)} %get-tuple-element.83), channel_id=1, source_target_pairs={{0,2},{1,3},{2,0},{3,1},{4,6},{5,7},{6,4},{7,5},{8,10},{9,11},{10,... | collective-permute-start | bytes 221192 | tf_op jit(solution)/shard_map/ppermute | solution.py:593
  113.0 17.9 %collective-permute-start.27 = (bf16[144,256]{1,0:T(8,128)(2,1)}, bf16[144,256]{1,0:T(8,128)(2,1)S(1)}, u32[]{:S(2)}, u32[]{:S(2)}) collective-permute-start(bf16[144,256]{1,0:T(8,128)(2,1)} %get-tuple-element.84), channel_id=1, source_target_pairs={{0,3},{1,0},{2,1},{3,2},{4,7},{5,4},{6,5},{7,6},{8,11},{9,8},{10,9... | collective-permute-start | bytes 221192 | tf_op jit(solution)/shard_map/ppermute | solution.py:593
  127.7 3.2 %copy-start.28 = (bf16[144,256]{1,0:T(8,128)(2,1)S(1)}, bf16[144,256]{1,0:T(8,128)(2,1)}, u32[]{:S(2)}) copy-start(bf16[144,256]{1,0:T(8,128)(2,1)} %get-tuple-element.81) | copy-start | bytes 221188
  127.8 6.9 %collective-permute-start.22 = (bf16[384,256]{1,0:T(8,128)(2,1)S(1)}, bf16[384,256]{1,0:T(8,128)(2,1)S(1)}, u32[]{:S(2)}, u32[]{:S(2)}) collective-permute-start(bf16[384,256]{1,0:T(8,128)(2,1)S(1)} %add_convert_fusion.1), channel_id=1, source_target_pairs={{0,24},{4,28},{8,16},{12,20},{16,8},{20,12},{24,0},{28,4},{1,25},{... | collective-permute-start | bytes 589832 | tf_op jit(solution)/shard_map/ppermute | solution.py:597
  129.1 11.5 %collective-permute-start.21 = (bf16[384,256]{1,0:T(8,128)(2,1)S(1)}, bf16[384,256]{1,0:T(8,128)(2,1)S(1)}, u32[]{:S(2)}, u32[]{:S(2)}) collective-permute-start(bf16[384,256]{1,0:T(8,128)(2,1)S(1)} %add_convert_fusion.1), channel_id=1, source_target_pairs={{0,16},{4,20},{8,24},{12,28},{16,0},{20,4},{24,8},{28,12},{1,17},{... | collective-permute-start | bytes 589832 | tf_op jit(solution)/shard_map/ppermute | solution.py:597
  130.2 10.5 %collective-permute-start.20 = (bf16[384,256]{1,0:T(8,128)(2,1)S(1)}, bf16[384,256]{1,0:T(8,128)(2,1)S(1)}, u32[]{:S(2)}, u32[]{:S(2)}) collective-permute-start(bf16[384,256]{1,0:T(8,128)(2,1)S(1)} %add_convert_fusion.1), channel_id=1, source_target_pairs={{0,8},{4,12},{8,0},{12,4},{16,24},{20,28},{24,16},{28,20},{1,9},{5... | collective-permute-start | bytes 589832 | tf_op jit(solution)/shard_map/ppermute | solution.py:597
  130.9 10.5 %collective-permute-start.30 = (bf16[144,256]{1,0:T(8,128)(2,1)S(1)}, bf16[144,256]{1,0:T(8,128)(2,1)S(1)}, u32[]{:S(2)}, u32[]{:S(2)}) collective-permute-start(bf16[144,256]{1,0:T(8,128)(2,1)S(1)} %add_convert_fusion.3), channel_id=1, source_target_pairs={{0,24},{4,28},{8,16},{12,20},{16,8},{20,12},{24,0},{28,4},{1,25},{... | collective-permute-start | bytes 221192 | tf_op jit(solution)/shard_map/ppermute | solution.py:597
  132.2 10.8 %collective-permute-start.29 = (bf16[144,256]{1,0:T(8,128)(2,1)S(1)}, bf16[144,256]{1,0:T(8,128)(2,1)S(1)}, u32[]{:S(2)}, u32[]{:S(2)}) collective-permute-start(bf16[144,256]{1,0:T(8,128)(2,1)S(1)} %add_convert_fusion.3), channel_id=1, source_target_pairs={{0,16},{4,20},{8,24},{12,28},{16,0},{20,4},{24,8},{28,12},{1,17},{... | collective-permute-start | bytes 221192 | tf_op jit(solution)/shard_map/ppermute | solution.py:597
  134.8 8.2 %collective-permute-start.28 = (bf16[144,256]{1,0:T(8,128)(2,1)S(1)}, bf16[144,256]{1,0:T(8,128)(2,1)S(1)}, u32[]{:S(2)}, u32[]{:S(2)}) collective-permute-start(bf16[144,256]{1,0:T(8,128)(2,1)S(1)} %add_convert_fusion.3), channel_id=1, source_target_pairs={{0,8},{4,12},{8,0},{12,4},{16,24},{20,28},{24,16},{28,20},{1,9},{5... | collective-permute-start | bytes 221192 | tf_op jit(solution)/shard_map/ppermute | solution.py:597
  140.7 3.8 %copy-start.1 = (bf16[384,256]{1,0:T(8,128)(2,1)}, bf16[384,256]{1,0:T(8,128)(2,1)S(1)}, u32[]{:S(2)}) copy-start(bf16[384,256]{1,0:T(8,128)(2,1)S(1)} %add_convert_fusion.lo_a) | copy-start | bytes 589828
  140.8 3.8 %collective-permute-start.23 = (bf16[384,256]{1,0:T(8,128)(2,1)S(1)}, bf16[384,256]{1,0:T(8,128)(2,1)S(1)}, u32[]{:S(2)}, u32[]{:S(2)}) collective-permute-start(bf16[384,256]{1,0:T(8,128)(2,1)S(1)} %add_convert_fusion.lo_a), channel_id=1, source_target_pairs={{0,4},{4,0},{8,12},{12,8},{16,20},{20,16},{24,28},{28,24},{1,5},{5... | collective-permute-start | bytes 589832 | tf_op jit(solution)/shard_map/ppermute | solution.py:597
  143.1 1.5 copy-start.7
  143.1 1.5 collective-permute-start.31
  (26 other events, 18.3 us)

commit v2 on v1

v2 whole, which is shorter than its diff:
```python
import functools

import jax
import jax.numpy as jnp
from jax import lax
from jax.experimental import pallas as pl
from jax.experimental.pallas import tpu as pltpu
from jax.sharding import PartitionSpec as P

HEADS = 8
HDIM = 32
PAIRS = HEADS // 2
SCALE = HDIM ** (-0.5)
EXP_SCALE = SCALE * 1.4426950408889634
EPS = 1e-06
NEG = -1e30
KEY_BLOCK = 768
SMALL_VMEM = 12 * 2**20
MAIN_VMEM = 16 * 2**20
WHOLE_VMEM = 58 * 2**20

bf16 = jnp.bfloat16
f32 = jnp.float32

(
    FIRST_G,
    FIRST_B,
    QUERY_B,
    REDUCE_B,
    KEYS_G,
    KEYS_B,
    VALUE_B,
    OUTPUT_B,
    SECOND_G,
    SECOND_B,
    RETURN_B,
    HIDDEN_B,
) = range(12)
VECS = 16


def mm(left, right):
    return jnp.dot(left, right, preferred_element_type=f32)


def mm_tn(left, right):
    return lax.dot_general(left, right, (((0,), (0,)), ((), ())), preferred_element_type=f32)


def mm_nt(left, right):
    return lax.dot_general(left, right, (((1,), (1,)), ((), ())), preferred_element_type=f32)


def normalize(rows):
    mean = jnp.mean(rows, axis=-1, keepdims=True)
    centered = rows - mean
    var = jnp.mean(centered * centered, axis=-1, keepdims=True)
    rstd = lax.rsqrt(var + EPS)
    return centered * rstd, rstd


def normalize_back(grad, normal, rstd, gain):
    scaled = grad * gain
    mean_a = jnp.mean(scaled, axis=-1, keepdims=True)
    mean_b = jnp.mean(scaled * normal, axis=-1, keepdims=True)
    return (scaled - mean_a - normal * mean_b) * rstd


def token_mask(first_row, rows, cols, width, height, image_width):
    row_ids = lax.broadcasted_iota(jnp.int32, (rows, cols, width), 0) + first_row
    col_ids = lax.broadcasted_iota(jnp.int32, (rows, cols, width), 1)
    valid = (row_ids < height) & (col_ids < image_width)
    return jnp.where(valid, 1.0, 0.0).astype(f32).reshape(rows * cols, width)


def pack_first_kernel(n_fs, *refs):
    smalls, (hidden_b, reduce_w, query_w, keyval_w, first, wide) = take(refs, HIDDEN_B)
    dim = reduce_w.shape[1]
    shard = dim // n_fs
    half = dim // 2
    rest = half + VECS
    fs = lax.axis_index("fs")
    is_low = lax.axis_index("sp") % 2 == 0

    @pl.when(is_low)
    def _():
        first[:half] = reduce_w[:half]
        first[rest : rest + shard] = query_w[...]
        first[rest + shard :] = keyval_w[: shard // 2, :dim]

    @pl.when(jnp.logical_not(is_low))
    def _():
        first[:half] = reduce_w[half:]
        first[rest : rest + shard // 2] = keyval_w[shard // 2 :, :dim]
        first[rest + shard // 2 :] = keyval_w[:, dim:]

    wide[...] = jnp.zeros_like(wide)
    for index, small in enumerate(smalls):
        row = small[...].astype(f32).reshape(1, shard)
        wide[index : index + 1, :] = jnp.concatenate([row] * n_fs, axis=1)
    lane = lax.broadcasted_iota(jnp.int32, wide.shape, 1)
    row = lax.broadcasted_iota(jnp.int32, wide.shape, 0)
    vectors = jnp.where(lane // shard == fs, wide[...], 0.0)
    hidden_row = hidden_b[...].astype(f32).reshape(1, dim)
    first[half:rest] = jnp.where(row == HIDDEN_B + fs, hidden_row, vectors).astype(bf16)


def both_halves(mine, other):
    is_low = lax.axis_index("sp") % 2 == 0
    a, b = mine[...], other[...]
    return jnp.where(is_low, a, b), jnp.where(is_low, b, a)


def shard_rows(place, rows):
    return pl.ds(pl.multiple_of(place * rows, rows), rows)


def begin_kernel(dims, sizes, tokens, reduce_w, query_w, keyval_w, hidden_w, return_w, output_w, packed, *outs):
    n_sp, batches, row_dev, cols, dim = dims
    normal_ref, mask_ref, bias_ref, own_r, own_q, own_kv, own_vec, second = outs
    tok = row_dev * cols
    half_cols = cols // 2
    rows_dev = row_dev // 2
    half = dim // 2
    shard = hidden_w.shape[0]
    sp = lax.axis_index("sp")
    own_r[...] = reduce_w[...]
    own_q[...] = query_w[...]
    own_kv[...] = keyval_w[...]
    own_vec[...] = packed[half : half + VECS].astype(f32)

    @pl.when(sp % 2 == 0)
    def _():
        for chunk in range(hidden_w.shape[1] // dim):
            second[chunk * shard : (chunk + 1) * shard] = hidden_w[:, chunk * dim : (chunk + 1) * dim]
        second[dim:] = output_w[: shard // 2]

    @pl.when(sp % 2 == 1)
    def _():
        second[:dim] = return_w[...]
        second[dim:] = output_w[shard // 2 :]

    for batch in range(batches):
        height, image_width = sizes[batch, 0, 0], sizes[batch, 0, 1]
        rows = slice(batch * tok, (batch + 1) * tok)
        normal_ref[rows], _ = normalize(tokens[batch, 0].reshape(tok, dim).astype(f32))
        mask_ref[rows] = token_mask(sp * row_dev, row_dev, cols, dim, height, image_width)
        col_ids = lax.broadcasted_iota(jnp.int32, (half_cols, dim), 0)

        def key_row_bias(index, _, batch=batch, height=height, image_width=image_width, col_ids=col_ids):
            key_row = index
            if n_sp == 8:
                key_row = (sp ^ (index // rows_dev)) * rows_dev + lax.rem(index, rows_dev)
            width = jnp.where(2 * key_row < height, image_width, 0)
            here = pl.ds(pl.multiple_of(index * half_cols, half_cols), half_cols)
            bias_ref[batch, here, :] = jnp.where(2 * col_ids < width, 0.0, NEG).astype(bf16)
            return 0

        lax.fori_loop(0, n_sp * rows_dev, key_row_bias, 0)


def reduce_kernel(dims, *refs):
    n_fs, batches, row_dev, cols, dim = dims
    ins, mine, other, outs = take(refs, 7, n_fs - 1, n_fs - 1)
    normal_in, mask_ref, own_w, own_q, own_kv, own_vec, second_in = ins
    normed_ref, patch_ref, reduced_ref, key_ref, weight_ref, wq, wkv, vec_ref, second, wide = outs
    half = dim // 2
    shard = dim // n_fs
    rest = half + VECS
    tok = row_dev * cols
    half_cols = cols // 2
    key_dev = tok // 4
    fs = lax.axis_index("fs")
    second[...] = second_in[...]
    weight_ref[fs] = own_w[...]
    here = shard_rows(fs, shard)
    wq[here, :] = own_q[...]
    wkv[here, :] = own_kv[...]
    vec = own_vec[...]
    for step in range(1, n_fs):
        low, high = both_halves(mine[step - 1], other[step - 1])
        place = lax.rem(fs + n_fs - step, n_fs)
        weight_ref[place, :half] = low[:half]
        weight_ref[place, half:] = high[:half]
        vec = vec + low[half:rest].astype(f32)
        here = shard_rows(place, shard)
        wq[here, :] = low[rest : rest + shard]
        wkv[here, :dim] = jnp.concatenate([low[rest + shard :], high[rest : rest + shard // 2]], axis=0)
        wkv[here, dim:] = high[rest + shard // 2 :]
    vec_ref[...] = vec
    for batch in range(batches):
        rows = slice(batch * tok, (batch + 1) * tok)
        low = (normal_in[rows] * vec[FIRST_G : FIRST_G + 1] + vec[FIRST_B : FIRST_B + 1]).astype(bf16)
        normed_ref[rows] = low
        masked = low.astype(f32) * mask_ref[rows]
        for part in range(dim // 128):
            wide[part] = masked[:, part * 128 : (part + 1) * 128]
        for row in range(row_dev // 2):
            start = batch * key_dev + row * half_cols
            for offset in range(4):
                dr, dc = offset // 2, offset % 2
                for part in range(dim // 128):
                    piece = wide[part, pl.ds((2 * row + dr) * cols + dc, half_cols, stride=2), :]
                    lanes = slice(offset * dim + part * 128, offset * dim + (part + 1) * 128)
                    patch_ref[start : start + half_cols, lanes] = piece.astype(bf16)
    reduced = mm(patch_ref[...], weight_ref[...].reshape(4 * dim, dim)) + vec[REDUCE_B : REDUCE_B + 1]
    reduced_ref[...] = reduced
    normal, _ = normalize(reduced)
    key_ref[...] = (normal * vec[KEYS_G : KEYS_G + 1] + vec[KEYS_B : KEYS_B + 1]).astype(bf16)


def relay_kernel(n, *refs):
    for source, target in zip(refs[:n], refs[n + 1 :]):
        target[...] = source[...]


def head_stack_t(values_t, pair, tok):
    both = jnp.concatenate([values_t, values_t], axis=1)
    head = lax.broadcasted_iota(jnp.int32, both.shape, 0) // HDIM
    want = 2 * pair + jnp.where(lax.broadcasted_iota(jnp.int32, both.shape, 1) >= tok, 1, 0)
    return jnp.where(head == want, both, jnp.zeros_like(both))


def head_stack(values, pair):
    head = lax.broadcasted_iota(jnp.int32, values.shape, 1) // HDIM
    zero = jnp.zeros_like(values)
    return jnp.concatenate(
        [jnp.where(head == 2 * pair, values, zero), jnp.where(head == 2 * pair + 1, values, zero)],
        axis=0,
    )


def split_pair(both, tok):
    return jnp.concatenate([both[:HDIM, :tok], both[HDIM:, tok:]], axis=0)


def key_rows_of(pieces, key_dev, per_block, batch, index):
    here = slice(batch * key_dev, (batch + 1) * key_dev)
    if len(pieces) > 1:
        return jnp.concatenate([part[here] for part in pieces], axis=0)
    dim = pieces[0].shape[2]
    devices = slice(index * per_block, (index + 1) * per_block)
    return pieces[0][devices, here, :].reshape(per_block * key_dev, dim)


def mask_lane(pair, dim):
    return 0 if pair == PAIRS - 1 else dim - 1


def with_bias(key_block, bias, lane_id):
    lane = lax.broadcasted_iota(jnp.int32, key_block.shape, 1)
    return jnp.where(lane == lane_id, bias.astype(f32), key_block.astype(f32)).astype(bf16)


def query_stack(queries_t, pair, lane_id, tok):
    stacked = head_stack_t(queries_t, pair, tok)
    row = lax.broadcasted_iota(jnp.int32, stacked.shape, 0)
    return jnp.where(row == lane_id, jnp.ones_like(stacked), stacked)


def take(refs, *counts):
    refs = list(refs)
    groups = []
    for count in counts:
        groups.append(refs[:count])
        refs = refs[count:]
    return groups + [refs]


def forward_kernel(dims, *refs):
    batches, tok, key_dev, keys, block, n_pieces = dims
    (normed, vec_ref, bias_ref, wq, wkv), pieces, (attended, *kept) = take(refs, 5, n_pieces)
    queries_out, kvs, attf, stats, probs = (
        kept[index * batches : (index + 1) * batches] for index in range(5)
    )
    dim = wq.shape[0]
    blocks = keys // block
    per_block = block // key_dev
    for batch in range(batches):
        rows = slice(batch * tok, (batch + 1) * tok)
        queries = (mm(normed[rows], wq[...]) + vec_ref[QUERY_B : QUERY_B + 1]).astype(bf16)
        queries_out[batch][...] = queries
        queries_t = queries.T
        for index in range(blocks):
            key_rows = key_rows_of(pieces, key_dev, per_block, batch, index)
            here = slice(index * block, (index + 1) * block)
            kvs[batch][here, :dim] = mm(key_rows, wkv[:, :dim]).astype(bf16)
            value_rows = mm(key_rows, wkv[:, dim:]) + vec_ref[VALUE_B : VALUE_B + 1]
            kvs[batch][here, dim:] = value_rows.astype(bf16)
        if blocks == 1:
            key_block = kvs[batch][:, :dim]
            values_t = kvs[batch][:, dim:].T
            bias = bias_ref[batch]
            masked = {lane_id: with_bias(key_block, bias, lane_id) for lane_id in (0, dim - 1)}
            for pair in range(PAIRS):
                lane_id = mask_lane(pair, dim)
                heads = slice(2 * HDIM * pair, 2 * HDIM * (pair + 1))
                scores = mm(masked[lane_id], query_stack(queries_t, pair, lane_id, tok))
                top = jnp.max(scores, axis=0, keepdims=True)
                weights = jnp.exp2((scores - top) * EXP_SCALE)
                inverse = 1.0 / jnp.sum(weights, axis=0, keepdims=True)
                low = weights.astype(bf16)
                probs[batch][pair] = low
                stats[batch][pair, 0:1] = inverse
                mixed = mm(values_t[heads], low) * inverse
                attf[batch][heads] = split_pair(mixed, tok)
        else:
            for pair in range(PAIRS):
                lane_id = mask_lane(pair, dim)
                heads = slice(2 * HDIM * pair, 2 * HDIM * (pair + 1))
                stacked = query_stack(queries_t, pair, lane_id, tok)

                def block_scores(index, stacked=stacked, lane_id=lane_id, batch=batch):
                    here = pl.ds(pl.multiple_of(index * block, block), block)
                    masked = with_bias(kvs[batch][here, :dim], bias_ref[batch, here, :], lane_id)
                    return here, mm(masked, stacked)

                def find_top(index, top, block_scores=block_scores):
                    _, scores = block_scores(index)
                    return jnp.maximum(top, jnp.max(scores, axis=0, keepdims=True))

                top = lax.fori_loop(0, blocks, find_top, jnp.full((1, 2 * tok), 4 * NEG, f32))

                def add_block(index, carry, block_scores=block_scores, top=top, heads=heads, batch=batch):
                    total, mixed = carry
                    here, scores = block_scores(index)
                    weights = jnp.exp2((scores - top) * EXP_SCALE)
                    values_t = kvs[batch][here, dim:].T
                    mixed = mixed + mm(values_t[heads], weights.astype(bf16))
                    return total + jnp.sum(weights, axis=0, keepdims=True), mixed

                start = (jnp.zeros((1, 2 * tok), f32), jnp.zeros((2 * HDIM, 2 * tok), f32))
                total, mixed = lax.fori_loop(0, blocks, add_block, start)
                inverse = 1.0 / total
                stats[batch][pair, 0:1] = inverse
                stats[batch][pair, 1:2] = top
                attf[batch][heads] = split_pair(mixed * inverse, tok)
        attended[rows] = attf[batch][...].T.astype(bf16)


def mlp_kernel(dims, *refs):
    n_fs, batches, row_dev, cols, dim, hid = dims
    ins, own, mine, other, outs, scratch = take(refs, 5, 3, n_fs - 1, n_fs - 1, 7)
    tokens, cotangent, mask_ref, attended, vec_ref = ins
    acts_ref, normal_ref, rstd_ref, grad_ref, keep_ref, send_ref, wo = outs
    wh, wr, bias_rows = scratch
    tok = row_dev * cols
    shard = dim // n_fs
    chunks = hid // dim
    fs = lax.axis_index("fs")
    is_low = lax.axis_index("sp") % 2 == 0
    wh[shard_rows(fs, shard), :] = own[0][...]
    wr[shard_rows(fs, dim), :] = own[1][...]
    wo[shard_rows(fs, shard), :] = own[2][...]
    for step in range(1, n_fs):
        low, high = both_halves(mine[step - 1], other[step - 1])
        place = lax.rem(fs + n_fs - step, n_fs)
        here = shard_rows(place, shard)
        for chunk in range(chunks):
            wh[here, chunk * dim : (chunk + 1) * dim] = low[chunk * shard : (chunk + 1) * shard]
        wr[shard_rows(place, dim), :] = high[:dim]
        wo[here, :] = jnp.concatenate([low[dim:], high[dim:]], axis=0)

    def vec(index):
        return vec_ref[index : index + 1, :]

    def store(low_half, owner, start, value):
        value = value.astype(bf16)
        here = slice(start, start + value.shape[0])
        keep = is_low if low_half else jnp.logical_not(is_low)

        @pl.when(keep)
        def _():
            keep_ref[owner, here, :] = value

        @pl.when(jnp.logical_not(keep))
        def _():
            send_ref[owner, here, :] = value

    x = jnp.concatenate([tokens[b, 0].reshape(tok, dim).astype(f32) for b in range(batches)], axis=0)
    mask = mask_ref[...]
    middle = x + mm(attended[...], wo[...]) + vec(OUTPUT_B)
    normal, rstd = normalize(middle)
    normal_ref[...] = normal
    rstd_ref[...] = jnp.broadcast_to(rstd, rstd_ref.shape)
    second = (normal * vec(SECOND_G) + vec(SECOND_B)).astype(bf16)
    grad_out = jnp.concatenate([cotangent[b, 0].reshape(tok, dim) for b in range(batches)], axis=0) * mask
    grad_mlp = grad_out.astype(bf16)
    total = middle + vec(RETURN_B)
    grad_second = jnp.zeros((batches * tok, dim), f32)
    bias_rows[...] = jnp.zeros_like(bias_rows)
    for chunk in range(chunks):
        lanes = slice(chunk * dim, (chunk + 1) * dim)
        hidden = mm(second, wh[:, lanes]) + vec(HIDDEN_B + chunk)
        phi = 0.5 + 0.5 * lax.erf(hidden * 0.7071067811865476)
        density = 0.3989422804014327 * jnp.exp2(hidden * hidden * (-0.5 * 1.4426950408889634))
        activated = (hidden * phi).astype(bf16)
        total = total + mm(activated, wr[lanes, :])
        grad_activated = mm_nt(grad_mlp, wr[lanes, :])
        grad_hidden = ((phi + hidden * density) * grad_activated).astype(bf16)
        bias_rows[chunk : chunk + 1] = jnp.sum(grad_hidden.astype(f32), axis=0, keepdims=True)
        grad_second = grad_second + mm_nt(grad_hidden, wh[:, lanes])
        store(False, chunk, 0, mm_tn(activated, grad_mlp))
        grad_wh = mm_tn(second, grad_hidden)
        for owner in range(n_fs):
            store(True, owner, chunk * shard, grad_wh[owner * shard : (owner + 1) * shard])
    total = total * mask
    for batch in range(batches):
        acts_ref[batch, 0] = total[batch * tok : (batch + 1) * tok].reshape(row_dev, cols, dim)
    rows = batches * tok
    grad_ref[:rows] = grad_second
    grad_ref[rows:] = bias_rows[...]


def middle_kernel(dims, cotangent, mask_ref, normal_ref, rstd_ref, grad_ref, vec_ref, wo, middle_ref, gatt, gvec_ref):
    batches, tok, chunks = dims
    dim = wo.shape[0]
    rows = batches * tok
    grad_out = jnp.concatenate([cotangent[b, 0].reshape(tok, dim) for b in range(batches)], axis=0)
    grad_out = grad_out * mask_ref[...]
    grad_second, normal = grad_ref[:rows], normal_ref[...]
    rstd = jnp.concatenate([rstd_ref[...]] * (dim // rstd_ref.shape[1]), axis=1)
    back = normalize_back(grad_second, normal, rstd, vec_ref[SECOND_G : SECOND_G + 1])
    grad_middle = grad_out + back
    middle_ref[...] = grad_middle
    grad_branch = grad_middle.astype(bf16)
    gatt[...] = mm_nt(grad_branch, wo[...]).astype(bf16)
    gvec_ref[...] = jnp.zeros_like(gvec_ref)
    for index, value in (
        (OUTPUT_B, grad_branch.astype(f32)),
        (SECOND_G, grad_second * normal),
        (SECOND_B, grad_second),
        (RETURN_B, grad_out.astype(bf16).astype(f32)),
    ):
        gvec_ref[index : index + 1] = jnp.sum(value, axis=0, keepdims=True)
    gvec_ref[HIDDEN_B : HIDDEN_B + chunks] = grad_ref[rows : rows + chunks]


def backward_kernel(dims, *refs):
    n_fs, n_sp, batch, last, tok, key_dev, keys, block, n_pieces, batches = dims
    ins, pieces, more, refs = take(refs, 8, n_pieces, 8 if last else 0)
    gatt, queries_ref, kvs, attf, stats, probs, bias_ref, wkv = ins
    if last:
        first_gq, first_gkv, first_gvec, normed, wq, attended, middle, _ = more
        keep_ref, send_ref, gnormed_ref, near_ref, far_ref, gvec_ref = refs[:6]
        gqs, gks, gvs = refs[6:]
    else:
        gq_ref, gkv_ref, gvec_ref, near_ref, far_ref = refs[:5]
        gqs, gks, gvs = refs[5:]
    dim = wkv.shape[0]
    shard = dim // n_fs
    blocks = keys // block
    per_block = block // key_dev
    rows = slice(batch * tok, (batch + 1) * tok)
    queries = queries_ref[...]
    grad_att_t = gatt[rows].astype(f32).T
    product = grad_att_t * attf[...]

    def pair_terms(pair):
        inverse = stats[pair, 0:1]
        piece = product[2 * HDIM * pair : 2 * HDIM * (pair + 1)]
        delta = jnp.concatenate(
            [jnp.sum(piece[:HDIM], axis=0, keepdims=True), jnp.sum(piece[HDIM:], axis=0, keepdims=True)],
            axis=1,
        )
        stacked = head_stack_t(grad_att_t, pair, tok) * inverse
        return delta * inverse, stacked.astype(bf16)

    if blocks == 1:
        keys_t = kvs[:, :dim].T
        values = kvs[:, dim:]
        grad_k = jnp.zeros((keys, dim), f32)
        grad_v = jnp.zeros((keys, dim), f32)
        for pair in range(PAIRS):
            heads = slice(2 * HDIM * pair, 2 * HDIM * (pair + 1))
            delta, stacked = pair_terms(pair)
            low = probs[pair]
            grad_probs = mm(values, stacked)
            grad_scores = (low.astype(f32) * (grad_probs - delta)).astype(bf16)
            gqs[heads] = split_pair(mm(keys_t[heads], grad_scores), tok)
            grad_k = grad_k + mm(grad_scores, head_stack(queries, pair))
            grad_v = grad_v + mm(low, stacked.T)
    else:
        gks[...] = jnp.zeros_like(gks)
        gvs[...] = jnp.zeros_like(gvs)
        queries_t = queries.T
        for pair in range(PAIRS):
            heads = slice(2 * HDIM * pair, 2 * HDIM * (pair + 1))
            lane_id = mask_lane(pair, dim)
            delta, stacked = pair_terms(pair)
            stacked_n = stacked.T
            query_t = query_stack(queries_t, pair, lane_id, tok)
            query_n = head_stack(queries, pair)
            top = stats[pair, 1:2]

            def back_block(index, gq, heads=heads, lane_id=lane_id, delta=delta, stacked=stacked, stacked_n=stacked_n, query_t=query_t, query_n=query_n, top=top):
                here = pl.ds(pl.multiple_of(index * block, block), block)
                key_block = kvs[here, :dim]
                masked = with_bias(key_block, bias_ref[batch, here, :], lane_id)
                weights = jnp.exp2((mm(masked, query_t) - top) * EXP_SCALE)
                grad_probs = mm(kvs[here, dim:], stacked)
                grad_scores = (weights * (grad_probs - delta)).astype(bf16)
                gks[here, :] += mm(grad_scores, query_n)
                gvs[here, :] += mm(weights.astype(bf16), stacked_n)
                return gq + mm(key_block.T[heads], grad_scores)

            gq = lax.fori_loop(0, blocks, back_block, jnp.zeros((2 * HDIM, 2 * tok), f32))
            gqs[heads] = split_pair(gq, tok)
    grad_queries = (gqs[...].T * SCALE).astype(bf16)
    grad_wk = jnp.zeros((dim, dim), f32)
    grad_wv = jnp.zeros((dim, dim), f32)
    bias_value = jnp.zeros((1, dim), f32)
    for index in range(blocks):
        if blocks > 1:
            here = slice(index * block, (index + 1) * block)
            grad_k, grad_v = gks[here], gvs[here]
        grad_k = (grad_k * SCALE).astype(bf16)
        bias_value = bias_value + jnp.sum(grad_v, axis=0, keepdims=True)
        grad_v = grad_v.astype(bf16)
        grad_key = (mm_nt(grad_k, wkv[:, :dim]) + mm_nt(grad_v, wkv[:, dim:])).astype(bf16)
        if n_pieces > 1:
            pairs = grad_key.reshape(n_sp // 2, 2, key_dev, dim)
            near_ref[...] = pairs[:, 0]
            far_ref[...] = pairs[:, 1]
        else:
            near_ref[index * per_block : (index + 1) * per_block] = grad_key.reshape(per_block, key_dev, dim)
        key_rows = key_rows_of(pieces, key_dev, per_block, batch, index)
        grad_wk = grad_wk + mm_tn(key_rows, grad_k)
        grad_wv = grad_wv + mm_tn(key_rows, grad_v)
    if not last:
        gq_ref[...] = grad_queries
        gkv_ref[:, :dim] = grad_wk
        gkv_ref[:, dim:] = grad_wv
        gvec_ref[...] = jnp.zeros_like(gvec_ref)
        gvec_ref[0:1] = bias_value
        return
    is_low = lax.axis_index("sp") % 2 == 0
    grad_wk = grad_wk + first_gkv[:, :dim]
    grad_wv = grad_wv + first_gkv[:, dim:]
    bias_value = bias_value + first_gvec[0:1]
    grad_queries = jnp.concatenate([first_gq[...], grad_queries], axis=0)
    grad_wq = mm_tn(normed[...], grad_queries)
    grad_wo = mm_tn(attended[...], middle[...].astype(bf16))
    for owner in range(n_fs):
        part = slice(owner * shard, (owner + 1) * shard)
        low = jnp.concatenate([grad_wq[part], grad_wk[part]], axis=0).astype(bf16)
        high = jnp.concatenate([grad_wv[part], grad_wo[part]], axis=0).astype(bf16)
        keep_ref[owner] = jnp.where(is_low, low, high)
        send_ref[owner] = jnp.where(is_low, high, low)
    gnormed_ref[...] = mm_nt(grad_queries, wq[...])
    gvec_ref[...] = jnp.zeros_like(gvec_ref)
    gvec_ref[QUERY_B : QUERY_B + 1] = jnp.sum(grad_queries.astype(f32), axis=0, keepdims=True)
    gvec_ref[VALUE_B : VALUE_B + 1] = bias_value


def sum_parts(parts):
    if len(parts) == 1:
        total = parts[0][0].astype(f32)
        for index in range(1, parts[0].shape[0]):
            total = total + parts[0][index].astype(f32)
        return total
    total = parts[0][...].astype(f32)
    for part in parts[1:]:
        total = total + part[...].astype(f32)
    return total


def reduction_kernel(n_parts, n_fs, patches, reduced, vec_ref, *refs):
    parts = refs[:n_parts]
    grad_ref, gvec_ref, keep_ref, send_ref = refs[-4:]
    dim = reduced.shape[1]
    half = dim // 2
    is_low = lax.axis_index("sp") % 2 == 0
    grad_key = sum_parts(parts)
    normal, rstd = normalize(reduced[...])
    grad_low = normalize_back(grad_key, normal, rstd, vec_ref[KEYS_G : KEYS_G + 1]).astype(bf16)
    grad_ref[...] = grad_low
    for owner in range(n_fs):
        grad_w = mm_tn(patches[:, owner * dim : (owner + 1) * dim], grad_low).astype(bf16)
        low, high = grad_w[:half], grad_w[half:]
        keep_ref[owner] = jnp.where(is_low, low, high)
        send_ref[owner] = jnp.where(is_low, high, low)
    gvec_ref[...] = jnp.zeros_like(gvec_ref)
    for index, value in (
        (REDUCE_B, grad_low.astype(f32)),
        (KEYS_G, grad_key * normal),
        (KEYS_B, grad_key),
    ):
        gvec_ref[index : index + 1] = jnp.sum(value, axis=0, keepdims=True)


def input_kernel(dims, tokens, middle, gnormed, mask_ref, grad_reduced, weight, vec_ref, vec_a, vec_b, vec_c, grad_ref, gvec_ref, wide):
    batches, row_dev, cols, dim = dims
    tok = row_dev * cols
    half_cols = cols // 2
    key_dev = tok // 4
    gain_first = jnp.zeros((1, dim), f32)
    bias_first = jnp.zeros((1, dim), f32)
    for batch in range(batches):
        for offset in range(4):
            dr, dc = offset // 2, offset % 2
            back = mm_nt(grad_reduced[batch * key_dev : (batch + 1) * key_dev], weight[offset])
            for row in range(row_dev // 2):
                for part in range(dim // 128):
                    wide[part, pl.ds((2 * row + dr) * cols + dc, half_cols, stride=2), :] = back[
                        row * half_cols : (row + 1) * half_cols, part * 128 : (part + 1) * 128
                    ]
        rows = slice(batch * tok, (batch + 1) * tok)
        spread = jnp.concatenate([wide[part] for part in range(dim // 128)], axis=1)
        grad_normed = gnormed[rows] + spread * mask_ref[rows]
        x = tokens[batch, 0].reshape(tok, dim).astype(f32)
        normal, rstd = normalize(x)
        grad_x = middle[rows] + normalize_back(grad_normed, normal, rstd, vec_ref[FIRST_G : FIRST_G + 1])
        grad_ref[batch, 0] = grad_x.reshape(row_dev, cols, dim)
        gain_first = gain_first + jnp.sum(grad_normed * normal, axis=0, keepdims=True)
        bias_first = bias_first + jnp.sum(grad_normed, axis=0, keepdims=True)
    index = lax.broadcasted_iota(jnp.int32, (VECS, dim), 0)
    vectors = vec_a[...] + vec_b[...] + vec_c[...]
    vectors = jnp.where(index == FIRST_G, gain_first, vectors)
    vectors = jnp.where(index == FIRST_B, bias_first, vectors)
    gvec_ref[...] = vectors.astype(bf16)


def key_sum_kernel(batches, *refs):
    near, far, outs = take(refs, batches, batches)
    for step, out in enumerate(outs):
        rows = near[0].shape[1]
        for batch in range(batches):
            total = near[batch][step].astype(f32) + far[batch][step].astype(f32)
            out[batch * rows : (batch + 1) * rows] = total.astype(out.dtype)


def owner_kernel(n, tail, keep, arrived, *refs):
    fs = lax.axis_index("fs")
    outs = refs[tail:]
    rows = keep.shape[1]
    for step, out in enumerate(outs):
        place = lax.rem(fs + step, n)
        out[:rows] = (keep[place].astype(f32) + arrived[place].astype(f32)).astype(out.dtype)
        if tail:
            out[rows:] = refs[0][...]


def chip_kernel(keep, arrived, *outs):
    chip = lax.axis_index("sp") // 2
    rows = outs[0].shape[1]
    for step, out in enumerate(outs):
        here = shard_rows(chip ^ step, rows)
        out[...] = (keep[:, here, :].astype(f32) + arrived[:, here, :].astype(f32)).astype(out.dtype)


def chip_sum_kernel(*refs):
    refs[-1][...] = sum_parts(refs[:-1]).astype(refs[-1].dtype)


def owners_kernel(total, keep, arrived, *outs):
    fs = lax.axis_index("fs")
    rows = total.shape[1]
    for step, out in enumerate(outs):
        place = lax.rem(fs + step, len(outs))
        out[:rows] = total[place]
        out[rows:] = (keep[place].astype(f32) + arrived[place].astype(f32)).astype(out.dtype)


def join_kernel(n, *refs):
    group_a, group_b, (out,) = take(refs, n, n)
    rows = group_a[0].shape[0]
    out[:rows] = sum_parts(group_a).astype(out.dtype)
    out[rows:] = sum_parts(group_b).astype(out.dtype)


def merge_kernel(rows, *refs):
    parts, out = refs[:4], refs[4]
    chip = lax.axis_index("sp") // 2
    for step, part in enumerate(parts):
        out[shard_rows(chip ^ step, rows), :] = part[:rows]
    rest = [part[rows:].astype(f32) for part in parts]
    out[4 * rows :] = ((rest[0] + rest[1]) + (rest[2] + rest[3])).astype(out.dtype)


def final_kernel(n_fs, mine, other, *outs):
    query_w, keyval_w, output_w, hidden_w, return_w, reduce_w = outs[:6]
    smalls, hidden_b = outs[6:-1], outs[-1]
    shard, dim = query_w.shape
    half = dim // 2
    fs = lax.axis_index("fs")
    low, high = both_halves(mine, other)
    low, high = low.astype(f32), high.astype(f32)
    for chunk in range(hidden_w.shape[1] // dim):
        hidden_w[:, chunk * dim : (chunk + 1) * dim] = low[chunk * shard : (chunk + 1) * shard]
    return_w[...] = high[:dim]
    low, high = low[dim:], high[dim:]
    query_w[...] = low[:shard]
    keyval_w[:, :dim] = low[shard : 2 * shard]
    keyval_w[:, dim:] = high[:shard]
    output_w[...] = high[shard : 2 * shard]
    low, high = low[2 * shard :], high[2 * shard :]
    reduce_w[:half] = low[:half]
    reduce_w[half:] = high[:half]
    vecs = low[half:] + high[half:]
    lane = lax.broadcasted_iota(jnp.int32, vecs.shape, 1)
    chosen = jnp.where(lane // shard == fs, vecs, 0.0)
    folded = chosen[:, :shard]
    for index in range(1, n_fs):
        folded = folded + chosen[:, index * shard : (index + 1) * shard]
    for index, small in enumerate(smalls):
        small[...] = folded[index : index + 1].reshape(shard)
    row = lax.broadcasted_iota(jnp.int32, vecs.shape, 0)
    hidden_b[...] = jnp.sum(jnp.where(row == HIDDEN_B + fs, vecs, 0.0), axis=0)


def rotate(value, n, step):
    return lax.ppermute(value, "fs", [(i, (i + step) % n) for i in range(n)])


def flip(value, n, bits):
    return lax.ppermute(value, "sp", [(i, i ^ bits) for i in range(n)])


def sum_over_rows(value, n_sp):
    bit = 2
    while bit < n_sp:
        if 2 * bit < n_sp:
            a, b, c = flip(value, n_sp, bit), flip(value, n_sp, 2 * bit), flip(value, n_sp, 3 * bit)
            value = (
                (value.astype(f32) + a.astype(f32)) + (b.astype(f32) + c.astype(f32))
            ).astype(value.dtype)
            bit = 4 * bit
        else:
            a = flip(value, n_sp, bit)
            value = (value.astype(f32) + a.astype(f32)).astype(value.dtype)
            bit = 2 * bit
    return value


def exchange(pieces, n_sp):
    return [pieces[0]] + [flip(pieces[step], n_sp, 2 * step) for step in range(1, n_sp // 2)]


def to_owners(pieces, n_fs):
    return [pieces[0]] + [rotate(pieces[step], n_fs, step) for step in range(1, n_fs)]


def call(kernel, out_shape, in_specs=None, scratch=(), limit=SMALL_VMEM):
    specs = {} if in_specs is None else {"in_specs": in_specs}
    return pl.pallas_call(
        kernel,
        out_shape=out_shape,
        **specs,
        scratch_shapes=scratch,
        compiler_params=pltpu.CompilerParams(vmem_limit_bytes=limit),
        cost_estimate=pl.CostEstimate(flops=0, bytes_accessed=0, transcendentals=0),
    )


def on_device(
    n_fs,
    n_sp,
    tokens,
    cotangent,
    image_sizes,
    first_gain,
    first_bias,
    query_weight,
    query_bias,
    reduce_weight,
    reduce_bias,
    keys_gain,
    keys_bias,
    keyval_weight,
    value_bias,
    output_weight,
    output_bias,
    second_gain,
    second_bias,
    hidden_weight,
    hidden_bias,
    return_weight,
    return_bias,
):
    batches, _, row_dev, cols, dim = tokens.shape
    hid = hidden_weight.shape[1]
    tok = row_dev * cols
    key_dev = tok // 4
    keys = n_sp * key_dev
    shard = dim // n_fs
    half = dim // 2
    vmem = pl.BlockSpec(memory_space=pltpu.VMEM)
    smem = pl.BlockSpec(memory_space=pltpu.SMEM)
    single = keys <= KEY_BLOCK
    split = n_sp == 8
    block = keys if single else KEY_BLOCK
    limit = MAIN_VMEM if single else WHOLE_VMEM

    def shape(*dims, dtype=bf16):
        return jax.ShapeDtypeStruct(dims, dtype)

    smalls = (
        first_gain,
        first_bias,
        query_bias,
        reduce_bias,
        keys_gain,
        keys_bias,
        value_bias,
        output_bias,
        second_gain,
        second_bias,
        return_bias,
    )
    first_half = call(
        functools.partial(pack_first_kernel, n_fs),
        shape(half + VECS + 3 * shard // 2, dim),
        scratch=[pltpu.VMEM((VECS, dim), f32)],
        limit=WHOLE_VMEM,
    )(*smalls, hidden_bias, reduce_weight, query_weight, keyval_weight)
    mine_first = to_owners([first_half] * n_fs, n_fs)[1:]

    begun = call(
        functools.partial(begin_kernel, (n_sp, batches, row_dev, cols, dim)),
        [
            shape(batches * tok, dim, dtype=f32),
            shape(batches * tok, dim, dtype=f32),
            shape(batches, keys, dim),
            shape(dim, dim),
            shape(shard, dim),
            shape(shard, 2 * dim),
            shape(VECS, dim, dtype=f32),
            shape(dim + shard // 2, dim),
        ],
        in_specs=[smem] + [vmem] * 8,
        limit=SMALL_VMEM if single else WHOLE_VMEM,
    )(
        image_sizes,
        tokens,
        reduce_weight,
        query_weight,
        keyval_weight,
        hidden_weight,
        return_weight,
        output_weight,
        first_half,
    )
    normal_first, mask, bias, own_r, own_q, own_kv, own_vec, second_half = begun
    mine_first = call(functools.partial(relay_kernel, n_fs - 1), [shape(*first_half.shape)] * (n_fs - 1))(
        *mine_first, own_vec
    )
    other_first = [flip(piece, n_sp, 1) for piece in mine_first]
    normed, patches, reduced, key_low, whole_reduce, wq, wkv, vec, second_half = call(
        functools.partial(reduce_kernel, (n_fs, batches, row_dev, cols, dim)),
        [
            shape(batches * tok, dim),
            shape(batches * key_dev, 4 * dim),
            shape(batches * key_dev, dim, dtype=f32),
            shape(batches * key_dev, dim),
            shape(n_fs, dim, dim),
            shape(dim, dim),
            shape(dim, 2 * dim),
            shape(VECS, dim, dtype=f32),
            shape(dim + shard // 2, dim),
        ],
        scratch=[pltpu.VMEM((dim // 128, tok, 128), f32)],
    )(normal_first, mask, own_r, own_q, own_kv, own_vec, second_half, *mine_first, *other_first)
    mine_second = to_owners([second_half] * n_fs, n_fs)[1:]

    if split:
        same = exchange([key_low] * (n_sp // 2), n_sp)
        key_pieces = [piece for part in same for piece in (part, flip(part, n_sp, 1))]
    else:
        key_pieces = [lax.all_gather(key_low, "sp")]
    n_pieces = len(key_pieces)

    attended, *kept = call(
        functools.partial(forward_kernel, (batches, tok, key_dev, keys, block, n_pieces)),
        [shape(batches * tok, dim)]
        + [shape(tok, dim)] * batches
        + [shape(keys, 2 * dim)] * batches
        + [shape(dim, tok, dtype=f32)] * batches
        + [shape(PAIRS, 8, 2 * tok, dtype=f32)] * batches
        + [shape(PAIRS, keys, 2 * tok) if single else shape(16, 128)] * batches,
        limit=limit,
    )(normed, vec, bias, wq, wkv, *key_pieces)
    kept = [kept[batch::batches] for batch in range(batches)]
    mine_second = call(functools.partial(relay_kernel, n_fs - 1), [shape(dim + shard // 2, dim)] * (n_fs - 1))(
        *mine_second, kept[0][3]
    )
    other_second = [flip(piece, n_sp, 1) for piece in mine_second]

    acts, normal, rstd, grad_second, keep_a, send_a, wo = call(
        functools.partial(mlp_kernel, (n_fs, batches, row_dev, cols, dim, hid)),
        [
            shape(batches, 1, row_dev, cols, dim, dtype=f32),
            shape(batches * tok, dim, dtype=f32),
            shape(batches * tok, 128, dtype=f32),
            shape(batches * tok + 8, dim, dtype=f32),
            shape(n_fs, dim, dim),
            shape(n_fs, dim, dim),
            shape(dim, dim),
        ],
        scratch=[pltpu.VMEM((dim, hid), bf16), pltpu.VMEM((hid, dim), bf16), pltpu.VMEM((8, dim), f32)],
        limit=limit,
    )(
        tokens,
        cotangent,
        mask,
        attended,
        vec,
        hidden_weight,
        return_weight,
        output_weight,
        *mine_second,
        *other_second,
    )
    arrived_a = flip(send_a, n_sp, 1)
    middle, gatt, gvec_a = call(
        functools.partial(middle_kernel, (batches, tok, hid // dim)),
        [shape(batches * tok, dim, dtype=f32), shape(batches * tok, dim), shape(VECS, dim, dtype=f32)],
        limit=limit,
    )(cotangent, mask, normal, rstd, grad_second, vec, wo)

    if split:
        pieces_a = call(chip_kernel, [shape(n_fs, dim // 4, dim)] * 4)(keep_a, arrived_a)
        total_a = call(chip_sum_kernel, shape(n_fs, dim // 4, dim))(*exchange(pieces_a, n_sp))
    else:
        total_a = vec
    near, far = [], []
    carried = ()
    gkey_dims = (n_sp // 2, key_dev, dim) if split else (n_sp, key_dev, dim)
    for batch in range(batches):
        last = batch == batches - 1
        scratch = [
            pltpu.VMEM((dim, tok), f32),
            pltpu.VMEM((8, 128) if single else (keys, dim), f32),
            pltpu.VMEM((8, 128) if single else (keys, dim), f32),
        ]
        if last:
            more = (*carried, normed, wq, attended, middle, total_a)
            out_shape = [
                shape(n_fs, half, dim),
                shape(n_fs, half, dim),
                shape(batches * tok, dim, dtype=f32),
                shape(*gkey_dims),
                shape(*(gkey_dims if split else (16, 128))),
                shape(VECS, dim, dtype=f32),
            ]
        else:
            more = ()
            out_shape = [
                shape(tok, dim),
                shape(dim, 2 * dim, dtype=f32),
                shape(8, dim, dtype=f32),
                shape(*gkey_dims),
                shape(*(gkey_dims if split else (16, 128))),
            ]
        queries, kvs, attf, stats, probs = kept[batch]
        results = call(
            functools.partial(
                backward_kernel,
                (n_fs, n_sp, batch, last, tok, key_dev, keys, block, n_pieces, batches),
            ),
            out_shape,
            scratch=scratch,
            limit=limit,
        )(gatt, queries, kvs, attf, stats, probs, bias, wkv, *key_pieces, *more)
        if last:
            keep_c, send_c, gnormed, near_b, far_b, gvec_c = results
        else:
            near_b, far_b = results[3:]
            carried = results[:3]
        near.append(near_b)
        far.append(flip(far_b, n_sp, 1) if split else far_b)

    arrived_c = flip(send_c, n_sp, 1)
    if split:
        sums = call(functools.partial(key_sum_kernel, batches), [shape(batches * key_dev, dim)] * 4)(*near, *far)
        parts = exchange(sums, n_sp)
        chunks = call(owners_kernel, [shape(dim // 4 + half, dim)] * n_fs)(total_a, keep_c, arrived_c)
        after = [chunks[0]]
    else:
        parts = [lax.all_to_all(jnp.concatenate(near, axis=1), "sp", 0, 0)]
        after = []

    grad_reduced, gvec_b, keep_b, send_b = call(
        functools.partial(reduction_kernel, len(parts), n_fs),
        [
            shape(batches * key_dev, dim),
            shape(VECS, dim, dtype=f32),
            shape(n_fs, half, dim),
            shape(n_fs, half, dim),
        ],
    )(patches, reduced, vec, *parts, *after)
    arrived_b = flip(send_b, n_sp, 1)
    grads, vectors = call(
        functools.partial(input_kernel, (batches, row_dev, cols, dim)),
        [shape(batches, 1, row_dev, cols, dim, dtype=f32), shape(VECS, dim)],
        scratch=[pltpu.VMEM((dim // 128, tok, 128), f32)],
    )(tokens, middle, gnormed, mask, grad_reduced, whole_reduce, vec, gvec_a, gvec_b, gvec_c)

    chunks_b = call(functools.partial(owner_kernel, n_fs, 1), [shape(half + VECS, dim)] * n_fs)(
        keep_b, arrived_b, vectors
    )
    group_b = to_owners(chunks_b, n_fs)
    if split:
        group_a = to_owners(chunks, n_fs)
        rows = group_a[0].shape[0] + group_b[0].shape[0]
        joined = call(functools.partial(join_kernel, n_fs), shape(rows, dim))(*group_a, *group_b)
        mine = call(functools.partial(merge_kernel, dim // 4), shape(rows + 3 * (dim // 4), dim))(
            *exchange([joined] * 4, n_sp)
        )
    else:
        groups = [group_b]
        for keep, arrived in ((keep_c, arrived_c), (keep_a, arrived_a)):
            pieces = call(functools.partial(owner_kernel, n_fs, 0), [shape(*keep.shape[1:])] * n_fs)(keep, arrived)
            groups.insert(0, to_owners(pieces, n_fs))
        mine = jnp.concatenate(
            [
                sum_over_rows(sum(piece.astype(f32) for piece in group).astype(bf16), n_sp)
                for group in groups
            ],
            axis=0,
        )

    gquery, gkeyval, goutput, ghidden, greturn, greduce, *vectors = call(
        functools.partial(final_kernel, n_fs),
        [
            shape(shard, dim, dtype=f32),
            shape(shard, 2 * dim, dtype=f32),
            shape(shard, dim, dtype=f32),
            shape(shard, hid, dtype=f32),
            shape(dim, dim, dtype=f32),
            shape(dim, dim, dtype=f32),
        ]
        + [shape(shard, dtype=f32)] * HIDDEN_B
        + [shape(dim, dtype=f32)],
    )(mine, flip(mine, n_sp, 1))
    return (
        acts,
        grads,
        vectors[FIRST_G],
        vectors[FIRST_B],
        gquery,
        vectors[QUERY_B],
        greduce,
        vectors[REDUCE_B],
        vectors[KEYS_G],
        vectors[KEYS_B],
        gkeyval,
        vectors[VALUE_B],
        goutput,
        vectors[OUTPUT_B],
        vectors[SECOND_G],
        vectors[SECOND_B],
        ghidden,
        vectors[HIDDEN_B],
        greturn,
        vectors[RETURN_B],
    )


def solution(mesh):
    vec, mat = P("fs"), P("fs", None)
    image = P(None, "fs", "sp", None, None)
    weights = (vec, vec, mat, vec, mat, vec, vec, vec, mat, vec, mat, vec, vec, vec, mat, vec, mat, vec)
    return jax.shard_map(
        functools.partial(on_device, mesh.shape["fs"], mesh.shape["sp"]),
        mesh=mesh,
        in_specs=(image, image, P(None, "fs", None)) + weights,
        out_specs=(image, image) + weights,
        check_vma=False,
    )
```

time: 151 us -> 113 us (0.75)
  waiting for transfers between devices: 45.9 us -> 31.7 us
  blocking collectives: 12.9 us -> 0 us
  Pallas kernels: 45.5 us -> 34.6 us
  starting transfers between devices: 31.2 us -> 36.9 us
  local copies, waits for them, and re-layouts: 13.2 us -> 7.67 us
    ppermute x12, waiting for transfers between devices: 31.1 us -> 9.81 us  [rotate(): return lax.ppermute(value, 'fs', [(i, (i + step) % n) for i in range(n)])]
    all_gather x1 -> x0, blocking collectives: 12.9 us -> none  [on_device(): keys_all = lax.all_gather(key_low, 'sp')]
    pallas_call x7 -> x20, Pallas kernels: 45.5 us -> 34.6 us  [the longest x2 11.3 us: on_device(): call(functools.partial(backward_kernel, (n_fs, n_sp, batch, last, tok, ke...]
    ppermute x20 -> x28, waiting for transfers between devices: 14.7 us -> 21.9 us  [flip(): return lax.ppermute(value, 'sp', [(i, i ^ bits) for i in range(n)])]
    ppermute x20 -> x28, starting transfers between devices: 19.6 us -> 22.6 us  [flip(): return lax.ppermute(value, 'sp', [(i, i ^ bits) for i in range(n)])]
    ppermute x12, starting transfers between devices: 11.6 us -> 14.3 us  [rotate(): return lax.ppermute(value, 'fs', [(i, (i + step) % n) for i in range(n)])]
    unnamed x92 -> x28, local copies, waits for them, and re-layouts: 10.2 us -> 7.67 us
    squeeze x1 -> x0, local copies, waits for them, and re-layouts: 1.53 us -> none  [on_device(): vectors = [gvecs[index, :shard] for index in range(HIDDEN_B)]]
  transfers between devices with their start and end apart: 32 -> 40, of which waited for: 12 -> 24; matrix products, arithmetic and copies ran while one was open for 1% -> 0% of each run, Pallas kernels for 9% -> 21%
where the time goes in v2:
time: 113 us; the launch traced here: 112 us
  starting transfers between devices  36.9 us (33%)
  Pallas kernels  34.6 us (31%)
  waiting for transfers between devices  31.7 us (28%)
  local copies, waits for them, and re-layouts  7.67 us (7%)
    ppermute x28, starting transfers between devices, flip(): return lax.ppermute(value, 'sp', [(i, i ^ bits) for i in range(n)])  22.6 us
    ppermute x28, waiting for transfers between devices, flip(): return lax.ppermute(value, 'sp', [(i, i ^ bits) for i in range(n)])  21.9 us
    ppermute x12, starting transfers between devices, rotate(): return lax.ppermute(value, 'fs', [(i, (i + step) % n) for i in range(n)])  14.3 us
    pallas_call x2, Pallas kernels, on_device(): call(functools.partial(backward_kernel, (n_fs, n_sp, batch, last, tok, ke...  11.3 us
    ppermute x12, waiting for transfers between devices, rotate(): return lax.ppermute(value, 'fs', [(i, (i + step) % n) for i in range(n)])  9.81 us
    pallas_call x1, Pallas kernels, on_device(): call(functools.partial(forward_kernel, (batches, tok, key_dev, keys, bloc...  8.35 us
    unnamed x28, local copies, waits for them, and re-layouts  7.67 us
    pallas_call x1, Pallas kernels, on_device(): call(functools.partial(mlp_kernel, (n_fs, batches, row_dev, cols, dim, hi...  6.71 us
  transfers between devices with their start and end apart: 40, of which 24 were waited for; matrix products, arithmetic and copies ran while one was open for 0% of the time, Pallas kernels for 21%

profile of v2, /device:TPU:9, one launch (start us, length us, event | category | flops | bytes accessed | tf_op | source)
XLA Modules:
  0.0 112.0 jit_solution(7842060404161243921)
XLA Ops:
  0.7 1.9 %shard_map.356.packed = bf16[240,256]{1,0:T(8,128)(2,1)} custom-call(bf16[64]{0:T(256)(128)(2,1)} %refs_0_.2, bf16[64]{0:T(256)(128)(2,1)} %refs_1_.2, bf16[64]{0:T(256)(128)(2,1)} %refs_2_.1, bf16[64]{0:T(256)(128)(2,1)} %refs_3_.1, bf16[64]{0:T(256)(128)(2,1)} %refs_4_.1, bf16[64]{0:T(256)(128)(2,1)} %refs_5_.2, bf16[64]{0:T(256)(128)(2,1)} %refs_6_.2, ...), custom_call_target="tpu_custom_call" | custom-call | tf_op jit(solution)/shard_map/pallas_call | solution.py:811
  2.6 2.5 %collective-permute-start.1 = (bf16[240,256]{1,0:T(8,128)(2,1)}, bf16[240,256]{1,0:T(8,128)(2,1)S(1)}, u32[]{:S(2)}, u32[]{:S(2)}) collective-permute-start(bf16[240,256]{1,0:T(8,128)(2,1)} %shard_map.356.packed), channel_id=1, source_target_pairs={{0,2},{1,3},{2,0},{3,1},{4,6},{5,7},{6,4},{7,5},{8,10},{9,11},{10,... | collective-permute-start | bytes 368648 | tf_op jit(solution)/shard_map/ppermute | solution.py:713
  5.0 2.2 %collective-permute-start = (bf16[240,256]{1,0:T(8,128)(2,1)}, bf16[240,256]{1,0:T(8,128)(2,1)S(1)}, u32[]{:S(2)}, u32[]{:S(2)}) collective-permute-start(bf16[240,256]{1,0:T(8,128)(2,1)} %shard_map.356.packed), channel_id=1, source_target_pairs={{0,1},{1,2},{2,3},{3,0},{4,5},{5,6},{6,7},{7,4},{8,9},{9,10},{10,1... | collective-permute-start | bytes 368648 | tf_op jit(solution)/shard_map/ppermute | solution.py:713
  7.2 1.0 copy-done
  8.2 0.9 copy-done.3
  9.1 0.9 copy-done.5
  10.0 0.9 copy-done.7
  10.9 0.9 copy-done.8
  14.9 1.2 %shard_map.357 = (f32[768,256]{1,0:T(8,128)S(1)}, f32[768,256]{1,0:T(8,128)S(1)}, bf16[2,768,256]{2,1,0:T(8,128)(2,1)S(1)}, bf16[256,256]{1,0:T(8,128)(2,1)S(1)}...) custom-call(s32[2,1,2]{2,1,0:T(1,128)S(1)} %copy-done.13, ...), custom_call_target="tpu_custom_call" | custom-call | tf_op jit(solution)/shard_map/pallas_call | solution.py:819
  16.2 1.6 %collective-permute-start.3 = (bf16[240,256]{1,0:T(8,128)(2,1)S(1)}, bf16[240,256]{1,0:T(8,128)(2,1)S(1)}, u32[]{:S(2)}, u32[]{:S(2)}) collective-permute-start(bf16[240,256]{1,0:T(8,128)(2,1)S(1)} %get-tuple-element.122.refs_7_), channel_id=1, source_target_pairs={{0,4},{4,0},{8,12},{12,8},{16,20},{20,16},{24,28},{28,24},{1,5},{5... | collective-permute-start | bytes 368648 | tf_op jit(solution)/shard_map/ppermute | solution.py:717
  20.0 2.2 %collective-permute-start.11 = (bf16[192,256]{1,0:T(8,128)(2,1)S(1)}, bf16[192,256]{1,0:T(8,128)(2,1)S(1)}, u32[]{:S(2)}, u32[]{:S(2)}) collective-permute-start(bf16[192,256]{1,0:T(8,128)(2,1)S(1)} %get-tuple-element.130.refs_5_.refs_8_), channel_id=1, source_target_pairs={{0,24},{4,28},{8,16},{12,20},{16,8},{20,12},{24,0},{28,4},{1,25},{... | collective-permute-start | bytes 294920 | tf_op jit(solution)/shard_map/ppermute | solution.py:717
  22.7 1.2 %collective-permute-start.6 = (bf16[192,256]{1,0:T(8,128)(2,1)S(1)}, bf16[192,256]{1,0:T(8,128)(2,1)S(1)}, u32[]{:S(2)}, u32[]{:S(2)}) collective-permute-start(bf16[192,256]{1,0:T(8,128)(2,1)S(1)} %get-tuple-element.130.refs_5_.refs_8_), channel_id=1, source_target_pairs={{0,4},{4,0},{8,12},{12,8},{16,20},{20,16},{24,28},{28,24},{1,5},{5... | collective-permute-start | bytes 294920 | tf_op jit(solution)/shard_map/ppermute | solution.py:717
  23.9 1.1 %collective-permute-done.11.refs_11_.refs_14_ = bf16[192,256]{1,0:T(8,128)(2,1)S(1)} collective-permute-done((bf16[192,256]{1,0:T(8,128)(2,1)S(1)}, bf16[192,256]{1,0:T(8,128)(2,1)S(1)}, u32[]{:S(2)}, u32[]{:S(2)}) %collective-permute-start.11) | collective-permute-done | bytes 98336 | tf_op jit(solution)/shard_map/ppermute | solution.py:717
  25.0 1.2 %collective-permute-start.12 = (bf16[192,256]{1,0:T(8,128)(2,1)S(1)}, bf16[192,256]{1,0:T(8,128)(2,1)S(1)}, u32[]{:S(2)}, u32[]{:S(2)}) collective-permute-start(bf16[192,256]{1,0:T(8,128)(2,1)S(1)} %collective-permute-done.11.refs_11_.refs_14_), channel_id=1, source_target_pairs={{0,4},{4,0},{8,12},{12,8},{16,20},{20,16},{24,28},{28,24},{1,5},{5... | collective-permute-start | bytes 294920 | tf_op jit(solution)/shard_map/ppermute | solution.py:717
  26.4 1.2 %collective-permute-done.9.refs_9_.refs_12_ = bf16[192,256]{1,0:T(8,128)(2,1)S(1)} collective-permute-done((bf16[192,256]{1,0:T(8,128)(2,1)S(1)}, bf16[192,256]{1,0:T(8,128)(2,1)S(1)}, u32[]{:S(2)}, u32[]{:S(2)}) %collective-permute-start.9) | collective-permute-done | bytes 98336 | tf_op jit(solution)/shard_map/ppermute | solution.py:717
  27.6 1.0 collective-permute-start.14
  29.2 0.9 collective-permute-start.10
  31.5 8.4 %shard_map.360 = (bf16[768,256]{1,0:T(8,128)(2,1)S(1)}, bf16[384,256]{1,0:T(8,128)(2,1)S(1)}, bf16[384,256]{1,0:T(8,128)(2,1)S(1)}, bf16[768,512]{1,0:T(8,128)(2...) custom-call(bf16[768,256]{1,0:T(8,128)(2,1)S(1)} %get-tuple-element., ...), custom_call_target="tpu_custom_call" | custom-call | tf_op jit(solution)/shard_map/pallas_call | solution.py:873
  39.8 1.0 collective-permute-done.13.refs_0_
  43.0 6.7 %shard_map.362 = (f32[2,1,2,192,256]{4,3,2,1,0:T(8,128)}, f32[768,256]{1,0:T(8,128)S(1)}, f32[768,128]{1,0:T(8,128)S(1)}, f32[776,256]{1,0:T(8,128)S(1)}, bf16[4...) custom-call(bf16[2,1,2,192,256]{4,3,2,1,0:T(8,128)(2,1)S(1)} %copy-done.1, ...), custom_call_target="tpu_custom_call" | custom-call | tf_op jit(solution)/shard_map/pallas_call | solution.py:889
  50.0 1.6 %collective-permute-done.19.arrived = bf16[4,256,256]{2,1,0:T(8,128)(2,1)S(1)} collective-permute-done((bf16[4,256,256]{2,1,0:T(8,128)(2,1)S(1)}, bf16[4,256,256]{2,1,0:T(8,128)(2,1)S(1)}, u32[]{:S(2)}, u32[]{:S(2)}) %collective-permute-start.19) | collective-permute-done | bytes 524320 | tf_op jit(solution)/shard_map/ppermute | solution.py:717
  51.8 1.9 %collective-permute-start.20 = (bf16[4,64,256]{2,1,0:T(8,128)(2,1)S(1)}, bf16[4,64,256]{2,1,0:T(8,128)(2,1)S(1)}, u32[]{:S(2)}, u32[]{:S(2)}) collective-permute-start(bf16[4,64,256]{2,1,0:T(8,128)(2,1)S(1)} %get-tuple-element.159), channel_id=1, source_target_pairs={{0,8},{4,12},{8,0},{12,4},{16,24},{20,28},{24,16},{28,20},{1,9},{5... | collective-permute-start | bytes 393224 | tf_op jit(solution)/shard_map/ppermute | solution.py:717
  53.6 1.4 %collective-permute-start.21 = (bf16[4,64,256]{2,1,0:T(8,128)(2,1)S(1)}, bf16[4,64,256]{2,1,0:T(8,128)(2,1)S(1)}, u32[]{:S(2)}, u32[]{:S(2)}) collective-permute-start(bf16[4,64,256]{2,1,0:T(8,128)(2,1)S(1)} %get-tuple-element.160), channel_id=1, source_target_pairs={{0,16},{4,20},{8,24},{12,28},{16,0},{20,4},{24,8},{28,12},{1,17},{... | collective-permute-start | bytes 393224 | tf_op jit(solution)/shard_map/ppermute | solution.py:717
  55.7 5.4 %shard_map.364 = (bf16[384,256]{1,0:T(8,128)(2,1)S(1)}, f32[256,512]{1,0:T(8,128)S(1)}, f32[8,256]{1,0:T(8,128)S(1)}, bf16[4,96,256]{2,1,0:T(8,128)(2,1)S(1)}, bf16[4,96,256]{2,1,0:T(8,128)(2,1)S(1)}) custom-call(bf16[768,256]{1,0:T(8,128)(2,1)S(1)} %get-tuple-element.143.refs_0_, bf16[384,256]{1,0:T(8,128)(2,1)S(1)} %get-tuple-element.149.refs_1_, ...), custom_call_target="tpu_custom_call" | custom-call | tf_op jit(solution)/shard_map/pallas_call | solution.py:956
  61.1 1.0 collective-permute-start.23
  62.2 5.8 %shard_map.367 = (bf16[4,128,256]{2,1,0:T(8,128)(2,1)S(1)}, bf16[4,128,256]{2,1,0:T(8,128)(2,1)S(1)}, f32[768,256]{1,0:T(8,128)S(1)}, bf16[4,96,256]{2,1,0:T(8,1...) custom-call(bf16[768,256]{1,0:T(8,128)(2,1)S(1)} %get-tuple-element.143.refs_0_, ...), custom_call_target="tpu_custom_call" | custom-call | tf_op jit(solution)/shard_map/pallas_call | solution.py:956
  68.6 0.9 collective-permute-done.24.refs_3_
  69.6 1.6 %collective-permute-start.25 = (bf16[192,256]{1,0:T(8,128)(2,1)S(1)}, bf16[192,256]{1,0:T(8,128)(2,1)S(1)}, u32[]{:S(2)}, u32[]{:S(2)}) collective-permute-start(bf16[192,256]{1,0:T(8,128)(2,1)S(1)} %get-tuple-element.170), channel_id=1, source_target_pairs={{0,8},{4,12},{8,0},{12,4},{16,24},{20,28},{24,16},{28,20},{1,9},{5... | collective-permute-start | bytes 294920 | tf_op jit(solution)/shard_map/ppermute | solution.py:717
  71.2 1.4 %collective-permute-start.26 = (bf16[192,256]{1,0:T(8,128)(2,1)S(1)}, bf16[192,256]{1,0:T(8,128)(2,1)S(1)}, u32[]{:S(2)}, u32[]{:S(2)}) collective-permute-start(bf16[192,256]{1,0:T(8,128)(2,1)S(1)} %get-tuple-element.171), channel_id=1, source_target_pairs={{0,16},{4,20},{8,24},{12,28},{16,0},{20,4},{24,8},{28,12},{1,17},{... | collective-permute-start | bytes 294920 | tf_op jit(solution)/shard_map/ppermute | solution.py:717
  72.7 1.3 %collective-permute-done.25.refs_1_ = bf16[192,256]{1,0:T(8,128)(2,1)S(1)} collective-permute-done((bf16[192,256]{1,0:T(8,128)(2,1)S(1)}, bf16[192,256]{1,0:T(8,128)(2,1)S(1)}, u32[]{:S(2)}, u32[]{:S(2)}) %collective-permute-start.25) | collective-permute-done | bytes 98336 | tf_op jit(solution)/shard_map/ppermute | solution.py:717
  74.0 1.2 %collective-permute-done.26.refs_2_ = bf16[192,256]{1,0:T(8,128)(2,1)S(1)} collective-permute-done((bf16[192,256]{1,0:T(8,128)(2,1)S(1)}, bf16[192,256]{1,0:T(8,128)(2,1)S(1)}, u32[]{:S(2)}, u32[]{:S(2)}) %collective-permute-start.26) | collective-permute-done | bytes 98336 | tf_op jit(solution)/shard_map/ppermute | solution.py:717
  75.2 1.8 %collective-permute-done.27.refs_3_ = bf16[192,256]{1,0:T(8,128)(2,1)S(1)} collective-permute-done((bf16[192,256]{1,0:T(8,128)(2,1)S(1)}, bf16[192,256]{1,0:T(8,128)(2,1)S(1)}, u32[]{:S(2)}, u32[]{:S(2)}) %collective-permute-start.27) | collective-permute-done | bytes 98336 | tf_op jit(solution)/shard_map/ppermute | solution.py:717
  77.6 1.9 %collective-permute-start.32 = (bf16[4,128,256]{2,1,0:T(8,128)(2,1)S(1)}, bf16[4,128,256]{2,1,0:T(8,128)(2,1)S(1)}, u32[]{:S(2)}, u32[]{:S(2)}) collective-permute-start(bf16[4,128,256]{2,1,0:T(8,128)(2,1)S(1)} %get-tuple-element.186), channel_id=1, source_target_pairs={{0,4},{4,0},{8,12},{12,8},{16,20},{20,16},{24,28},{28,24},{1,5},{5... | collective-permute-start | bytes 786440 | tf_op jit(solution)/shard_map/ppermute | solution.py:717
  79.5 2.2 %collective-permute-start.29 = (bf16[192,256]{1,0:T(8,128)(2,1)S(1)}, bf16[192,256]{1,0:T(8,128)(2,1)S(1)}, u32[]{:S(2)}, u32[]{:S(2)}) collective-permute-start(bf16[192,256]{1,0:T(8,128)(2,1)S(1)} %get-tuple-element.182), channel_id=1, source_target_pairs={{0,1},{1,2},{2,3},{3,0},{4,5},{5,6},{6,7},{7,4},{8,9},{9,10},{10,1... | collective-permute-start | bytes 294920 | tf_op jit(solution)/shard_map/ppermute | solution.py:713
  81.7 1.7 %collective-permute-start.30 = (bf16[192,256]{1,0:T(8,128)(2,1)S(1)}, bf16[192,256]{1,0:T(8,128)(2,1)S(1)}, u32[]{:S(2)}, u32[]{:S(2)}) collective-permute-start(bf16[192,256]{1,0:T(8,128)(2,1)S(1)} %get-tuple-element.183), channel_id=1, source_target_pairs={{0,2},{1,3},{2,0},{3,1},{4,6},{5,7},{6,4},{7,5},{8,10},{9,11},{10,... | collective-permute-start | bytes 294920 | tf_op jit(solution)/shard_map/ppermute | solution.py:713
  83.4 1.7 %shard_map.371 = (f32[2,1,2,192,256]{4,3,2,1,0:T(8,128)}, bf16[16,256]{1,0:T(8,128)(2,1)S(1)}) custom-call(bf16[2,1,2,192,256]{4,3,2,1,0:T(8,128)(2,1)S(1)} %copy-done.1, f32[768,256]{1,0:T(8,128)S(1)} %get-tuple-element.142.refs_22_.middle, f32[768,256]{1,0:T(8,128)S(1)} %get-tuple-element.162.gnormed, ...), custom_call_target="tpu_custom_call" | custom-call | tf_op jit(solution)/shard_map/pallas_call | solution.py:993
  85.1 1.5 %collective-permute-start.33 = (bf16[144,256]{1,0:T(8,128)(2,1)S(1)}, bf16[144,256]{1,0:T(8,128)(2,1)S(1)}, u32[]{:S(2)}, u32[]{:S(2)}) collective-permute-start(bf16[144,256]{1,0:T(8,128)(2,1)S(1)} %get-tuple-element.189), channel_id=1, source_target_pairs={{0,1},{1,2},{2,3},{3,0},{4,5},{5,6},{6,7},{7,4},{8,9},{9,10},{10,1... | collective-permute-start | bytes 221192 | tf_op jit(solution)/shard_map/ppermute | solution.py:713
  86.6 2.5 %collective-permute-start.34 = (bf16[144,256]{1,0:T(8,128)(2,1)S(1)}, bf16[144,256]{1,0:T(8,128)(2,1)S(1)}, u32[]{:S(2)}, u32[]{:S(2)}) collective-permute-start(bf16[144,256]{1,0:T(8,128)(2,1)S(1)} %get-tuple-element.190), channel_id=1, source_target_pairs={{0,2},{1,3},{2,0},{3,1},{4,6},{5,7},{6,4},{7,5},{8,10},{9,11},{10,... | collective-permute-start | bytes 221192 | tf_op jit(solution)/shard_map/ppermute | solution.py:713
  89.1 3.3 %collective-permute-done.30.refs_2_ = bf16[192,256]{1,0:T(8,128)(2,1)S(1)} collective-permute-done((bf16[192,256]{1,0:T(8,128)(2,1)S(1)}, bf16[192,256]{1,0:T(8,128)(2,1)S(1)}, u32[]{:S(2)}, u32[]{:S(2)}) %collective-permute-start.30) | collective-permute-done | bytes 98336 | tf_op jit(solution)/shard_map/ppermute | solution.py:713
  92.4 2.1 %collective-permute-done.31.refs_3_ = bf16[192,256]{1,0:T(8,128)(2,1)S(1)} collective-permute-done((bf16[192,256]{1,0:T(8,128)(2,1)S(1)}, bf16[192,256]{1,0:T(8,128)(2,1)S(1)}, u32[]{:S(2)}, u32[]{:S(2)}) %collective-permute-start.31) | collective-permute-done | bytes 98336 | tf_op jit(solution)/shard_map/ppermute | solution.py:713
  94.9 1.6 %collective-permute-done.34.refs_6_ = bf16[144,256]{1,0:T(8,128)(2,1)S(1)} collective-permute-done((bf16[144,256]{1,0:T(8,128)(2,1)S(1)}, bf16[144,256]{1,0:T(8,128)(2,1)S(1)}, u32[]{:S(2)}, u32[]{:S(2)}) %collective-permute-start.34) | collective-permute-done | bytes 73760 | tf_op jit(solution)/shard_map/ppermute | solution.py:713
  96.5 1.4 %collective-permute-done.35.refs_7_ = bf16[144,256]{1,0:T(8,128)(2,1)S(1)} collective-permute-done((bf16[144,256]{1,0:T(8,128)(2,1)S(1)}, bf16[144,256]{1,0:T(8,128)(2,1)S(1)}, u32[]{:S(2)}, u32[]{:S(2)}) %collective-permute-start.35) | collective-permute-done | bytes 73760 | tf_op jit(solution)/shard_map/ppermute | solution.py:713
  98.0 1.1 collective-permute-start.38
  99.1 1.0 collective-permute-start.37
  100.7 3.2 %collective-permute-done.38.refs_3_ = bf16[336,256]{1,0:T(8,128)(2,1)S(1)} collective-permute-done((bf16[336,256]{1,0:T(8,128)(2,1)S(1)}, bf16[336,256]{1,0:T(8,128)(2,1)S(1)}, u32[]{:S(2)}, u32[]{:S(2)}) %collective-permute-start.38) | collective-permute-done | bytes 172064 | tf_op jit(solution)/shard_map/ppermute | solution.py:717
  103.9 5.0 %collective-permute-done.37.refs_2_ = bf16[336,256]{1,0:T(8,128)(2,1)S(1)} collective-permute-done((bf16[336,256]{1,0:T(8,128)(2,1)S(1)}, bf16[336,256]{1,0:T(8,128)(2,1)S(1)}, u32[]{:S(2)}, u32[]{:S(2)}) %collective-permute-start.37) | collective-permute-done | bytes 172064 | tf_op jit(solution)/shard_map/ppermute | solution.py:717
  109.6 1.2 %collective-permute-done.39.other = bf16[528,256]{1,0:T(8,128)(2,1)S(1)} collective-permute-done((bf16[528,256]{1,0:T(8,128)(2,1)S(1)}, bf16[528,256]{1,0:T(8,128)(2,1)S(1)}, u32[]{:S(2)}, u32[]{:S(2)}) %collective-permute-start.39) | collective-permute-done | bytes 270368 | tf_op jit(solution)/shard_map/ppermute | solution.py:717
  110.8 1.0 shard_map.375
  (80 shorter events, 14.3 us)
Async XLA Ops:
  0.7 42.3 %copy-start.6 = (bf16[256,256]{1,0:T(8,128)(2,1)S(1)}, bf16[256,256]{1,0:T(8,128)(2,1)}, u32[]{:S(2)}) copy-start(bf16[256,256]{1,0:T(8,128)(2,1)} %refs_6_.3) | copy-start | bytes 393220
  0.7 42.3 %copy-start.4 = (bf16[64,1024]{1,0:T(8,128)(2,1)S(1)}, bf16[64,1024]{1,0:T(8,128)(2,1)}, u32[]{:S(2)}) copy-start(bf16[64,1024]{1,0:T(8,128)(2,1)} %refs_5_.3) | copy-start | bytes 393220
  0.7 42.3 %copy-start.11 = (bf16[64,256]{1,0:T(8,128)(2,1)S(1)}, bf16[64,256]{1,0:T(8,128)(2,1)}, u32[]{:S(2)}) copy-start(bf16[64,256]{1,0:T(8,128)(2,1)} %refs_7_.3) | copy-start | bytes 98308
  2.6 13.5 %collective-permute-start.2 = (bf16[240,256]{1,0:T(8,128)(2,1)}, bf16[240,256]{1,0:T(8,128)(2,1)S(1)}, u32[]{:S(2)}, u32[]{:S(2)}) collective-permute-start(bf16[240,256]{1,0:T(8,128)(2,1)} %shard_map.356.packed), channel_id=1, source_target_pairs={{0,3},{1,0},{2,1},{3,2},{4,7},{5,4},{6,5},{7,6},{8,11},{9,8},{10,9... | collective-permute-start | bytes 368648 | tf_op jit(solution)/shard_map/ppermute | solution.py:713
  2.6 13.5 %collective-permute-start.1 = (bf16[240,256]{1,0:T(8,128)(2,1)}, bf16[240,256]{1,0:T(8,128)(2,1)S(1)}, u32[]{:S(2)}, u32[]{:S(2)}) collective-permute-start(bf16[240,256]{1,0:T(8,128)(2,1)} %shard_map.356.packed), channel_id=1, source_target_pairs={{0,2},{1,3},{2,0},{3,1},{4,6},{5,7},{6,4},{7,5},{8,10},{9,11},{10,... | collective-permute-start | bytes 368648 | tf_op jit(solution)/shard_map/ppermute | solution.py:713
  5.0 11.1 %collective-permute-start = (bf16[240,256]{1,0:T(8,128)(2,1)}, bf16[240,256]{1,0:T(8,128)(2,1)S(1)}, u32[]{:S(2)}, u32[]{:S(2)}) collective-permute-start(bf16[240,256]{1,0:T(8,128)(2,1)} %shard_map.356.packed), channel_id=1, source_target_pairs={{0,1},{1,2},{2,3},{3,0},{4,5},{5,6},{6,7},{7,4},{8,9},{9,10},{10,1... | collective-permute-start | bytes 368648 | tf_op jit(solution)/shard_map/ppermute | solution.py:713
  7.2 1.0 copy-start
  9.1 0.9 copy-start.5
  10.0 0.9 copy-start.7
  14.9 28.1 %copy-start.1 = (bf16[2,1,2,192,256]{4,3,2,1,0:T(8,128)(2,1)S(1)}, bf16[2,1,2,192,256]{4,3,2,1,0:T(8,128)(2,1)}, u32[]{:S(2)}) copy-start(bf16[2,1,2,192,256]{4,3,2,1,0:T(8,128)(2,1)} %tokens.3) | copy-start | bytes 1179652
  14.9 28.1 %copy-start.2 = (f32[2,1,2,192,256]{4,3,2,1,0:T(8,128)S(1)}, f32[2,1,2,192,256]{4,3,2,1,0:T(8,128)}, u32[]{:S(2)}) copy-start(f32[2,1,2,192,256]{4,3,2,1,0:T(8,128)} %cotangent.1) | copy-start | bytes 2359300
  16.2 2.6 %collective-permute-start.3 = (bf16[240,256]{1,0:T(8,128)(2,1)S(1)}, bf16[240,256]{1,0:T(8,128)(2,1)S(1)}, u32[]{:S(2)}, u32[]{:S(2)}) collective-permute-start(bf16[240,256]{1,0:T(8,128)(2,1)S(1)} %get-tuple-element.122.refs_7_), channel_id=1, source_target_pairs={{0,4},{4,0},{8,12},{12,8},{16,20},{20,16},{24,28},{28,24},{1,5},{5... | collective-permute-start | bytes 368648 | tf_op jit(solution)/shard_map/ppermute | solution.py:717
  17.7 1.3 %collective-permute-start.4 = (bf16[240,256]{1,0:T(8,128)(2,1)S(1)}, bf16[240,256]{1,0:T(8,128)(2,1)S(1)}, u32[]{:S(2)}, u32[]{:S(2)}) collective-permute-start(bf16[240,256]{1,0:T(8,128)(2,1)S(1)} %get-tuple-element.123.refs_8_), channel_id=1, source_target_pairs={{0,4},{4,0},{8,12},{12,8},{16,20},{20,16},{24,28},{28,24},{1,5},{5... | collective-permute-start | bytes 368648 | tf_op jit(solution)/shard_map/ppermute | solution.py:717
  17.8 1.4 %collective-permute-start.5 = (bf16[240,256]{1,0:T(8,128)(2,1)S(1)}, bf16[240,256]{1,0:T(8,128)(2,1)S(1)}, u32[]{:S(2)}, u32[]{:S(2)}) collective-permute-start(bf16[240,256]{1,0:T(8,128)(2,1)S(1)} %get-tuple-element.124.refs_9_), channel_id=1, source_target_pairs={{0,4},{4,0},{8,12},{12,8},{16,20},{20,16},{24,28},{28,24},{1,5},{5... | collective-permute-start | bytes 368648 | tf_op jit(solution)/shard_map/ppermute | solution.py:717
  20.0 5.0 %collective-permute-start.11 = (bf16[192,256]{1,0:T(8,128)(2,1)S(1)}, bf16[192,256]{1,0:T(8,128)(2,1)S(1)}, u32[]{:S(2)}, u32[]{:S(2)}) collective-permute-start(bf16[192,256]{1,0:T(8,128)(2,1)S(1)} %get-tuple-element.130.refs_5_.refs_8_), channel_id=1, source_target_pairs={{0,24},{4,28},{8,16},{12,20},{16,8},{20,12},{24,0},{28,4},{1,25},{... | collective-permute-start | bytes 294920 | tf_op jit(solution)/shard_map/ppermute | solution.py:717
  22.2 5.4 %collective-permute-start.9 = (bf16[192,256]{1,0:T(8,128)(2,1)S(1)}, bf16[192,256]{1,0:T(8,128)(2,1)S(1)}, u32[]{:S(2)}, u32[]{:S(2)}) collective-permute-start(bf16[192,256]{1,0:T(8,128)(2,1)S(1)} %get-tuple-element.130.refs_5_.refs_8_), channel_id=1, source_target_pairs={{0,16},{4,20},{8,24},{12,28},{16,0},{20,4},{24,8},{28,12},{1,17},{... | collective-permute-start | bytes 294920 | tf_op jit(solution)/shard_map/ppermute | solution.py:717
  22.4 6.2 %collective-permute-start.7 = (bf16[192,256]{1,0:T(8,128)(2,1)S(1)}, bf16[192,256]{1,0:T(8,128)(2,1)S(1)}, u32[]{:S(2)}, u32[]{:S(2)}) collective-permute-start(bf16[192,256]{1,0:T(8,128)(2,1)S(1)} %get-tuple-element.130.refs_5_.refs_8_), channel_id=1, source_target_pairs={{0,8},{4,12},{8,0},{12,4},{16,24},{20,28},{24,16},{28,20},{1,9},{5... | collective-permute-start | bytes 294920 | tf_op jit(solution)/shard_map/ppermute | solution.py:717
  22.7 6.5 %collective-permute-start.6 = (bf16[192,256]{1,0:T(8,128)(2,1)S(1)}, bf16[192,256]{1,0:T(8,128)(2,1)S(1)}, u32[]{:S(2)}, u32[]{:S(2)}) collective-permute-start(bf16[192,256]{1,0:T(8,128)(2,1)S(1)} %get-tuple-element.130.refs_5_.refs_8_), channel_id=1, source_target_pairs={{0,4},{4,0},{8,12},{12,8},{16,20},{20,16},{24,28},{28,24},{1,5},{5... | collective-permute-start | bytes 294920 | tf_op jit(solution)/shard_map/ppermute | solution.py:717
  25.0 5.2 %collective-permute-start.12 = (bf16[192,256]{1,0:T(8,128)(2,1)S(1)}, bf16[192,256]{1,0:T(8,128)(2,1)S(1)}, u32[]{:S(2)}, u32[]{:S(2)}) collective-permute-start(bf16[192,256]{1,0:T(8,128)(2,1)S(1)} %collective-permute-done.11.refs_11_.refs_14_), channel_id=1, source_target_pairs={{0,4},{4,0},{8,12},{12,8},{16,20},{20,16},{24,28},{28,24},{1,5},{5... | collective-permute-start | bytes 294920 | tf_op jit(solution)/shard_map/ppermute | solution.py:717
  26.2 13.6 %collective-permute-start.15 = (bf16[288,256]{1,0:T(8,128)(2,1)S(1)}, bf16[288,256]{1,0:T(8,128)(2,1)S(1)}, u32[]{:S(2)}, u32[]{:S(2)}) collective-permute-start(bf16[288,256]{1,0:T(8,128)(2,1)S(1)} %get-tuple-element.132), channel_id=1, source_target_pairs={{0,3},{1,0},{2,1},{3,2},{4,7},{5,4},{6,5},{7,6},{8,11},{9,8},{10,9... | collective-permute-start | bytes 442376 | tf_op jit(solution)/shard_map/ppermute | solution.py:713
  27.6 12.2 %collective-permute-start.14 = (bf16[288,256]{1,0:T(8,128)(2,1)S(1)}, bf16[288,256]{1,0:T(8,128)(2,1)S(1)}, u32[]{:S(2)}, u32[]{:S(2)}) collective-permute-start(bf16[288,256]{1,0:T(8,128)(2,1)S(1)} %get-tuple-element.132), channel_id=1, source_target_pairs={{0,2},{1,3},{2,0},{3,1},{4,6},{5,7},{6,4},{7,5},{8,10},{9,11},{10,... | collective-permute-start | bytes 442376 | tf_op jit(solution)/shard_map/ppermute | solution.py:713
  28.7 12.2 %collective-permute-start.13 = (bf16[288,256]{1,0:T(8,128)(2,1)S(1)}, bf16[288,256]{1,0:T(8,128)(2,1)S(1)}, u32[]{:S(2)}, u32[]{:S(2)}) collective-permute-start(bf16[288,256]{1,0:T(8,128)(2,1)S(1)} %get-tuple-element.132), channel_id=1, source_target_pairs={{0,1},{1,2},{2,3},{3,0},{4,5},{5,6},{6,7},{7,4},{8,9},{9,10},{10,1... | collective-permute-start | bytes 442376 | tf_op jit(solution)/shard_map/ppermute | solution.py:713
  29.2 1.9 %collective-permute-start.10 = (bf16[192,256]{1,0:T(8,128)(2,1)S(1)}, bf16[192,256]{1,0:T(8,128)(2,1)S(1)}, u32[]{:S(2)}, u32[]{:S(2)}) collective-permute-start(bf16[192,256]{1,0:T(8,128)(2,1)S(1)} %collective-permute-done.9.refs_9_.refs_12_), channel_id=1, source_target_pairs={{0,4},{4,0},{8,12},{12,8},{16,20},{20,16},{24,28},{28,24},{1,5},{5... | collective-permute-start | bytes 294920 | tf_op jit(solution)/shard_map/ppermute | solution.py:717
  30.2 1.3 %collective-permute-start.8 = (bf16[192,256]{1,0:T(8,128)(2,1)S(1)}, bf16[192,256]{1,0:T(8,128)(2,1)S(1)}, u32[]{:S(2)}, u32[]{:S(2)}) collective-permute-start(bf16[192,256]{1,0:T(8,128)(2,1)S(1)} %collective-permute-done.7.refs_7_.refs_10_), channel_id=1, source_target_pairs={{0,4},{4,0},{8,12},{12,8},{16,20},{20,16},{24,28},{28,24},{1,5},{5... | collective-permute-start | bytes 294920 | tf_op jit(solution)/shard_map/ppermute | solution.py:717
  40.9 1.5 %collective-permute-start.16 = (bf16[288,256]{1,0:T(8,128)(2,1)S(1)}, bf16[288,256]{1,0:T(8,128)(2,1)S(1)}, u32[]{:S(2)}, u32[]{:S(2)}) collective-permute-start(bf16[288,256]{1,0:T(8,128)(2,1)S(1)} %get-tuple-element.134.refs_8_), channel_id=1, source_target_pairs={{0,4},{4,0},{8,12},{12,8},{16,20},{20,16},{24,28},{28,24},{1,5},{5... | collective-permute-start | bytes 442376 | tf_op jit(solution)/shard_map/ppermute | solution.py:717
  41.4 1.4 %collective-permute-start.17 = (bf16[288,256]{1,0:T(8,128)(2,1)S(1)}, bf16[288,256]{1,0:T(8,128)(2,1)S(1)}, u32[]{:S(2)}, u32[]{:S(2)}) collective-permute-start(bf16[288,256]{1,0:T(8,128)(2,1)S(1)} %get-tuple-element.135.refs_9_), channel_id=1, source_target_pairs={{0,4},{4,0},{8,12},{12,8},{16,20},{20,16},{24,28},{28,24},{1,5},{5... | collective-permute-start | bytes 442376 | tf_op jit(solution)/shard_map/ppermute | solution.py:717
  41.5 1.5 %collective-permute-start.18 = (bf16[288,256]{1,0:T(8,128)(2,1)S(1)}, bf16[288,256]{1,0:T(8,128)(2,1)S(1)}, u32[]{:S(2)}, u32[]{:S(2)}) collective-permute-start(bf16[288,256]{1,0:T(8,128)(2,1)S(1)} %get-tuple-element.136.refs_10_), channel_id=1, source_target_pairs={{0,4},{4,0},{8,12},{12,8},{16,20},{20,16},{24,28},{28,24},{1,5},{5... | collective-permute-start | bytes 442376 | tf_op jit(solution)/shard_map/ppermute | solution.py:717
  49.7 1.9 %collective-permute-start.19 = (bf16[4,256,256]{2,1,0:T(8,128)(2,1)S(1)}, bf16[4,256,256]{2,1,0:T(8,128)(2,1)S(1)}, u32[]{:S(2)}, u32[]{:S(2)}) collective-permute-start(bf16[4,256,256]{2,1,0:T(8,128)(2,1)S(1)} %get-tuple-element.157), channel_id=1, source_target_pairs={{0,4},{4,0},{8,12},{12,8},{16,20},{20,16},{24,28},{28,24},{1,5},{5... | collective-permute-start | bytes 1572872 | tf_op jit(solution)/shard_map/ppermute | solution.py:717
  51.8 10.3 %collective-permute-start.20 = (bf16[4,64,256]{2,1,0:T(8,128)(2,1)S(1)}, bf16[4,64,256]{2,1,0:T(8,128)(2,1)S(1)}, u32[]{:S(2)}, u32[]{:S(2)}) collective-permute-start(bf16[4,64,256]{2,1,0:T(8,128)(2,1)S(1)} %get-tuple-element.159), channel_id=1, source_target_pairs={{0,8},{4,12},{8,0},{12,4},{16,24},{20,28},{24,16},{28,20},{1,9},{5... | collective-permute-start | bytes 393224 | tf_op jit(solution)/shard_map/ppermute | solution.py:717
  53.6 8.5 %collective-permute-start.21 = (bf16[4,64,256]{2,1,0:T(8,128)(2,1)S(1)}, bf16[4,64,256]{2,1,0:T(8,128)(2,1)S(1)}, u32[]{:S(2)}, u32[]{:S(2)}) collective-permute-start(bf16[4,64,256]{2,1,0:T(8,128)(2,1)S(1)} %get-tuple-element.160), channel_id=1, source_target_pairs={{0,16},{4,20},{8,24},{12,28},{16,0},{20,4},{24,8},{28,12},{1,17},{... | collective-permute-start | bytes 393224 | tf_op jit(solution)/shard_map/ppermute | solution.py:717
  55.0 7.1 %collective-permute-start.22 = (bf16[4,64,256]{2,1,0:T(8,128)(2,1)S(1)}, bf16[4,64,256]{2,1,0:T(8,128)(2,1)S(1)}, u32[]{:S(2)}, u32[]{:S(2)}) collective-permute-start(bf16[4,64,256]{2,1,0:T(8,128)(2,1)S(1)} %get-tuple-element.161), channel_id=1, source_target_pairs={{0,24},{4,28},{8,16},{12,20},{16,8},{20,12},{24,0},{28,4},{1,25},{... | collective-permute-start | bytes 393224 | tf_op jit(solution)/shard_map/ppermute | solution.py:717
  61.1 7.5 %collective-permute-start.23 = (bf16[4,96,256]{2,1,0:T(8,128)(2,1)S(1)}, bf16[4,96,256]{2,1,0:T(8,128)(2,1)S(1)}, u32[]{:S(2)}, u32[]{:S(2)}) collective-permute-start(bf16[4,96,256]{2,1,0:T(8,128)(2,1)S(1)} %get-tuple-element.167), channel_id=1, source_target_pairs={{0,4},{4,0},{8,12},{12,8},{16,20},{20,16},{24,28},{28,24},{1,5},{5... | collective-permute-start | bytes 589832 | tf_op jit(solution)/shard_map/ppermute | solution.py:717
  68.0 1.5 %collective-permute-start.24 = (bf16[4,96,256]{2,1,0:T(8,128)(2,1)S(1)}, bf16[4,96,256]{2,1,0:T(8,128)(2,1)S(1)}, u32[]{:S(2)}, u32[]{:S(2)}) collective-permute-start(bf16[4,96,256]{2,1,0:T(8,128)(2,1)S(1)} %get-tuple-element.168), channel_id=1, source_target_pairs={{0,4},{4,0},{8,12},{12,8},{16,20},{20,16},{24,28},{28,24},{1,5},{5... | collective-permute-start | bytes 589832 | tf_op jit(solution)/shard_map/ppermute | solution.py:717
  68.3 4.3 %collective-permute-start.28 = (bf16[4,128,256]{2,1,0:T(8,128)(2,1)S(1)}, bf16[4,128,256]{2,1,0:T(8,128)(2,1)S(1)}, u32[]{:S(2)}, u32[]{:S(2)}) collective-permute-start(bf16[4,128,256]{2,1,0:T(8,128)(2,1)S(1)} %get-tuple-element.174), channel_id=1, source_target_pairs={{0,4},{4,0},{8,12},{12,8},{16,20},{20,16},{24,28},{28,24},{1,5},{5... | collective-permute-start | bytes 786440 | tf_op jit(solution)/shard_map/ppermute | solution.py:717
  69.6 4.3 %collective-permute-start.25 = (bf16[192,256]{1,0:T(8,128)(2,1)S(1)}, bf16[192,256]{1,0:T(8,128)(2,1)S(1)}, u32[]{:S(2)}, u32[]{:S(2)}) collective-permute-start(bf16[192,256]{1,0:T(8,128)(2,1)S(1)} %get-tuple-element.170), channel_id=1, source_target_pairs={{0,8},{4,12},{8,0},{12,4},{16,24},{20,28},{24,16},{28,20},{1,9},{5... | collective-permute-start | bytes 294920 | tf_op jit(solution)/shard_map/ppermute | solution.py:717
  71.2 3.9 %collective-permute-start.26 = (bf16[192,256]{1,0:T(8,128)(2,1)S(1)}, bf16[192,256]{1,0:T(8,128)(2,1)S(1)}, u32[]{:S(2)}, u32[]{:S(2)}) collective-permute-start(bf16[192,256]{1,0:T(8,128)(2,1)S(1)} %get-tuple-element.171), channel_id=1, source_target_pairs={{0,16},{4,20},{8,24},{12,28},{16,0},{20,4},{24,8},{28,12},{1,17},{... | collective-permute-start | bytes 294920 | tf_op jit(solution)/shard_map/ppermute | solution.py:717
  72.6 4.4 %collective-permute-start.27 = (bf16[192,256]{1,0:T(8,128)(2,1)S(1)}, bf16[192,256]{1,0:T(8,128)(2,1)S(1)}, u32[]{:S(2)}, u32[]{:S(2)}) collective-permute-start(bf16[192,256]{1,0:T(8,128)(2,1)S(1)} %get-tuple-element.172), channel_id=1, source_target_pairs={{0,24},{4,28},{8,16},{12,20},{16,8},{20,12},{24,0},{28,4},{1,25},{... | collective-permute-start | bytes 294920 | tf_op jit(solution)/shard_map/ppermute | solution.py:717
  77.6 7.5 %collective-permute-start.32 = (bf16[4,128,256]{2,1,0:T(8,128)(2,1)S(1)}, bf16[4,128,256]{2,1,0:T(8,128)(2,1)S(1)}, u32[]{:S(2)}, u32[]{:S(2)}) collective-permute-start(bf16[4,128,256]{2,1,0:T(8,128)(2,1)S(1)} %get-tuple-element.186), channel_id=1, source_target_pairs={{0,4},{4,0},{8,12},{12,8},{16,20},{20,16},{24,28},{28,24},{1,5},{5... | collective-permute-start | bytes 786440 | tf_op jit(solution)/shard_map/ppermute | solution.py:717
  79.5 9.6 %collective-permute-start.29 = (bf16[192,256]{1,0:T(8,128)(2,1)S(1)}, bf16[192,256]{1,0:T(8,128)(2,1)S(1)}, u32[]{:S(2)}, u32[]{:S(2)}) collective-permute-start(bf16[192,256]{1,0:T(8,128)(2,1)S(1)} %get-tuple-element.182), channel_id=1, source_target_pairs={{0,1},{1,2},{2,3},{3,0},{4,5},{5,6},{6,7},{7,4},{8,9},{9,10},{10,1... | collective-permute-start | bytes 294920 | tf_op jit(solution)/shard_map/ppermute | solution.py:713
  81.7 10.7 %collective-permute-start.30 = (bf16[192,256]{1,0:T(8,128)(2,1)S(1)}, bf16[192,256]{1,0:T(8,128)(2,1)S(1)}, u32[]{:S(2)}, u32[]{:S(2)}) collective-permute-start(bf16[192,256]{1,0:T(8,128)(2,1)S(1)} %get-tuple-element.183), channel_id=1, source_target_pairs={{0,2},{1,3},{2,0},{3,1},{4,6},{5,7},{6,4},{7,5},{8,10},{9,11},{10,... | collective-permute-start | bytes 294920 | tf_op jit(solution)/shard_map/ppermute | solution.py:713
  83.4 11.1 %collective-permute-start.31 = (bf16[192,256]{1,0:T(8,128)(2,1)S(1)}, bf16[192,256]{1,0:T(8,128)(2,1)S(1)}, u32[]{:S(2)}, u32[]{:S(2)}) collective-permute-start(bf16[192,256]{1,0:T(8,128)(2,1)S(1)} %get-tuple-element.184), channel_id=1, source_target_pairs={{0,3},{1,0},{2,1},{3,2},{4,7},{5,4},{6,5},{7,6},{8,11},{9,8},{10,9... | collective-permute-start | bytes 294920 | tf_op jit(solution)/shard_map/ppermute | solution.py:713
  85.1 9.8 %collective-permute-start.33 = (bf16[144,256]{1,0:T(8,128)(2,1)S(1)}, bf16[144,256]{1,0:T(8,128)(2,1)S(1)}, u32[]{:S(2)}, u32[]{:S(2)}) collective-permute-start(bf16[144,256]{1,0:T(8,128)(2,1)S(1)} %get-tuple-element.189), channel_id=1, source_target_pairs={{0,1},{1,2},{2,3},{3,0},{4,5},{5,6},{6,7},{7,4},{8,9},{9,10},{10,1... | collective-permute-start | bytes 221192 | tf_op jit(solution)/shard_map/ppermute | solution.py:713
  86.6 9.8 %collective-permute-start.34 = (bf16[144,256]{1,0:T(8,128)(2,1)S(1)}, bf16[144,256]{1,0:T(8,128)(2,1)S(1)}, u32[]{:S(2)}, u32[]{:S(2)}) collective-permute-start(bf16[144,256]{1,0:T(8,128)(2,1)S(1)} %get-tuple-element.190), channel_id=1, source_target_pairs={{0,2},{1,3},{2,0},{3,1},{4,6},{5,7},{6,4},{7,5},{8,10},{9,11},{10,... | collective-permute-start | bytes 221192 | tf_op jit(solution)/shard_map/ppermute | solution.py:713
  89.1 8.8 %collective-permute-start.35 = (bf16[144,256]{1,0:T(8,128)(2,1)S(1)}, bf16[144,256]{1,0:T(8,128)(2,1)S(1)}, u32[]{:S(2)}, u32[]{:S(2)}) collective-permute-start(bf16[144,256]{1,0:T(8,128)(2,1)S(1)} %get-tuple-element.191), channel_id=1, source_target_pairs={{0,3},{1,0},{2,1},{3,2},{4,7},{5,4},{6,5},{7,6},{8,11},{9,8},{10,9... | collective-permute-start | bytes 221192 | tf_op jit(solution)/shard_map/ppermute | solution.py:713
  98.0 5.9 %collective-permute-start.38 = (bf16[336,256]{1,0:T(8,128)(2,1)S(1)}, bf16[336,256]{1,0:T(8,128)(2,1)S(1)}, u32[]{:S(2)}, u32[]{:S(2)}) collective-permute-start(bf16[336,256]{1,0:T(8,128)(2,1)S(1)} %shard_map.373.refs_0_), channel_id=1, source_target_pairs={{0,24},{4,28},{8,16},{12,20},{16,8},{20,12},{24,0},{28,4},{1,25},{... | collective-permute-start | bytes 516104 | tf_op jit(solution)/shard_map/ppermute | solution.py:717
  99.1 9.9 %collective-permute-start.37 = (bf16[336,256]{1,0:T(8,128)(2,1)S(1)}, bf16[336,256]{1,0:T(8,128)(2,1)S(1)}, u32[]{:S(2)}, u32[]{:S(2)}) collective-permute-start(bf16[336,256]{1,0:T(8,128)(2,1)S(1)} %shard_map.373.refs_0_), channel_id=1, source_target_pairs={{0,16},{4,20},{8,24},{12,28},{16,0},{20,4},{24,8},{28,12},{1,17},{... | collective-permute-start | bytes 516104 | tf_op jit(solution)/shard_map/ppermute | solution.py:717
  100.1 8.9 %collective-permute-start.36 = (bf16[336,256]{1,0:T(8,128)(2,1)S(1)}, bf16[336,256]{1,0:T(8,128)(2,1)S(1)}, u32[]{:S(2)}, u32[]{:S(2)}) collective-permute-start(bf16[336,256]{1,0:T(8,128)(2,1)S(1)} %shard_map.373.refs_0_), channel_id=1, source_target_pairs={{0,8},{4,12},{8,0},{12,4},{16,24},{20,28},{24,16},{28,20},{1,9},{5... | collective-permute-start | bytes 516104 | tf_op jit(solution)/shard_map/ppermute | solution.py:717
  109.0 1.7 %collective-permute-start.39 = (bf16[528,256]{1,0:T(8,128)(2,1)S(1)}, bf16[528,256]{1,0:T(8,128)(2,1)S(1)}, u32[]{:S(2)}, u32[]{:S(2)}) collective-permute-start(bf16[528,256]{1,0:T(8,128)(2,1)S(1)} %shard_map.374.mine), channel_id=1, source_target_pairs={{0,4},{4,0},{8,12},{12,8},{16,20},{20,16},{24,28},{28,24},{1,5},{5... | collective-permute-start | bytes 811016 | tf_op jit(solution)/shard_map/ppermute | solution.py:717
  (6 other events, 4.8 us)

commit v3 on v2

--- a/solution.py
+++ b/solution.py
@@ -117,7 +117,7 @@
 
 def begin_kernel(dims, sizes, tokens, reduce_w, query_w, keyval_w, hidden_w, return_w, output_w, packed, *outs):
     n_sp, batches, row_dev, cols, dim = dims
-    normal_ref, mask_ref, bias_ref, own_r, own_q, own_kv, own_vec, second = outs
+    normal_ref, rstd_ref, mask_ref, bias_ref, own_r, own_q, own_kv, own_vec, second = outs
     tok = row_dev * cols
     half_cols = cols // 2
     rows_dev = row_dev // 2
@@ -143,7 +143,9 @@
     for batch in range(batches):
         height, image_width = sizes[batch, 0, 0], sizes[batch, 0, 1]
         rows = slice(batch * tok, (batch + 1) * tok)
-        normal_ref[rows], _ = normalize(tokens[batch, 0].reshape(tok, dim).astype(f32))
+        normal, rstd = normalize(tokens[batch, 0].reshape(tok, dim).astype(f32))
+        normal_ref[rows] = normal
+        rstd_ref[rows] = jnp.broadcast_to(rstd, (tok, 128))
         mask_ref[rows] = token_mask(sp * row_dev, row_dev, cols, dim, height, image_width)
         col_ids = lax.broadcasted_iota(jnp.int32, (half_cols, dim), 0)
 
@@ -163,7 +165,7 @@
     n_fs, batches, row_dev, cols, dim = dims
     ins, mine, other, outs = take(refs, 7, n_fs - 1, n_fs - 1)
     normal_in, mask_ref, own_w, own_q, own_kv, own_vec, second_in = ins
-    normed_ref, patch_ref, reduced_ref, key_ref, weight_ref, wq, wkv, vec_ref, second, wide = outs
+    normed_ref, cols_ref, send_ref, reduced_ref, key_ref, weight_ref, wq, wkv, vec_ref, second, patch_ref, wide = outs
     half = dim // 2
     shard = dim // n_fs
     rest = half + VECS
@@ -203,6 +205,12 @@
                     piece = wide[part, pl.ds((2 * row + dr) * cols + dc, half_cols, stride=2), :]
                     lanes = slice(offset * dim + part * 128, offset * dim + (part + 1) * 128)
                     patch_ref[start : start + half_cols, lanes] = piece.astype(bf16)
+    is_low = lax.axis_index("sp") % 2 == 0
+    for offset in range(4):
+        low = patch_ref[:, offset * dim : offset * dim + half]
+        high = patch_ref[:, offset * dim + half : (offset + 1) * dim]
+        cols_ref[offset] = jnp.where(is_low, low, high)
+        send_ref[offset] = jnp.where(is_low, high, low)
     reduced = mm(patch_ref[...], weight_ref[...].reshape(4 * dim, dim)) + vec[REDUCE_B : REDUCE_B + 1]
     reduced_ref[...] = reduced
     normal, _ = normalize(reduced)
@@ -269,46 +277,58 @@
 
 def forward_kernel(dims, *refs):
     batches, tok, key_dev, keys, block, n_pieces = dims
-    (normed, vec_ref, bias_ref, wq, wkv), pieces, (attended, *kept) = take(refs, 5, n_pieces)
+    (normed, vec_ref, bias_ref, wq, wkv), pieces, (attended, *kept, wide) = take(refs, 5, n_pieces)
     queries_out, kvs, attf, stats, probs = (
         kept[index * batches : (index + 1) * batches] for index in range(5)
     )
     dim = wq.shape[0]
     blocks = keys // block
     per_block = block // key_dev
+    queries_t, values_t, masked = [], [], []
     for batch in range(batches):
         rows = slice(batch * tok, (batch + 1) * tok)
         queries = (mm(normed[rows], wq[...]) + vec_ref[QUERY_B : QUERY_B + 1]).astype(bf16)
         queries_out[batch][...] = queries
-        queries_t = queries.T
+        queries_t.append(queries.T)
         for index in range(blocks):
             key_rows = key_rows_of(pieces, key_dev, per_block, batch, index)
             here = slice(index * block, (index + 1) * block)
             kvs[batch][here, :dim] = mm(key_rows, wkv[:, :dim]).astype(bf16)
             value_rows = mm(key_rows, wkv[:, dim:]) + vec_ref[VALUE_B : VALUE_B + 1]
             kvs[batch][here, dim:] = value_rows.astype(bf16)
-        if blocks == 1:
+    if blocks == 1:
+        for batch in range(batches):
             key_block = kvs[batch][:, :dim]
-            values_t = kvs[batch][:, dim:].T
             bias = bias_ref[batch]
-            masked = {lane_id: with_bias(key_block, bias, lane_id) for lane_id in (0, dim - 1)}
+            values_t.append(kvs[batch][:, dim:].T)
+            masked.append({lane_id: with_bias(key_block, bias, lane_id) for lane_id in (0, dim - 1)})
+        todo = [(batch, pair) for batch in range(batches) for pair in range(PAIRS)]
+
+        def score(index):
+            batch, pair = todo[index]
+            lane_id = mask_lane(pair, dim)
+            wide[index % 2] = mm(masked[batch][lane_id], query_stack(queries_t[batch], pair, lane_id, tok))
+
+        score(0)
+        for index, (batch, pair) in enumerate(todo):
+            if index + 1 < len(todo):
+                score(index + 1)
+            heads = slice(2 * HDIM * pair, 2 * HDIM * (pair + 1))
+            scores = wide[index % 2]
+            top = jnp.max(scores, axis=0, keepdims=True)
+            weights = jnp.exp2((scores - top) * EXP_SCALE)
+            inverse = 1.0 / jnp.sum(weights, axis=0, keepdims=True)
+            low = weights.astype(bf16)
+            probs[batch][pair] = low
+            stats[batch][pair, 0:1] = inverse
+            mixed = mm(values_t[batch][heads], low) * inverse
+            attf[batch][heads] = split_pair(mixed, tok)
+    else:
+        for batch in range(batches):
             for pair in range(PAIRS):
                 lane_id = mask_lane(pair, dim)
                 heads = slice(2 * HDIM * pair, 2 * HDIM * (pair + 1))
-                scores = mm(masked[lane_id], query_stack(queries_t, pair, lane_id, tok))
-                top = jnp.max(scores, axis=0, keepdims=True)
-                weights = jnp.exp2((scores - top) * EXP_SCALE)
-                inverse = 1.0 / jnp.sum(weights, axis=0, keepdims=True)
-                low = weights.astype(bf16)
-                probs[batch][pair] = low
-                stats[batch][pair, 0:1] = inverse
-                mixed = mm(values_t[heads], low) * inverse
-                attf[batch][heads] = split_pair(mixed, tok)
-        else:
-            for pair in range(PAIRS):
-                lane_id = mask_lane(pair, dim)
-                heads = slice(2 * HDIM * pair, 2 * HDIM * (pair + 1))
-                stacked = query_stack(queries_t, pair, lane_id, tok)
+                stacked = query_stack(queries_t[batch], pair, lane_id, tok)
 
                 def block_scores(index, stacked=stacked, lane_id=lane_id, batch=batch):
                     here = pl.ds(pl.multiple_of(index * block, block), block)
@@ -335,15 +355,16 @@
                 stats[batch][pair, 0:1] = inverse
                 stats[batch][pair, 1:2] = top
                 attf[batch][heads] = split_pair(mixed * inverse, tok)
-        attended[rows] = attf[batch][...].T.astype(bf16)
+    for batch in range(batches):
+        attended[batch * tok : (batch + 1) * tok] = attf[batch][...].T.astype(bf16)
 
 
 def mlp_kernel(dims, *refs):
     n_fs, batches, row_dev, cols, dim, hid = dims
-    ins, own, mine, other, outs, scratch = take(refs, 5, 3, n_fs - 1, n_fs - 1, 7)
+    ins, own, mine, other, _, outs, scratch = take(refs, 5, 3, n_fs - 1, n_fs - 1, 1, 7)
     tokens, cotangent, mask_ref, attended, vec_ref = ins
     acts_ref, normal_ref, rstd_ref, grad_ref, keep_ref, send_ref, wo = outs
-    wh, wr, bias_rows = scratch
+    wh, wr, bias_rows, lows, highs = scratch
     tok = row_dev * cols
     shard = dim // n_fs
     chunks = hid // dim
@@ -363,19 +384,6 @@
 
     def vec(index):
         return vec_ref[index : index + 1, :]
-
-    def store(low_half, owner, start, value):
-        value = value.astype(bf16)
-        here = slice(start, start + value.shape[0])
-        keep = is_low if low_half else jnp.logical_not(is_low)
-
-        @pl.when(keep)
-        def _():
-            keep_ref[owner, here, :] = value
-
-        @pl.when(jnp.logical_not(keep))
-        def _():
-            send_ref[owner, here, :] = value
 
     x = jnp.concatenate([tokens[b, 0].reshape(tok, dim).astype(f32) for b in range(batches)], axis=0)
     mask = mask_ref[...]
@@ -400,10 +408,13 @@
         grad_hidden = ((phi + hidden * density) * grad_activated).astype(bf16)
         bias_rows[chunk : chunk + 1] = jnp.sum(grad_hidden.astype(f32), axis=0, keepdims=True)
         grad_second = grad_second + mm_nt(grad_hidden, wh[:, lanes])
-        store(False, chunk, 0, mm_tn(activated, grad_mlp))
-        grad_wh = mm_tn(second, grad_hidden)
+        highs[chunk] = mm_tn(activated, grad_mlp).astype(bf16)
+        grad_wh = mm_tn(second, grad_hidden).astype(bf16)
         for owner in range(n_fs):
-            store(True, owner, chunk * shard, grad_wh[owner * shard : (owner + 1) * shard])
+            lows[owner, chunk * shard : (chunk + 1) * shard] = grad_wh[owner * shard : (owner + 1) * shard]
+    low, high = lows[...], highs[...]
+    keep_ref[...] = jnp.where(is_low, low, high)
+    send_ref[...] = jnp.where(is_low, high, low)
     total = total * mask
     for batch in range(batches):
         acts_ref[batch, 0] = total[batch * tok : (batch + 1) * tok].reshape(row_dev, cols, dim)
@@ -437,18 +448,10 @@
 
 
 def backward_kernel(dims, *refs):
-    n_fs, n_sp, batch, last, tok, key_dev, keys, block, n_pieces, batches = dims
-    ins, pieces, more, refs = take(refs, 8, n_pieces, 8 if last else 0)
-    gatt, queries_ref, kvs, attf, stats, probs, bias_ref, wkv = ins
-    if last:
-        first_gq, first_gkv, first_gvec, normed, wq, attended, middle, _ = more
-        keep_ref, send_ref, gnormed_ref, near_ref, far_ref, gvec_ref = refs[:6]
-        gqs, gks, gvs = refs[6:]
-    else:
-        gq_ref, gkv_ref, gvec_ref, near_ref, far_ref = refs[:5]
-        gqs, gks, gvs = refs[5:]
+    n_sp, batch, tok, key_dev, keys, block, n_pieces = dims
+    gatt, queries_ref, kvs, attf, stats, probs, bias_ref, wkv, _ = refs[:9]
+    near_ref, far_ref, scores_ref, gks, gvs, gvec_ref = refs[9:15]
     dim = wkv.shape[0]
-    shard = dim // n_fs
     blocks = keys // block
     per_block = block // key_dev
     rows = slice(batch * tok, (batch + 1) * tok)
@@ -467,22 +470,21 @@
         return delta * inverse, stacked.astype(bf16)
 
     if blocks == 1:
-        keys_t = kvs[:, :dim].T
         values = kvs[:, dim:]
         grad_k = jnp.zeros((keys, dim), f32)
         grad_v = jnp.zeros((keys, dim), f32)
         for pair in range(PAIRS):
-            heads = slice(2 * HDIM * pair, 2 * HDIM * (pair + 1))
             delta, stacked = pair_terms(pair)
             low = probs[pair]
             grad_probs = mm(values, stacked)
             grad_scores = (low.astype(f32) * (grad_probs - delta)).astype(bf16)
-            gqs[heads] = split_pair(mm(keys_t[heads], grad_scores), tok)
+            scores_ref[pair] = grad_scores
             grad_k = grad_k + mm(grad_scores, head_stack(queries, pair))
             grad_v = grad_v + mm(low, stacked.T)
     else:
-        gks[...] = jnp.zeros_like(gks)
-        gvs[...] = jnp.zeros_like(gvs)
+        wide_k, wide_v = refs[15:]
+        wide_k[...] = jnp.zeros_like(wide_k)
+        wide_v[...] = jnp.zeros_like(wide_v)
         queries_t = queries.T
         for pair in range(PAIRS):
             heads = slice(2 * HDIM * pair, 2 * HDIM * (pair + 1))
@@ -500,23 +502,22 @@
                 weights = jnp.exp2((mm(masked, query_t) - top) * EXP_SCALE)
                 grad_probs = mm(kvs[here, dim:], stacked)
                 grad_scores = (weights * (grad_probs - delta)).astype(bf16)
-                gks[here, :] += mm(grad_scores, query_n)
-                gvs[here, :] += mm(weights.astype(bf16), stacked_n)
+                wide_k[here, :] += mm(grad_scores, query_n)
+                wide_v[here, :] += mm(weights.astype(bf16), stacked_n)
                 return gq + mm(key_block.T[heads], grad_scores)
 
             gq = lax.fori_loop(0, blocks, back_block, jnp.zeros((2 * HDIM, 2 * tok), f32))
-            gqs[heads] = split_pair(gq, tok)
-    grad_queries = (gqs[...].T * SCALE).astype(bf16)
-    grad_wk = jnp.zeros((dim, dim), f32)
-    grad_wv = jnp.zeros((dim, dim), f32)
+            scores_ref[heads] = split_pair(gq, tok)
     bias_value = jnp.zeros((1, dim), f32)
     for index in range(blocks):
+        here = slice(index * block, (index + 1) * block)
         if blocks > 1:
-            here = slice(index * block, (index + 1) * block)
-            grad_k, grad_v = gks[here], gvs[here]
+            grad_k, grad_v = wide_k[here], wide_v[here]
         grad_k = (grad_k * SCALE).astype(bf16)
         bias_value = bias_value + jnp.sum(grad_v, axis=0, keepdims=True)
         grad_v = grad_v.astype(bf16)
+        gks[here] = grad_k
+        gvs[here] = grad_v
         grad_key = (mm_nt(grad_k, wkv[:, :dim]) + mm_nt(grad_v, wkv[:, dim:])).astype(bf16)
         if n_pieces > 1:
             pairs = grad_key.reshape(n_sp // 2, 2, key_dev, dim)
@@ -524,23 +525,40 @@
             far_ref[...] = pairs[:, 1]
         else:
             near_ref[index * per_block : (index + 1) * per_block] = grad_key.reshape(per_block, key_dev, dim)
-        key_rows = key_rows_of(pieces, key_dev, per_block, batch, index)
-        grad_wk = grad_wk + mm_tn(key_rows, grad_k)
-        grad_wv = grad_wv + mm_tn(key_rows, grad_v)
-    if not last:
-        gq_ref[...] = grad_queries
-        gkv_ref[:, :dim] = grad_wk
-        gkv_ref[:, dim:] = grad_wv
-        gvec_ref[...] = jnp.zeros_like(gvec_ref)
-        gvec_ref[0:1] = bias_value
-        return
-    is_low = lax.axis_index("sp") % 2 == 0
-    grad_wk = grad_wk + first_gkv[:, :dim]
-    grad_wv = grad_wv + first_gkv[:, dim:]
-    bias_value = bias_value + first_gvec[0:1]
-    grad_queries = jnp.concatenate([first_gq[...], grad_queries], axis=0)
+    gvec_ref[...] = jnp.broadcast_to(bias_value, gvec_ref.shape)
+
+
+def query_kernel(dims, *refs):
+    n_fs, batches, tok, key_dev, keys, block, n_pieces = dims
+    ins, kvs, scores, gks, gvs, gvecs, pieces, outs = take(refs, 5, *([batches] * 5), n_pieces)
+    normed, wq, attended, middle, _ = ins
+    keep_ref, send_ref, gnormed_ref, gvec_ref, wide = outs
+    dim = wq.shape[0]
+    shard = dim // n_fs
+    blocks = keys // block
+    per_block = block // key_dev
+    grad_queries = []
+    grad_wk = jnp.zeros((dim, dim), f32)
+    grad_wv = jnp.zeros((dim, dim), f32)
+    for batch in range(batches):
+        if blocks == 1:
+            keys_t = kvs[batch][:, :dim].T
+            for pair in range(PAIRS):
+                heads = slice(2 * HDIM * pair, 2 * HDIM * (pair + 1))
+                wide[heads] = split_pair(mm(keys_t[heads], scores[batch][pair]), tok)
+            grad_t = wide[...]
+        else:
+            grad_t = scores[batch][...]
+        grad_queries.append((grad_t.T * SCALE).astype(bf16))
+        for index in range(blocks):
+            here = slice(index * block, (index + 1) * block)
+            key_rows = key_rows_of(pieces, key_dev, per_block, batch, index)
+            grad_wk = grad_wk + mm_tn(key_rows, gks[batch][here])
+            grad_wv = grad_wv + mm_tn(key_rows, gvs[batch][here])
+    grad_queries = jnp.concatenate(grad_queries, axis=0)
     grad_wq = mm_tn(normed[...], grad_queries)
     grad_wo = mm_tn(attended[...], middle[...].astype(bf16))
+    is_low = lax.axis_index("sp") % 2 == 0
     for owner in range(n_fs):
         part = slice(owner * shard, (owner + 1) * shard)
         low = jnp.concatenate([grad_wq[part], grad_wk[part]], axis=0).astype(bf16)
@@ -550,6 +568,9 @@
     gnormed_ref[...] = mm_nt(grad_queries, wq[...])
     gvec_ref[...] = jnp.zeros_like(gvec_ref)
     gvec_ref[QUERY_B : QUERY_B + 1] = jnp.sum(grad_queries.astype(f32), axis=0, keepdims=True)
+    bias_value = gvecs[0][0:1]
+    for gvec in gvecs[1:]:
+        bias_value = bias_value + gvec[0:1]
     gvec_ref[VALUE_B : VALUE_B + 1] = bias_value
 
 
@@ -565,21 +586,14 @@
     return total
 
 
-def reduction_kernel(n_parts, n_fs, patches, reduced, vec_ref, *refs):
-    parts = refs[:n_parts]
-    grad_ref, gvec_ref, keep_ref, send_ref = refs[-4:]
-    dim = reduced.shape[1]
-    half = dim // 2
-    is_low = lax.axis_index("sp") % 2 == 0
+def reduction_kernel(n_parts, batches, reduced, vec_ref, *refs):
+    parts, gvec_ref, outs = refs[:n_parts], refs[-1], refs[-1 - batches : -1]
     grad_key = sum_parts(parts)
     normal, rstd = normalize(reduced[...])
     grad_low = normalize_back(grad_key, normal, rstd, vec_ref[KEYS_G : KEYS_G + 1]).astype(bf16)
-    grad_ref[...] = grad_low
-    for owner in range(n_fs):
-        grad_w = mm_tn(patches[:, owner * dim : (owner + 1) * dim], grad_low).astype(bf16)
-        low, high = grad_w[:half], grad_w[half:]
-        keep_ref[owner] = jnp.where(is_low, low, high)
-        send_ref[owner] = jnp.where(is_low, high, low)
+    rows = outs[0].shape[0]
+    for batch, out in enumerate(outs):
+        out[...] = grad_low[batch * rows : (batch + 1) * rows]
     gvec_ref[...] = jnp.zeros_like(gvec_ref)
     for index, value in (
         (REDUCE_B, grad_low.astype(f32)),
@@ -589,17 +603,29 @@
         gvec_ref[index : index + 1] = jnp.sum(value, axis=0, keepdims=True)
 
 
-def input_kernel(dims, tokens, middle, gnormed, mask_ref, grad_reduced, weight, vec_ref, vec_a, vec_b, vec_c, grad_ref, gvec_ref, wide):
+def weight_kernel(batches, *refs):
+    (own_cols, other_cols), own, other, (vectors, *outs) = take(refs, 2, batches, batches)
+    fs = lax.axis_index("fs")
+    own = jnp.concatenate([part[...] for part in own], axis=0)
+    other = jnp.concatenate([part[...] for part in other], axis=0)
+    rows = own_cols.shape[2]
+    for step, out in enumerate(outs):
+        place = lax.rem(fs + step, len(outs))
+        out[:rows] = (mm_tn(own_cols[place], own) + mm_tn(other_cols[place], other)).astype(out.dtype)
+        out[rows:] = vectors[...]
+
+
+def normed_kernel(dims, gnormed, mask_ref, weight, normal_ref, vec_a, vec_b, vec_c, *refs):
     batches, row_dev, cols, dim = dims
+    grads, (grad_ref, gvec_ref, wide) = take(refs, batches)
     tok = row_dev * cols
     half_cols = cols // 2
-    key_dev = tok // 4
     gain_first = jnp.zeros((1, dim), f32)
     bias_first = jnp.zeros((1, dim), f32)
     for batch in range(batches):
         for offset in range(4):
             dr, dc = offset // 2, offset % 2
-            back = mm_nt(grad_reduced[batch * key_dev : (batch + 1) * key_dev], weight[offset])
+            back = mm_nt(grads[batch][...], weight[offset])
             for row in range(row_dev // 2):
                 for part in range(dim // 128):
                     wide[part, pl.ds((2 * row + dr) * cols + dc, half_cols, stride=2), :] = back[
@@ -608,11 +634,8 @@
         rows = slice(batch * tok, (batch + 1) * tok)
         spread = jnp.concatenate([wide[part] for part in range(dim // 128)], axis=1)
         grad_normed = gnormed[rows] + spread * mask_ref[rows]
-        x = tokens[batch, 0].reshape(tok, dim).astype(f32)
-        normal, rstd = normalize(x)
-        grad_x = middle[rows] + normalize_back(grad_normed, normal, rstd, vec_ref[FIRST_G : FIRST_G + 1])
-        grad_ref[batch, 0] = grad_x.reshape(row_dev, cols, dim)
-        gain_first = gain_first + jnp.sum(grad_normed * normal, axis=0, keepdims=True)
+        grad_ref[rows] = grad_normed
+        gain_first = gain_first + jnp.sum(grad_normed * normal_ref[rows], axis=0, keepdims=True)
         bias_first = bias_first + jnp.sum(grad_normed, axis=0, keepdims=True)
     index = lax.broadcasted_iota(jnp.int32, (VECS, dim), 0)
     vectors = vec_a[...] + vec_b[...] + vec_c[...]
@@ -621,8 +644,19 @@
     gvec_ref[...] = vectors.astype(bf16)
 
 
+def input_kernel(dims, middle, grad_normed, normal_ref, rstd_ref, vec_ref, grad_ref, done_ref):
+    batches, row_dev, cols, dim = dims
+    tok = row_dev * cols
+    rstd = jnp.concatenate([rstd_ref[...]] * (dim // rstd_ref.shape[1]), axis=1)
+    back = normalize_back(grad_normed[...], normal_ref[...], rstd, vec_ref[FIRST_G : FIRST_G + 1])
+    grad_x = middle[...] + back
+    for batch in range(batches):
+        grad_ref[batch, 0] = grad_x[batch * tok : (batch + 1) * tok].reshape(row_dev, cols, dim)
+    done_ref[...] = jnp.zeros_like(done_ref)
+
+
 def key_sum_kernel(batches, *refs):
-    near, far, outs = take(refs, batches, batches)
+    near, far, _, outs = take(refs, batches, batches, 2)
     for step, out in enumerate(outs):
         rows = near[0].shape[1]
         for batch in range(batches):
@@ -630,18 +664,14 @@
             out[batch * rows : (batch + 1) * rows] = total.astype(out.dtype)
 
 
-def owner_kernel(n, tail, keep, arrived, *refs):
+def owner_kernel(keep, arrived, *outs):
     fs = lax.axis_index("fs")
-    outs = refs[tail:]
-    rows = keep.shape[1]
     for step, out in enumerate(outs):
-        place = lax.rem(fs + step, n)
-        out[:rows] = (keep[place].astype(f32) + arrived[place].astype(f32)).astype(out.dtype)
-        if tail:
-            out[rows:] = refs[0][...]
-
-
-def chip_kernel(keep, arrived, *outs):
+        place = lax.rem(fs + step, len(outs))
+        out[...] = (keep[place].astype(f32) + arrived[place].astype(f32)).astype(out.dtype)
+
+
+def chip_kernel(keep, arrived, _, *outs):
     chip = lax.axis_index("sp") // 2
     rows = outs[0].shape[1]
     for step, out in enumerate(outs):
@@ -663,27 +693,21 @@
 
 
 def join_kernel(n, *refs):
-    group_a, group_b, (out,) = take(refs, n, n)
-    rows = group_a[0].shape[0]
-    out[:rows] = sum_parts(group_a).astype(out.dtype)
-    out[rows:] = sum_parts(group_b).astype(out.dtype)
+    refs[-1][...] = sum_parts(refs[:n]).astype(refs[-1].dtype)
 
 
 def merge_kernel(rows, *refs):
-    parts, out = refs[:4], refs[4]
+    parts, out = refs[:4], refs[5]
     chip = lax.axis_index("sp") // 2
-    for step, part in enumerate(parts):
-        out[shard_rows(chip ^ step, rows), :] = part[:rows]
+    if rows:
+        for step, part in enumerate(parts):
+            out[shard_rows(chip ^ step, rows), :] = part[:rows]
     rest = [part[rows:].astype(f32) for part in parts]
     out[4 * rows :] = ((rest[0] + rest[1]) + (rest[2] + rest[3])).astype(out.dtype)
 
 
-def final_kernel(n_fs, mine, other, *outs):
-    query_w, keyval_w, output_w, hidden_w, return_w, reduce_w = outs[:6]
-    smalls, hidden_b = outs[6:-1], outs[-1]
+def final_kernel(mine, other, query_w, keyval_w, output_w, hidden_w, return_w):
     shard, dim = query_w.shape
-    half = dim // 2
-    fs = lax.axis_index("fs")
     low, high = both_halves(mine, other)
     low, high = low.astype(f32), high.astype(f32)
     for chunk in range(hidden_w.shape[1] // dim):
@@ -694,7 +718,16 @@
     keyval_w[:, :dim] = low[shard : 2 * shard]
     keyval_w[:, dim:] = high[:shard]
     output_w[...] = high[shard : 2 * shard]
-    low, high = low[2 * shard :], high[2 * shard :]
+
+
+def final_small_kernel(n_fs, mine, other, reduce_w, *outs):
+    smalls, hidden_b = outs[:-1], outs[-1]
+    dim = reduce_w.shape[0]
+    shard = dim // n_fs
+    half = dim // 2
+    fs = lax.axis_index("fs")
+    low, high = both_halves(mine, other)
+    low, high = low.astype(f32), high.astype(f32)
     reduce_w[:half] = low[:half]
     reduce_w[half:] = high[:half]
     vecs = low[half:] + high[half:]
@@ -741,7 +774,7 @@
     return [pieces[0]] + [rotate(pieces[step], n_fs, step) for step in range(1, n_fs)]
 
 
-def call(kernel, out_shape, in_specs=None, scratch=(), limit=SMALL_VMEM):
+def call(kernel, out_shape, in_specs=None, scratch=(), limit=SMALL_VMEM, micros=0):
     specs = {} if in_specs is None else {"in_specs": in_specs}
     return pl.pallas_call(
         kernel,
@@ -749,7 +782,7 @@
         **specs,
         scratch_shapes=scratch,
         compiler_params=pltpu.CompilerParams(vmem_limit_bytes=limit),
-        cost_estimate=pl.CostEstimate(flops=0, bytes_accessed=0, transcendentals=0),
+        cost_estimate=pl.CostEstimate(flops=int(micros * 1e9), bytes_accessed=0, transcendentals=0),
     )
 
 
@@ -820,6 +853,7 @@
         functools.partial(begin_kernel, (n_sp, batches, row_dev, cols, dim)),
         [
             shape(batches * tok, dim, dtype=f32),
+            shape(batches * tok, 128, dtype=f32),
             shape(batches * tok, dim, dtype=f32),
             shape(batches, keys, dim),
             shape(dim, dim),
@@ -841,16 +875,17 @@
         output_weight,
         first_half,
     )
-    normal_first, mask, bias, own_r, own_q, own_kv, own_vec, second_half = begun
+    normal_first, rstd_first, mask, bias, own_r, own_q, own_kv, own_vec, second_half = begun
     mine_first = call(functools.partial(relay_kernel, n_fs - 1), [shape(*first_half.shape)] * (n_fs - 1))(
         *mine_first, own_vec
     )
     other_first = [flip(piece, n_sp, 1) for piece in mine_first]
-    normed, patches, reduced, key_low, whole_reduce, wq, wkv, vec, second_half = call(
+    normed, patch_cols, patch_send, reduced, key_low, whole_reduce, wq, wkv, vec, second_half = call(
         functools.partial(reduce_kernel, (n_fs, batches, row_dev, cols, dim)),
         [
             shape(batches * tok, dim),
-            shape(batches * key_dev, 4 * dim),
+            shape(4, batches * key_dev, half),
+            shape(4, batches * key_dev, half),
             shape(batches * key_dev, dim, dtype=f32),
             shape(batches * key_dev, dim),
             shape(n_fs, dim, dim),
@@ -859,7 +894,7 @@
             shape(VECS, dim, dtype=f32),
             shape(dim + shard // 2, dim),
         ],
-        scratch=[pltpu.VMEM((dim // 128, tok, 128), f32)],
+        scratch=[pltpu.VMEM((batches * key_dev, 4 * dim), bf16), pltpu.VMEM((dim // 128, tok, 128), f32)],
     )(normal_first, mask, own_r, own_q, own_kv, own_vec, second_half, *mine_first, *other_first)
     mine_second = to_owners([second_half] * n_fs, n_fs)[1:]
 
@@ -878,12 +913,14 @@
         + [shape(dim, tok, dtype=f32)] * batches
         + [shape(PAIRS, 8, 2 * tok, dtype=f32)] * batches
         + [shape(PAIRS, keys, 2 * tok) if single else shape(16, 128)] * batches,
+        scratch=[pltpu.VMEM((2, block, 2 * tok) if single else (8, 128), f32)],
         limit=limit,
     )(normed, vec, bias, wq, wkv, *key_pieces)
     kept = [kept[batch::batches] for batch in range(batches)]
     mine_second = call(functools.partial(relay_kernel, n_fs - 1), [shape(dim + shard // 2, dim)] * (n_fs - 1))(
         *mine_second, kept[0][3]
     )
+    patch_other = flip(patch_send, n_sp, 1)
     other_second = [flip(piece, n_sp, 1) for piece in mine_second]
 
     acts, normal, rstd, grad_second, keep_a, send_a, wo = call(
@@ -897,7 +934,13 @@
             shape(n_fs, dim, dim),
             shape(dim, dim),
         ],
-        scratch=[pltpu.VMEM((dim, hid), bf16), pltpu.VMEM((hid, dim), bf16), pltpu.VMEM((8, dim), f32)],
+        scratch=[
+            pltpu.VMEM((dim, hid), bf16),
+            pltpu.VMEM((hid, dim), bf16),
+            pltpu.VMEM((8, dim), f32),
+            pltpu.VMEM((n_fs, dim, dim), bf16),
+            pltpu.VMEM((n_fs, dim, dim), bf16),
+        ],
         limit=limit,
     )(
         tokens,
@@ -910,6 +953,7 @@
         output_weight,
         *mine_second,
         *other_second,
+        patch_other,
     )
     arrived_a = flip(send_a, n_sp, 1)
     middle, gatt, gvec_a = call(
@@ -918,121 +962,118 @@
         limit=limit,
     )(cotangent, mask, normal, rstd, grad_second, vec, wo)
 
-    if split:
-        pieces_a = call(chip_kernel, [shape(n_fs, dim // 4, dim)] * 4)(keep_a, arrived_a)
-        total_a = call(chip_sum_kernel, shape(n_fs, dim // 4, dim))(*exchange(pieces_a, n_sp))
-    else:
-        total_a = vec
-    near, far = [], []
-    carried = ()
     gkey_dims = (n_sp // 2, key_dev, dim) if split else (n_sp, key_dev, dim)
+    back = []
     for batch in range(batches):
-        last = batch == batches - 1
-        scratch = [
-            pltpu.VMEM((dim, tok), f32),
-            pltpu.VMEM((8, 128) if single else (keys, dim), f32),
-            pltpu.VMEM((8, 128) if single else (keys, dim), f32),
-        ]
-        if last:
-            more = (*carried, normed, wq, attended, middle, total_a)
-            out_shape = [
-                shape(n_fs, half, dim),
-                shape(n_fs, half, dim),
-                shape(batches * tok, dim, dtype=f32),
-                shape(*gkey_dims),
-                shape(*(gkey_dims if split else (16, 128))),
-                shape(VECS, dim, dtype=f32),
-            ]
-        else:
-            more = ()
-            out_shape = [
-                shape(tok, dim),
-                shape(dim, 2 * dim, dtype=f32),
-                shape(8, dim, dtype=f32),
-                shape(*gkey_dims),
-                shape(*(gkey_dims if split else (16, 128))),
-            ]
         queries, kvs, attf, stats, probs = kept[batch]
-        results = call(
-            functools.partial(
-                backward_kernel,
-                (n_fs, n_sp, batch, last, tok, key_dev, keys, block, n_pieces, batches),
-            ),
-            out_shape,
-            scratch=scratch,
-            limit=limit,
-        )(gatt, queries, kvs, attf, stats, probs, bias, wkv, *key_pieces, *more)
-        if last:
-            keep_c, send_c, gnormed, near_b, far_b, gvec_c = results
-        else:
-            near_b, far_b = results[3:]
-            carried = results[:3]
-        near.append(near_b)
-        far.append(flip(far_b, n_sp, 1) if split else far_b)
-
+        order = vec
+        if split and batch == batches - 1:
+            pieces_a = call(chip_kernel, [shape(n_fs, dim // 4, dim)] * 4)(keep_a, arrived_a, back[0][5])
+            total_a = call(chip_sum_kernel, shape(n_fs, dim // 4, dim), micros=5)(*exchange(pieces_a, n_sp))
+            order = pieces_a[0]
+        back.append(
+            call(
+                functools.partial(backward_kernel, (n_sp, batch, tok, key_dev, keys, block, n_pieces)),
+                [
+                    shape(*gkey_dims),
+                    shape(*(gkey_dims if split else (16, 128))),
+                    shape(PAIRS, keys, 2 * tok) if single else shape(dim, tok, dtype=f32),
+                    shape(keys, dim),
+                    shape(keys, dim),
+                    shape(8, dim, dtype=f32),
+                ],
+                scratch=() if single else [pltpu.VMEM((keys, dim), f32)] * 2,
+                limit=limit,
+            )(gatt, queries, kvs, attf, stats, probs, bias, wkv, order)
+        )
+    near = [results[0] for results in back]
+    keep_c, send_c, gnormed, gvec_c = call(
+        functools.partial(query_kernel, (n_fs, batches, tok, key_dev, keys, block, n_pieces)),
+        [
+            shape(n_fs, half, dim),
+            shape(n_fs, half, dim),
+            shape(batches * tok, dim, dtype=f32),
+            shape(VECS, dim, dtype=f32),
+        ],
+        scratch=[pltpu.VMEM((dim, tok), f32)],
+        limit=limit,
+    )(
+        normed,
+        wq,
+        attended,
+        middle,
+        vec,
+        *[kept[batch][1] for batch in range(batches)],
+        *[results[2] for results in back],
+        *[results[3] for results in back],
+        *[results[4] for results in back],
+        *[results[5] for results in back],
+        *key_pieces,
+    )
     arrived_c = flip(send_c, n_sp, 1)
     if split:
-        sums = call(functools.partial(key_sum_kernel, batches), [shape(batches * key_dev, dim)] * 4)(*near, *far)
+        far = [flip(results[1], n_sp, 1) for results in back]
+        sums = call(functools.partial(key_sum_kernel, batches), [shape(batches * key_dev, dim)] * 4)(
+            *near, *far, total_a, gvec_c
+        )
         parts = exchange(sums, n_sp)
-        chunks = call(owners_kernel, [shape(dim // 4 + half, dim)] * n_fs)(total_a, keep_c, arrived_c)
-        after = [chunks[0]]
     else:
         parts = [lax.all_to_all(jnp.concatenate(near, axis=1), "sp", 0, 0)]
-        after = []
-
-    grad_reduced, gvec_b, keep_b, send_b = call(
-        functools.partial(reduction_kernel, len(parts), n_fs),
-        [
-            shape(batches * key_dev, dim),
-            shape(VECS, dim, dtype=f32),
-            shape(n_fs, half, dim),
-            shape(n_fs, half, dim),
-        ],
-    )(patches, reduced, vec, *parts, *after)
-    arrived_b = flip(send_b, n_sp, 1)
-    grads, vectors = call(
+    *grad_reduced, gvec_b = call(
+        functools.partial(reduction_kernel, len(parts), batches),
+        [shape(key_dev, dim)] * batches + [shape(VECS, dim, dtype=f32)],
+    )(reduced, vec, *parts)
+    grad_other = [flip(part, n_sp, 1) for part in grad_reduced]
+    grad_normed, vectors = call(
+        functools.partial(normed_kernel, (batches, row_dev, cols, dim)),
+        [shape(batches * tok, dim, dtype=f32), shape(VECS, dim)],
+        scratch=[pltpu.VMEM((dim // 128, tok, 128), f32)],
+    )(gnormed, mask, whole_reduce, normal_first, gvec_a, gvec_b, gvec_c, *grad_reduced)
+    grads, done = call(
         functools.partial(input_kernel, (batches, row_dev, cols, dim)),
-        [shape(batches, 1, row_dev, cols, dim, dtype=f32), shape(VECS, dim)],
-        scratch=[pltpu.VMEM((dim // 128, tok, 128), f32)],
-    )(tokens, middle, gnormed, mask, grad_reduced, whole_reduce, vec, gvec_a, gvec_b, gvec_c)
-
-    chunks_b = call(functools.partial(owner_kernel, n_fs, 1), [shape(half + VECS, dim)] * n_fs)(
-        keep_b, arrived_b, vectors
+        [shape(batches, 1, row_dev, cols, dim, dtype=f32), shape(8, 128, dtype=f32)],
+    )(middle, grad_normed, normal_first, rstd_first, vec)
+
+    chunks_b = call(functools.partial(weight_kernel, batches), [shape(half + VECS, dim)] * n_fs)(
+        patch_cols, patch_other, *grad_reduced, *grad_other, vectors
     )
-    group_b = to_owners(chunks_b, n_fs)
     if split:
-        group_a = to_owners(chunks, n_fs)
-        rows = group_a[0].shape[0] + group_b[0].shape[0]
-        joined = call(functools.partial(join_kernel, n_fs), shape(rows, dim))(*group_a, *group_b)
-        mine = call(functools.partial(merge_kernel, dim // 4), shape(rows + 3 * (dim // 4), dim))(
-            *exchange([joined] * 4, n_sp)
+        rows = dim // 4
+        chunks = call(owners_kernel, [shape(rows + half, dim)] * n_fs)(total_a, keep_c, arrived_c)
+        join = functools.partial(join_kernel, n_fs)
+        joined_a = call(join, shape(rows + half, dim))(*to_owners(chunks, n_fs), done)
+        joined_b = call(join, shape(half + VECS, dim), micros=1)(*to_owners(chunks_b, n_fs), done)
+        mine = call(functools.partial(merge_kernel, rows), shape(4 * rows + half, dim))(
+            *exchange([joined_a] * 4, n_sp), joined_b
+        )
+        mine_b = call(functools.partial(merge_kernel, 0), shape(half + VECS, dim))(
+            *exchange([joined_b] * 4, n_sp), mine
         )
     else:
-        groups = [group_b]
+        groups = [to_owners(chunks_b, n_fs)]
         for keep, arrived in ((keep_c, arrived_c), (keep_a, arrived_a)):
-            pieces = call(functools.partial(owner_kernel, n_fs, 0), [shape(*keep.shape[1:])] * n_fs)(keep, arrived)
+            pieces = call(owner_kernel, [shape(*keep.shape[1:])] * n_fs)(keep, arrived)
             groups.insert(0, to_owners(pieces, n_fs))
-        mine = jnp.concatenate(
-            [
-                sum_over_rows(sum(piece.astype(f32) for piece in group).astype(bf16), n_sp)
-                for group in groups
-            ],
-            axis=0,
+        mine_a, mine_c, mine_b = (
+            sum_over_rows(sum(piece.astype(f32) for piece in group).astype(bf16), n_sp) for group in groups
         )
-
-    gquery, gkeyval, goutput, ghidden, greturn, greduce, *vectors = call(
-        functools.partial(final_kernel, n_fs),
+        mine = jnp.concatenate([mine_a, mine_c], axis=0)
+
+    gquery, gkeyval, goutput, ghidden, greturn = call(
+        final_kernel,
         [
             shape(shard, dim, dtype=f32),
             shape(shard, 2 * dim, dtype=f32),
             shape(shard, dim, dtype=f32),
             shape(shard, hid, dtype=f32),
             shape(dim, dim, dtype=f32),
-            shape(dim, dim, dtype=f32),
-        ]
-        + [shape(shard, dtype=f32)] * HIDDEN_B
-        + [shape(dim, dtype=f32)],
+        ],
     )(mine, flip(mine, n_sp, 1))
+    greduce, *vectors = call(
+        functools.partial(final_small_kernel, n_fs),
+        [shape(dim, dim, dtype=f32)] + [shape(shard, dtype=f32)] * HIDDEN_B + [shape(dim, dtype=f32)],
+        micros=10,
+    )(mine_b, flip(mine_b, n_sp, 1))
     return (
         acts,
         grads,

time: 113 us -> 103 us (0.912)
  waiting for transfers between devices: 31.7 us -> 20.8 us
  starting transfers between devices: 36.9 us -> 40.1 us
  Pallas kernels: 34.6 us -> 32.4 us
    ppermute x28 -> x34, waiting for transfers between devices: 21.9 us -> 13.1 us  [flip(): return lax.ppermute(value, 'sp', [(i, i ^ bits) for i in range(n)])]
    ppermute x28 -> x34, starting transfers between devices: 22.6 us -> 25.7 us  [flip(): return lax.ppermute(value, 'sp', [(i, i ^ bits) for i in range(n)])]
    pallas_call x1, Pallas kernels: 6.71 us -> 4.21 us  [on_device(): call(functools.partial(mlp_kernel, (n_fs, batches, row_dev, cols, dim, hi...]
    ppermute x12, waiting for transfers between devices: 9.81 us -> 7.69 us  [rotate(): return lax.ppermute(value, 'fs', [(i, (i + step) % n) for i in range(n)])]
    pallas_call x10 -> x15, Pallas kernels: 13.3 us -> 15.1 us  [the longest x2 9.22 us: on_device(): call(functools.partial(backward_kernel, (n_sp, batch, tok, key_dev, keys,...]
  transfers between devices with their start and end apart: 40 -> 46, of which waited for: 24 -> 17; matrix products, arithmetic and copies ran while one was open for 0% -> 0% of each run, Pallas kernels for 21% -> 24%
where the time goes in v3:
time: 103 us; the launch traced here: 102 us
  starting transfers between devices  40.1 us (39%)
  Pallas kernels  32.4 us (31%)
  waiting for transfers between devices  20.8 us (20%)
  local copies, waits for them, and re-layouts  7.66 us (7%)
    ppermute x34, starting transfers between devices, flip(): return lax.ppermute(value, 'sp', [(i, i ^ bits) for i in range(n)])  25.7 us
    ppermute x12, starting transfers between devices, rotate(): return lax.ppermute(value, 'fs', [(i, (i + step) % n) for i in range(n)])  14.4 us
    ppermute x34, waiting for transfers between devices, flip(): return lax.ppermute(value, 'sp', [(i, i ^ bits) for i in range(n)])  13.1 us
    pallas_call x2, Pallas kernels, on_device(): call(functools.partial(backward_kernel, (n_sp, batch, tok, key_dev, keys,...  9.22 us
    ppermute x12, waiting for transfers between devices, rotate(): return lax.ppermute(value, 'fs', [(i, (i + step) % n) for i in range(n)])  7.69 us
    unnamed x28, local copies, waits for them, and re-layouts  7.66 us
    pallas_call x1, Pallas kernels, on_device(): call(functools.partial(forward_kernel, (batches, tok, key_dev, keys, bloc...  7.23 us
    pallas_call x1, Pallas kernels, on_device(): call(functools.partial(mlp_kernel, (n_fs, batches, row_dev, cols, dim, hi...  4.21 us
  transfers between devices with their start and end apart: 46, of which 17 were waited for; matrix products, arithmetic and copies ran while one was open for 0% of the time, Pallas kernels for 24%

profile of v3, /device:TPU:9, one launch (start us, length us, event | category | flops | bytes accessed | tf_op | source)
XLA Modules:
  0.0 101.9 jit_solution(7739115943542359723)
XLA Ops:
  0.7 1.9 %shard_map.356.packed = bf16[240,256]{1,0:T(8,128)(2,1)} custom-call(bf16[64]{0:T(256)(128)(2,1)} %refs_0_.2, bf16[64]{0:T(256)(128)(2,1)} %refs_1_.2, bf16[64]{0:T(256)(128)(2,1)} %refs_2_.1, bf16[64]{0:T(256)(128)(2,1)} %refs_3_.1, bf16[64]{0:T(256)(128)(2,1)} %refs_4_.1, bf16[64]{0:T(256)(128)(2,1)} %refs_5_.2, bf16[64]{0:T(256)(128)(2,1)} %refs_6_.2, ...), custom_call_target="tpu_custom_call" | custom-call | tf_op jit(solution)/shard_map/pallas_call | solution.py:844
  2.5 2.5 %collective-permute-start.1 = (bf16[240,256]{1,0:T(8,128)(2,1)}, bf16[240,256]{1,0:T(8,128)(2,1)S(1)}, u32[]{:S(2)}, u32[]{:S(2)}) collective-permute-start(bf16[240,256]{1,0:T(8,128)(2,1)} %shard_map.356.packed), channel_id=1, source_target_pairs={{0,2},{1,3},{2,0},{3,1},{4,6},{5,7},{6,4},{7,5},{8,10},{9,11},{10,... | collective-permute-start | bytes 368648 | tf_op jit(solution)/shard_map/ppermute | solution.py:746
  5.0 2.2 %collective-permute-start = (bf16[240,256]{1,0:T(8,128)(2,1)}, bf16[240,256]{1,0:T(8,128)(2,1)S(1)}, u32[]{:S(2)}, u32[]{:S(2)}) collective-permute-start(bf16[240,256]{1,0:T(8,128)(2,1)} %shard_map.356.packed), channel_id=1, source_target_pairs={{0,1},{1,2},{2,3},{3,0},{4,5},{5,6},{6,7},{7,4},{8,9},{9,10},{10,1... | collective-permute-start | bytes 368648 | tf_op jit(solution)/shard_map/ppermute | solution.py:746
  7.2 1.0 copy-done.1
  8.2 0.9 copy-done.3
  9.1 0.9 copy-done.5
  10.0 0.9 copy-done.7
  10.9 0.9 copy-done.8
  11.8 0.8 copy-done.9
  12.7 0.8 copy-done.10
  13.4 0.8 copy-done.12
  14.9 1.2 %shard_map.357 = (f32[768,256]{1,0:T(8,128)S(1)}, f32[768,128]{1,0:T(8,128)S(1)}, f32[768,256]{1,0:T(8,128)S(1)}, bf16[2,768,256]{2,1,0:T(8,128)(2,1)S(1)}, bf16...) custom-call(s32[2,1,2]{2,1,0:T(1,128)S(1)} %copy-done.13, ...), custom_call_target="tpu_custom_call" | custom-call | tf_op jit(solution)/shard_map/pallas_call | solution.py:852
  16.2 1.6 %collective-permute-start.3 = (bf16[240,256]{1,0:T(8,128)(2,1)S(1)}, bf16[240,256]{1,0:T(8,128)(2,1)S(1)}, u32[]{:S(2)}, u32[]{:S(2)}) collective-permute-start(bf16[240,256]{1,0:T(8,128)(2,1)S(1)} %get-tuple-element.130.refs_7_), channel_id=1, source_target_pairs={{0,4},{4,0},{8,12},{12,8},{16,20},{20,16},{24,28},{28,24},{1,5},{5... | collective-permute-start | bytes 368648 | tf_op jit(solution)/shard_map/ppermute | solution.py:750
  20.0 2.2 %collective-permute-start.11 = (bf16[192,256]{1,0:T(8,128)(2,1)S(1)}, bf16[192,256]{1,0:T(8,128)(2,1)S(1)}, u32[]{:S(2)}, u32[]{:S(2)}) collective-permute-start(bf16[192,256]{1,0:T(8,128)(2,1)S(1)} %get-tuple-element.138.refs_5_.refs_15_), channel_id=1, source_target_pairs={{0,24},{4,28},{8,16},{12,20},{16,8},{20,12},{24,0},{28,4},{1,25},{... | collective-permute-start | bytes 294920 | tf_op jit(solution)/shard_map/ppermute | solution.py:750
  22.7 1.2 %collective-permute-start.6 = (bf16[192,256]{1,0:T(8,128)(2,1)S(1)}, bf16[192,256]{1,0:T(8,128)(2,1)S(1)}, u32[]{:S(2)}, u32[]{:S(2)}) collective-permute-start(bf16[192,256]{1,0:T(8,128)(2,1)S(1)} %get-tuple-element.138.refs_5_.refs_15_), channel_id=1, source_target_pairs={{0,4},{4,0},{8,12},{12,8},{16,20},{20,16},{24,28},{28,24},{1,5},{5... | collective-permute-start | bytes 294920 | tf_op jit(solution)/shard_map/ppermute | solution.py:750
  23.9 1.1 %collective-permute-done.11.refs_11_.refs_21_ = bf16[192,256]{1,0:T(8,128)(2,1)S(1)} collective-permute-done((bf16[192,256]{1,0:T(8,128)(2,1)S(1)}, bf16[192,256]{1,0:T(8,128)(2,1)S(1)}, u32[]{:S(2)}, u32[]{:S(2)}) %collective-permute-start.11) | collective-permute-done | bytes 98336 | tf_op jit(solution)/shard_map/ppermute | solution.py:750
  25.0 1.2 %collective-permute-start.12 = (bf16[192,256]{1,0:T(8,128)(2,1)S(1)}, bf16[192,256]{1,0:T(8,128)(2,1)S(1)}, u32[]{:S(2)}, u32[]{:S(2)}) collective-permute-start(bf16[192,256]{1,0:T(8,128)(2,1)S(1)} %collective-permute-done.11.refs_11_.refs_21_), channel_id=1, source_target_pairs={{0,4},{4,0},{8,12},{12,8},{16,20},{20,16},{24,28},{28,24},{1,5},{5... | collective-permute-start | bytes 294920 | tf_op jit(solution)/shard_map/ppermute | solution.py:750
  26.4 1.2 %collective-permute-done.9.refs_9_.refs_19_ = bf16[192,256]{1,0:T(8,128)(2,1)S(1)} collective-permute-done((bf16[192,256]{1,0:T(8,128)(2,1)S(1)}, bf16[192,256]{1,0:T(8,128)(2,1)S(1)}, u32[]{:S(2)}, u32[]{:S(2)}) %collective-permute-start.9) | collective-permute-done | bytes 98336 | tf_op jit(solution)/shard_map/ppermute | solution.py:750
  27.6 1.0 %collective-permute-start.14 = (bf16[288,256]{1,0:T(8,128)(2,1)S(1)}, bf16[288,256]{1,0:T(8,128)(2,1)S(1)}, u32[]{:S(2)}, u32[]{:S(2)}) collective-permute-start(bf16[288,256]{1,0:T(8,128)(2,1)S(1)} %get-tuple-element.140), channel_id=1, source_target_pairs={{0,2},{1,3},{2,0},{3,1},{4,6},{5,7},{6,4},{7,5},{8,10},{9,11},{10,... | collective-permute-start | bytes 442376 | tf_op jit(solution)/shard_map/ppermute | solution.py:746
  29.3 0.9 collective-permute-start.10
  30.3 0.9 collective-permute-done.10.refs_10_.refs_20_
  31.5 7.2 %shard_map.360 = (bf16[768,256]{1,0:T(8,128)(2,1)S(1)}, bf16[384,256]{1,0:T(8,128)(2,1)S(1)}, bf16[384,256]{1,0:T(8,128)(2,1)S(1)}, bf16[768,512]{1,0:T(8,128)(2...) custom-call(bf16[768,256]{1,0:T(8,128)(2,1)S(1)} %get-tuple-element., ...), custom_call_target="tpu_custom_call" | custom-call | tf_op jit(solution)/shard_map/pallas_call | solution.py:908
  38.7 2.1 %collective-permute-done.13.refs_0_ = bf16[288,256]{1,0:T(8,128)(2,1)S(1)} collective-permute-done((bf16[288,256]{1,0:T(8,128)(2,1)S(1)}, bf16[288,256]{1,0:T(8,128)(2,1)S(1)}, u32[]{:S(2)}, u32[]{:S(2)}) %collective-permute-start.13) | collective-permute-done | bytes 147488 | tf_op jit(solution)/shard_map/ppermute | solution.py:746
  43.0 4.2 %shard_map.362 = (f32[2,1,2,192,256]{4,3,2,1,0:T(8,128)}, f32[768,256]{1,0:T(8,128)S(1)}, f32[768,128]{1,0:T(8,128)S(1)}, f32[776,256]{1,0:T(8,128)S(1)}, bf16[4...) custom-call(bf16[2,1,2,192,256]{4,3,2,1,0:T(8,128)(2,1)S(1)} %copy-done.2, ...), custom_call_target="tpu_custom_call" | custom-call | tf_op jit(solution)/shard_map/pallas_call | solution.py:926
  48.2 4.7 %shard_map.364 = (bf16[4,96,256]{2,1,0:T(8,128)(2,1)S(1)}, bf16[4,96,256]{2,1,0:T(8,128)(2,1)S(1)}, bf16[4,768,768]{2,1,0:T(8,128)(2,1)S(1)}, bf16[768,256]{1,0:...) custom-call(bf16[768,256]{1,0:T(8,128)(2,1)S(1)} %get-tuple-element.154.refs_0_, ...), custom_call_target="tpu_custom_call" | custom-call | tf_op jit(solution)/shard_map/pallas_call | solution.py:975
  53.1 1.9 %collective-permute-start.23 = (bf16[4,64,256]{2,1,0:T(8,128)(2,1)S(1)}, bf16[4,64,256]{2,1,0:T(8,128)(2,1)S(1)}, u32[]{:S(2)}, u32[]{:S(2)}) collective-permute-start(bf16[4,64,256]{2,1,0:T(8,128)(2,1)S(1)} %get-tuple-element.181), channel_id=1, source_target_pairs={{0,8},{4,12},{8,0},{12,4},{16,24},{20,28},{24,16},{28,20},{1,9},{5... | collective-permute-start | bytes 393224 | tf_op jit(solution)/shard_map/ppermute | solution.py:750
  55.0 1.4 %collective-permute-start.24 = (bf16[4,64,256]{2,1,0:T(8,128)(2,1)S(1)}, bf16[4,64,256]{2,1,0:T(8,128)(2,1)S(1)}, u32[]{:S(2)}, u32[]{:S(2)}) collective-permute-start(bf16[4,64,256]{2,1,0:T(8,128)(2,1)S(1)} %get-tuple-element.182), channel_id=1, source_target_pairs={{0,16},{4,20},{8,24},{12,28},{16,0},{20,4},{24,8},{28,12},{1,17},{... | collective-permute-start | bytes 393224 | tf_op jit(solution)/shard_map/ppermute | solution.py:750
  56.4 0.8 collective-permute-start.21
  57.2 4.5 %shard_map.366 = (bf16[4,96,256]{2,1,0:T(8,128)(2,1)S(1)}, bf16[4,96,256]{2,1,0:T(8,128)(2,1)S(1)}, bf16[4,768,768]{2,1,0:T(8,128)(2,1)S(1)}, bf16[768,256]{1,0:...) custom-call(bf16[768,256]{1,0:T(8,128)(2,1)S(1)} %get-tuple-element.154.refs_0_, ...), custom_call_target="tpu_custom_call" | custom-call | tf_op jit(solution)/shard_map/pallas_call | solution.py:975
  61.7 2.6 %shard_map.367 = (bf16[4,128,256]{2,1,0:T(8,128)(2,1)S(1)}, bf16[4,128,256]{2,1,0:T(8,128)(2,1)S(1)}, f32[768,256]{1,0:T(8,128)S(1)}, f32[16,256]{1,0:T(8,128)S(1)}) custom-call(bf16[768,256]{1,0:T(8,128)(2,1)S(1)} %get-tuple-element.133.refs_0_, bf16[256,256]{1,0:T(8,128)(2,1)S(1)} %get-tuple-element.136.refs_3_.refs_1_, ...), custom_call_target="tpu_custom_call" | custom-call | tf_op jit(solution)/shard_map/pallas_call | solution.py:990
  65.1 1.6 %collective-permute-start.26 = (bf16[192,256]{1,0:T(8,128)(2,1)S(1)}, bf16[192,256]{1,0:T(8,128)(2,1)S(1)}, u32[]{:S(2)}, u32[]{:S(2)}) collective-permute-start(bf16[192,256]{1,0:T(8,128)(2,1)S(1)} %get-tuple-element.186), channel_id=1, source_target_pairs={{0,8},{4,12},{8,0},{12,4},{16,24},{20,28},{24,16},{28,20},{1,9},{5... | collective-permute-start | bytes 294920 | tf_op jit(solution)/shard_map/ppermute | solution.py:750
  66.7 1.4 %collective-permute-start.27 = (bf16[192,256]{1,0:T(8,128)(2,1)S(1)}, bf16[192,256]{1,0:T(8,128)(2,1)S(1)}, u32[]{:S(2)}, u32[]{:S(2)}) collective-permute-start(bf16[192,256]{1,0:T(8,128)(2,1)S(1)} %get-tuple-element.187), channel_id=1, source_target_pairs={{0,16},{4,20},{8,24},{12,28},{16,0},{20,4},{24,8},{28,12},{1,17},{... | collective-permute-start | bytes 294920 | tf_op jit(solution)/shard_map/ppermute | solution.py:750
  68.1 2.3 %collective-permute-start.38 = (bf16[192,256]{1,0:T(8,128)(2,1)S(1)}, bf16[192,256]{1,0:T(8,128)(2,1)S(1)}, u32[]{:S(2)}, u32[]{:S(2)}) collective-permute-start(bf16[192,256]{1,0:T(8,128)(2,1)S(1)} %get-tuple-element.205), channel_id=1, source_target_pairs={{0,1},{1,2},{2,3},{3,0},{4,5},{5,6},{6,7},{7,4},{8,9},{9,10},{10,1... | collective-permute-start | bytes 294920 | tf_op jit(solution)/shard_map/ppermute | solution.py:746
  70.8 1.7 %collective-permute-done.28.refs_3_ = bf16[192,256]{1,0:T(8,128)(2,1)S(1)} collective-permute-done((bf16[192,256]{1,0:T(8,128)(2,1)S(1)}, bf16[192,256]{1,0:T(8,128)(2,1)S(1)}, u32[]{:S(2)}, u32[]{:S(2)}) %collective-permute-start.28) | collective-permute-done | bytes 98336 | tf_op jit(solution)/shard_map/ppermute | solution.py:750
  72.7 1.8 %collective-permute-start.29 = (bf16[96,256]{1,0:T(8,128)(2,1)S(1)}, bf16[96,256]{1,0:T(8,128)(2,1)S(1)}, u32[]{:S(2)}, u32[]{:S(2)}) collective-permute-start(bf16[96,256]{1,0:T(8,128)(2,1)S(1)} %get-tuple-element.190.refs_0_.refs_2_), channel_id=1, source_target_pairs={{0,4},{4,0},{8,12},{12,8},{16,20},{20,16},{24,28},{28,24},{1,5},{5... | collective-permute-start | bytes 147464 | tf_op jit(solution)/shard_map/ppermute | solution.py:750
  74.7 3.3 %collective-permute-start.40 = (bf16[192,256]{1,0:T(8,128)(2,1)S(1)}, bf16[192,256]{1,0:T(8,128)(2,1)S(1)}, u32[]{:S(2)}, u32[]{:S(2)}) collective-permute-start(bf16[192,256]{1,0:T(8,128)(2,1)S(1)} %get-tuple-element.207), channel_id=1, source_target_pairs={{0,3},{1,0},{2,1},{3,2},{4,7},{5,4},{6,5},{7,6},{8,11},{9,8},{10,9... | collective-permute-start | bytes 294920 | tf_op jit(solution)/shard_map/ppermute | solution.py:746
  79.0 2.2 %collective-permute-start.32 = (bf16[144,256]{1,0:T(8,128)(2,1)S(1)}, bf16[144,256]{1,0:T(8,128)(2,1)S(1)}, u32[]{:S(2)}, u32[]{:S(2)}) collective-permute-start(bf16[144,256]{1,0:T(8,128)(2,1)S(1)} %get-tuple-element.199), channel_id=1, source_target_pairs={{0,2},{1,3},{2,0},{3,1},{4,6},{5,7},{6,4},{7,5},{8,10},{9,11},{10,... | collective-permute-start | bytes 221192 | tf_op jit(solution)/shard_map/ppermute | solution.py:746
  81.2 1.3 %shard_map.372 = (f32[2,1,2,192,256]{4,3,2,1,0:T(8,128)}, f32[8,128]{1,0:T(8,128)S(1)}) custom-call(f32[768,256]{1,0:T(8,128)S(1)} %get-tuple-element.151.refs_3_.middle, f32[768,256]{1,0:T(8,128)S(1)} %get-tuple-element.192.grad_normed, f32[768,256]{1,0:T(8,128)S(1)} %get-tuple-element.124.refs_0_.normal_ref, f32[768,128]{1,0:T(8,128)S(1)} %get-tuple-element.193.rstd_ref, ...), custom_call_target="tpu_custom_call" | custom-call | tf_op jit(solution)/shard_map/pallas_call | solution.py:1032
  82.5 5.2 %collective-permute-done.40.refs_3_ = bf16[192,256]{1,0:T(8,128)(2,1)S(1)} collective-permute-done((bf16[192,256]{1,0:T(8,128)(2,1)S(1)}, bf16[192,256]{1,0:T(8,128)(2,1)S(1)}, u32[]{:S(2)}, u32[]{:S(2)}) %collective-permute-start.40) | collective-permute-done | bytes 98336 | tf_op jit(solution)/shard_map/ppermute | solution.py:746
  87.7 1.2 %collective-permute-start.43 = (bf16[192,256]{1,0:T(8,128)(2,1)S(1)}, bf16[192,256]{1,0:T(8,128)(2,1)S(1)}, u32[]{:S(2)}, u32[]{:S(2)}) collective-permute-start(bf16[192,256]{1,0:T(8,128)(2,1)S(1)} %shard_map.376.refs_0_), channel_id=1, source_target_pairs={{0,24},{4,28},{8,16},{12,20},{16,8},{20,12},{24,0},{28,4},{1,25},{... | collective-permute-start | bytes 294920 | tf_op jit(solution)/shard_map/ppermute | solution.py:750
  88.9 1.0 collective-permute-start.42
  90.9 1.2 %collective-permute-start.36 = (bf16[144,256]{1,0:T(8,128)(2,1)S(1)}, bf16[144,256]{1,0:T(8,128)(2,1)S(1)}, u32[]{:S(2)}, u32[]{:S(2)}) collective-permute-start(bf16[144,256]{1,0:T(8,128)(2,1)S(1)} %shard_map.374.refs_4_.refs_0_), channel_id=1, source_target_pairs={{0,24},{4,28},{8,16},{12,20},{16,8},{20,12},{24,0},{28,4},{1,25},{... | collective-permute-start | bytes 221192 | tf_op jit(solution)/shard_map/ppermute | solution.py:750
  92.0 1.0 collective-permute-start.35
  93.6 2.7 %collective-permute-done.42.refs_2_ = bf16[192,256]{1,0:T(8,128)(2,1)S(1)} collective-permute-done((bf16[192,256]{1,0:T(8,128)(2,1)S(1)}, bf16[192,256]{1,0:T(8,128)(2,1)S(1)}, u32[]{:S(2)}, u32[]{:S(2)}) %collective-permute-start.42) | collective-permute-done | bytes 98336 | tf_op jit(solution)/shard_map/ppermute | solution.py:750
  96.4 2.2 %collective-permute-done.35.refs_2_ = bf16[144,256]{1,0:T(8,128)(2,1)S(1)} collective-permute-done((bf16[144,256]{1,0:T(8,128)(2,1)S(1)}, bf16[144,256]{1,0:T(8,128)(2,1)S(1)}, u32[]{:S(2)}, u32[]{:S(2)}) %collective-permute-start.35) | collective-permute-done | bytes 73760 | tf_op jit(solution)/shard_map/ppermute | solution.py:750
  99.4 0.8 collective-permute-done.44.other
  100.3 0.8 shard_map.379
  101.0 0.9 shard_map.380
  (97 shorter events, 13.0 us)
Async XLA Ops:
  0.7 42.4 %copy-start = (f32[2,1,2,192,256]{4,3,2,1,0:T(8,128)S(1)}, f32[2,1,2,192,256]{4,3,2,1,0:T(8,128)}, u32[]{:S(2)}) copy-start(f32[2,1,2,192,256]{4,3,2,1,0:T(8,128)} %cotangent.1) | copy-start | bytes 2359300
  2.5 13.6 %collective-permute-start.2 = (bf16[240,256]{1,0:T(8,128)(2,1)}, bf16[240,256]{1,0:T(8,128)(2,1)S(1)}, u32[]{:S(2)}, u32[]{:S(2)}) collective-permute-start(bf16[240,256]{1,0:T(8,128)(2,1)} %shard_map.356.packed), channel_id=1, source_target_pairs={{0,3},{1,0},{2,1},{3,2},{4,7},{5,4},{6,5},{7,6},{8,11},{9,8},{10,9... | collective-permute-start | bytes 368648 | tf_op jit(solution)/shard_map/ppermute | solution.py:746
  2.5 13.6 %collective-permute-start.1 = (bf16[240,256]{1,0:T(8,128)(2,1)}, bf16[240,256]{1,0:T(8,128)(2,1)S(1)}, u32[]{:S(2)}, u32[]{:S(2)}) collective-permute-start(bf16[240,256]{1,0:T(8,128)(2,1)} %shard_map.356.packed), channel_id=1, source_target_pairs={{0,2},{1,3},{2,0},{3,1},{4,6},{5,7},{6,4},{7,5},{8,10},{9,11},{10,... | collective-permute-start | bytes 368648 | tf_op jit(solution)/shard_map/ppermute | solution.py:746
  5.0 11.1 %collective-permute-start = (bf16[240,256]{1,0:T(8,128)(2,1)}, bf16[240,256]{1,0:T(8,128)(2,1)S(1)}, u32[]{:S(2)}, u32[]{:S(2)}) collective-permute-start(bf16[240,256]{1,0:T(8,128)(2,1)} %shard_map.356.packed), channel_id=1, source_target_pairs={{0,1},{1,2},{2,3},{3,0},{4,5},{5,6},{6,7},{7,4},{8,9},{9,10},{10,1... | collective-permute-start | bytes 368648 | tf_op jit(solution)/shard_map/ppermute | solution.py:746
  14.9 28.2 %copy-start.11 = (bf16[64,256]{1,0:T(8,128)(2,1)S(1)}, bf16[64,256]{1,0:T(8,128)(2,1)}, u32[]{:S(2)}) copy-start(bf16[64,256]{1,0:T(8,128)(2,1)} %refs_7_.3) | copy-start | bytes 98308
  16.2 2.6 %collective-permute-start.3 = (bf16[240,256]{1,0:T(8,128)(2,1)S(1)}, bf16[240,256]{1,0:T(8,128)(2,1)S(1)}, u32[]{:S(2)}, u32[]{:S(2)}) collective-permute-start(bf16[240,256]{1,0:T(8,128)(2,1)S(1)} %get-tuple-element.130.refs_7_), channel_id=1, source_target_pairs={{0,4},{4,0},{8,12},{12,8},{16,20},{20,16},{24,28},{28,24},{1,5},{5... | collective-permute-start | bytes 368648 | tf_op jit(solution)/shard_map/ppermute | solution.py:750
  17.7 1.3 %collective-permute-start.4 = (bf16[240,256]{1,0:T(8,128)(2,1)S(1)}, bf16[240,256]{1,0:T(8,128)(2,1)S(1)}, u32[]{:S(2)}, u32[]{:S(2)}) collective-permute-start(bf16[240,256]{1,0:T(8,128)(2,1)S(1)} %get-tuple-element.131.refs_8_), channel_id=1, source_target_pairs={{0,4},{4,0},{8,12},{12,8},{16,20},{20,16},{24,28},{28,24},{1,5},{5... | collective-permute-start | bytes 368648 | tf_op jit(solution)/shard_map/ppermute | solution.py:750
  17.8 1.4 %collective-permute-start.5 = (bf16[240,256]{1,0:T(8,128)(2,1)S(1)}, bf16[240,256]{1,0:T(8,128)(2,1)S(1)}, u32[]{:S(2)}, u32[]{:S(2)}) collective-permute-start(bf16[240,256]{1,0:T(8,128)(2,1)S(1)} %get-tuple-element.132.refs_9_), channel_id=1, source_target_pairs={{0,4},{4,0},{8,12},{12,8},{16,20},{20,16},{24,28},{28,24},{1,5},{5... | collective-permute-start | bytes 368648 | tf_op jit(solution)/shard_map/ppermute | solution.py:750
  20.0 5.0 %collective-permute-start.11 = (bf16[192,256]{1,0:T(8,128)(2,1)S(1)}, bf16[192,256]{1,0:T(8,128)(2,1)S(1)}, u32[]{:S(2)}, u32[]{:S(2)}) collective-permute-start(bf16[192,256]{1,0:T(8,128)(2,1)S(1)} %get-tuple-element.138.refs_5_.refs_15_), channel_id=1, source_target_pairs={{0,24},{4,28},{8,16},{12,20},{16,8},{20,12},{24,0},{28,4},{1,25},{... | collective-permute-start | bytes 294920 | tf_op jit(solution)/shard_map/ppermute | solution.py:750
  22.2 5.4 %collective-permute-start.9 = (bf16[192,256]{1,0:T(8,128)(2,1)S(1)}, bf16[192,256]{1,0:T(8,128)(2,1)S(1)}, u32[]{:S(2)}, u32[]{:S(2)}) collective-permute-start(bf16[192,256]{1,0:T(8,128)(2,1)S(1)} %get-tuple-element.138.refs_5_.refs_15_), channel_id=1, source_target_pairs={{0,16},{4,20},{8,24},{12,28},{16,0},{20,4},{24,8},{28,12},{1,17},{... | collective-permute-start | bytes 294920 | tf_op jit(solution)/shard_map/ppermute | solution.py:750
  22.5 6.2 %collective-permute-start.7 = (bf16[192,256]{1,0:T(8,128)(2,1)S(1)}, bf16[192,256]{1,0:T(8,128)(2,1)S(1)}, u32[]{:S(2)}, u32[]{:S(2)}) collective-permute-start(bf16[192,256]{1,0:T(8,128)(2,1)S(1)} %get-tuple-element.138.refs_5_.refs_15_), channel_id=1, source_target_pairs={{0,8},{4,12},{8,0},{12,4},{16,24},{20,28},{24,16},{28,20},{1,9},{5... | collective-permute-start | bytes 294920 | tf_op jit(solution)/shard_map/ppermute | solution.py:750
  22.7 6.5 %collective-permute-start.6 = (bf16[192,256]{1,0:T(8,128)(2,1)S(1)}, bf16[192,256]{1,0:T(8,128)(2,1)S(1)}, u32[]{:S(2)}, u32[]{:S(2)}) collective-permute-start(bf16[192,256]{1,0:T(8,128)(2,1)S(1)} %get-tuple-element.138.refs_5_.refs_15_), channel_id=1, source_target_pairs={{0,4},{4,0},{8,12},{12,8},{16,20},{20,16},{24,28},{28,24},{1,5},{5... | collective-permute-start | bytes 294920 | tf_op jit(solution)/shard_map/ppermute | solution.py:750
  25.0 5.2 %collective-permute-start.12 = (bf16[192,256]{1,0:T(8,128)(2,1)S(1)}, bf16[192,256]{1,0:T(8,128)(2,1)S(1)}, u32[]{:S(2)}, u32[]{:S(2)}) collective-permute-start(bf16[192,256]{1,0:T(8,128)(2,1)S(1)} %collective-permute-done.11.refs_11_.refs_21_), channel_id=1, source_target_pairs={{0,4},{4,0},{8,12},{12,8},{16,20},{20,16},{24,28},{28,24},{1,5},{5... | collective-permute-start | bytes 294920 | tf_op jit(solution)/shard_map/ppermute | solution.py:750
  26.3 12.5 %collective-permute-start.15 = (bf16[288,256]{1,0:T(8,128)(2,1)S(1)}, bf16[288,256]{1,0:T(8,128)(2,1)S(1)}, u32[]{:S(2)}, u32[]{:S(2)}) collective-permute-start(bf16[288,256]{1,0:T(8,128)(2,1)S(1)} %get-tuple-element.140), channel_id=1, source_target_pairs={{0,3},{1,0},{2,1},{3,2},{4,7},{5,4},{6,5},{7,6},{8,11},{9,8},{10,9... | collective-permute-start | bytes 442376 | tf_op jit(solution)/shard_map/ppermute | solution.py:746
  27.6 11.1 %collective-permute-start.14 = (bf16[288,256]{1,0:T(8,128)(2,1)S(1)}, bf16[288,256]{1,0:T(8,128)(2,1)S(1)}, u32[]{:S(2)}, u32[]{:S(2)}) collective-permute-start(bf16[288,256]{1,0:T(8,128)(2,1)S(1)} %get-tuple-element.140), channel_id=1, source_target_pairs={{0,2},{1,3},{2,0},{3,1},{4,6},{5,7},{6,4},{7,5},{8,10},{9,11},{10,... | collective-permute-start | bytes 442376 | tf_op jit(solution)/shard_map/ppermute | solution.py:746
  28.7 12.2 %collective-permute-start.13 = (bf16[288,256]{1,0:T(8,128)(2,1)S(1)}, bf16[288,256]{1,0:T(8,128)(2,1)S(1)}, u32[]{:S(2)}, u32[]{:S(2)}) collective-permute-start(bf16[288,256]{1,0:T(8,128)(2,1)S(1)} %get-tuple-element.140), channel_id=1, source_target_pairs={{0,1},{1,2},{2,3},{3,0},{4,5},{5,6},{6,7},{7,4},{8,9},{9,10},{10,1... | collective-permute-start | bytes 442376 | tf_op jit(solution)/shard_map/ppermute | solution.py:746
  29.3 1.9 %collective-permute-start.10 = (bf16[192,256]{1,0:T(8,128)(2,1)S(1)}, bf16[192,256]{1,0:T(8,128)(2,1)S(1)}, u32[]{:S(2)}, u32[]{:S(2)}) collective-permute-start(bf16[192,256]{1,0:T(8,128)(2,1)S(1)} %collective-permute-done.9.refs_9_.refs_19_), channel_id=1, source_target_pairs={{0,4},{4,0},{8,12},{12,8},{16,20},{20,16},{24,28},{28,24},{1,5},{5... | collective-permute-start | bytes 294920 | tf_op jit(solution)/shard_map/ppermute | solution.py:750
  30.2 1.3 %collective-permute-start.8 = (bf16[192,256]{1,0:T(8,128)(2,1)S(1)}, bf16[192,256]{1,0:T(8,128)(2,1)S(1)}, u32[]{:S(2)}, u32[]{:S(2)}) collective-permute-start(bf16[192,256]{1,0:T(8,128)(2,1)S(1)} %collective-permute-done.7.refs_7_.refs_17_), channel_id=1, source_target_pairs={{0,4},{4,0},{8,12},{12,8},{16,20},{20,16},{24,28},{28,24},{1,5},{5... | collective-permute-start | bytes 294920 | tf_op jit(solution)/shard_map/ppermute | solution.py:750
  31.1 10.8 %collective-permute-start.19 = (bf16[4,192,128]{2,1,0:T(8,128)(2,1)S(1)}, bf16[4,192,128]{2,1,0:T(8,128)(2,1)S(1)}, u32[]{:S(2)}, u32[]{:S(2)}) collective-permute-start(bf16[4,192,128]{2,1,0:T(8,128)(2,1)S(1)} %get-tuple-element.145), channel_id=1, source_target_pairs={{0,4},{4,0},{8,12},{12,8},{16,20},{20,16},{24,28},{28,24},{1,5},{5... | collective-permute-start | bytes 589832 | tf_op jit(solution)/shard_map/ppermute | solution.py:750
  40.9 1.5 %collective-permute-start.16 = (bf16[288,256]{1,0:T(8,128)(2,1)S(1)}, bf16[288,256]{1,0:T(8,128)(2,1)S(1)}, u32[]{:S(2)}, u32[]{:S(2)}) collective-permute-start(bf16[288,256]{1,0:T(8,128)(2,1)S(1)} %get-tuple-element.142.refs_8_), channel_id=1, source_target_pairs={{0,4},{4,0},{8,12},{12,8},{16,20},{20,16},{24,28},{28,24},{1,5},{5... | collective-permute-start | bytes 442376 | tf_op jit(solution)/shard_map/ppermute | solution.py:750
  41.4 1.4 %collective-permute-start.17 = (bf16[288,256]{1,0:T(8,128)(2,1)S(1)}, bf16[288,256]{1,0:T(8,128)(2,1)S(1)}, u32[]{:S(2)}, u32[]{:S(2)}) collective-permute-start(bf16[288,256]{1,0:T(8,128)(2,1)S(1)} %get-tuple-element.143.refs_9_), channel_id=1, source_target_pairs={{0,4},{4,0},{8,12},{12,8},{16,20},{20,16},{24,28},{28,24},{1,5},{5... | collective-permute-start | bytes 442376 | tf_op jit(solution)/shard_map/ppermute | solution.py:750
  41.5 1.5 %collective-permute-start.18 = (bf16[288,256]{1,0:T(8,128)(2,1)S(1)}, bf16[288,256]{1,0:T(8,128)(2,1)S(1)}, u32[]{:S(2)}, u32[]{:S(2)}) collective-permute-start(bf16[288,256]{1,0:T(8,128)(2,1)S(1)} %get-tuple-element.144.refs_10_), channel_id=1, source_target_pairs={{0,4},{4,0},{8,12},{12,8},{16,20},{20,16},{24,28},{28,24},{1,5},{5... | collective-permute-start | bytes 442376 | tf_op jit(solution)/shard_map/ppermute | solution.py:750
  47.3 5.7 %collective-permute-start.20 = (bf16[4,256,256]{2,1,0:T(8,128)(2,1)S(1)}, bf16[4,256,256]{2,1,0:T(8,128)(2,1)S(1)}, u32[]{:S(2)}, u32[]{:S(2)}) collective-permute-start(bf16[4,256,256]{2,1,0:T(8,128)(2,1)S(1)} %get-tuple-element.164), channel_id=1, source_target_pairs={{0,4},{4,0},{8,12},{12,8},{16,20},{20,16},{24,28},{28,24},{1,5},{5... | collective-permute-start | bytes 1572872 | tf_op jit(solution)/shard_map/ppermute | solution.py:750
  53.1 11.2 %collective-permute-start.23 = (bf16[4,64,256]{2,1,0:T(8,128)(2,1)S(1)}, bf16[4,64,256]{2,1,0:T(8,128)(2,1)S(1)}, u32[]{:S(2)}, u32[]{:S(2)}) collective-permute-start(bf16[4,64,256]{2,1,0:T(8,128)(2,1)S(1)} %get-tuple-element.181), channel_id=1, source_target_pairs={{0,8},{4,12},{8,0},{12,4},{16,24},{20,28},{24,16},{28,20},{1,9},{5... | collective-permute-start | bytes 393224 | tf_op jit(solution)/shard_map/ppermute | solution.py:750
  55.0 9.9 %collective-permute-start.24 = (bf16[4,64,256]{2,1,0:T(8,128)(2,1)S(1)}, bf16[4,64,256]{2,1,0:T(8,128)(2,1)S(1)}, u32[]{:S(2)}, u32[]{:S(2)}) collective-permute-start(bf16[4,64,256]{2,1,0:T(8,128)(2,1)S(1)} %get-tuple-element.182), channel_id=1, source_target_pairs={{0,16},{4,20},{8,24},{12,28},{16,0},{20,4},{24,8},{28,12},{1,17},{... | collective-permute-start | bytes 393224 | tf_op jit(solution)/shard_map/ppermute | solution.py:750
  56.4 8.5 %collective-permute-start.25 = (bf16[4,64,256]{2,1,0:T(8,128)(2,1)S(1)}, bf16[4,64,256]{2,1,0:T(8,128)(2,1)S(1)}, u32[]{:S(2)}, u32[]{:S(2)}) collective-permute-start(bf16[4,64,256]{2,1,0:T(8,128)(2,1)S(1)} %get-tuple-element.183), channel_id=1, source_target_pairs={{0,24},{4,28},{8,16},{12,20},{16,8},{20,12},{24,0},{28,4},{1,25},{... | collective-permute-start | bytes 393224 | tf_op jit(solution)/shard_map/ppermute | solution.py:750
  56.4 8.6 %collective-permute-start.21 = (bf16[4,96,256]{2,1,0:T(8,128)(2,1)S(1)}, bf16[4,96,256]{2,1,0:T(8,128)(2,1)S(1)}, u32[]{:S(2)}, u32[]{:S(2)}) collective-permute-start(bf16[4,96,256]{2,1,0:T(8,128)(2,1)S(1)} %get-tuple-element.179), channel_id=1, source_target_pairs={{0,4},{4,0},{8,12},{12,8},{16,20},{20,16},{24,28},{28,24},{1,5},{5... | collective-permute-start | bytes 589832 | tf_op jit(solution)/shard_map/ppermute | solution.py:750
  61.6 3.3 %collective-permute-start.22 = (bf16[4,96,256]{2,1,0:T(8,128)(2,1)S(1)}, bf16[4,96,256]{2,1,0:T(8,128)(2,1)S(1)}, u32[]{:S(2)}, u32[]{:S(2)}) collective-permute-start(bf16[4,96,256]{2,1,0:T(8,128)(2,1)S(1)} %get-tuple-element.180), channel_id=1, source_target_pairs={{0,4},{4,0},{8,12},{12,8},{16,20},{20,16},{24,28},{28,24},{1,5},{5... | collective-permute-start | bytes 589832 | tf_op jit(solution)/shard_map/ppermute | solution.py:750
  64.3 3.7 %collective-permute-start.37 = (bf16[4,128,256]{2,1,0:T(8,128)(2,1)S(1)}, bf16[4,128,256]{2,1,0:T(8,128)(2,1)S(1)}, u32[]{:S(2)}, u32[]{:S(2)}) collective-permute-start(bf16[4,128,256]{2,1,0:T(8,128)(2,1)S(1)} %get-tuple-element.203), channel_id=1, source_target_pairs={{0,4},{4,0},{8,12},{12,8},{16,20},{20,16},{24,28},{28,24},{1,5},{5... | collective-permute-start | bytes 786440 | tf_op jit(solution)/shard_map/ppermute | solution.py:750
  65.1 5.3 %collective-permute-start.26 = (bf16[192,256]{1,0:T(8,128)(2,1)S(1)}, bf16[192,256]{1,0:T(8,128)(2,1)S(1)}, u32[]{:S(2)}, u32[]{:S(2)}) collective-permute-start(bf16[192,256]{1,0:T(8,128)(2,1)S(1)} %get-tuple-element.186), channel_id=1, source_target_pairs={{0,8},{4,12},{8,0},{12,4},{16,24},{20,28},{24,16},{28,20},{1,9},{5... | collective-permute-start | bytes 294920 | tf_op jit(solution)/shard_map/ppermute | solution.py:750
  66.7 4.1 %collective-permute-start.27 = (bf16[192,256]{1,0:T(8,128)(2,1)S(1)}, bf16[192,256]{1,0:T(8,128)(2,1)S(1)}, u32[]{:S(2)}, u32[]{:S(2)}) collective-permute-start(bf16[192,256]{1,0:T(8,128)(2,1)S(1)} %get-tuple-element.187), channel_id=1, source_target_pairs={{0,16},{4,20},{8,24},{12,28},{16,0},{20,4},{24,8},{28,12},{1,17},{... | collective-permute-start | bytes 294920 | tf_op jit(solution)/shard_map/ppermute | solution.py:750
  68.1 4.4 %collective-permute-start.28 = (bf16[192,256]{1,0:T(8,128)(2,1)S(1)}, bf16[192,256]{1,0:T(8,128)(2,1)S(1)}, u32[]{:S(2)}, u32[]{:S(2)}) collective-permute-start(bf16[192,256]{1,0:T(8,128)(2,1)S(1)} %get-tuple-element.188), channel_id=1, source_target_pairs={{0,24},{4,28},{8,16},{12,20},{16,8},{20,12},{24,0},{28,4},{1,25},{... | collective-permute-start | bytes 294920 | tf_op jit(solution)/shard_map/ppermute | solution.py:750
  68.1 13.1 %collective-permute-start.38 = (bf16[192,256]{1,0:T(8,128)(2,1)S(1)}, bf16[192,256]{1,0:T(8,128)(2,1)S(1)}, u32[]{:S(2)}, u32[]{:S(2)}) collective-permute-start(bf16[192,256]{1,0:T(8,128)(2,1)S(1)} %get-tuple-element.205), channel_id=1, source_target_pairs={{0,1},{1,2},{2,3},{3,0},{4,5},{5,6},{6,7},{7,4},{8,9},{9,10},{10,1... | collective-permute-start | bytes 294920 | tf_op jit(solution)/shard_map/ppermute | solution.py:746
  72.7 5.8 %collective-permute-start.29 = (bf16[96,256]{1,0:T(8,128)(2,1)S(1)}, bf16[96,256]{1,0:T(8,128)(2,1)S(1)}, u32[]{:S(2)}, u32[]{:S(2)}) collective-permute-start(bf16[96,256]{1,0:T(8,128)(2,1)S(1)} %get-tuple-element.190.refs_0_.refs_2_), channel_id=1, source_target_pairs={{0,4},{4,0},{8,12},{12,8},{16,20},{20,16},{24,28},{28,24},{1,5},{5... | collective-permute-start | bytes 147464 | tf_op jit(solution)/shard_map/ppermute | solution.py:750
  74.5 4.0 %collective-permute-start.30 = (bf16[96,256]{1,0:T(8,128)(2,1)S(1)}, bf16[96,256]{1,0:T(8,128)(2,1)S(1)}, u32[]{:S(2)}, u32[]{:S(2)}) collective-permute-start(bf16[96,256]{1,0:T(8,128)(2,1)S(1)} %get-tuple-element.191.refs_1_.refs_3_), channel_id=1, source_target_pairs={{0,4},{4,0},{8,12},{12,8},{16,20},{20,16},{24,28},{28,24},{1,5},{5... | collective-permute-start | bytes 147464 | tf_op jit(solution)/shard_map/ppermute | solution.py:750
  74.6 7.9 %collective-permute-start.39 = (bf16[192,256]{1,0:T(8,128)(2,1)S(1)}, bf16[192,256]{1,0:T(8,128)(2,1)S(1)}, u32[]{:S(2)}, u32[]{:S(2)}) collective-permute-start(bf16[192,256]{1,0:T(8,128)(2,1)S(1)} %get-tuple-element.206), channel_id=1, source_target_pairs={{0,2},{1,3},{2,0},{3,1},{4,6},{5,7},{6,4},{7,5},{8,10},{9,11},{10,... | collective-permute-start | bytes 294920 | tf_op jit(solution)/shard_map/ppermute | solution.py:746
  74.7 12.9 %collective-permute-start.40 = (bf16[192,256]{1,0:T(8,128)(2,1)S(1)}, bf16[192,256]{1,0:T(8,128)(2,1)S(1)}, u32[]{:S(2)}, u32[]{:S(2)}) collective-permute-start(bf16[192,256]{1,0:T(8,128)(2,1)S(1)} %get-tuple-element.207), channel_id=1, source_target_pairs={{0,3},{1,0},{2,1},{3,2},{4,7},{5,4},{6,5},{7,6},{8,11},{9,8},{10,9... | collective-permute-start | bytes 294920 | tf_op jit(solution)/shard_map/ppermute | solution.py:746
  78.9 11.0 %collective-permute-start.31 = (bf16[144,256]{1,0:T(8,128)(2,1)S(1)}, bf16[144,256]{1,0:T(8,128)(2,1)S(1)}, u32[]{:S(2)}, u32[]{:S(2)}) collective-permute-start(bf16[144,256]{1,0:T(8,128)(2,1)S(1)} %get-tuple-element.198), channel_id=1, source_target_pairs={{0,1},{1,2},{2,3},{3,0},{4,5},{5,6},{6,7},{7,4},{8,9},{9,10},{10,1... | collective-permute-start | bytes 221192 | tf_op jit(solution)/shard_map/ppermute | solution.py:746
  79.0 11.5 %collective-permute-start.32 = (bf16[144,256]{1,0:T(8,128)(2,1)S(1)}, bf16[144,256]{1,0:T(8,128)(2,1)S(1)}, u32[]{:S(2)}, u32[]{:S(2)}) collective-permute-start(bf16[144,256]{1,0:T(8,128)(2,1)S(1)} %get-tuple-element.199), channel_id=1, source_target_pairs={{0,2},{1,3},{2,0},{3,1},{4,6},{5,7},{6,4},{7,5},{8,10},{9,11},{10,... | collective-permute-start | bytes 221192 | tf_op jit(solution)/shard_map/ppermute | solution.py:746
  81.2 9.6 %collective-permute-start.33 = (bf16[144,256]{1,0:T(8,128)(2,1)S(1)}, bf16[144,256]{1,0:T(8,128)(2,1)S(1)}, u32[]{:S(2)}, u32[]{:S(2)}) collective-permute-start(bf16[144,256]{1,0:T(8,128)(2,1)S(1)} %get-tuple-element.200), channel_id=1, source_target_pairs={{0,3},{1,0},{2,1},{3,2},{4,7},{5,4},{6,5},{7,6},{8,11},{9,8},{10,9... | collective-permute-start | bytes 221192 | tf_op jit(solution)/shard_map/ppermute | solution.py:746
  87.7 5.3 %collective-permute-start.43 = (bf16[192,256]{1,0:T(8,128)(2,1)S(1)}, bf16[192,256]{1,0:T(8,128)(2,1)S(1)}, u32[]{:S(2)}, u32[]{:S(2)}) collective-permute-start(bf16[192,256]{1,0:T(8,128)(2,1)S(1)} %shard_map.376.refs_0_), channel_id=1, source_target_pairs={{0,24},{4,28},{8,16},{12,20},{16,8},{20,12},{24,0},{28,4},{1,25},{... | collective-permute-start | bytes 294920 | tf_op jit(solution)/shard_map/ppermute | solution.py:750
  88.9 7.4 %collective-permute-start.42 = (bf16[192,256]{1,0:T(8,128)(2,1)S(1)}, bf16[192,256]{1,0:T(8,128)(2,1)S(1)}, u32[]{:S(2)}, u32[]{:S(2)}) collective-permute-start(bf16[192,256]{1,0:T(8,128)(2,1)S(1)} %shard_map.376.refs_0_), channel_id=1, source_target_pairs={{0,16},{4,20},{8,24},{12,28},{16,0},{20,4},{24,8},{28,12},{1,17},{... | collective-permute-start | bytes 294920 | tf_op jit(solution)/shard_map/ppermute | solution.py:750
  89.9 6.4 %collective-permute-start.41 = (bf16[192,256]{1,0:T(8,128)(2,1)S(1)}, bf16[192,256]{1,0:T(8,128)(2,1)S(1)}, u32[]{:S(2)}, u32[]{:S(2)}) collective-permute-start(bf16[192,256]{1,0:T(8,128)(2,1)S(1)} %shard_map.376.refs_0_), channel_id=1, source_target_pairs={{0,8},{4,12},{8,0},{12,4},{16,24},{20,28},{24,16},{28,20},{1,9},{5... | collective-permute-start | bytes 294920 | tf_op jit(solution)/shard_map/ppermute | solution.py:750
  90.9 5.5 %collective-permute-start.36 = (bf16[144,256]{1,0:T(8,128)(2,1)S(1)}, bf16[144,256]{1,0:T(8,128)(2,1)S(1)}, u32[]{:S(2)}, u32[]{:S(2)}) collective-permute-start(bf16[144,256]{1,0:T(8,128)(2,1)S(1)} %shard_map.374.refs_4_.refs_0_), channel_id=1, source_target_pairs={{0,24},{4,28},{8,16},{12,20},{16,8},{20,12},{24,0},{28,4},{1,25},{... | collective-permute-start | bytes 221192 | tf_op jit(solution)/shard_map/ppermute | solution.py:750
  92.0 6.5 %collective-permute-start.35 = (bf16[144,256]{1,0:T(8,128)(2,1)S(1)}, bf16[144,256]{1,0:T(8,128)(2,1)S(1)}, u32[]{:S(2)}, u32[]{:S(2)}) collective-permute-start(bf16[144,256]{1,0:T(8,128)(2,1)S(1)} %shard_map.374.refs_4_.refs_0_), channel_id=1, source_target_pairs={{0,16},{4,20},{8,24},{12,28},{16,0},{20,4},{24,8},{28,12},{1,17},{... | collective-permute-start | bytes 221192 | tf_op jit(solution)/shard_map/ppermute | solution.py:750
  93.0 5.5 %collective-permute-start.34 = (bf16[144,256]{1,0:T(8,128)(2,1)S(1)}, bf16[144,256]{1,0:T(8,128)(2,1)S(1)}, u32[]{:S(2)}, u32[]{:S(2)}) collective-permute-start(bf16[144,256]{1,0:T(8,128)(2,1)S(1)} %shard_map.374.refs_4_.refs_0_), channel_id=1, source_target_pairs={{0,8},{4,12},{8,0},{12,4},{16,24},{20,28},{24,16},{28,20},{1,9},{5... | collective-permute-start | bytes 221192 | tf_op jit(solution)/shard_map/ppermute | solution.py:750
  98.6 1.6 %collective-permute-start.44 = (bf16[144,256]{1,0:T(8,128)(2,1)S(1)}, bf16[144,256]{1,0:T(8,128)(2,1)S(1)}, u32[]{:S(2)}, u32[]{:S(2)}) collective-permute-start(bf16[144,256]{1,0:T(8,128)(2,1)S(1)} %shard_map.378.mine), channel_id=1, source_target_pairs={{0,4},{4,0},{8,12},{12,8},{16,20},{20,16},{24,28},{28,24},{1,5},{5... | collective-permute-start | bytes 221192 | tf_op jit(solution)/shard_map/ppermute | solution.py:750
  99.3 1.7 %collective-permute-start.45 = (bf16[384,256]{1,0:T(8,128)(2,1)S(1)}, bf16[384,256]{1,0:T(8,128)(2,1)S(1)}, u32[]{:S(2)}, u32[]{:S(2)}) collective-permute-start(bf16[384,256]{1,0:T(8,128)(2,1)S(1)} %shard_map.377.refs_4_.mine), channel_id=1, source_target_pairs={{0,4},{4,0},{8,12},{12,8},{16,20},{20,16},{24,28},{28,24},{1,5},{5... | collective-permute-start | bytes 589832 | tf_op jit(solution)/shard_map/ppermute | solution.py:750
  (12 other events, 92.1 us)

commit v4 on v3

--- a/solution.py
+++ b/solution.py
@@ -163,9 +163,9 @@
 
 def reduce_kernel(dims, *refs):
     n_fs, batches, row_dev, cols, dim = dims
-    ins, mine, other, outs = take(refs, 7, n_fs - 1, n_fs - 1)
-    normal_in, mask_ref, own_w, own_q, own_kv, own_vec, second_in = ins
-    normed_ref, cols_ref, send_ref, reduced_ref, key_ref, weight_ref, wq, wkv, vec_ref, second, patch_ref, wide = outs
+    ins, mine, other, outs = take(refs, 6, n_fs - 1, n_fs - 1)
+    normal_in, mask_ref, own_w, own_q, own_kv, own_vec = ins
+    normed_ref, cols_ref, send_ref, reduced_ref, key_ref, weight_ref, wq, wkv, vec_ref, patch_ref, wide = outs
     half = dim // 2
     shard = dim // n_fs
     rest = half + VECS
@@ -173,7 +173,6 @@
     half_cols = cols // 2
     key_dev = tok // 4
     fs = lax.axis_index("fs")
-    second[...] = second_in[...]
     weight_ref[fs] = own_w[...]
     here = shard_rows(fs, shard)
     wq[here, :] = own_q[...]
@@ -276,95 +275,84 @@
 
 
 def forward_kernel(dims, *refs):
-    batches, tok, key_dev, keys, block, n_pieces = dims
-    (normed, vec_ref, bias_ref, wq, wkv), pieces, (attended, *kept, wide) = take(refs, 5, n_pieces)
-    queries_out, kvs, attf, stats, probs = (
-        kept[index * batches : (index + 1) * batches] for index in range(5)
-    )
+    batch, tok, key_dev, keys, block, n_pieces = dims
+    (normed, vec_ref, bias_ref, wq, wkv), pieces, outs = take(refs, 5, n_pieces)
+    attended, queries_out, kvs, attf, stats, probs, wide = outs
     dim = wq.shape[0]
     blocks = keys // block
     per_block = block // key_dev
-    queries_t, values_t, masked = [], [], []
-    for batch in range(batches):
-        rows = slice(batch * tok, (batch + 1) * tok)
-        queries = (mm(normed[rows], wq[...]) + vec_ref[QUERY_B : QUERY_B + 1]).astype(bf16)
-        queries_out[batch][...] = queries
-        queries_t.append(queries.T)
-        for index in range(blocks):
-            key_rows = key_rows_of(pieces, key_dev, per_block, batch, index)
-            here = slice(index * block, (index + 1) * block)
-            kvs[batch][here, :dim] = mm(key_rows, wkv[:, :dim]).astype(bf16)
-            value_rows = mm(key_rows, wkv[:, dim:]) + vec_ref[VALUE_B : VALUE_B + 1]
-            kvs[batch][here, dim:] = value_rows.astype(bf16)
+    queries = (mm(normed[batch * tok : (batch + 1) * tok], wq[...]) + vec_ref[QUERY_B : QUERY_B + 1]).astype(bf16)
+    queries_out[...] = queries
+    queries_t = queries.T
+    for index in range(blocks):
+        key_rows = key_rows_of(pieces, key_dev, per_block, batch, index)
+        here = slice(index * block, (index + 1) * block)
+        kvs[here, :dim] = mm(key_rows, wkv[:, :dim]).astype(bf16)
+        value_rows = mm(key_rows, wkv[:, dim:]) + vec_ref[VALUE_B : VALUE_B + 1]
+        kvs[here, dim:] = value_rows.astype(bf16)
     if blocks == 1:
-        for batch in range(batches):
-            key_block = kvs[batch][:, :dim]
-            bias = bias_ref[batch]
-            values_t.append(kvs[batch][:, dim:].T)
-            masked.append({lane_id: with_bias(key_block, bias, lane_id) for lane_id in (0, dim - 1)})
-        todo = [(batch, pair) for batch in range(batches) for pair in range(PAIRS)]
-
-        def score(index):
-            batch, pair = todo[index]
+        key_block = kvs[:, :dim]
+        values_t = kvs[:, dim:].T
+        masked = {lane_id: with_bias(key_block, bias_ref[batch], lane_id) for lane_id in (0, dim - 1)}
+
+        def score(pair):
             lane_id = mask_lane(pair, dim)
-            wide[index % 2] = mm(masked[batch][lane_id], query_stack(queries_t[batch], pair, lane_id, tok))
+            wide[pair % 2] = mm(masked[lane_id], query_stack(queries_t, pair, lane_id, tok))
 
         score(0)
-        for index, (batch, pair) in enumerate(todo):
-            if index + 1 < len(todo):
-                score(index + 1)
+        for pair in range(PAIRS):
+            if pair + 1 < PAIRS:
+                score(pair + 1)
             heads = slice(2 * HDIM * pair, 2 * HDIM * (pair + 1))
-            scores = wide[index % 2]
+            scores = wide[pair % 2]
             top = jnp.max(scores, axis=0, keepdims=True)
             weights = jnp.exp2((scores - top) * EXP_SCALE)
             inverse = 1.0 / jnp.sum(weights, axis=0, keepdims=True)
             low = weights.astype(bf16)
-            probs[batch][pair] = low
-            stats[batch][pair, 0:1] = inverse
-            mixed = mm(values_t[batch][heads], low) * inverse
-            attf[batch][heads] = split_pair(mixed, tok)
+            probs[pair] = low
+            stats[pair, 0:1] = inverse
+            mixed = mm(values_t[heads], low) * inverse
+            attf[heads] = split_pair(mixed, tok)
     else:
-        for batch in range(batches):
-            for pair in range(PAIRS):
-                lane_id = mask_lane(pair, dim)
-                heads = slice(2 * HDIM * pair, 2 * HDIM * (pair + 1))
-                stacked = query_stack(queries_t[batch], pair, lane_id, tok)
-
-                def block_scores(index, stacked=stacked, lane_id=lane_id, batch=batch):
-                    here = pl.ds(pl.multiple_of(index * block, block), block)
-                    masked = with_bias(kvs[batch][here, :dim], bias_ref[batch, here, :], lane_id)
-                    return here, mm(masked, stacked)
-
-                def find_top(index, top, block_scores=block_scores):
-                    _, scores = block_scores(index)
-                    return jnp.maximum(top, jnp.max(scores, axis=0, keepdims=True))
-
-                top = lax.fori_loop(0, blocks, find_top, jnp.full((1, 2 * tok), 4 * NEG, f32))
-
-                def add_block(index, carry, block_scores=block_scores, top=top, heads=heads, batch=batch):
-                    total, mixed = carry
-                    here, scores = block_scores(index)
-                    weights = jnp.exp2((scores - top) * EXP_SCALE)
-                    values_t = kvs[batch][here, dim:].T
-                    mixed = mixed + mm(values_t[heads], weights.astype(bf16))
-                    return total + jnp.sum(weights, axis=0, keepdims=True), mixed
-
-                start = (jnp.zeros((1, 2 * tok), f32), jnp.zeros((2 * HDIM, 2 * tok), f32))
-                total, mixed = lax.fori_loop(0, blocks, add_block, start)
-                inverse = 1.0 / total
-                stats[batch][pair, 0:1] = inverse
-                stats[batch][pair, 1:2] = top
-                attf[batch][heads] = split_pair(mixed * inverse, tok)
-    for batch in range(batches):
-        attended[batch * tok : (batch + 1) * tok] = attf[batch][...].T.astype(bf16)
+        for pair in range(PAIRS):
+            lane_id = mask_lane(pair, dim)
+            heads = slice(2 * HDIM * pair, 2 * HDIM * (pair + 1))
+            stacked = query_stack(queries_t, pair, lane_id, tok)
+
+            def block_scores(index, stacked=stacked, lane_id=lane_id):
+                here = pl.ds(pl.multiple_of(index * block, block), block)
+                masked = with_bias(kvs[here, :dim], bias_ref[batch, here, :], lane_id)
+                return here, mm(masked, stacked)
+
+            def find_top(index, top, block_scores=block_scores):
+                _, scores = block_scores(index)
+                return jnp.maximum(top, jnp.max(scores, axis=0, keepdims=True))
+
+            top = lax.fori_loop(0, blocks, find_top, jnp.full((1, 2 * tok), 4 * NEG, f32))
+
+            def add_block(index, carry, block_scores=block_scores, top=top, heads=heads):
+                total, mixed = carry
+                here, scores = block_scores(index)
+                weights = jnp.exp2((scores - top) * EXP_SCALE)
+                values_t = kvs[here, dim:].T
+                mixed = mixed + mm(values_t[heads], weights.astype(bf16))
+                return total + jnp.sum(weights, axis=0, keepdims=True), mixed
+
+            start = (jnp.zeros((1, 2 * tok), f32), jnp.zeros((2 * HDIM, 2 * tok), f32))
+            total, mixed = lax.fori_loop(0, blocks, add_block, start)
+            inverse = 1.0 / total
+            stats[pair, 0:1] = inverse
+            stats[pair, 1:2] = top
+            attf[heads] = split_pair(mixed * inverse, tok)
+    attended[...] = attf[...].T.astype(bf16)
 
 
 def mlp_kernel(dims, *refs):
     n_fs, batches, row_dev, cols, dim, hid = dims
-    ins, own, mine, other, _, outs, scratch = take(refs, 5, 3, n_fs - 1, n_fs - 1, 1, 7)
-    tokens, cotangent, mask_ref, attended, vec_ref = ins
-    acts_ref, normal_ref, rstd_ref, grad_ref, keep_ref, send_ref, wo = outs
-    wh, wr, bias_rows, lows, highs = scratch
+    ins, attended, own, mine, other, _, outs, scratch = take(refs, 4, batches, 3, n_fs - 1, n_fs - 1, 1, 6)
+    tokens, cotangent, mask_ref, vec_ref = ins
+    acts_ref, middle_ref, gatt, keep_ref, send_ref, gvec_ref = outs
+    wh, wr, wo, lows, highs = scratch
     tok = row_dev * cols
     shard = dim // n_fs
     chunks = hid // dim
@@ -375,7 +363,7 @@
     wo[shard_rows(fs, shard), :] = own[2][...]
     for step in range(1, n_fs):
         low, high = both_halves(mine[step - 1], other[step - 1])
-        place = lax.rem(fs + n_fs - step, n_fs)
+        place = fs ^ step
         here = shard_rows(place, shard)
         for chunk in range(chunks):
             wh[here, chunk * dim : (chunk + 1) * dim] = low[chunk * shard : (chunk + 1) * shard]
@@ -387,16 +375,15 @@
 
     x = jnp.concatenate([tokens[b, 0].reshape(tok, dim).astype(f32) for b in range(batches)], axis=0)
     mask = mask_ref[...]
-    middle = x + mm(attended[...], wo[...]) + vec(OUTPUT_B)
+    attended = jnp.concatenate([part[...] for part in attended], axis=0)
+    middle = x + mm(attended, wo[...]) + vec(OUTPUT_B)
     normal, rstd = normalize(middle)
-    normal_ref[...] = normal
-    rstd_ref[...] = jnp.broadcast_to(rstd, rstd_ref.shape)
     second = (normal * vec(SECOND_G) + vec(SECOND_B)).astype(bf16)
     grad_out = jnp.concatenate([cotangent[b, 0].reshape(tok, dim) for b in range(batches)], axis=0) * mask
     grad_mlp = grad_out.astype(bf16)
     total = middle + vec(RETURN_B)
     grad_second = jnp.zeros((batches * tok, dim), f32)
-    bias_rows[...] = jnp.zeros_like(bias_rows)
+    gvec_ref[...] = jnp.zeros_like(gvec_ref)
     for chunk in range(chunks):
         lanes = slice(chunk * dim, (chunk + 1) * dim)
         hidden = mm(second, wh[:, lanes]) + vec(HIDDEN_B + chunk)
@@ -406,7 +393,9 @@
         total = total + mm(activated, wr[lanes, :])
         grad_activated = mm_nt(grad_mlp, wr[lanes, :])
         grad_hidden = ((phi + hidden * density) * grad_activated).astype(bf16)
-        bias_rows[chunk : chunk + 1] = jnp.sum(grad_hidden.astype(f32), axis=0, keepdims=True)
+        gvec_ref[HIDDEN_B + chunk : HIDDEN_B + chunk + 1] = jnp.sum(
+            grad_hidden.astype(f32), axis=0, keepdims=True
+        )
         grad_second = grad_second + mm_nt(grad_hidden, wh[:, lanes])
         highs[chunk] = mm_tn(activated, grad_mlp).astype(bf16)
         grad_wh = mm_tn(second, grad_hidden).astype(bf16)
@@ -418,33 +407,17 @@
     total = total * mask
     for batch in range(batches):
         acts_ref[batch, 0] = total[batch * tok : (batch + 1) * tok].reshape(row_dev, cols, dim)
-    rows = batches * tok
-    grad_ref[:rows] = grad_second
-    grad_ref[rows:] = bias_rows[...]
-
-
-def middle_kernel(dims, cotangent, mask_ref, normal_ref, rstd_ref, grad_ref, vec_ref, wo, middle_ref, gatt, gvec_ref):
-    batches, tok, chunks = dims
-    dim = wo.shape[0]
-    rows = batches * tok
-    grad_out = jnp.concatenate([cotangent[b, 0].reshape(tok, dim) for b in range(batches)], axis=0)
-    grad_out = grad_out * mask_ref[...]
-    grad_second, normal = grad_ref[:rows], normal_ref[...]
-    rstd = jnp.concatenate([rstd_ref[...]] * (dim // rstd_ref.shape[1]), axis=1)
-    back = normalize_back(grad_second, normal, rstd, vec_ref[SECOND_G : SECOND_G + 1])
-    grad_middle = grad_out + back
+    grad_middle = grad_out + normalize_back(grad_second, normal, rstd, vec(SECOND_G))
     middle_ref[...] = grad_middle
     grad_branch = grad_middle.astype(bf16)
     gatt[...] = mm_nt(grad_branch, wo[...]).astype(bf16)
-    gvec_ref[...] = jnp.zeros_like(gvec_ref)
     for index, value in (
         (OUTPUT_B, grad_branch.astype(f32)),
         (SECOND_G, grad_second * normal),
         (SECOND_B, grad_second),
-        (RETURN_B, grad_out.astype(bf16).astype(f32)),
+        (RETURN_B, grad_mlp.astype(f32)),
     ):
         gvec_ref[index : index + 1] = jnp.sum(value, axis=0, keepdims=True)
-    gvec_ref[HIDDEN_B : HIDDEN_B + chunks] = grad_ref[rows : rows + chunks]
 
 
 def backward_kernel(dims, *refs):
@@ -470,14 +443,24 @@
         return delta * inverse, stacked.astype(bf16)
 
     if blocks == 1:
+        (wide,) = refs[15:]
         values = kvs[:, dim:]
         grad_k = jnp.zeros((keys, dim), f32)
         grad_v = jnp.zeros((keys, dim), f32)
+        terms = []
+
+        def grad_prob(pair):
+            delta, stacked = pair_terms(pair)
+            wide[pair % 2] = mm(values, stacked)
+            terms.append((delta, stacked))
+
+        grad_prob(0)
         for pair in range(PAIRS):
-            delta, stacked = pair_terms(pair)
+            if pair + 1 < PAIRS:
+                grad_prob(pair + 1)
+            delta, stacked = terms[pair]
             low = probs[pair]
-            grad_probs = mm(values, stacked)
-            grad_scores = (low.astype(f32) * (grad_probs - delta)).astype(bf16)
+            grad_scores = (low.astype(f32) * (wide[pair % 2] - delta)).astype(bf16)
             scores_ref[pair] = grad_scores
             grad_k = grad_k + mm(grad_scores, head_stack(queries, pair))
             grad_v = grad_v + mm(low, stacked.T)
@@ -530,8 +513,8 @@
 
 def query_kernel(dims, *refs):
     n_fs, batches, tok, key_dev, keys, block, n_pieces = dims
-    ins, kvs, scores, gks, gvs, gvecs, pieces, outs = take(refs, 5, *([batches] * 5), n_pieces)
-    normed, wq, attended, middle, _ = ins
+    ins, attended, kvs, scores, gks, gvs, gvecs, pieces, outs = take(refs, 3, *([batches] * 6), n_pieces)
+    normed, wq, middle = ins
     keep_ref, send_ref, gnormed_ref, gvec_ref, wide = outs
     dim = wq.shape[0]
     shard = dim // n_fs
@@ -557,7 +540,8 @@
             grad_wv = grad_wv + mm_tn(key_rows, gvs[batch][here])
     grad_queries = jnp.concatenate(grad_queries, axis=0)
     grad_wq = mm_tn(normed[...], grad_queries)
-    grad_wo = mm_tn(attended[...], middle[...].astype(bf16))
+    attended = jnp.concatenate([part[...] for part in attended], axis=0)
+    grad_wo = mm_tn(attended, middle[...].astype(bf16))
     is_low = lax.axis_index("sp") % 2 == 0
     for owner in range(n_fs):
         part = slice(owner * shard, (owner + 1) * shard)
@@ -644,7 +628,7 @@
     gvec_ref[...] = vectors.astype(bf16)
 
 
-def input_kernel(dims, middle, grad_normed, normal_ref, rstd_ref, vec_ref, grad_ref, done_ref):
+def input_kernel(dims, middle, grad_normed, normal_ref, rstd_ref, vec_ref, _, grad_ref, done_ref):
     batches, row_dev, cols, dim = dims
     tok = row_dev * cols
     rstd = jnp.concatenate([rstd_ref[...]] * (dim // rstd_ref.shape[1]), axis=1)
@@ -744,6 +728,10 @@
 
 def rotate(value, n, step):
     return lax.ppermute(value, "fs", [(i, (i + step) % n) for i in range(n)])
+
+
+def swap(value, n, bits):
+    return lax.ppermute(value, "fs", [(i, i ^ bits) for i in range(n)])
 
 
 def flip(value, n, bits):
@@ -880,7 +868,7 @@
         *mine_first, own_vec
     )
     other_first = [flip(piece, n_sp, 1) for piece in mine_first]
-    normed, patch_cols, patch_send, reduced, key_low, whole_reduce, wq, wkv, vec, second_half = call(
+    normed, patch_cols, patch_send, reduced, key_low, whole_reduce, wq, wkv, vec = call(
         functools.partial(reduce_kernel, (n_fs, batches, row_dev, cols, dim)),
         [
             shape(batches * tok, dim),
@@ -892,11 +880,12 @@
             shape(dim, dim),
             shape(dim, 2 * dim),
             shape(VECS, dim, dtype=f32),
-            shape(dim + shard // 2, dim),
         ],
         scratch=[pltpu.VMEM((batches * key_dev, 4 * dim), bf16), pltpu.VMEM((dim // 128, tok, 128), f32)],
-    )(normal_first, mask, own_r, own_q, own_kv, own_vec, second_half, *mine_first, *other_first)
-    mine_second = to_owners([second_half] * n_fs, n_fs)[1:]
+    )(normal_first, mask, own_r, own_q, own_kv, own_vec, *mine_first, *other_first)
+    across = swap(second_half, n_fs, 2)
+    passed = call(functools.partial(relay_kernel, 1), [shape(dim + shard // 2, dim)], micros=15)(across, own_vec)
+    mine_second = [swap(second_half, n_fs, 1), across, swap(passed[0], n_fs, 1)]
 
     if split:
         same = exchange([key_low] * (n_sp // 2), n_sp)
@@ -905,39 +894,44 @@
         key_pieces = [lax.all_gather(key_low, "sp")]
     n_pieces = len(key_pieces)
 
-    attended, *kept = call(
-        functools.partial(forward_kernel, (batches, tok, key_dev, keys, block, n_pieces)),
-        [shape(batches * tok, dim)]
-        + [shape(tok, dim)] * batches
-        + [shape(keys, 2 * dim)] * batches
-        + [shape(dim, tok, dtype=f32)] * batches
-        + [shape(PAIRS, 8, 2 * tok, dtype=f32)] * batches
-        + [shape(PAIRS, keys, 2 * tok) if single else shape(16, 128)] * batches,
-        scratch=[pltpu.VMEM((2, block, 2 * tok) if single else (8, 128), f32)],
-        limit=limit,
-    )(normed, vec, bias, wq, wkv, *key_pieces)
-    kept = [kept[batch::batches] for batch in range(batches)]
+    kept = [
+        call(
+            functools.partial(forward_kernel, (batch, tok, key_dev, keys, block, n_pieces)),
+            [
+                shape(tok, dim),
+                shape(tok, dim),
+                shape(keys, 2 * dim),
+                shape(dim, tok, dtype=f32),
+                shape(PAIRS, 8, 2 * tok, dtype=f32),
+                shape(PAIRS, keys, 2 * tok) if single else shape(16, 128),
+            ],
+            scratch=[pltpu.VMEM((2, block, 2 * tok) if single else (8, 128), f32)],
+            limit=limit,
+        )(normed, vec, bias, wq, wkv, *key_pieces)
+        for batch in range(batches)
+    ]
+    attended = [results[0] for results in kept]
+    kept = [results[1:] for results in kept]
     mine_second = call(functools.partial(relay_kernel, n_fs - 1), [shape(dim + shard // 2, dim)] * (n_fs - 1))(
         *mine_second, kept[0][3]
     )
     patch_other = flip(patch_send, n_sp, 1)
     other_second = [flip(piece, n_sp, 1) for piece in mine_second]
 
-    acts, normal, rstd, grad_second, keep_a, send_a, wo = call(
+    acts, middle, gatt, keep_a, send_a, gvec_a = call(
         functools.partial(mlp_kernel, (n_fs, batches, row_dev, cols, dim, hid)),
         [
             shape(batches, 1, row_dev, cols, dim, dtype=f32),
             shape(batches * tok, dim, dtype=f32),
-            shape(batches * tok, 128, dtype=f32),
-            shape(batches * tok + 8, dim, dtype=f32),
+            shape(batches * tok, dim),
             shape(n_fs, dim, dim),
             shape(n_fs, dim, dim),
-            shape(dim, dim),
+            shape(VECS, dim, dtype=f32),
         ],
         scratch=[
             pltpu.VMEM((dim, hid), bf16),
             pltpu.VMEM((hid, dim), bf16),
-            pltpu.VMEM((8, dim), f32),
+            pltpu.VMEM((dim, dim), bf16),
             pltpu.VMEM((n_fs, dim, dim), bf16),
             pltpu.VMEM((n_fs, dim, dim), bf16),
         ],
@@ -946,8 +940,8 @@
         tokens,
         cotangent,
         mask,
-        attended,
         vec,
+        *attended,
         hidden_weight,
         return_weight,
         output_weight,
@@ -956,12 +950,6 @@
         patch_other,
     )
     arrived_a = flip(send_a, n_sp, 1)
-    middle, gatt, gvec_a = call(
-        functools.partial(middle_kernel, (batches, tok, hid // dim)),
-        [shape(batches * tok, dim, dtype=f32), shape(batches * tok, dim), shape(VECS, dim, dtype=f32)],
-        limit=limit,
-    )(cotangent, mask, normal, rstd, grad_second, vec, wo)
-
     gkey_dims = (n_sp // 2, key_dev, dim) if split else (n_sp, key_dev, dim)
     back = []
     for batch in range(batches):
@@ -982,7 +970,7 @@
                     shape(keys, dim),
                     shape(8, dim, dtype=f32),
                 ],
-                scratch=() if single else [pltpu.VMEM((keys, dim), f32)] * 2,
+                scratch=[pltpu.VMEM((2, keys, 2 * tok), f32)] if single else [pltpu.VMEM((keys, dim), f32)] * 2,
                 limit=limit,
             )(gatt, queries, kvs, attf, stats, probs, bias, wkv, order)
         )
@@ -1000,9 +988,8 @@
     )(
         normed,
         wq,
-        attended,
         middle,
-        vec,
+        *attended,
         *[kept[batch][1] for batch in range(batches)],
         *[results[2] for results in back],
         *[results[3] for results in back],
@@ -1029,11 +1016,6 @@
         [shape(batches * tok, dim, dtype=f32), shape(VECS, dim)],
         scratch=[pltpu.VMEM((dim // 128, tok, 128), f32)],
     )(gnormed, mask, whole_reduce, normal_first, gvec_a, gvec_b, gvec_c, *grad_reduced)
-    grads, done = call(
-        functools.partial(input_kernel, (batches, row_dev, cols, dim)),
-        [shape(batches, 1, row_dev, cols, dim, dtype=f32), shape(8, 128, dtype=f32)],
-    )(middle, grad_normed, normal_first, rstd_first, vec)
-
     chunks_b = call(functools.partial(weight_kernel, batches), [shape(half + VECS, dim)] * n_fs)(
         patch_cols, patch_other, *grad_reduced, *grad_other, vectors
     )
@@ -1041,7 +1023,16 @@
         rows = dim // 4
         chunks = call(owners_kernel, [shape(rows + half, dim)] * n_fs)(total_a, keep_c, arrived_c)
         join = functools.partial(join_kernel, n_fs)
-        joined_a = call(join, shape(rows + half, dim))(*to_owners(chunks, n_fs), done)
+        joined_a = call(join, shape(rows + half, dim), micros=5)(*to_owners(chunks, n_fs), vec)
+        order = joined_a
+    else:
+        order = vec
+    grads, done = call(
+        functools.partial(input_kernel, (batches, row_dev, cols, dim)),
+        [shape(batches, 1, row_dev, cols, dim, dtype=f32), shape(8, 128, dtype=f32)],
+    )(middle, grad_normed, normal_first, rstd_first, vec, order)
+
+    if split:
         joined_b = call(join, shape(half + VECS, dim), micros=1)(*to_owners(chunks_b, n_fs), done)
         mine = call(functools.partial(merge_kernel, rows), shape(4 * rows + half, dim))(
             *exchange([joined_a] * 4, n_sp), joined_b
@@ -1072,7 +1063,7 @@
     greduce, *vectors = call(
         functools.partial(final_small_kernel, n_fs),
         [shape(dim, dim, dtype=f32)] + [shape(shard, dtype=f32)] * HIDDEN_B + [shape(dim, dtype=f32)],
-        micros=10,
+        micros=3,
     )(mine_b, flip(mine_b, n_sp, 1))
     return (
         acts,

time: 103 us -> 94.9 us (0.921)
  waiting for transfers between devices: 20.8 us -> 15 us
  starting transfers between devices: 40.1 us -> 38.6 us
    ppermute x12 -> x9, waiting for transfers between devices: 7.69 us -> 4.41 us  [rotate(): return lax.ppermute(value, 'fs', [(i, (i + step) % n) for i in range(n)])]
    ppermute x12 -> x9, starting transfers between devices: 14.4 us -> 11.4 us  [rotate(): return lax.ppermute(value, 'fs', [(i, (i + step) % n) for i in range(n)])]
    ppermute x34, waiting for transfers between devices: 13.1 us -> 10.5 us  [flip(): return lax.ppermute(value, 'sp', [(i, i ^ bits) for i in range(n)])]
    ppermute x0 -> x3, starting transfers between devices: none -> 1.75 us  [swap(): return lax.ppermute(value, 'fs', [(i, i ^ bits) for i in range(n)])]
    pallas_call x3 -> x4, Pallas kernels: 7.93 us -> 7.75 us  [the longest x2 7.69 us: on_device(): call(functools.partial(forward_kernel, (batch, tok, key_dev, keys, block,...]
  transfers between devices with their start and end apart: 46 -> 46, of which waited for: 17 -> 18; matrix products, arithmetic and copies ran while one was open for 0% -> 0% of each run, Pallas kernels for 24% -> 26%
where the time goes in v4:
time: 94.9 us; the launch traced here: 94.4 us
  starting transfers between devices  38.6 us (41%)
  Pallas kernels  32.1 us (34%)
  waiting for transfers between devices  15 us (16%)
  local copies, waits for them, and re-layouts  7.67 us (8%)
  between operations  1.02 us (1%)
    ppermute x34, starting transfers between devices, flip(): return lax.ppermute(value, 'sp', [(i, i ^ bits) for i in range(n)])  25.4 us
    ppermute x9, starting transfers between devices, rotate(): return lax.ppermute(value, 'fs', [(i, (i + step) % n) for i in range(n)])  11.4 us
    ppermute x34, waiting for transfers between devices, flip(): return lax.ppermute(value, 'sp', [(i, i ^ bits) for i in range(n)])  10.5 us
    pallas_call x2, Pallas kernels, on_device(): call(functools.partial(backward_kernel, (n_sp, batch, tok, key_dev, keys,...  8.51 us
    pallas_call x2, Pallas kernels, on_device(): call(functools.partial(forward_kernel, (batch, tok, key_dev, keys, block,...  7.69 us
    unnamed x28, local copies, waits for them, and re-layouts  7.67 us
    pallas_call x1, Pallas kernels, on_device(): call(functools.partial(mlp_kernel, (n_fs, batches, row_dev, cols, dim, hi...  4.91 us
    ppermute x9, waiting for transfers between devices, rotate(): return lax.ppermute(value, 'fs', [(i, (i + step) % n) for i in range(n)])  4.41 us
  transfers between devices with their start and end apart: 46, of which 18 were waited for; matrix products, arithmetic and copies ran while one was open for 0% of the time, Pallas kernels for 26%

profile of v4, /device:TPU:9, one launch (start us, length us, event | category | flops | bytes accessed | tf_op | source)
XLA Modules:
  0.0 94.4 jit_solution(7271061357557867229)
XLA Ops:
  0.7 1.8 %shard_map.356.packed = bf16[240,256]{1,0:T(8,128)(2,1)} custom-call(bf16[64]{0:T(256)(128)(2,1)} %refs_0_.2, bf16[64]{0:T(256)(128)(2,1)} %refs_1_.2, bf16[64]{0:T(256)(128)(2,1)} %refs_2_.1, bf16[64]{0:T(256)(128)(2,1)} %refs_3_.1, bf16[64]{0:T(256)(128)(2,1)} %refs_4_.1, bf16[64]{0:T(256)(128)(2,1)} %refs_5_.1, bf16[64]{0:T(256)(128)(2,1)} %refs_6_.2, ...), custom_call_target="tpu_custom_call" | custom-call | tf_op jit(solution)/shard_map/pallas_call | solution.py:832
  2.5 2.5 %collective-permute-start.1 = (bf16[240,256]{1,0:T(8,128)(2,1)}, bf16[240,256]{1,0:T(8,128)(2,1)S(1)}, u32[]{:S(2)}, u32[]{:S(2)}) collective-permute-start(bf16[240,256]{1,0:T(8,128)(2,1)} %shard_map.356.packed), channel_id=1, source_target_pairs={{0,2},{1,3},{2,0},{3,1},{4,6},{5,7},{6,4},{7,5},{8,10},{9,11},{10,... | collective-permute-start | bytes 368648 | tf_op jit(solution)/shard_map/ppermute | solution.py:730
  5.0 2.2 %collective-permute-start = (bf16[240,256]{1,0:T(8,128)(2,1)}, bf16[240,256]{1,0:T(8,128)(2,1)S(1)}, u32[]{:S(2)}, u32[]{:S(2)}) collective-permute-start(bf16[240,256]{1,0:T(8,128)(2,1)} %shard_map.356.packed), channel_id=1, source_target_pairs={{0,1},{1,2},{2,3},{3,0},{4,5},{5,6},{6,7},{7,4},{8,9},{9,10},{10,1... | collective-permute-start | bytes 368648 | tf_op jit(solution)/shard_map/ppermute | solution.py:730
  7.2 1.0 %copy-done = bf16[2,1,2,192,256]{4,3,2,1,0:T(8,128)(2,1)S(1)} copy-done((bf16[2,1,2,192,256]{4,3,2,1,0:T(8,128)(2,1)S(1)}, bf16[2,1,2,192,256]{4,3,2,1,0:T(8,128)(2,1)}, u32[]{:S(2)}) %copy-start) | copy-done | bytes 393240
  8.1 0.9 copy-done.3
  9.1 0.9 copy-done.5
  10.0 0.9 copy-done.7
  10.9 0.9 copy-done.8
  11.8 0.8 copy-done.9
  12.6 0.8 copy-done.10
  13.4 0.8 copy-done.12
  14.8 1.2 %shard_map.357 = (f32[768,256]{1,0:T(8,128)S(1)}, f32[768,128]{1,0:T(8,128)S(1)}, f32[768,256]{1,0:T(8,128)S(1)}, bf16[2,768,256]{2,1,0:T(8,128)(2,1)S(1)}, bf16...) custom-call(s32[2,1,2]{2,1,0:T(1,128)S(1)} %copy-done.13, ...), custom_call_target="tpu_custom_call" | custom-call | tf_op jit(solution)/shard_map/pallas_call | solution.py:840
  16.0 1.0 %collective-permute-start.14 = (bf16[288,256]{1,0:T(8,128)(2,1)S(1)}, bf16[288,256]{1,0:T(8,128)(2,1)S(1)}, u32[]{:S(2)}, u32[]{:S(2)}) collective-permute-start(bf16[288,256]{1,0:T(8,128)(2,1)S(1)} %get-tuple-element.136), channel_id=1, source_target_pairs={{0,2},{1,3},{2,0},{3,1},{4,6},{5,7},{6,4},{7,5},{8,10},{9,11},{10,... | collective-permute-start | bytes 442376 | tf_op jit(solution)/shard_map/ppermute | solution.py:734
  17.0 1.6 %collective-permute-start.3 = (bf16[240,256]{1,0:T(8,128)(2,1)S(1)}, bf16[240,256]{1,0:T(8,128)(2,1)S(1)}, u32[]{:S(2)}, u32[]{:S(2)}) collective-permute-start(bf16[240,256]{1,0:T(8,128)(2,1)S(1)} %get-tuple-element.125.refs_6_), channel_id=1, source_target_pairs={{0,4},{4,0},{8,12},{12,8},{16,20},{20,16},{24,28},{28,24},{1,5},{5... | collective-permute-start | bytes 368648 | tf_op jit(solution)/shard_map/ppermute | solution.py:738
  20.1 0.7 shard_map.359
  20.9 2.2 %collective-permute-start.11 = (bf16[192,256]{1,0:T(8,128)(2,1)S(1)}, bf16[192,256]{1,0:T(8,128)(2,1)S(1)}, u32[]{:S(2)}, u32[]{:S(2)}) collective-permute-start(bf16[192,256]{1,0:T(8,128)(2,1)S(1)} %get-tuple-element.133.refs_5_.refs_15_), channel_id=1, source_target_pairs={{0,24},{4,28},{8,16},{12,20},{16,8},{20,12},{24,0},{28,4},{1,25},{... | collective-permute-start | bytes 294920 | tf_op jit(solution)/shard_map/ppermute | solution.py:738
  23.7 1.1 %collective-permute-start.6 = (bf16[192,256]{1,0:T(8,128)(2,1)S(1)}, bf16[192,256]{1,0:T(8,128)(2,1)S(1)}, u32[]{:S(2)}, u32[]{:S(2)}) collective-permute-start(bf16[192,256]{1,0:T(8,128)(2,1)S(1)} %get-tuple-element.133.refs_5_.refs_15_), channel_id=1, source_target_pairs={{0,4},{4,0},{8,12},{12,8},{16,20},{20,16},{24,28},{28,24},{1,5},{5... | collective-permute-start | bytes 294920 | tf_op jit(solution)/shard_map/ppermute | solution.py:738
  24.9 1.0 %collective-permute-done.11.refs_11_.refs_21_ = bf16[192,256]{1,0:T(8,128)(2,1)S(1)} collective-permute-done((bf16[192,256]{1,0:T(8,128)(2,1)S(1)}, bf16[192,256]{1,0:T(8,128)(2,1)S(1)}, u32[]{:S(2)}, u32[]{:S(2)}) %collective-permute-start.11) | collective-permute-done | bytes 98336 | tf_op jit(solution)/shard_map/ppermute | solution.py:738
  26.4 2.1 %collective-permute-done.9.refs_9_.refs_19_ = bf16[192,256]{1,0:T(8,128)(2,1)S(1)} collective-permute-done((bf16[192,256]{1,0:T(8,128)(2,1)S(1)}, bf16[192,256]{1,0:T(8,128)(2,1)S(1)}, u32[]{:S(2)}, u32[]{:S(2)}) %collective-permute-start.9) | collective-permute-done | bytes 98336 | tf_op jit(solution)/shard_map/ppermute | solution.py:738
  30.6 3.8 %shard_map.360 = (bf16[384,256]{1,0:T(8,128)(2,1)S(1)}, bf16[384,256]{1,0:T(8,128)(2,1)S(1)}, bf16[768,512]{1,0:T(8,128)(2,1)S(1)}, f32[256,384]{1,0:T(8,128)S(1...) custom-call(bf16[768,256]{1,0:T(8,128)(2,1)S(1)} %get-tuple-element.129.refs_0_, ...), custom_call_target="tpu_custom_call" | custom-call | tf_op jit(solution)/shard_map/pallas_call | solution.py:898
  35.5 3.8 %shard_map.361 = (bf16[384,256]{1,0:T(8,128)(2,1)S(1)}, bf16[384,256]{1,0:T(8,128)(2,1)S(1)}, bf16[768,512]{1,0:T(8,128)(2,1)S(1)}, f32[256,384]{1,0:T(8,128)S(1...) custom-call(bf16[768,256]{1,0:T(8,128)(2,1)S(1)} %get-tuple-element.129.refs_0_, ...), custom_call_target="tpu_custom_call" | custom-call | tf_op jit(solution)/shard_map/pallas_call | solution.py:898
  39.4 4.9 %shard_map.364 = (f32[2,1,2,192,256]{4,3,2,1,0:T(8,128)}, f32[768,256]{1,0:T(8,128)S(1)}, bf16[768,256]{1,0:T(8,128)(2,1)S(1)}, bf16[4,256,256]{2,1,0:T(8,128)(2...) custom-call(bf16[2,1,2,192,256]{4,3,2,1,0:T(8,128)(2,1)S(1)} %copy-done.1, ...), custom_call_target="tpu_custom_call" | custom-call | tf_op jit(solution)/shard_map/pallas_call | solution.py:921
  44.5 4.3 %shard_map.365 = (bf16[4,96,256]{2,1,0:T(8,128)(2,1)S(1)}, bf16[4,96,256]{2,1,0:T(8,128)(2,1)S(1)}, bf16[4,768,768]{2,1,0:T(8,128)(2,1)S(1)}, bf16[768,256]{1,0:...) custom-call(bf16[768,256]{1,0:T(8,128)(2,1)S(1)} %get-tuple-element.146.refs_0_, ...), custom_call_target="tpu_custom_call" | custom-call | tf_op jit(solution)/shard_map/pallas_call | solution.py:963
  48.9 1.3 %collective-permute-start.23 = (bf16[4,64,256]{2,1,0:T(8,128)(2,1)S(1)}, bf16[4,64,256]{2,1,0:T(8,128)(2,1)S(1)}, u32[]{:S(2)}, u32[]{:S(2)}) collective-permute-start(bf16[4,64,256]{2,1,0:T(8,128)(2,1)S(1)} %get-tuple-element.173), channel_id=1, source_target_pairs={{0,8},{4,12},{8,0},{12,4},{16,24},{20,28},{24,16},{28,20},{1,9},{5... | collective-permute-start | bytes 393224 | tf_op jit(solution)/shard_map/ppermute | solution.py:738
  50.2 0.7 collective-permute-start.24
  51.6 1.2 %collective-permute-start.21 = (bf16[4,96,256]{2,1,0:T(8,128)(2,1)S(1)}, bf16[4,96,256]{2,1,0:T(8,128)(2,1)S(1)}, u32[]{:S(2)}, u32[]{:S(2)}) collective-permute-start(bf16[4,96,256]{2,1,0:T(8,128)(2,1)S(1)} %get-tuple-element.171), channel_id=1, source_target_pairs={{0,4},{4,0},{8,12},{12,8},{16,20},{20,16},{24,28},{28,24},{1,5},{5... | collective-permute-start | bytes 589832 | tf_op jit(solution)/shard_map/ppermute | solution.py:738
  52.8 4.3 %shard_map.367 = (bf16[4,96,256]{2,1,0:T(8,128)(2,1)S(1)}, bf16[4,96,256]{2,1,0:T(8,128)(2,1)S(1)}, bf16[4,768,768]{2,1,0:T(8,128)(2,1)S(1)}, bf16[768,256]{1,0:...) custom-call(bf16[768,256]{1,0:T(8,128)(2,1)S(1)} %get-tuple-element.146.refs_0_, ...), custom_call_target="tpu_custom_call" | custom-call | tf_op jit(solution)/shard_map/pallas_call | solution.py:963
  57.1 2.6 %shard_map.368 = (bf16[4,128,256]{2,1,0:T(8,128)(2,1)S(1)}, bf16[4,128,256]{2,1,0:T(8,128)(2,1)S(1)}, f32[768,256]{1,0:T(8,128)S(1)}, f32[16,256]{1,0:T(8,128)S(1)}) custom-call(bf16[768,256]{1,0:T(8,128)(2,1)S(1)} %get-tuple-element.129.refs_0_, bf16[256,256]{1,0:T(8,128)(2,1)S(1)} %get-tuple-element.131.refs_3_.refs_1_, ...), custom_call_target="tpu_custom_call" | custom-call | tf_op jit(solution)/shard_map/pallas_call | solution.py:978
  60.5 1.3 %collective-permute-start.26 = (bf16[192,256]{1,0:T(8,128)(2,1)S(1)}, bf16[192,256]{1,0:T(8,128)(2,1)S(1)}, u32[]{:S(2)}, u32[]{:S(2)}) collective-permute-start(bf16[192,256]{1,0:T(8,128)(2,1)S(1)} %get-tuple-element.178), channel_id=1, source_target_pairs={{0,8},{4,12},{8,0},{12,4},{16,24},{20,28},{24,16},{28,20},{1,9},{5... | collective-permute-start | bytes 294920 | tf_op jit(solution)/shard_map/ppermute | solution.py:738
  61.7 0.7 collective-permute-start.27
  63.3 1.3 %collective-permute-start.30 = (bf16[192,256]{1,0:T(8,128)(2,1)S(1)}, bf16[192,256]{1,0:T(8,128)(2,1)S(1)}, u32[]{:S(2)}, u32[]{:S(2)}) collective-permute-start(bf16[192,256]{1,0:T(8,128)(2,1)S(1)} %get-tuple-element.189), channel_id=1, source_target_pairs={{0,1},{1,2},{2,3},{3,0},{4,5},{5,6},{6,7},{7,4},{8,9},{9,10},{10,1... | collective-permute-start | bytes 294920 | tf_op jit(solution)/shard_map/ppermute | solution.py:730
  64.6 1.5 %collective-permute-start.31 = (bf16[192,256]{1,0:T(8,128)(2,1)S(1)}, bf16[192,256]{1,0:T(8,128)(2,1)S(1)}, u32[]{:S(2)}, u32[]{:S(2)}) collective-permute-start(bf16[192,256]{1,0:T(8,128)(2,1)S(1)} %get-tuple-element.190), channel_id=1, source_target_pairs={{0,2},{1,3},{2,0},{3,1},{4,6},{5,7},{6,4},{7,5},{8,10},{9,11},{10,... | collective-permute-start | bytes 294920 | tf_op jit(solution)/shard_map/ppermute | solution.py:730
  66.8 0.9 collective-permute-done.28.refs_3_
  67.9 1.5 %collective-permute-start.33 = (bf16[96,256]{1,0:T(8,128)(2,1)S(1)}, bf16[96,256]{1,0:T(8,128)(2,1)S(1)}, u32[]{:S(2)}, u32[]{:S(2)}) collective-permute-start(bf16[96,256]{1,0:T(8,128)(2,1)S(1)} %get-tuple-element.182.refs_0_.refs_2_), channel_id=1, source_target_pairs={{0,4},{4,0},{8,12},{12,8},{16,20},{20,16},{24,28},{28,24},{1,5},{5... | collective-permute-start | bytes 147464 | tf_op jit(solution)/shard_map/ppermute | solution.py:738
  71.0 1.1 %collective-permute-start.35 = (bf16[144,256]{1,0:T(8,128)(2,1)S(1)}, bf16[144,256]{1,0:T(8,128)(2,1)S(1)}, u32[]{:S(2)}, u32[]{:S(2)}) collective-permute-start(bf16[144,256]{1,0:T(8,128)(2,1)S(1)} %get-tuple-element.196), channel_id=1, source_target_pairs={{0,1},{1,2},{2,3},{3,0},{4,5},{5,6},{6,7},{7,4},{8,9},{9,10},{10,1... | collective-permute-start | bytes 221192 | tf_op jit(solution)/shard_map/ppermute | solution.py:730
  72.1 1.8 %collective-permute-start.36 = (bf16[144,256]{1,0:T(8,128)(2,1)S(1)}, bf16[144,256]{1,0:T(8,128)(2,1)S(1)}, u32[]{:S(2)}, u32[]{:S(2)}) collective-permute-start(bf16[144,256]{1,0:T(8,128)(2,1)S(1)} %get-tuple-element.197), channel_id=1, source_target_pairs={{0,2},{1,3},{2,0},{3,1},{4,6},{5,7},{6,4},{7,5},{8,10},{9,11},{10,... | collective-permute-start | bytes 221192 | tf_op jit(solution)/shard_map/ppermute | solution.py:730
  74.3 4.4 %collective-permute-done.32.refs_3_ = bf16[192,256]{1,0:T(8,128)(2,1)S(1)} collective-permute-done((bf16[192,256]{1,0:T(8,128)(2,1)S(1)}, bf16[192,256]{1,0:T(8,128)(2,1)S(1)}, u32[]{:S(2)}, u32[]{:S(2)}) %collective-permute-start.32) | collective-permute-done | bytes 98336 | tf_op jit(solution)/shard_map/ppermute | solution.py:730
  78.8 2.4 %collective-permute-start.42 = (bf16[192,256]{1,0:T(8,128)(2,1)S(1)}, bf16[192,256]{1,0:T(8,128)(2,1)S(1)}, u32[]{:S(2)}, u32[]{:S(2)}) collective-permute-start(bf16[192,256]{1,0:T(8,128)(2,1)S(1)} %shard_map.374._.refs_0_), channel_id=1, source_target_pairs={{0,16},{4,20},{8,24},{12,28},{16,0},{20,4},{24,8},{28,12},{1,17},{... | collective-permute-start | bytes 294920 | tf_op jit(solution)/shard_map/ppermute | solution.py:738
  81.2 1.2 %shard_map.375 = (f32[2,1,2,192,256]{4,3,2,1,0:T(8,128)}, f32[8,128]{1,0:T(8,128)S(1)}) custom-call(f32[768,256]{1,0:T(8,128)S(1)} %get-tuple-element.143.refs_2_.middle, f32[768,256]{1,0:T(8,128)S(1)} %get-tuple-element.184.grad_normed, f32[768,256]{1,0:T(8,128)S(1)} %get-tuple-element.120.refs_0_.normal_ref, f32[768,128]{1,0:T(8,128)S(1)} %get-tuple-element.185.rstd_ref, ...), custom_call_target="tpu_custom_call" | custom-call | tf_op jit(solution)/shard_map/pallas_call | solution.py:1030
  82.8 1.0 %collective-permute-start.40 = (bf16[144,256]{1,0:T(8,128)(2,1)S(1)}, bf16[144,256]{1,0:T(8,128)(2,1)S(1)}, u32[]{:S(2)}, u32[]{:S(2)}) collective-permute-start(bf16[144,256]{1,0:T(8,128)(2,1)S(1)} %shard_map.377.refs_4_.refs_0_), channel_id=1, source_target_pairs={{0,24},{4,28},{8,16},{12,20},{16,8},{20,12},{24,0},{28,4},{1,25},{... | collective-permute-start | bytes 221192 | tf_op jit(solution)/shard_map/ppermute | solution.py:738
  83.8 1.4 %collective-permute-start.39 = (bf16[144,256]{1,0:T(8,128)(2,1)S(1)}, bf16[144,256]{1,0:T(8,128)(2,1)S(1)}, u32[]{:S(2)}, u32[]{:S(2)}) collective-permute-start(bf16[144,256]{1,0:T(8,128)(2,1)S(1)} %shard_map.377.refs_4_.refs_0_), channel_id=1, source_target_pairs={{0,16},{4,20},{8,24},{12,28},{16,0},{20,4},{24,8},{28,12},{1,17},{... | collective-permute-start | bytes 221192 | tf_op jit(solution)/shard_map/ppermute | solution.py:738
  86.3 0.8 collective-permute-done.40.refs_3_
  87.0 1.2 %collective-permute-done.39.refs_2_ = bf16[144,256]{1,0:T(8,128)(2,1)S(1)} collective-permute-done((bf16[144,256]{1,0:T(8,128)(2,1)S(1)}, bf16[144,256]{1,0:T(8,128)(2,1)S(1)}, u32[]{:S(2)}, u32[]{:S(2)}) %collective-permute-start.39) | collective-permute-done | bytes 73760 | tf_op jit(solution)/shard_map/ppermute | solution.py:738
  88.2 1.0 %collective-permute-done.38.refs_1_ = bf16[144,256]{1,0:T(8,128)(2,1)S(1)} collective-permute-done((bf16[144,256]{1,0:T(8,128)(2,1)S(1)}, bf16[144,256]{1,0:T(8,128)(2,1)S(1)}, u32[]{:S(2)}, u32[]{:S(2)}) %collective-permute-start.38) | collective-permute-done | bytes 73760 | tf_op jit(solution)/shard_map/ppermute | solution.py:738
  89.2 2.6 %collective-permute-start.44 = (bf16[144,256]{1,0:T(8,128)(2,1)S(1)}, bf16[144,256]{1,0:T(8,128)(2,1)S(1)}, u32[]{:S(2)}, u32[]{:S(2)}) collective-permute-start(bf16[144,256]{1,0:T(8,128)(2,1)S(1)} %shard_map.379.mine), channel_id=1, source_target_pairs={{0,4},{4,0},{8,12},{12,8},{16,20},{20,16},{24,28},{28,24},{1,5},{5... | collective-permute-start | bytes 221192 | tf_op jit(solution)/shard_map/ppermute | solution.py:738
  91.9 0.8 collective-permute-done.44.other
  92.7 0.8 shard_map.380
  93.5 0.9 shard_map.381
  (98 shorter events, 13.5 us)
Async XLA Ops:
  2.5 14.5 %collective-permute-start.2 = (bf16[240,256]{1,0:T(8,128)(2,1)}, bf16[240,256]{1,0:T(8,128)(2,1)S(1)}, u32[]{:S(2)}, u32[]{:S(2)}) collective-permute-start(bf16[240,256]{1,0:T(8,128)(2,1)} %shard_map.356.packed), channel_id=1, source_target_pairs={{0,3},{1,0},{2,1},{3,2},{4,7},{5,4},{6,5},{7,6},{8,11},{9,8},{10,9... | collective-permute-start | bytes 368648 | tf_op jit(solution)/shard_map/ppermute | solution.py:730
  2.5 14.5 %collective-permute-start.1 = (bf16[240,256]{1,0:T(8,128)(2,1)}, bf16[240,256]{1,0:T(8,128)(2,1)S(1)}, u32[]{:S(2)}, u32[]{:S(2)}) collective-permute-start(bf16[240,256]{1,0:T(8,128)(2,1)} %shard_map.356.packed), channel_id=1, source_target_pairs={{0,2},{1,3},{2,0},{3,1},{4,6},{5,7},{6,4},{7,5},{8,10},{9,11},{10,... | collective-permute-start | bytes 368648 | tf_op jit(solution)/shard_map/ppermute | solution.py:730
  5.0 12.0 %collective-permute-start = (bf16[240,256]{1,0:T(8,128)(2,1)}, bf16[240,256]{1,0:T(8,128)(2,1)S(1)}, u32[]{:S(2)}, u32[]{:S(2)}) collective-permute-start(bf16[240,256]{1,0:T(8,128)(2,1)} %shard_map.356.packed), channel_id=1, source_target_pairs={{0,1},{1,2},{2,3},{3,0},{4,5},{5,6},{6,7},{7,4},{8,9},{9,10},{10,1... | collective-permute-start | bytes 368648 | tf_op jit(solution)/shard_map/ppermute | solution.py:730
  16.0 7.7 %collective-permute-start.14 = (bf16[288,256]{1,0:T(8,128)(2,1)S(1)}, bf16[288,256]{1,0:T(8,128)(2,1)S(1)}, u32[]{:S(2)}, u32[]{:S(2)}) collective-permute-start(bf16[288,256]{1,0:T(8,128)(2,1)S(1)} %get-tuple-element.136), channel_id=1, source_target_pairs={{0,2},{1,3},{2,0},{3,1},{4,6},{5,7},{6,4},{7,5},{8,10},{9,11},{10,... | collective-permute-start | bytes 442376 | tf_op jit(solution)/shard_map/ppermute | solution.py:734
  17.0 2.6 %collective-permute-start.3 = (bf16[240,256]{1,0:T(8,128)(2,1)S(1)}, bf16[240,256]{1,0:T(8,128)(2,1)S(1)}, u32[]{:S(2)}, u32[]{:S(2)}) collective-permute-start(bf16[240,256]{1,0:T(8,128)(2,1)S(1)} %get-tuple-element.125.refs_6_), channel_id=1, source_target_pairs={{0,4},{4,0},{8,12},{12,8},{16,20},{20,16},{24,28},{28,24},{1,5},{5... | collective-permute-start | bytes 368648 | tf_op jit(solution)/shard_map/ppermute | solution.py:738
  18.6 1.3 %collective-permute-start.4 = (bf16[240,256]{1,0:T(8,128)(2,1)S(1)}, bf16[240,256]{1,0:T(8,128)(2,1)S(1)}, u32[]{:S(2)}, u32[]{:S(2)}) collective-permute-start(bf16[240,256]{1,0:T(8,128)(2,1)S(1)} %get-tuple-element.126.refs_7_), channel_id=1, source_target_pairs={{0,4},{4,0},{8,12},{12,8},{16,20},{20,16},{24,28},{28,24},{1,5},{5... | collective-permute-start | bytes 368648 | tf_op jit(solution)/shard_map/ppermute | solution.py:738
  18.7 1.4 %collective-permute-start.5 = (bf16[240,256]{1,0:T(8,128)(2,1)S(1)}, bf16[240,256]{1,0:T(8,128)(2,1)S(1)}, u32[]{:S(2)}, u32[]{:S(2)}) collective-permute-start(bf16[240,256]{1,0:T(8,128)(2,1)S(1)} %get-tuple-element.127.refs_8_), channel_id=1, source_target_pairs={{0,4},{4,0},{8,12},{12,8},{16,20},{20,16},{24,28},{28,24},{1,5},{5... | collective-permute-start | bytes 368648 | tf_op jit(solution)/shard_map/ppermute | solution.py:738
  19.1 15.4 %collective-permute-start.13 = (bf16[288,256]{1,0:T(8,128)(2,1)S(1)}, bf16[288,256]{1,0:T(8,128)(2,1)S(1)}, u32[]{:S(2)}, u32[]{:S(2)}) collective-permute-start(bf16[288,256]{1,0:T(8,128)(2,1)S(1)} %get-tuple-element.136), channel_id=1, source_target_pairs={{0,1},{1,0},{2,3},{3,2},{4,5},{5,4},{6,7},{7,6},{8,9},{9,8},{10,11... | collective-permute-start | bytes 442376 | tf_op jit(solution)/shard_map/ppermute | solution.py:734
  20.9 5.0 %collective-permute-start.11 = (bf16[192,256]{1,0:T(8,128)(2,1)S(1)}, bf16[192,256]{1,0:T(8,128)(2,1)S(1)}, u32[]{:S(2)}, u32[]{:S(2)}) collective-permute-start(bf16[192,256]{1,0:T(8,128)(2,1)S(1)} %get-tuple-element.133.refs_5_.refs_15_), channel_id=1, source_target_pairs={{0,24},{4,28},{8,16},{12,20},{16,8},{20,12},{24,0},{28,4},{1,25},{... | collective-permute-start | bytes 294920 | tf_op jit(solution)/shard_map/ppermute | solution.py:738
  23.1 5.4 %collective-permute-start.9 = (bf16[192,256]{1,0:T(8,128)(2,1)S(1)}, bf16[192,256]{1,0:T(8,128)(2,1)S(1)}, u32[]{:S(2)}, u32[]{:S(2)}) collective-permute-start(bf16[192,256]{1,0:T(8,128)(2,1)S(1)} %get-tuple-element.133.refs_5_.refs_15_), channel_id=1, source_target_pairs={{0,16},{4,20},{8,24},{12,28},{16,0},{20,4},{24,8},{28,12},{1,17},{... | collective-permute-start | bytes 294920 | tf_op jit(solution)/shard_map/ppermute | solution.py:738
  23.3 5.8 %collective-permute-start.7 = (bf16[192,256]{1,0:T(8,128)(2,1)S(1)}, bf16[192,256]{1,0:T(8,128)(2,1)S(1)}, u32[]{:S(2)}, u32[]{:S(2)}) collective-permute-start(bf16[192,256]{1,0:T(8,128)(2,1)S(1)} %get-tuple-element.133.refs_5_.refs_15_), channel_id=1, source_target_pairs={{0,8},{4,12},{8,0},{12,4},{16,24},{20,28},{24,16},{28,20},{1,9},{5... | collective-permute-start | bytes 294920 | tf_op jit(solution)/shard_map/ppermute | solution.py:738
  23.7 5.5 %collective-permute-start.6 = (bf16[192,256]{1,0:T(8,128)(2,1)S(1)}, bf16[192,256]{1,0:T(8,128)(2,1)S(1)}, u32[]{:S(2)}, u32[]{:S(2)}) collective-permute-start(bf16[192,256]{1,0:T(8,128)(2,1)S(1)} %get-tuple-element.133.refs_5_.refs_15_), channel_id=1, source_target_pairs={{0,4},{4,0},{8,12},{12,8},{16,20},{20,16},{24,28},{28,24},{1,5},{5... | collective-permute-start | bytes 294920 | tf_op jit(solution)/shard_map/ppermute | solution.py:738
  24.9 14.5 %copy-start.1 = (bf16[2,1,2,192,256]{4,3,2,1,0:T(8,128)(2,1)S(1)}, bf16[2,1,2,192,256]{4,3,2,1,0:T(8,128)(2,1)}, u32[]{:S(2)}) copy-start(bf16[2,1,2,192,256]{4,3,2,1,0:T(8,128)(2,1)} %refs_0_.3) | copy-start | bytes 1179652
  24.9 14.5 %copy-start.2 = (f32[2,1,2,192,256]{4,3,2,1,0:T(8,128)S(1)}, f32[2,1,2,192,256]{4,3,2,1,0:T(8,128)}, u32[]{:S(2)}) copy-start(f32[2,1,2,192,256]{4,3,2,1,0:T(8,128)} %refs_1_.3) | copy-start | bytes 2359300
  25.9 8.6 %collective-permute-start.15 = (bf16[288,256]{1,0:T(8,128)(2,1)S(1)}, bf16[288,256]{1,0:T(8,128)(2,1)S(1)}, u32[]{:S(2)}, u32[]{:S(2)}) collective-permute-start(bf16[288,256]{1,0:T(8,128)(2,1)S(1)} %shard_map.362), channel_id=1, source_target_pairs={{0,1},{1,0},{2,3},{3,2},{4,5},{5,4},{6,7},{7,6},{8,9},{9,8},{10,11... | collective-permute-start | bytes 442376 | tf_op jit(solution)/shard_map/ppermute | solution.py:734
  28.5 1.6 %collective-permute-start.12 = (bf16[192,256]{1,0:T(8,128)(2,1)S(1)}, bf16[192,256]{1,0:T(8,128)(2,1)S(1)}, u32[]{:S(2)}, u32[]{:S(2)}) collective-permute-start(bf16[192,256]{1,0:T(8,128)(2,1)S(1)} %collective-permute-done.11.refs_11_.refs_21_), channel_id=1, source_target_pairs={{0,4},{4,0},{8,12},{12,8},{16,20},{20,16},{24,28},{28,24},{1,5},{5... | collective-permute-start | bytes 294920 | tf_op jit(solution)/shard_map/ppermute | solution.py:738
  29.1 1.3 %collective-permute-start.10 = (bf16[192,256]{1,0:T(8,128)(2,1)S(1)}, bf16[192,256]{1,0:T(8,128)(2,1)S(1)}, u32[]{:S(2)}, u32[]{:S(2)}) collective-permute-start(bf16[192,256]{1,0:T(8,128)(2,1)S(1)} %collective-permute-done.9.refs_9_.refs_19_), channel_id=1, source_target_pairs={{0,4},{4,0},{8,12},{12,8},{16,20},{20,16},{24,28},{28,24},{1,5},{5... | collective-permute-start | bytes 294920 | tf_op jit(solution)/shard_map/ppermute | solution.py:738
  29.2 1.4 %collective-permute-start.8 = (bf16[192,256]{1,0:T(8,128)(2,1)S(1)}, bf16[192,256]{1,0:T(8,128)(2,1)S(1)}, u32[]{:S(2)}, u32[]{:S(2)}) collective-permute-start(bf16[192,256]{1,0:T(8,128)(2,1)S(1)} %collective-permute-done.7.refs_7_.refs_17_), channel_id=1, source_target_pairs={{0,4},{4,0},{8,12},{12,8},{16,20},{20,16},{24,28},{28,24},{1,5},{5... | collective-permute-start | bytes 294920 | tf_op jit(solution)/shard_map/ppermute | solution.py:738
  30.1 9.2 %collective-permute-start.19 = (bf16[4,192,128]{2,1,0:T(8,128)(2,1)S(1)}, bf16[4,192,128]{2,1,0:T(8,128)(2,1)S(1)}, u32[]{:S(2)}, u32[]{:S(2)}) collective-permute-start(bf16[4,192,128]{2,1,0:T(8,128)(2,1)S(1)} %get-tuple-element.141), channel_id=1, source_target_pairs={{0,4},{4,0},{8,12},{12,8},{16,20},{20,16},{24,28},{28,24},{1,5},{5... | collective-permute-start | bytes 589832 | tf_op jit(solution)/shard_map/ppermute | solution.py:738
  34.5 4.8 %collective-permute-start.16 = (bf16[288,256]{1,0:T(8,128)(2,1)S(1)}, bf16[288,256]{1,0:T(8,128)(2,1)S(1)}, u32[]{:S(2)}, u32[]{:S(2)}) collective-permute-start(bf16[288,256]{1,0:T(8,128)(2,1)S(1)} %get-tuple-element.138.refs_9_), channel_id=1, source_target_pairs={{0,4},{4,0},{8,12},{12,8},{16,20},{20,16},{24,28},{28,24},{1,5},{5... | collective-permute-start | bytes 442376 | tf_op jit(solution)/shard_map/ppermute | solution.py:738
  34.9 4.4 %collective-permute-start.17 = (bf16[288,256]{1,0:T(8,128)(2,1)S(1)}, bf16[288,256]{1,0:T(8,128)(2,1)S(1)}, u32[]{:S(2)}, u32[]{:S(2)}) collective-permute-start(bf16[288,256]{1,0:T(8,128)(2,1)S(1)} %get-tuple-element.139.refs_10_), channel_id=1, source_target_pairs={{0,4},{4,0},{8,12},{12,8},{16,20},{20,16},{24,28},{28,24},{1,5},{5... | collective-permute-start | bytes 442376 | tf_op jit(solution)/shard_map/ppermute | solution.py:738
  35.1 4.2 %collective-permute-start.18 = (bf16[288,256]{1,0:T(8,128)(2,1)S(1)}, bf16[288,256]{1,0:T(8,128)(2,1)S(1)}, u32[]{:S(2)}, u32[]{:S(2)}) collective-permute-start(bf16[288,256]{1,0:T(8,128)(2,1)S(1)} %get-tuple-element.140.refs_11_), channel_id=1, source_target_pairs={{0,4},{4,0},{8,12},{12,8},{16,20},{20,16},{24,28},{28,24},{1,5},{5... | collective-permute-start | bytes 442376 | tf_op jit(solution)/shard_map/ppermute | solution.py:738
  44.3 4.4 %collective-permute-start.20 = (bf16[4,256,256]{2,1,0:T(8,128)(2,1)S(1)}, bf16[4,256,256]{2,1,0:T(8,128)(2,1)S(1)}, u32[]{:S(2)}, u32[]{:S(2)}) collective-permute-start(bf16[4,256,256]{2,1,0:T(8,128)(2,1)S(1)} %get-tuple-element.156), channel_id=1, source_target_pairs={{0,4},{4,0},{8,12},{12,8},{16,20},{20,16},{24,28},{28,24},{1,5},{5... | collective-permute-start | bytes 1572872 | tf_op jit(solution)/shard_map/ppermute | solution.py:738
  48.9 10.8 %collective-permute-start.23 = (bf16[4,64,256]{2,1,0:T(8,128)(2,1)S(1)}, bf16[4,64,256]{2,1,0:T(8,128)(2,1)S(1)}, u32[]{:S(2)}, u32[]{:S(2)}) collective-permute-start(bf16[4,64,256]{2,1,0:T(8,128)(2,1)S(1)} %get-tuple-element.173), channel_id=1, source_target_pairs={{0,8},{4,12},{8,0},{12,4},{16,24},{20,28},{24,16},{28,20},{1,9},{5... | collective-permute-start | bytes 393224 | tf_op jit(solution)/shard_map/ppermute | solution.py:738
  50.2 10.1 %collective-permute-start.24 = (bf16[4,64,256]{2,1,0:T(8,128)(2,1)S(1)}, bf16[4,64,256]{2,1,0:T(8,128)(2,1)S(1)}, u32[]{:S(2)}, u32[]{:S(2)}) collective-permute-start(bf16[4,64,256]{2,1,0:T(8,128)(2,1)S(1)} %get-tuple-element.174), channel_id=1, source_target_pairs={{0,16},{4,20},{8,24},{12,28},{16,0},{20,4},{24,8},{28,12},{1,17},{... | collective-permute-start | bytes 393224 | tf_op jit(solution)/shard_map/ppermute | solution.py:738
  50.9 9.4 %collective-permute-start.25 = (bf16[4,64,256]{2,1,0:T(8,128)(2,1)S(1)}, bf16[4,64,256]{2,1,0:T(8,128)(2,1)S(1)}, u32[]{:S(2)}, u32[]{:S(2)}) collective-permute-start(bf16[4,64,256]{2,1,0:T(8,128)(2,1)S(1)} %get-tuple-element.175), channel_id=1, source_target_pairs={{0,24},{4,28},{8,16},{12,20},{16,8},{20,12},{24,0},{28,4},{1,25},{... | collective-permute-start | bytes 393224 | tf_op jit(solution)/shard_map/ppermute | solution.py:738
  51.6 8.7 %collective-permute-start.21 = (bf16[4,96,256]{2,1,0:T(8,128)(2,1)S(1)}, bf16[4,96,256]{2,1,0:T(8,128)(2,1)S(1)}, u32[]{:S(2)}, u32[]{:S(2)}) collective-permute-start(bf16[4,96,256]{2,1,0:T(8,128)(2,1)S(1)} %get-tuple-element.171), channel_id=1, source_target_pairs={{0,4},{4,0},{8,12},{12,8},{16,20},{20,16},{24,28},{28,24},{1,5},{5... | collective-permute-start | bytes 589832 | tf_op jit(solution)/shard_map/ppermute | solution.py:738
  57.1 3.3 %collective-permute-start.22 = (bf16[4,96,256]{2,1,0:T(8,128)(2,1)S(1)}, bf16[4,96,256]{2,1,0:T(8,128)(2,1)S(1)}, u32[]{:S(2)}, u32[]{:S(2)}) collective-permute-start(bf16[4,96,256]{2,1,0:T(8,128)(2,1)S(1)} %get-tuple-element.172), channel_id=1, source_target_pairs={{0,4},{4,0},{8,12},{12,8},{16,20},{20,16},{24,28},{28,24},{1,5},{5... | collective-permute-start | bytes 589832 | tf_op jit(solution)/shard_map/ppermute | solution.py:738
  59.7 3.5 %collective-permute-start.29 = (bf16[4,128,256]{2,1,0:T(8,128)(2,1)S(1)}, bf16[4,128,256]{2,1,0:T(8,128)(2,1)S(1)}, u32[]{:S(2)}, u32[]{:S(2)}) collective-permute-start(bf16[4,128,256]{2,1,0:T(8,128)(2,1)S(1)} %get-tuple-element.187), channel_id=1, source_target_pairs={{0,4},{4,0},{8,12},{12,8},{16,20},{20,16},{24,28},{28,24},{1,5},{5... | collective-permute-start | bytes 786440 | tf_op jit(solution)/shard_map/ppermute | solution.py:738
  60.5 5.6 %collective-permute-start.26 = (bf16[192,256]{1,0:T(8,128)(2,1)S(1)}, bf16[192,256]{1,0:T(8,128)(2,1)S(1)}, u32[]{:S(2)}, u32[]{:S(2)}) collective-permute-start(bf16[192,256]{1,0:T(8,128)(2,1)S(1)} %get-tuple-element.178), channel_id=1, source_target_pairs={{0,8},{4,12},{8,0},{12,4},{16,24},{20,28},{24,16},{28,20},{1,9},{5... | collective-permute-start | bytes 294920 | tf_op jit(solution)/shard_map/ppermute | solution.py:738
  61.7 5.0 %collective-permute-start.27 = (bf16[192,256]{1,0:T(8,128)(2,1)S(1)}, bf16[192,256]{1,0:T(8,128)(2,1)S(1)}, u32[]{:S(2)}, u32[]{:S(2)}) collective-permute-start(bf16[192,256]{1,0:T(8,128)(2,1)S(1)} %get-tuple-element.179), channel_id=1, source_target_pairs={{0,16},{4,20},{8,24},{12,28},{16,0},{20,4},{24,8},{28,12},{1,17},{... | collective-permute-start | bytes 294920 | tf_op jit(solution)/shard_map/ppermute | solution.py:738
  62.5 5.1 %collective-permute-start.28 = (bf16[192,256]{1,0:T(8,128)(2,1)S(1)}, bf16[192,256]{1,0:T(8,128)(2,1)S(1)}, u32[]{:S(2)}, u32[]{:S(2)}) collective-permute-start(bf16[192,256]{1,0:T(8,128)(2,1)S(1)} %get-tuple-element.180), channel_id=1, source_target_pairs={{0,24},{4,28},{8,16},{12,20},{16,8},{20,12},{24,0},{28,4},{1,25},{... | collective-permute-start | bytes 294920 | tf_op jit(solution)/shard_map/ppermute | solution.py:738
  63.3 10.7 %collective-permute-start.30 = (bf16[192,256]{1,0:T(8,128)(2,1)S(1)}, bf16[192,256]{1,0:T(8,128)(2,1)S(1)}, u32[]{:S(2)}, u32[]{:S(2)}) collective-permute-start(bf16[192,256]{1,0:T(8,128)(2,1)S(1)} %get-tuple-element.189), channel_id=1, source_target_pairs={{0,1},{1,2},{2,3},{3,0},{4,5},{5,6},{6,7},{7,4},{8,9},{9,10},{10,1... | collective-permute-start | bytes 294920 | tf_op jit(solution)/shard_map/ppermute | solution.py:730
  64.6 9.7 %collective-permute-start.31 = (bf16[192,256]{1,0:T(8,128)(2,1)S(1)}, bf16[192,256]{1,0:T(8,128)(2,1)S(1)}, u32[]{:S(2)}, u32[]{:S(2)}) collective-permute-start(bf16[192,256]{1,0:T(8,128)(2,1)S(1)} %get-tuple-element.190), channel_id=1, source_target_pairs={{0,2},{1,3},{2,0},{3,1},{4,6},{5,7},{6,4},{7,5},{8,10},{9,11},{10,... | collective-permute-start | bytes 294920 | tf_op jit(solution)/shard_map/ppermute | solution.py:730
  66.1 12.6 %collective-permute-start.32 = (bf16[192,256]{1,0:T(8,128)(2,1)S(1)}, bf16[192,256]{1,0:T(8,128)(2,1)S(1)}, u32[]{:S(2)}, u32[]{:S(2)}) collective-permute-start(bf16[192,256]{1,0:T(8,128)(2,1)S(1)} %get-tuple-element.191), channel_id=1, source_target_pairs={{0,3},{1,0},{2,1},{3,2},{4,7},{5,4},{6,5},{7,6},{8,11},{9,8},{10,9... | collective-permute-start | bytes 294920 | tf_op jit(solution)/shard_map/ppermute | solution.py:730
  67.9 2.4 %collective-permute-start.33 = (bf16[96,256]{1,0:T(8,128)(2,1)S(1)}, bf16[96,256]{1,0:T(8,128)(2,1)S(1)}, u32[]{:S(2)}, u32[]{:S(2)}) collective-permute-start(bf16[96,256]{1,0:T(8,128)(2,1)S(1)} %get-tuple-element.182.refs_0_.refs_2_), channel_id=1, source_target_pairs={{0,4},{4,0},{8,12},{12,8},{16,20},{20,16},{24,28},{28,24},{1,5},{5... | collective-permute-start | bytes 147464 | tf_op jit(solution)/shard_map/ppermute | solution.py:738
  69.4 1.2 %collective-permute-start.34 = (bf16[96,256]{1,0:T(8,128)(2,1)S(1)}, bf16[96,256]{1,0:T(8,128)(2,1)S(1)}, u32[]{:S(2)}, u32[]{:S(2)}) collective-permute-start(bf16[96,256]{1,0:T(8,128)(2,1)S(1)} %get-tuple-element.183.refs_1_.refs_3_), channel_id=1, source_target_pairs={{0,4},{4,0},{8,12},{12,8},{16,20},{20,16},{24,28},{28,24},{1,5},{5... | collective-permute-start | bytes 147464 | tf_op jit(solution)/shard_map/ppermute | solution.py:738
  71.0 11.4 %collective-permute-start.35 = (bf16[144,256]{1,0:T(8,128)(2,1)S(1)}, bf16[144,256]{1,0:T(8,128)(2,1)S(1)}, u32[]{:S(2)}, u32[]{:S(2)}) collective-permute-start(bf16[144,256]{1,0:T(8,128)(2,1)S(1)} %get-tuple-element.196), channel_id=1, source_target_pairs={{0,1},{1,2},{2,3},{3,0},{4,5},{5,6},{6,7},{7,4},{8,9},{9,10},{10,1... | collective-permute-start | bytes 221192 | tf_op jit(solution)/shard_map/ppermute | solution.py:730
  72.1 10.6 %collective-permute-start.36 = (bf16[144,256]{1,0:T(8,128)(2,1)S(1)}, bf16[144,256]{1,0:T(8,128)(2,1)S(1)}, u32[]{:S(2)}, u32[]{:S(2)}) collective-permute-start(bf16[144,256]{1,0:T(8,128)(2,1)S(1)} %get-tuple-element.197), channel_id=1, source_target_pairs={{0,2},{1,3},{2,0},{3,1},{4,6},{5,7},{6,4},{7,5},{8,10},{9,11},{10,... | collective-permute-start | bytes 221192 | tf_op jit(solution)/shard_map/ppermute | solution.py:730
  74.0 8.7 %collective-permute-start.37 = (bf16[144,256]{1,0:T(8,128)(2,1)S(1)}, bf16[144,256]{1,0:T(8,128)(2,1)S(1)}, u32[]{:S(2)}, u32[]{:S(2)}) collective-permute-start(bf16[144,256]{1,0:T(8,128)(2,1)S(1)} %get-tuple-element.198), channel_id=1, source_target_pairs={{0,3},{1,0},{2,1},{3,2},{4,7},{5,4},{6,5},{7,6},{8,11},{9,8},{10,9... | collective-permute-start | bytes 221192 | tf_op jit(solution)/shard_map/ppermute | solution.py:730
  78.8 6.5 %collective-permute-start.43 = (bf16[192,256]{1,0:T(8,128)(2,1)S(1)}, bf16[192,256]{1,0:T(8,128)(2,1)S(1)}, u32[]{:S(2)}, u32[]{:S(2)}) collective-permute-start(bf16[192,256]{1,0:T(8,128)(2,1)S(1)} %shard_map.374._.refs_0_), channel_id=1, source_target_pairs={{0,24},{4,28},{8,16},{12,20},{16,8},{20,12},{24,0},{28,4},{1,25},{... | collective-permute-start | bytes 294920 | tf_op jit(solution)/shard_map/ppermute | solution.py:738
  78.8 7.1 %collective-permute-start.42 = (bf16[192,256]{1,0:T(8,128)(2,1)S(1)}, bf16[192,256]{1,0:T(8,128)(2,1)S(1)}, u32[]{:S(2)}, u32[]{:S(2)}) collective-permute-start(bf16[192,256]{1,0:T(8,128)(2,1)S(1)} %shard_map.374._.refs_0_), channel_id=1, source_target_pairs={{0,16},{4,20},{8,24},{12,28},{16,0},{20,4},{24,8},{28,12},{1,17},{... | collective-permute-start | bytes 294920 | tf_op jit(solution)/shard_map/ppermute | solution.py:738
  82.4 3.8 %collective-permute-start.41 = (bf16[192,256]{1,0:T(8,128)(2,1)S(1)}, bf16[192,256]{1,0:T(8,128)(2,1)S(1)}, u32[]{:S(2)}, u32[]{:S(2)}) collective-permute-start(bf16[192,256]{1,0:T(8,128)(2,1)S(1)} %shard_map.374._.refs_0_), channel_id=1, source_target_pairs={{0,8},{4,12},{8,0},{12,4},{16,24},{20,28},{24,16},{28,20},{1,9},{5... | collective-permute-start | bytes 294920 | tf_op jit(solution)/shard_map/ppermute | solution.py:738
  82.8 4.3 %collective-permute-start.40 = (bf16[144,256]{1,0:T(8,128)(2,1)S(1)}, bf16[144,256]{1,0:T(8,128)(2,1)S(1)}, u32[]{:S(2)}, u32[]{:S(2)}) collective-permute-start(bf16[144,256]{1,0:T(8,128)(2,1)S(1)} %shard_map.377.refs_4_.refs_0_), channel_id=1, source_target_pairs={{0,24},{4,28},{8,16},{12,20},{16,8},{20,12},{24,0},{28,4},{1,25},{... | collective-permute-start | bytes 221192 | tf_op jit(solution)/shard_map/ppermute | solution.py:738
  83.8 4.4 %collective-permute-start.39 = (bf16[144,256]{1,0:T(8,128)(2,1)S(1)}, bf16[144,256]{1,0:T(8,128)(2,1)S(1)}, u32[]{:S(2)}, u32[]{:S(2)}) collective-permute-start(bf16[144,256]{1,0:T(8,128)(2,1)S(1)} %shard_map.377.refs_4_.refs_0_), channel_id=1, source_target_pairs={{0,16},{4,20},{8,24},{12,28},{16,0},{20,4},{24,8},{28,12},{1,17},{... | collective-permute-start | bytes 221192 | tf_op jit(solution)/shard_map/ppermute | solution.py:738
  85.2 4.0 %collective-permute-start.38 = (bf16[144,256]{1,0:T(8,128)(2,1)S(1)}, bf16[144,256]{1,0:T(8,128)(2,1)S(1)}, u32[]{:S(2)}, u32[]{:S(2)}) collective-permute-start(bf16[144,256]{1,0:T(8,128)(2,1)S(1)} %shard_map.377.refs_4_.refs_0_), channel_id=1, source_target_pairs={{0,8},{4,12},{8,0},{12,4},{16,24},{20,28},{24,16},{28,20},{1,9},{5... | collective-permute-start | bytes 221192 | tf_op jit(solution)/shard_map/ppermute | solution.py:738
  89.2 3.5 %collective-permute-start.44 = (bf16[144,256]{1,0:T(8,128)(2,1)S(1)}, bf16[144,256]{1,0:T(8,128)(2,1)S(1)}, u32[]{:S(2)}, u32[]{:S(2)}) collective-permute-start(bf16[144,256]{1,0:T(8,128)(2,1)S(1)} %shard_map.379.mine), channel_id=1, source_target_pairs={{0,4},{4,0},{8,12},{12,8},{16,20},{20,16},{24,28},{28,24},{1,5},{5... | collective-permute-start | bytes 221192 | tf_op jit(solution)/shard_map/ppermute | solution.py:738
  91.8 1.7 %collective-permute-start.45 = (bf16[384,256]{1,0:T(8,128)(2,1)S(1)}, bf16[384,256]{1,0:T(8,128)(2,1)S(1)}, u32[]{:S(2)}, u32[]{:S(2)}) collective-permute-start(bf16[384,256]{1,0:T(8,128)(2,1)S(1)} %shard_map.378.refs_4_.mine), channel_id=1, source_target_pairs={{0,4},{4,0},{8,12},{12,8},{16,20},{20,16},{24,28},{28,24},{1,5},{5... | collective-permute-start | bytes 589832 | tf_op jit(solution)/shard_map/ppermute | solution.py:738
  (12 other events, 51.1 us)

commit v5 on v4

--- a/solution.py
+++ b/solution.py
@@ -381,6 +381,7 @@
     second = (normal * vec(SECOND_G) + vec(SECOND_B)).astype(bf16)
     grad_out = jnp.concatenate([cotangent[b, 0].reshape(tok, dim) for b in range(batches)], axis=0) * mask
     grad_mlp = grad_out.astype(bf16)
+    second_t, grad_mlp_t = second.T, grad_mlp.T
     total = middle + vec(RETURN_B)
     grad_second = jnp.zeros((batches * tok, dim), f32)
     gvec_ref[...] = jnp.zeros_like(gvec_ref)
@@ -397,8 +398,8 @@
             grad_hidden.astype(f32), axis=0, keepdims=True
         )
         grad_second = grad_second + mm_nt(grad_hidden, wh[:, lanes])
-        highs[chunk] = mm_tn(activated, grad_mlp).astype(bf16)
-        grad_wh = mm_tn(second, grad_hidden).astype(bf16)
+        highs[chunk] = mm(grad_mlp_t, activated).T.astype(bf16)
+        grad_wh = mm(second_t, grad_hidden).astype(bf16)
         for owner in range(n_fs):
             lows[owner, chunk * shard : (chunk + 1) * shard] = grad_wh[owner * shard : (owner + 1) * shard]
     low, high = lows[...], highs[...]
@@ -1023,7 +1024,9 @@
         rows = dim // 4
         chunks = call(owners_kernel, [shape(rows + half, dim)] * n_fs)(total_a, keep_c, arrived_c)
         join = functools.partial(join_kernel, n_fs)
-        joined_a = call(join, shape(rows + half, dim), micros=5)(*to_owners(chunks, n_fs), vec)
+        *first_a, last_a = to_owners(chunks, n_fs)
+        joined_a = call(functools.partial(join_kernel, n_fs - 1), shape(rows + half, dim), micros=5)(*first_a, vec)
+        joined_a = call(functools.partial(join_kernel, 2), shape(rows + half, dim))(joined_a, last_a, vec)
         order = joined_a
     else:
         order = vec
@@ -1063,7 +1066,7 @@
     greduce, *vectors = call(
         functools.partial(final_small_kernel, n_fs),
         [shape(dim, dim, dtype=f32)] + [shape(shard, dtype=f32)] * HIDDEN_B + [shape(dim, dtype=f32)],
-        micros=3,
+        micros=1,
     )(mine_b, flip(mine_b, n_sp, 1))
     return (
         acts,

time: 94.9 us -> 93.4 us (0.984)
  waiting for transfers between devices: 15 us -> 11.2 us
  starting transfers between devices: 38.6 us -> 40.4 us
    ppermute x9, waiting for transfers between devices: 4.41 us -> 2.05 us  [rotate(): return lax.ppermute(value, 'fs', [(i, (i + step) % n) for i in range(n)])]
    ppermute x34, waiting for transfers between devices: 10.5 us -> 8.99 us  [flip(): return lax.ppermute(value, 'sp', [(i, i ^ bits) for i in range(n)])]
    ppermute x34, starting transfers between devices: 25.4 us -> 26.4 us  [flip(): return lax.ppermute(value, 'sp', [(i, i ^ bits) for i in range(n)])]
  transfers between devices with their start and end apart: 46 -> 46, of which waited for: 18 -> 16; matrix products, arithmetic and copies ran while one was open for 0% -> 0% of each run, Pallas kernels for 26% -> 27%
where the time goes in v5:
time: 93.4 us; the launch traced here: 92.1 us
  starting transfers between devices  40.4 us (43%)
  Pallas kernels  31.8 us (34%)
  waiting for transfers between devices  11.2 us (12%)
  local copies, waits for them, and re-layouts  7.67 us (8%)
  between operations  1.04 us (1%)
    ppermute x34, starting transfers between devices, flip(): return lax.ppermute(value, 'sp', [(i, i ^ bits) for i in range(n)])  26.4 us
    ppermute x9, starting transfers between devices, rotate(): return lax.ppermute(value, 'fs', [(i, (i + step) % n) for i in range(n)])  12.2 us
    ppermute x34, waiting for transfers between devices, flip(): return lax.ppermute(value, 'sp', [(i, i ^ bits) for i in range(n)])  8.99 us
    pallas_call x2, Pallas kernels, on_device(): call(functools.partial(backward_kernel, (n_sp, batch, tok, key_dev, keys,...  8.51 us
    pallas_call x2, Pallas kernels, on_device(): call(functools.partial(forward_kernel, (batch, tok, key_dev, keys, block,...  7.69 us
    unnamed x28, local copies, waits for them, and re-layouts  7.67 us
    pallas_call x1, Pallas kernels, on_device(): call(functools.partial(mlp_kernel, (n_fs, batches, row_dev, cols, dim, hi...  4.38 us
    pallas_call x1, Pallas kernels, on_device(): call(functools.partial(query_kernel, (n_fs, batches, tok, key_dev, keys,...  2.57 us
  transfers between devices with their start and end apart: 46, of which 16 were waited for; matrix products, arithmetic and copies ran while one was open for 0% of the time, Pallas kernels for 27%

profile of v5, /device:TPU:9, one launch (start us, length us, event | category | flops | bytes accessed | tf_op | source)
XLA Modules:
  0.0 92.1 jit_solution(3155450241258281165)
XLA Ops:
  0.7 1.8 %shard_map.356.packed = bf16[240,256]{1,0:T(8,128)(2,1)} custom-call(bf16[64]{0:T(256)(128)(2,1)} %refs_0_.2, bf16[64]{0:T(256)(128)(2,1)} %refs_1_.2, bf16[64]{0:T(256)(128)(2,1)} %refs_2_.1, bf16[64]{0:T(256)(128)(2,1)} %refs_3_.1, bf16[64]{0:T(256)(128)(2,1)} %refs_4_.1, bf16[64]{0:T(256)(128)(2,1)} %refs_5_.1, bf16[64]{0:T(256)(128)(2,1)} %refs_6_.2, ...), custom_call_target="tpu_custom_call" | custom-call | tf_op jit(solution)/shard_map/pallas_call | solution.py:833
  2.5 2.5 %collective-permute-start.1 = (bf16[240,256]{1,0:T(8,128)(2,1)}, bf16[240,256]{1,0:T(8,128)(2,1)S(1)}, u32[]{:S(2)}, u32[]{:S(2)}) collective-permute-start(bf16[240,256]{1,0:T(8,128)(2,1)} %shard_map.356.packed), channel_id=1, source_target_pairs={{0,2},{1,3},{2,0},{3,1},{4,6},{5,7},{6,4},{7,5},{8,10},{9,11},{10,... | collective-permute-start | bytes 368648 | tf_op jit(solution)/shard_map/ppermute | solution.py:731
  5.0 2.2 %collective-permute-start = (bf16[240,256]{1,0:T(8,128)(2,1)}, bf16[240,256]{1,0:T(8,128)(2,1)S(1)}, u32[]{:S(2)}, u32[]{:S(2)}) collective-permute-start(bf16[240,256]{1,0:T(8,128)(2,1)} %shard_map.356.packed), channel_id=1, source_target_pairs={{0,1},{1,2},{2,3},{3,0},{4,5},{5,6},{6,7},{7,4},{8,9},{9,10},{10,1... | collective-permute-start | bytes 368648 | tf_op jit(solution)/shard_map/ppermute | solution.py:731
  7.2 1.0 %copy-done = bf16[2,1,2,192,256]{4,3,2,1,0:T(8,128)(2,1)S(1)} copy-done((bf16[2,1,2,192,256]{4,3,2,1,0:T(8,128)(2,1)S(1)}, bf16[2,1,2,192,256]{4,3,2,1,0:T(8,128)(2,1)}, u32[]{:S(2)}) %copy-start) | copy-done | bytes 393240
  8.1 0.9 copy-done.3
  9.1 0.9 copy-done.5
  10.0 0.9 copy-done.7
  10.9 0.9 copy-done.8
  11.8 0.8 copy-done.9
  12.6 0.8 copy-done.10
  13.4 0.8 copy-done.12
  14.8 1.2 %shard_map.357 = (f32[768,256]{1,0:T(8,128)S(1)}, f32[768,128]{1,0:T(8,128)S(1)}, f32[768,256]{1,0:T(8,128)S(1)}, bf16[2,768,256]{2,1,0:T(8,128)(2,1)S(1)}, bf16...) custom-call(s32[2,1,2]{2,1,0:T(1,128)S(1)} %copy-done.13, ...), custom_call_target="tpu_custom_call" | custom-call | tf_op jit(solution)/shard_map/pallas_call | solution.py:841
  16.0 1.0 %collective-permute-start.14 = (bf16[288,256]{1,0:T(8,128)(2,1)S(1)}, bf16[288,256]{1,0:T(8,128)(2,1)S(1)}, u32[]{:S(2)}, u32[]{:S(2)}) collective-permute-start(bf16[288,256]{1,0:T(8,128)(2,1)S(1)} %get-tuple-element.136), channel_id=1, source_target_pairs={{0,2},{1,3},{2,0},{3,1},{4,6},{5,7},{6,4},{7,5},{8,10},{9,11},{10,... | collective-permute-start | bytes 442376 | tf_op jit(solution)/shard_map/ppermute | solution.py:735
  17.0 1.6 %collective-permute-start.3 = (bf16[240,256]{1,0:T(8,128)(2,1)S(1)}, bf16[240,256]{1,0:T(8,128)(2,1)S(1)}, u32[]{:S(2)}, u32[]{:S(2)}) collective-permute-start(bf16[240,256]{1,0:T(8,128)(2,1)S(1)} %get-tuple-element.125.refs_6_), channel_id=1, source_target_pairs={{0,4},{4,0},{8,12},{12,8},{16,20},{20,16},{24,28},{28,24},{1,5},{5... | collective-permute-start | bytes 368648 | tf_op jit(solution)/shard_map/ppermute | solution.py:739
  20.1 0.7 shard_map.359
  20.9 2.2 %collective-permute-start.11 = (bf16[192,256]{1,0:T(8,128)(2,1)S(1)}, bf16[192,256]{1,0:T(8,128)(2,1)S(1)}, u32[]{:S(2)}, u32[]{:S(2)}) collective-permute-start(bf16[192,256]{1,0:T(8,128)(2,1)S(1)} %get-tuple-element.133.refs_5_.refs_15_), channel_id=1, source_target_pairs={{0,24},{4,28},{8,16},{12,20},{16,8},{20,12},{24,0},{28,4},{1,25},{... | collective-permute-start | bytes 294920 | tf_op jit(solution)/shard_map/ppermute | solution.py:739
  23.7 1.1 %collective-permute-start.6 = (bf16[192,256]{1,0:T(8,128)(2,1)S(1)}, bf16[192,256]{1,0:T(8,128)(2,1)S(1)}, u32[]{:S(2)}, u32[]{:S(2)}) collective-permute-start(bf16[192,256]{1,0:T(8,128)(2,1)S(1)} %get-tuple-element.133.refs_5_.refs_15_), channel_id=1, source_target_pairs={{0,4},{4,0},{8,12},{12,8},{16,20},{20,16},{24,28},{28,24},{1,5},{5... | collective-permute-start | bytes 294920 | tf_op jit(solution)/shard_map/ppermute | solution.py:739
  24.9 1.0 %collective-permute-done.11.refs_11_.refs_21_ = bf16[192,256]{1,0:T(8,128)(2,1)S(1)} collective-permute-done((bf16[192,256]{1,0:T(8,128)(2,1)S(1)}, bf16[192,256]{1,0:T(8,128)(2,1)S(1)}, u32[]{:S(2)}, u32[]{:S(2)}) %collective-permute-start.11) | collective-permute-done | bytes 98336 | tf_op jit(solution)/shard_map/ppermute | solution.py:739
  26.4 2.1 %collective-permute-done.9.refs_9_.refs_19_ = bf16[192,256]{1,0:T(8,128)(2,1)S(1)} collective-permute-done((bf16[192,256]{1,0:T(8,128)(2,1)S(1)}, bf16[192,256]{1,0:T(8,128)(2,1)S(1)}, u32[]{:S(2)}, u32[]{:S(2)}) %collective-permute-start.9) | collective-permute-done | bytes 98336 | tf_op jit(solution)/shard_map/ppermute | solution.py:739
  30.6 3.8 %shard_map.360 = (bf16[384,256]{1,0:T(8,128)(2,1)S(1)}, bf16[384,256]{1,0:T(8,128)(2,1)S(1)}, bf16[768,512]{1,0:T(8,128)(2,1)S(1)}, f32[256,384]{1,0:T(8,128)S(1...) custom-call(bf16[768,256]{1,0:T(8,128)(2,1)S(1)} %get-tuple-element.129.refs_0_, ...), custom_call_target="tpu_custom_call" | custom-call | tf_op jit(solution)/shard_map/pallas_call | solution.py:899
  35.5 3.8 %shard_map.361 = (bf16[384,256]{1,0:T(8,128)(2,1)S(1)}, bf16[384,256]{1,0:T(8,128)(2,1)S(1)}, bf16[768,512]{1,0:T(8,128)(2,1)S(1)}, f32[256,384]{1,0:T(8,128)S(1...) custom-call(bf16[768,256]{1,0:T(8,128)(2,1)S(1)} %get-tuple-element.129.refs_0_, ...), custom_call_target="tpu_custom_call" | custom-call | tf_op jit(solution)/shard_map/pallas_call | solution.py:899
  39.4 4.4 %shard_map.364 = (f32[2,1,2,192,256]{4,3,2,1,0:T(8,128)}, f32[768,256]{1,0:T(8,128)S(1)}, bf16[768,256]{1,0:T(8,128)(2,1)S(1)}, bf16[4,256,256]{2,1,0:T(8,128)(2...) custom-call(bf16[2,1,2,192,256]{4,3,2,1,0:T(8,128)(2,1)S(1)} %copy-done.1, ...), custom_call_target="tpu_custom_call" | custom-call | tf_op jit(solution)/shard_map/pallas_call | solution.py:922
  43.9 4.3 %shard_map.365 = (bf16[4,96,256]{2,1,0:T(8,128)(2,1)S(1)}, bf16[4,96,256]{2,1,0:T(8,128)(2,1)S(1)}, bf16[4,768,768]{2,1,0:T(8,128)(2,1)S(1)}, bf16[768,256]{1,0:...) custom-call(bf16[768,256]{1,0:T(8,128)(2,1)S(1)} %get-tuple-element.146.refs_0_, ...), custom_call_target="tpu_custom_call" | custom-call | tf_op jit(solution)/shard_map/pallas_call | solution.py:964
  48.4 1.3 %collective-permute-start.23 = (bf16[4,64,256]{2,1,0:T(8,128)(2,1)S(1)}, bf16[4,64,256]{2,1,0:T(8,128)(2,1)S(1)}, u32[]{:S(2)}, u32[]{:S(2)}) collective-permute-start(bf16[4,64,256]{2,1,0:T(8,128)(2,1)S(1)} %get-tuple-element.173), channel_id=1, source_target_pairs={{0,8},{4,12},{8,0},{12,4},{16,24},{20,28},{24,16},{28,20},{1,9},{5... | collective-permute-start | bytes 393224 | tf_op jit(solution)/shard_map/ppermute | solution.py:739
  49.6 0.7 collective-permute-start.24
  51.1 1.2 %collective-permute-start.21 = (bf16[4,96,256]{2,1,0:T(8,128)(2,1)S(1)}, bf16[4,96,256]{2,1,0:T(8,128)(2,1)S(1)}, u32[]{:S(2)}, u32[]{:S(2)}) collective-permute-start(bf16[4,96,256]{2,1,0:T(8,128)(2,1)S(1)} %get-tuple-element.171), channel_id=1, source_target_pairs={{0,4},{4,0},{8,12},{12,8},{16,20},{20,16},{24,28},{28,24},{1,5},{5... | collective-permute-start | bytes 589832 | tf_op jit(solution)/shard_map/ppermute | solution.py:739
  52.3 4.3 %shard_map.367 = (bf16[4,96,256]{2,1,0:T(8,128)(2,1)S(1)}, bf16[4,96,256]{2,1,0:T(8,128)(2,1)S(1)}, bf16[4,768,768]{2,1,0:T(8,128)(2,1)S(1)}, bf16[768,256]{1,0:...) custom-call(bf16[768,256]{1,0:T(8,128)(2,1)S(1)} %get-tuple-element.146.refs_0_, ...), custom_call_target="tpu_custom_call" | custom-call | tf_op jit(solution)/shard_map/pallas_call | solution.py:964
  56.6 2.6 %shard_map.368 = (bf16[4,128,256]{2,1,0:T(8,128)(2,1)S(1)}, bf16[4,128,256]{2,1,0:T(8,128)(2,1)S(1)}, f32[768,256]{1,0:T(8,128)S(1)}, f32[16,256]{1,0:T(8,128)S(1)}) custom-call(bf16[768,256]{1,0:T(8,128)(2,1)S(1)} %get-tuple-element.129.refs_0_, bf16[256,256]{1,0:T(8,128)(2,1)S(1)} %get-tuple-element.131.refs_3_.refs_1_, ...), custom_call_target="tpu_custom_call" | custom-call | tf_op jit(solution)/shard_map/pallas_call | solution.py:979
  59.9 1.3 %collective-permute-start.26 = (bf16[192,256]{1,0:T(8,128)(2,1)S(1)}, bf16[192,256]{1,0:T(8,128)(2,1)S(1)}, u32[]{:S(2)}, u32[]{:S(2)}) collective-permute-start(bf16[192,256]{1,0:T(8,128)(2,1)S(1)} %get-tuple-element.178), channel_id=1, source_target_pairs={{0,8},{4,12},{8,0},{12,4},{16,24},{20,28},{24,16},{28,20},{1,9},{5... | collective-permute-start | bytes 294920 | tf_op jit(solution)/shard_map/ppermute | solution.py:739
  61.2 0.7 collective-permute-start.27
  62.9 1.1 %collective-permute-start.30 = (bf16[192,256]{1,0:T(8,128)(2,1)S(1)}, bf16[192,256]{1,0:T(8,128)(2,1)S(1)}, u32[]{:S(2)}, u32[]{:S(2)}) collective-permute-start(bf16[192,256]{1,0:T(8,128)(2,1)S(1)} %get-tuple-element.189), channel_id=1, source_target_pairs={{0,1},{1,2},{2,3},{3,0},{4,5},{5,6},{6,7},{7,4},{8,9},{9,10},{10,1... | collective-permute-start | bytes 294920 | tf_op jit(solution)/shard_map/ppermute | solution.py:731
  64.1 1.5 %collective-permute-start.31 = (bf16[192,256]{1,0:T(8,128)(2,1)S(1)}, bf16[192,256]{1,0:T(8,128)(2,1)S(1)}, u32[]{:S(2)}, u32[]{:S(2)}) collective-permute-start(bf16[192,256]{1,0:T(8,128)(2,1)S(1)} %get-tuple-element.190), channel_id=1, source_target_pairs={{0,2},{1,3},{2,0},{3,1},{4,6},{5,7},{6,4},{7,5},{8,10},{9,11},{10,... | collective-permute-start | bytes 294920 | tf_op jit(solution)/shard_map/ppermute | solution.py:731
  65.6 1.5 %collective-permute-done.28.refs_3_ = bf16[192,256]{1,0:T(8,128)(2,1)S(1)} collective-permute-done((bf16[192,256]{1,0:T(8,128)(2,1)S(1)}, bf16[192,256]{1,0:T(8,128)(2,1)S(1)}, u32[]{:S(2)}, u32[]{:S(2)}) %collective-permute-start.28) | collective-permute-done | bytes 98336 | tf_op jit(solution)/shard_map/ppermute | solution.py:739
  67.4 1.5 %collective-permute-start.33 = (bf16[96,256]{1,0:T(8,128)(2,1)S(1)}, bf16[96,256]{1,0:T(8,128)(2,1)S(1)}, u32[]{:S(2)}, u32[]{:S(2)}) collective-permute-start(bf16[96,256]{1,0:T(8,128)(2,1)S(1)} %get-tuple-element.182.refs_0_.refs_2_), channel_id=1, source_target_pairs={{0,4},{4,0},{8,12},{12,8},{16,20},{20,16},{24,28},{28,24},{1,5},{5... | collective-permute-start | bytes 147464 | tf_op jit(solution)/shard_map/ppermute | solution.py:739
  70.5 1.1 %collective-permute-start.35 = (bf16[144,256]{1,0:T(8,128)(2,1)S(1)}, bf16[144,256]{1,0:T(8,128)(2,1)S(1)}, u32[]{:S(2)}, u32[]{:S(2)}) collective-permute-start(bf16[144,256]{1,0:T(8,128)(2,1)S(1)} %get-tuple-element.196), channel_id=1, source_target_pairs={{0,1},{1,2},{2,3},{3,0},{4,5},{5,6},{6,7},{7,4},{8,9},{9,10},{10,1... | collective-permute-start | bytes 221192 | tf_op jit(solution)/shard_map/ppermute | solution.py:731
  71.6 3.3 %collective-permute-start.36 = (bf16[144,256]{1,0:T(8,128)(2,1)S(1)}, bf16[144,256]{1,0:T(8,128)(2,1)S(1)}, u32[]{:S(2)}, u32[]{:S(2)}) collective-permute-start(bf16[144,256]{1,0:T(8,128)(2,1)S(1)} %get-tuple-element.197), channel_id=1, source_target_pairs={{0,2},{1,3},{2,0},{3,1},{4,6},{5,7},{6,4},{7,5},{8,10},{9,11},{10,... | collective-permute-start | bytes 221192 | tf_op jit(solution)/shard_map/ppermute | solution.py:731
  75.2 1.3 %collective-permute-start.43 = (bf16[192,256]{1,0:T(8,128)(2,1)S(1)}, bf16[192,256]{1,0:T(8,128)(2,1)S(1)}, u32[]{:S(2)}, u32[]{:S(2)}) collective-permute-start(bf16[192,256]{1,0:T(8,128)(2,1)S(1)} %shard_map.375._.refs_0_), channel_id=1, source_target_pairs={{0,24},{4,28},{8,16},{12,20},{16,8},{20,12},{24,0},{28,4},{1,25},{... | collective-permute-start | bytes 294920 | tf_op jit(solution)/shard_map/ppermute | solution.py:739
  76.6 1.1 %collective-permute-start.42 = (bf16[192,256]{1,0:T(8,128)(2,1)S(1)}, bf16[192,256]{1,0:T(8,128)(2,1)S(1)}, u32[]{:S(2)}, u32[]{:S(2)}) collective-permute-start(bf16[192,256]{1,0:T(8,128)(2,1)S(1)} %shard_map.375._.refs_0_), channel_id=1, source_target_pairs={{0,16},{4,20},{8,24},{12,28},{16,0},{20,4},{24,8},{28,12},{1,17},{... | collective-permute-start | bytes 294920 | tf_op jit(solution)/shard_map/ppermute | solution.py:739
  77.7 1.2 %shard_map.376 = (f32[2,1,2,192,256]{4,3,2,1,0:T(8,128)}, f32[8,128]{1,0:T(8,128)S(1)}) custom-call(f32[768,256]{1,0:T(8,128)S(1)} %get-tuple-element.143.refs_2_.middle, f32[768,256]{1,0:T(8,128)S(1)} %get-tuple-element.184.grad_normed, f32[768,256]{1,0:T(8,128)S(1)} %get-tuple-element.120.refs_0_.normal_ref, f32[768,128]{1,0:T(8,128)S(1)} %get-tuple-element.185.rstd_ref, ...), custom_call_target="tpu_custom_call" | custom-call | tf_op jit(solution)/shard_map/pallas_call | solution.py:1033
  79.2 1.2 %collective-permute-done.36.refs_2_ = bf16[144,256]{1,0:T(8,128)(2,1)S(1)} collective-permute-done((bf16[144,256]{1,0:T(8,128)(2,1)S(1)}, bf16[144,256]{1,0:T(8,128)(2,1)S(1)}, u32[]{:S(2)}, u32[]{:S(2)}) %collective-permute-start.36) | collective-permute-done | bytes 73760 | tf_op jit(solution)/shard_map/ppermute | solution.py:731
  81.1 1.9 %collective-permute-start.40 = (bf16[144,256]{1,0:T(8,128)(2,1)S(1)}, bf16[144,256]{1,0:T(8,128)(2,1)S(1)}, u32[]{:S(2)}, u32[]{:S(2)}) collective-permute-start(bf16[144,256]{1,0:T(8,128)(2,1)S(1)} %shard_map.378.refs_4_.refs_0_), channel_id=1, source_target_pairs={{0,24},{4,28},{8,16},{12,20},{16,8},{20,12},{24,0},{28,4},{1,25},{... | collective-permute-start | bytes 221192 | tf_op jit(solution)/shard_map/ppermute | solution.py:739
  82.9 0.9 collective-permute-start.39
  83.9 1.9 %collective-permute-start.45 = (bf16[384,256]{1,0:T(8,128)(2,1)S(1)}, bf16[384,256]{1,0:T(8,128)(2,1)S(1)}, u32[]{:S(2)}, u32[]{:S(2)}) collective-permute-start(bf16[384,256]{1,0:T(8,128)(2,1)S(1)} %shard_map.379.refs_4_.mine), channel_id=1, source_target_pairs={{0,4},{4,0},{8,12},{12,8},{16,20},{20,16},{24,28},{28,24},{1,5},{5... | collective-permute-start | bytes 589832 | tf_op jit(solution)/shard_map/ppermute | solution.py:739
  85.8 1.7 %collective-permute-done.39.refs_2_ = bf16[144,256]{1,0:T(8,128)(2,1)S(1)} collective-permute-done((bf16[144,256]{1,0:T(8,128)(2,1)S(1)}, bf16[144,256]{1,0:T(8,128)(2,1)S(1)}, u32[]{:S(2)}, u32[]{:S(2)}) %collective-permute-start.39) | collective-permute-done | bytes 73760 | tf_op jit(solution)/shard_map/ppermute | solution.py:739
  87.9 1.7 %collective-permute-start.44 = (bf16[144,256]{1,0:T(8,128)(2,1)S(1)}, bf16[144,256]{1,0:T(8,128)(2,1)S(1)}, u32[]{:S(2)}, u32[]{:S(2)}) collective-permute-start(bf16[144,256]{1,0:T(8,128)(2,1)S(1)} %shard_map.380.mine), channel_id=1, source_target_pairs={{0,4},{4,0},{8,12},{12,8},{16,20},{20,16},{24,28},{28,24},{1,5},{5... | collective-permute-start | bytes 221192 | tf_op jit(solution)/shard_map/ppermute | solution.py:739
  89.5 0.9 collective-permute-done.44.other
  90.4 0.8 shard_map.381
  91.2 0.9 shard_map.382
  (99 shorter events, 12.7 us)
Async XLA Ops:
  2.5 14.5 %collective-permute-start.2 = (bf16[240,256]{1,0:T(8,128)(2,1)}, bf16[240,256]{1,0:T(8,128)(2,1)S(1)}, u32[]{:S(2)}, u32[]{:S(2)}) collective-permute-start(bf16[240,256]{1,0:T(8,128)(2,1)} %shard_map.356.packed), channel_id=1, source_target_pairs={{0,3},{1,0},{2,1},{3,2},{4,7},{5,4},{6,5},{7,6},{8,11},{9,8},{10,9... | collective-permute-start | bytes 368648 | tf_op jit(solution)/shard_map/ppermute | solution.py:731
  2.5 14.5 %collective-permute-start.1 = (bf16[240,256]{1,0:T(8,128)(2,1)}, bf16[240,256]{1,0:T(8,128)(2,1)S(1)}, u32[]{:S(2)}, u32[]{:S(2)}) collective-permute-start(bf16[240,256]{1,0:T(8,128)(2,1)} %shard_map.356.packed), channel_id=1, source_target_pairs={{0,2},{1,3},{2,0},{3,1},{4,6},{5,7},{6,4},{7,5},{8,10},{9,11},{10,... | collective-permute-start | bytes 368648 | tf_op jit(solution)/shard_map/ppermute | solution.py:731
  5.0 12.0 %collective-permute-start = (bf16[240,256]{1,0:T(8,128)(2,1)}, bf16[240,256]{1,0:T(8,128)(2,1)S(1)}, u32[]{:S(2)}, u32[]{:S(2)}) collective-permute-start(bf16[240,256]{1,0:T(8,128)(2,1)} %shard_map.356.packed), channel_id=1, source_target_pairs={{0,1},{1,2},{2,3},{3,0},{4,5},{5,6},{6,7},{7,4},{8,9},{9,10},{10,1... | collective-permute-start | bytes 368648 | tf_op jit(solution)/shard_map/ppermute | solution.py:731
  16.0 7.7 %collective-permute-start.14 = (bf16[288,256]{1,0:T(8,128)(2,1)S(1)}, bf16[288,256]{1,0:T(8,128)(2,1)S(1)}, u32[]{:S(2)}, u32[]{:S(2)}) collective-permute-start(bf16[288,256]{1,0:T(8,128)(2,1)S(1)} %get-tuple-element.136), channel_id=1, source_target_pairs={{0,2},{1,3},{2,0},{3,1},{4,6},{5,7},{6,4},{7,5},{8,10},{9,11},{10,... | collective-permute-start | bytes 442376 | tf_op jit(solution)/shard_map/ppermute | solution.py:735
  17.0 2.6 %collective-permute-start.3 = (bf16[240,256]{1,0:T(8,128)(2,1)S(1)}, bf16[240,256]{1,0:T(8,128)(2,1)S(1)}, u32[]{:S(2)}, u32[]{:S(2)}) collective-permute-start(bf16[240,256]{1,0:T(8,128)(2,1)S(1)} %get-tuple-element.125.refs_6_), channel_id=1, source_target_pairs={{0,4},{4,0},{8,12},{12,8},{16,20},{20,16},{24,28},{28,24},{1,5},{5... | collective-permute-start | bytes 368648 | tf_op jit(solution)/shard_map/ppermute | solution.py:739
  18.6 1.3 %collective-permute-start.4 = (bf16[240,256]{1,0:T(8,128)(2,1)S(1)}, bf16[240,256]{1,0:T(8,128)(2,1)S(1)}, u32[]{:S(2)}, u32[]{:S(2)}) collective-permute-start(bf16[240,256]{1,0:T(8,128)(2,1)S(1)} %get-tuple-element.126.refs_7_), channel_id=1, source_target_pairs={{0,4},{4,0},{8,12},{12,8},{16,20},{20,16},{24,28},{28,24},{1,5},{5... | collective-permute-start | bytes 368648 | tf_op jit(solution)/shard_map/ppermute | solution.py:739
  18.7 1.4 %collective-permute-start.5 = (bf16[240,256]{1,0:T(8,128)(2,1)S(1)}, bf16[240,256]{1,0:T(8,128)(2,1)S(1)}, u32[]{:S(2)}, u32[]{:S(2)}) collective-permute-start(bf16[240,256]{1,0:T(8,128)(2,1)S(1)} %get-tuple-element.127.refs_8_), channel_id=1, source_target_pairs={{0,4},{4,0},{8,12},{12,8},{16,20},{20,16},{24,28},{28,24},{1,5},{5... | collective-permute-start | bytes 368648 | tf_op jit(solution)/shard_map/ppermute | solution.py:739
  19.1 15.4 %collective-permute-start.13 = (bf16[288,256]{1,0:T(8,128)(2,1)S(1)}, bf16[288,256]{1,0:T(8,128)(2,1)S(1)}, u32[]{:S(2)}, u32[]{:S(2)}) collective-permute-start(bf16[288,256]{1,0:T(8,128)(2,1)S(1)} %get-tuple-element.136), channel_id=1, source_target_pairs={{0,1},{1,0},{2,3},{3,2},{4,5},{5,4},{6,7},{7,6},{8,9},{9,8},{10,11... | collective-permute-start | bytes 442376 | tf_op jit(solution)/shard_map/ppermute | solution.py:735
  20.9 5.0 %collective-permute-start.11 = (bf16[192,256]{1,0:T(8,128)(2,1)S(1)}, bf16[192,256]{1,0:T(8,128)(2,1)S(1)}, u32[]{:S(2)}, u32[]{:S(2)}) collective-permute-start(bf16[192,256]{1,0:T(8,128)(2,1)S(1)} %get-tuple-element.133.refs_5_.refs_15_), channel_id=1, source_target_pairs={{0,24},{4,28},{8,16},{12,20},{16,8},{20,12},{24,0},{28,4},{1,25},{... | collective-permute-start | bytes 294920 | tf_op jit(solution)/shard_map/ppermute | solution.py:739
  23.1 5.4 %collective-permute-start.9 = (bf16[192,256]{1,0:T(8,128)(2,1)S(1)}, bf16[192,256]{1,0:T(8,128)(2,1)S(1)}, u32[]{:S(2)}, u32[]{:S(2)}) collective-permute-start(bf16[192,256]{1,0:T(8,128)(2,1)S(1)} %get-tuple-element.133.refs_5_.refs_15_), channel_id=1, source_target_pairs={{0,16},{4,20},{8,24},{12,28},{16,0},{20,4},{24,8},{28,12},{1,17},{... | collective-permute-start | bytes 294920 | tf_op jit(solution)/shard_map/ppermute | solution.py:739
  23.3 5.8 %collective-permute-start.7 = (bf16[192,256]{1,0:T(8,128)(2,1)S(1)}, bf16[192,256]{1,0:T(8,128)(2,1)S(1)}, u32[]{:S(2)}, u32[]{:S(2)}) collective-permute-start(bf16[192,256]{1,0:T(8,128)(2,1)S(1)} %get-tuple-element.133.refs_5_.refs_15_), channel_id=1, source_target_pairs={{0,8},{4,12},{8,0},{12,4},{16,24},{20,28},{24,16},{28,20},{1,9},{5... | collective-permute-start | bytes 294920 | tf_op jit(solution)/shard_map/ppermute | solution.py:739
  23.7 5.5 %collective-permute-start.6 = (bf16[192,256]{1,0:T(8,128)(2,1)S(1)}, bf16[192,256]{1,0:T(8,128)(2,1)S(1)}, u32[]{:S(2)}, u32[]{:S(2)}) collective-permute-start(bf16[192,256]{1,0:T(8,128)(2,1)S(1)} %get-tuple-element.133.refs_5_.refs_15_), channel_id=1, source_target_pairs={{0,4},{4,0},{8,12},{12,8},{16,20},{20,16},{24,28},{28,24},{1,5},{5... | collective-permute-start | bytes 294920 | tf_op jit(solution)/shard_map/ppermute | solution.py:739
  24.9 14.5 %copy-start.1 = (bf16[2,1,2,192,256]{4,3,2,1,0:T(8,128)(2,1)S(1)}, bf16[2,1,2,192,256]{4,3,2,1,0:T(8,128)(2,1)}, u32[]{:S(2)}) copy-start(bf16[2,1,2,192,256]{4,3,2,1,0:T(8,128)(2,1)} %refs_0_.3) | copy-start | bytes 1179652
  24.9 14.5 %copy-start.2 = (f32[2,1,2,192,256]{4,3,2,1,0:T(8,128)S(1)}, f32[2,1,2,192,256]{4,3,2,1,0:T(8,128)}, u32[]{:S(2)}) copy-start(f32[2,1,2,192,256]{4,3,2,1,0:T(8,128)} %refs_1_.3) | copy-start | bytes 2359300
  25.9 8.6 %collective-permute-start.15 = (bf16[288,256]{1,0:T(8,128)(2,1)S(1)}, bf16[288,256]{1,0:T(8,128)(2,1)S(1)}, u32[]{:S(2)}, u32[]{:S(2)}) collective-permute-start(bf16[288,256]{1,0:T(8,128)(2,1)S(1)} %shard_map.362), channel_id=1, source_target_pairs={{0,1},{1,0},{2,3},{3,2},{4,5},{5,4},{6,7},{7,6},{8,9},{9,8},{10,11... | collective-permute-start | bytes 442376 | tf_op jit(solution)/shard_map/ppermute | solution.py:735
  28.5 1.6 %collective-permute-start.12 = (bf16[192,256]{1,0:T(8,128)(2,1)S(1)}, bf16[192,256]{1,0:T(8,128)(2,1)S(1)}, u32[]{:S(2)}, u32[]{:S(2)}) collective-permute-start(bf16[192,256]{1,0:T(8,128)(2,1)S(1)} %collective-permute-done.11.refs_11_.refs_21_), channel_id=1, source_target_pairs={{0,4},{4,0},{8,12},{12,8},{16,20},{20,16},{24,28},{28,24},{1,5},{5... | collective-permute-start | bytes 294920 | tf_op jit(solution)/shard_map/ppermute | solution.py:739
  29.1 1.3 %collective-permute-start.10 = (bf16[192,256]{1,0:T(8,128)(2,1)S(1)}, bf16[192,256]{1,0:T(8,128)(2,1)S(1)}, u32[]{:S(2)}, u32[]{:S(2)}) collective-permute-start(bf16[192,256]{1,0:T(8,128)(2,1)S(1)} %collective-permute-done.9.refs_9_.refs_19_), channel_id=1, source_target_pairs={{0,4},{4,0},{8,12},{12,8},{16,20},{20,16},{24,28},{28,24},{1,5},{5... | collective-permute-start | bytes 294920 | tf_op jit(solution)/shard_map/ppermute | solution.py:739
  29.2 1.4 %collective-permute-start.8 = (bf16[192,256]{1,0:T(8,128)(2,1)S(1)}, bf16[192,256]{1,0:T(8,128)(2,1)S(1)}, u32[]{:S(2)}, u32[]{:S(2)}) collective-permute-start(bf16[192,256]{1,0:T(8,128)(2,1)S(1)} %collective-permute-done.7.refs_7_.refs_17_), channel_id=1, source_target_pairs={{0,4},{4,0},{8,12},{12,8},{16,20},{20,16},{24,28},{28,24},{1,5},{5... | collective-permute-start | bytes 294920 | tf_op jit(solution)/shard_map/ppermute | solution.py:739
  30.1 9.2 %collective-permute-start.19 = (bf16[4,192,128]{2,1,0:T(8,128)(2,1)S(1)}, bf16[4,192,128]{2,1,0:T(8,128)(2,1)S(1)}, u32[]{:S(2)}, u32[]{:S(2)}) collective-permute-start(bf16[4,192,128]{2,1,0:T(8,128)(2,1)S(1)} %get-tuple-element.141), channel_id=1, source_target_pairs={{0,4},{4,0},{8,12},{12,8},{16,20},{20,16},{24,28},{28,24},{1,5},{5... | collective-permute-start | bytes 589832 | tf_op jit(solution)/shard_map/ppermute | solution.py:739
  34.5 4.8 %collective-permute-start.16 = (bf16[288,256]{1,0:T(8,128)(2,1)S(1)}, bf16[288,256]{1,0:T(8,128)(2,1)S(1)}, u32[]{:S(2)}, u32[]{:S(2)}) collective-permute-start(bf16[288,256]{1,0:T(8,128)(2,1)S(1)} %get-tuple-element.138.refs_9_), channel_id=1, source_target_pairs={{0,4},{4,0},{8,12},{12,8},{16,20},{20,16},{24,28},{28,24},{1,5},{5... | collective-permute-start | bytes 442376 | tf_op jit(solution)/shard_map/ppermute | solution.py:739
  34.9 4.4 %collective-permute-start.17 = (bf16[288,256]{1,0:T(8,128)(2,1)S(1)}, bf16[288,256]{1,0:T(8,128)(2,1)S(1)}, u32[]{:S(2)}, u32[]{:S(2)}) collective-permute-start(bf16[288,256]{1,0:T(8,128)(2,1)S(1)} %get-tuple-element.139.refs_10_), channel_id=1, source_target_pairs={{0,4},{4,0},{8,12},{12,8},{16,20},{20,16},{24,28},{28,24},{1,5},{5... | collective-permute-start | bytes 442376 | tf_op jit(solution)/shard_map/ppermute | solution.py:739
  35.1 4.2 %collective-permute-start.18 = (bf16[288,256]{1,0:T(8,128)(2,1)S(1)}, bf16[288,256]{1,0:T(8,128)(2,1)S(1)}, u32[]{:S(2)}, u32[]{:S(2)}) collective-permute-start(bf16[288,256]{1,0:T(8,128)(2,1)S(1)} %get-tuple-element.140.refs_11_), channel_id=1, source_target_pairs={{0,4},{4,0},{8,12},{12,8},{16,20},{20,16},{24,28},{28,24},{1,5},{5... | collective-permute-start | bytes 442376 | tf_op jit(solution)/shard_map/ppermute | solution.py:739
  43.8 4.4 %collective-permute-start.20 = (bf16[4,256,256]{2,1,0:T(8,128)(2,1)S(1)}, bf16[4,256,256]{2,1,0:T(8,128)(2,1)S(1)}, u32[]{:S(2)}, u32[]{:S(2)}) collective-permute-start(bf16[4,256,256]{2,1,0:T(8,128)(2,1)S(1)} %get-tuple-element.156), channel_id=1, source_target_pairs={{0,4},{4,0},{8,12},{12,8},{16,20},{20,16},{24,28},{28,24},{1,5},{5... | collective-permute-start | bytes 1572872 | tf_op jit(solution)/shard_map/ppermute | solution.py:739
  48.4 10.8 %collective-permute-start.23 = (bf16[4,64,256]{2,1,0:T(8,128)(2,1)S(1)}, bf16[4,64,256]{2,1,0:T(8,128)(2,1)S(1)}, u32[]{:S(2)}, u32[]{:S(2)}) collective-permute-start(bf16[4,64,256]{2,1,0:T(8,128)(2,1)S(1)} %get-tuple-element.173), channel_id=1, source_target_pairs={{0,8},{4,12},{8,0},{12,4},{16,24},{20,28},{24,16},{28,20},{1,9},{5... | collective-permute-start | bytes 393224 | tf_op jit(solution)/shard_map/ppermute | solution.py:739
  49.6 10.1 %collective-permute-start.24 = (bf16[4,64,256]{2,1,0:T(8,128)(2,1)S(1)}, bf16[4,64,256]{2,1,0:T(8,128)(2,1)S(1)}, u32[]{:S(2)}, u32[]{:S(2)}) collective-permute-start(bf16[4,64,256]{2,1,0:T(8,128)(2,1)S(1)} %get-tuple-element.174), channel_id=1, source_target_pairs={{0,16},{4,20},{8,24},{12,28},{16,0},{20,4},{24,8},{28,12},{1,17},{... | collective-permute-start | bytes 393224 | tf_op jit(solution)/shard_map/ppermute | solution.py:739
  50.4 9.4 %collective-permute-start.25 = (bf16[4,64,256]{2,1,0:T(8,128)(2,1)S(1)}, bf16[4,64,256]{2,1,0:T(8,128)(2,1)S(1)}, u32[]{:S(2)}, u32[]{:S(2)}) collective-permute-start(bf16[4,64,256]{2,1,0:T(8,128)(2,1)S(1)} %get-tuple-element.175), channel_id=1, source_target_pairs={{0,24},{4,28},{8,16},{12,20},{16,8},{20,12},{24,0},{28,4},{1,25},{... | collective-permute-start | bytes 393224 | tf_op jit(solution)/shard_map/ppermute | solution.py:739
  51.1 8.7 %collective-permute-start.21 = (bf16[4,96,256]{2,1,0:T(8,128)(2,1)S(1)}, bf16[4,96,256]{2,1,0:T(8,128)(2,1)S(1)}, u32[]{:S(2)}, u32[]{:S(2)}) collective-permute-start(bf16[4,96,256]{2,1,0:T(8,128)(2,1)S(1)} %get-tuple-element.171), channel_id=1, source_target_pairs={{0,4},{4,0},{8,12},{12,8},{16,20},{20,16},{24,28},{28,24},{1,5},{5... | collective-permute-start | bytes 589832 | tf_op jit(solution)/shard_map/ppermute | solution.py:739
  56.5 3.3 %collective-permute-start.22 = (bf16[4,96,256]{2,1,0:T(8,128)(2,1)S(1)}, bf16[4,96,256]{2,1,0:T(8,128)(2,1)S(1)}, u32[]{:S(2)}, u32[]{:S(2)}) collective-permute-start(bf16[4,96,256]{2,1,0:T(8,128)(2,1)S(1)} %get-tuple-element.172), channel_id=1, source_target_pairs={{0,4},{4,0},{8,12},{12,8},{16,20},{20,16},{24,28},{28,24},{1,5},{5... | collective-permute-start | bytes 589832 | tf_op jit(solution)/shard_map/ppermute | solution.py:739
  59.2 3.5 %collective-permute-start.29 = (bf16[4,128,256]{2,1,0:T(8,128)(2,1)S(1)}, bf16[4,128,256]{2,1,0:T(8,128)(2,1)S(1)}, u32[]{:S(2)}, u32[]{:S(2)}) collective-permute-start(bf16[4,128,256]{2,1,0:T(8,128)(2,1)S(1)} %get-tuple-element.187), channel_id=1, source_target_pairs={{0,4},{4,0},{8,12},{12,8},{16,20},{20,16},{24,28},{28,24},{1,5},{5... | collective-permute-start | bytes 786440 | tf_op jit(solution)/shard_map/ppermute | solution.py:739
  59.9 5.6 %collective-permute-start.26 = (bf16[192,256]{1,0:T(8,128)(2,1)S(1)}, bf16[192,256]{1,0:T(8,128)(2,1)S(1)}, u32[]{:S(2)}, u32[]{:S(2)}) collective-permute-start(bf16[192,256]{1,0:T(8,128)(2,1)S(1)} %get-tuple-element.178), channel_id=1, source_target_pairs={{0,8},{4,12},{8,0},{12,4},{16,24},{20,28},{24,16},{28,20},{1,9},{5... | collective-permute-start | bytes 294920 | tf_op jit(solution)/shard_map/ppermute | solution.py:739
  61.2 4.4 %collective-permute-start.27 = (bf16[192,256]{1,0:T(8,128)(2,1)S(1)}, bf16[192,256]{1,0:T(8,128)(2,1)S(1)}, u32[]{:S(2)}, u32[]{:S(2)}) collective-permute-start(bf16[192,256]{1,0:T(8,128)(2,1)S(1)} %get-tuple-element.179), channel_id=1, source_target_pairs={{0,16},{4,20},{8,24},{12,28},{16,0},{20,4},{24,8},{28,12},{1,17},{... | collective-permute-start | bytes 294920 | tf_op jit(solution)/shard_map/ppermute | solution.py:739
  61.9 5.1 %collective-permute-start.28 = (bf16[192,256]{1,0:T(8,128)(2,1)S(1)}, bf16[192,256]{1,0:T(8,128)(2,1)S(1)}, u32[]{:S(2)}, u32[]{:S(2)}) collective-permute-start(bf16[192,256]{1,0:T(8,128)(2,1)S(1)} %get-tuple-element.180), channel_id=1, source_target_pairs={{0,24},{4,28},{8,16},{12,20},{16,8},{20,12},{24,0},{28,4},{1,25},{... | collective-permute-start | bytes 294920 | tf_op jit(solution)/shard_map/ppermute | solution.py:739
  62.9 12.0 %collective-permute-start.30 = (bf16[192,256]{1,0:T(8,128)(2,1)S(1)}, bf16[192,256]{1,0:T(8,128)(2,1)S(1)}, u32[]{:S(2)}, u32[]{:S(2)}) collective-permute-start(bf16[192,256]{1,0:T(8,128)(2,1)S(1)} %get-tuple-element.189), channel_id=1, source_target_pairs={{0,1},{1,2},{2,3},{3,0},{4,5},{5,6},{6,7},{7,4},{8,9},{9,10},{10,1... | collective-permute-start | bytes 294920 | tf_op jit(solution)/shard_map/ppermute | solution.py:731
  64.1 10.9 %collective-permute-start.31 = (bf16[192,256]{1,0:T(8,128)(2,1)S(1)}, bf16[192,256]{1,0:T(8,128)(2,1)S(1)}, u32[]{:S(2)}, u32[]{:S(2)}) collective-permute-start(bf16[192,256]{1,0:T(8,128)(2,1)S(1)} %get-tuple-element.190), channel_id=1, source_target_pairs={{0,2},{1,3},{2,0},{3,1},{4,6},{5,7},{6,4},{7,5},{8,10},{9,11},{10,... | collective-permute-start | bytes 294920 | tf_op jit(solution)/shard_map/ppermute | solution.py:731
  67.4 2.6 %collective-permute-start.33 = (bf16[96,256]{1,0:T(8,128)(2,1)S(1)}, bf16[96,256]{1,0:T(8,128)(2,1)S(1)}, u32[]{:S(2)}, u32[]{:S(2)}) collective-permute-start(bf16[96,256]{1,0:T(8,128)(2,1)S(1)} %get-tuple-element.182.refs_0_.refs_2_), channel_id=1, source_target_pairs={{0,4},{4,0},{8,12},{12,8},{16,20},{20,16},{24,28},{28,24},{1,5},{5... | collective-permute-start | bytes 147464 | tf_op jit(solution)/shard_map/ppermute | solution.py:739
  68.9 1.2 %collective-permute-start.34 = (bf16[96,256]{1,0:T(8,128)(2,1)S(1)}, bf16[96,256]{1,0:T(8,128)(2,1)S(1)}, u32[]{:S(2)}, u32[]{:S(2)}) collective-permute-start(bf16[96,256]{1,0:T(8,128)(2,1)S(1)} %get-tuple-element.183.refs_1_.refs_3_), channel_id=1, source_target_pairs={{0,4},{4,0},{8,12},{12,8},{16,20},{20,16},{24,28},{28,24},{1,5},{5... | collective-permute-start | bytes 147464 | tf_op jit(solution)/shard_map/ppermute | solution.py:739
  69.0 6.2 %collective-permute-start.32 = (bf16[192,256]{1,0:T(8,128)(2,1)S(1)}, bf16[192,256]{1,0:T(8,128)(2,1)S(1)}, u32[]{:S(2)}, u32[]{:S(2)}) collective-permute-start(bf16[192,256]{1,0:T(8,128)(2,1)S(1)} %get-tuple-element.191), channel_id=1, source_target_pairs={{0,3},{1,0},{2,1},{3,2},{4,7},{5,4},{6,5},{7,6},{8,11},{9,8},{10,9... | collective-permute-start | bytes 294920 | tf_op jit(solution)/shard_map/ppermute | solution.py:731
  70.5 8.4 %collective-permute-start.35 = (bf16[144,256]{1,0:T(8,128)(2,1)S(1)}, bf16[144,256]{1,0:T(8,128)(2,1)S(1)}, u32[]{:S(2)}, u32[]{:S(2)}) collective-permute-start(bf16[144,256]{1,0:T(8,128)(2,1)S(1)} %get-tuple-element.196), channel_id=1, source_target_pairs={{0,1},{1,2},{2,3},{3,0},{4,5},{5,6},{6,7},{7,4},{8,9},{9,10},{10,1... | collective-permute-start | bytes 221192 | tf_op jit(solution)/shard_map/ppermute | solution.py:731
  71.6 8.8 %collective-permute-start.36 = (bf16[144,256]{1,0:T(8,128)(2,1)S(1)}, bf16[144,256]{1,0:T(8,128)(2,1)S(1)}, u32[]{:S(2)}, u32[]{:S(2)}) collective-permute-start(bf16[144,256]{1,0:T(8,128)(2,1)S(1)} %get-tuple-element.197), channel_id=1, source_target_pairs={{0,2},{1,3},{2,0},{3,1},{4,6},{5,7},{6,4},{7,5},{8,10},{9,11},{10,... | collective-permute-start | bytes 221192 | tf_op jit(solution)/shard_map/ppermute | solution.py:731
  74.9 6.1 %collective-permute-start.37 = (bf16[144,256]{1,0:T(8,128)(2,1)S(1)}, bf16[144,256]{1,0:T(8,128)(2,1)S(1)}, u32[]{:S(2)}, u32[]{:S(2)}) collective-permute-start(bf16[144,256]{1,0:T(8,128)(2,1)S(1)} %get-tuple-element.198), channel_id=1, source_target_pairs={{0,3},{1,0},{2,1},{3,2},{4,7},{5,4},{6,5},{7,6},{8,11},{9,8},{10,9... | collective-permute-start | bytes 221192 | tf_op jit(solution)/shard_map/ppermute | solution.py:731
  75.2 8.6 %collective-permute-start.43 = (bf16[192,256]{1,0:T(8,128)(2,1)S(1)}, bf16[192,256]{1,0:T(8,128)(2,1)S(1)}, u32[]{:S(2)}, u32[]{:S(2)}) collective-permute-start(bf16[192,256]{1,0:T(8,128)(2,1)S(1)} %shard_map.375._.refs_0_), channel_id=1, source_target_pairs={{0,24},{4,28},{8,16},{12,20},{16,8},{20,12},{24,0},{28,4},{1,25},{... | collective-permute-start | bytes 294920 | tf_op jit(solution)/shard_map/ppermute | solution.py:739
  76.6 7.3 %collective-permute-start.42 = (bf16[192,256]{1,0:T(8,128)(2,1)S(1)}, bf16[192,256]{1,0:T(8,128)(2,1)S(1)}, u32[]{:S(2)}, u32[]{:S(2)}) collective-permute-start(bf16[192,256]{1,0:T(8,128)(2,1)S(1)} %shard_map.375._.refs_0_), channel_id=1, source_target_pairs={{0,16},{4,20},{8,24},{12,28},{16,0},{20,4},{24,8},{28,12},{1,17},{... | collective-permute-start | bytes 294920 | tf_op jit(solution)/shard_map/ppermute | solution.py:739
  78.9 4.9 %collective-permute-start.41 = (bf16[192,256]{1,0:T(8,128)(2,1)S(1)}, bf16[192,256]{1,0:T(8,128)(2,1)S(1)}, u32[]{:S(2)}, u32[]{:S(2)}) collective-permute-start(bf16[192,256]{1,0:T(8,128)(2,1)S(1)} %shard_map.375._.refs_0_), channel_id=1, source_target_pairs={{0,8},{4,12},{8,0},{12,4},{16,24},{20,28},{24,16},{28,20},{1,9},{5... | collective-permute-start | bytes 294920 | tf_op jit(solution)/shard_map/ppermute | solution.py:739
  81.1 4.8 %collective-permute-start.40 = (bf16[144,256]{1,0:T(8,128)(2,1)S(1)}, bf16[144,256]{1,0:T(8,128)(2,1)S(1)}, u32[]{:S(2)}, u32[]{:S(2)}) collective-permute-start(bf16[144,256]{1,0:T(8,128)(2,1)S(1)} %shard_map.378.refs_4_.refs_0_), channel_id=1, source_target_pairs={{0,24},{4,28},{8,16},{12,20},{16,8},{20,12},{24,0},{28,4},{1,25},{... | collective-permute-start | bytes 221192 | tf_op jit(solution)/shard_map/ppermute | solution.py:739
  82.9 4.5 %collective-permute-start.39 = (bf16[144,256]{1,0:T(8,128)(2,1)S(1)}, bf16[144,256]{1,0:T(8,128)(2,1)S(1)}, u32[]{:S(2)}, u32[]{:S(2)}) collective-permute-start(bf16[144,256]{1,0:T(8,128)(2,1)S(1)} %shard_map.378.refs_4_.refs_0_), channel_id=1, source_target_pairs={{0,16},{4,20},{8,24},{12,28},{16,0},{20,4},{24,8},{28,12},{1,17},{... | collective-permute-start | bytes 221192 | tf_op jit(solution)/shard_map/ppermute | solution.py:739
  83.8 4.0 %collective-permute-start.38 = (bf16[144,256]{1,0:T(8,128)(2,1)S(1)}, bf16[144,256]{1,0:T(8,128)(2,1)S(1)}, u32[]{:S(2)}, u32[]{:S(2)}) collective-permute-start(bf16[144,256]{1,0:T(8,128)(2,1)S(1)} %shard_map.378.refs_4_.refs_0_), channel_id=1, source_target_pairs={{0,8},{4,12},{8,0},{12,4},{16,24},{20,28},{24,16},{28,20},{1,9},{5... | collective-permute-start | bytes 221192 | tf_op jit(solution)/shard_map/ppermute | solution.py:739
  83.9 7.3 %collective-permute-start.45 = (bf16[384,256]{1,0:T(8,128)(2,1)S(1)}, bf16[384,256]{1,0:T(8,128)(2,1)S(1)}, u32[]{:S(2)}, u32[]{:S(2)}) collective-permute-start(bf16[384,256]{1,0:T(8,128)(2,1)S(1)} %shard_map.379.refs_4_.mine), channel_id=1, source_target_pairs={{0,4},{4,0},{8,12},{12,8},{16,20},{20,16},{24,28},{28,24},{1,5},{5... | collective-permute-start | bytes 589832 | tf_op jit(solution)/shard_map/ppermute | solution.py:739
  87.9 2.6 %collective-permute-start.44 = (bf16[144,256]{1,0:T(8,128)(2,1)S(1)}, bf16[144,256]{1,0:T(8,128)(2,1)S(1)}, u32[]{:S(2)}, u32[]{:S(2)}) collective-permute-start(bf16[144,256]{1,0:T(8,128)(2,1)S(1)} %shard_map.380.mine), channel_id=1, source_target_pairs={{0,4},{4,0},{8,12},{12,8},{16,20},{20,16},{24,28},{28,24},{1,5},{5... | collective-permute-start | bytes 221192 | tf_op jit(solution)/shard_map/ppermute | solution.py:739
  (12 other events, 51.1 us)

commit v6 on v5

--- a/solution.py
+++ b/solution.py
@@ -691,8 +691,12 @@
     out[4 * rows :] = ((rest[0] + rest[1]) + (rest[2] + rest[3])).astype(out.dtype)
 
 
-def final_kernel(mine, other, query_w, keyval_w, output_w, hidden_w, return_w):
+def final_kernel(n_fs, mine, other, mine_b, other_b, *outs):
+    query_w, keyval_w, output_w, hidden_w, return_w, reduce_w = outs[:6]
+    smalls, hidden_b = outs[6:-1], outs[-1]
     shard, dim = query_w.shape
+    half = dim // 2
+    fs = lax.axis_index("fs")
     low, high = both_halves(mine, other)
     low, high = low.astype(f32), high.astype(f32)
     for chunk in range(hidden_w.shape[1] // dim):
@@ -703,15 +707,7 @@
     keyval_w[:, :dim] = low[shard : 2 * shard]
     keyval_w[:, dim:] = high[:shard]
     output_w[...] = high[shard : 2 * shard]
-
-
-def final_small_kernel(n_fs, mine, other, reduce_w, *outs):
-    smalls, hidden_b = outs[:-1], outs[-1]
-    dim = reduce_w.shape[0]
-    shard = dim // n_fs
-    half = dim // 2
-    fs = lax.axis_index("fs")
-    low, high = both_halves(mine, other)
+    low, high = both_halves(mine_b, other_b)
     low, high = low.astype(f32), high.astype(f32)
     reduce_w[:half] = low[:half]
     reduce_w[half:] = high[:half]
@@ -1024,26 +1020,17 @@
         rows = dim // 4
         chunks = call(owners_kernel, [shape(rows + half, dim)] * n_fs)(total_a, keep_c, arrived_c)
         join = functools.partial(join_kernel, n_fs)
-        *first_a, last_a = to_owners(chunks, n_fs)
+        first_a = to_owners(chunks, n_fs)
+        last_a = first_a.pop(1)
         joined_a = call(functools.partial(join_kernel, n_fs - 1), shape(rows + half, dim), micros=5)(*first_a, vec)
         joined_a = call(functools.partial(join_kernel, 2), shape(rows + half, dim))(joined_a, last_a, vec)
-        order = joined_a
-    else:
-        order = vec
-    grads, done = call(
-        functools.partial(input_kernel, (batches, row_dev, cols, dim)),
-        [shape(batches, 1, row_dev, cols, dim, dtype=f32), shape(8, 128, dtype=f32)],
-    )(middle, grad_normed, normal_first, rstd_first, vec, order)
-
-    if split:
-        joined_b = call(join, shape(half + VECS, dim), micros=1)(*to_owners(chunks_b, n_fs), done)
+        joined_b = call(join, shape(half + VECS, dim), micros=1)(*to_owners(chunks_b, n_fs), vec)
         mine = call(functools.partial(merge_kernel, rows), shape(4 * rows + half, dim))(
             *exchange([joined_a] * 4, n_sp), joined_b
         )
-        mine_b = call(functools.partial(merge_kernel, 0), shape(half + VECS, dim))(
-            *exchange([joined_b] * 4, n_sp), mine
-        )
+        order = mine
     else:
+        order = vec
         groups = [to_owners(chunks_b, n_fs)]
         for keep, arrived in ((keep_c, arrived_c), (keep_a, arrived_a)):
             pieces = call(owner_kernel, [shape(*keep.shape[1:])] * n_fs)(keep, arrived)
@@ -1053,21 +1040,31 @@
         )
         mine = jnp.concatenate([mine_a, mine_c], axis=0)
 
-    gquery, gkeyval, goutput, ghidden, greturn = call(
-        final_kernel,
+    grads, done = call(
+        functools.partial(input_kernel, (batches, row_dev, cols, dim)),
+        [shape(batches, 1, row_dev, cols, dim, dtype=f32), shape(8, 128, dtype=f32)],
+    )(middle, grad_normed, normal_first, rstd_first, vec, order)
+
+    if split:
+        mine_b = call(functools.partial(merge_kernel, 0), shape(half + VECS, dim))(
+            *exchange([joined_b] * 4, n_sp), done
+        )
+    (other_b,) = call(functools.partial(relay_kernel, 1), [shape(half + VECS, dim)], micros=1)(
+        flip(mine_b, n_sp, 1), vec
+    )
+    gquery, gkeyval, goutput, ghidden, greturn, greduce, *vectors = call(
+        functools.partial(final_kernel, n_fs),
         [
             shape(shard, dim, dtype=f32),
             shape(shard, 2 * dim, dtype=f32),
             shape(shard, dim, dtype=f32),
             shape(shard, hid, dtype=f32),
             shape(dim, dim, dtype=f32),
-        ],
-    )(mine, flip(mine, n_sp, 1))
-    greduce, *vectors = call(
-        functools.partial(final_small_kernel, n_fs),
-        [shape(dim, dim, dtype=f32)] + [shape(shard, dtype=f32)] * HIDDEN_B + [shape(dim, dtype=f32)],
-        micros=1,
-    )(mine_b, flip(mine_b, n_sp, 1))
+            shape(dim, dim, dtype=f32),
+        ]
+        + [shape(shard, dtype=f32)] * HIDDEN_B
+        + [shape(dim, dtype=f32)],
+    )(mine, flip(mine, n_sp, 1), mine_b, other_b)
     return (
         acts,
         grads,

time: 93.4 us -> 92.1 us (0.986)
    ppermute x9, starting transfers between devices: 12.2 us -> 11.1 us  [rotate(): return lax.ppermute(value, 'fs', [(i, (i + step) % n) for i in range(n)])]
    ppermute x34, waiting for transfers between devices: 8.99 us -> 8 us  [flip(): return lax.ppermute(value, 'sp', [(i, i ^ bits) for i in range(n)])]
  transfers between devices with their start and end apart: 46 -> 46, of which waited for: 16 -> 14; matrix products, arithmetic and copies ran while one was open for 0% -> 0% of each run, Pallas kernels for 27% -> 26%
where the time goes in v6:
time: 92.1 us; the launch traced here: 91 us
  starting transfers between devices  40.1 us (44%)
  Pallas kernels  31.2 us (34%)
  waiting for transfers between devices  10.9 us (12%)
  local copies, waits for them, and re-layouts  7.67 us (8%)
  between operations  1.21 us (1%)
    ppermute x34, starting transfers between devices, flip(): return lax.ppermute(value, 'sp', [(i, i ^ bits) for i in range(n)])  27.3 us
    ppermute x9, starting transfers between devices, rotate(): return lax.ppermute(value, 'fs', [(i, (i + step) % n) for i in range(n)])  11.1 us
    pallas_call x2, Pallas kernels, on_device(): call(functools.partial(backward_kernel, (n_sp, batch, tok, key_dev, keys,...  8.51 us
    ppermute x34, waiting for transfers between devices, flip(): return lax.ppermute(value, 'sp', [(i, i ^ bits) for i in range(n)])  8 us
    pallas_call x2, Pallas kernels, on_device(): call(functools.partial(forward_kernel, (batch, tok, key_dev, keys, block,...  7.69 us
    unnamed x28, local copies, waits for them, and re-layouts  7.67 us
    pallas_call x1, Pallas kernels, on_device(): call(functools.partial(mlp_kernel, (n_fs, batches, row_dev, cols, dim, hi...  4.38 us
    ppermute x9, waiting for transfers between devices, rotate(): return lax.ppermute(value, 'fs', [(i, (i + step) % n) for i in range(n)])  2.72 us
  transfers between devices with their start and end apart: 46, of which 14 were waited for; matrix products, arithmetic and copies ran while one was open for 0% of the time, Pallas kernels for 26%

profile of v6, /device:TPU:9, one launch (start us, length us, event | category | flops | bytes accessed | tf_op | source)
XLA Modules:
  0.0 91.0 jit_solution(10423760600346502364)
XLA Ops:
  0.7 1.8 %shard_map.356.packed = bf16[240,256]{1,0:T(8,128)(2,1)} custom-call(bf16[64]{0:T(256)(128)(2,1)} %refs_0_.2, bf16[64]{0:T(256)(128)(2,1)} %refs_1_.2, bf16[64]{0:T(256)(128)(2,1)} %refs_2_.1, bf16[64]{0:T(256)(128)(2,1)} %refs_3_.1, bf16[64]{0:T(256)(128)(2,1)} %refs_4_.1, bf16[64]{0:T(256)(128)(2,1)} %refs_5_.1, bf16[64]{0:T(256)(128)(2,1)} %refs_6_.2, ...), custom_call_target="tpu_custom_call" | custom-call | tf_op jit(solution)/shard_map/pallas_call | solution.py:829
  2.5 2.5 %collective-permute-start.1 = (bf16[240,256]{1,0:T(8,128)(2,1)}, bf16[240,256]{1,0:T(8,128)(2,1)S(1)}, u32[]{:S(2)}, u32[]{:S(2)}) collective-permute-start(bf16[240,256]{1,0:T(8,128)(2,1)} %shard_map.356.packed), channel_id=1, source_target_pairs={{0,2},{1,3},{2,0},{3,1},{4,6},{5,7},{6,4},{7,5},{8,10},{9,11},{10,... | collective-permute-start | bytes 368648 | tf_op jit(solution)/shard_map/ppermute | solution.py:727
  5.0 2.2 %collective-permute-start = (bf16[240,256]{1,0:T(8,128)(2,1)}, bf16[240,256]{1,0:T(8,128)(2,1)S(1)}, u32[]{:S(2)}, u32[]{:S(2)}) collective-permute-start(bf16[240,256]{1,0:T(8,128)(2,1)} %shard_map.356.packed), channel_id=1, source_target_pairs={{0,1},{1,2},{2,3},{3,0},{4,5},{5,6},{6,7},{7,4},{8,9},{9,10},{10,1... | collective-permute-start | bytes 368648 | tf_op jit(solution)/shard_map/ppermute | solution.py:727
  7.2 1.0 %copy-done = bf16[2,1,2,192,256]{4,3,2,1,0:T(8,128)(2,1)S(1)} copy-done((bf16[2,1,2,192,256]{4,3,2,1,0:T(8,128)(2,1)S(1)}, bf16[2,1,2,192,256]{4,3,2,1,0:T(8,128)(2,1)}, u32[]{:S(2)}) %copy-start) | copy-done | bytes 393240
  8.1 0.9 copy-done.3
  9.1 0.9 copy-done.5
  10.0 0.9 copy-done.7
  10.9 0.9 copy-done.8
  11.8 0.8 copy-done.9
  12.6 0.8 copy-done.10
  13.4 0.8 copy-done.12
  14.8 1.2 %shard_map.357 = (f32[768,256]{1,0:T(8,128)S(1)}, f32[768,128]{1,0:T(8,128)S(1)}, f32[768,256]{1,0:T(8,128)S(1)}, bf16[2,768,256]{2,1,0:T(8,128)(2,1)S(1)}, bf16...) custom-call(s32[2,1,2]{2,1,0:T(1,128)S(1)} %copy-done.13, ...), custom_call_target="tpu_custom_call" | custom-call | tf_op jit(solution)/shard_map/pallas_call | solution.py:837
  16.0 1.0 %collective-permute-start.14 = (bf16[288,256]{1,0:T(8,128)(2,1)S(1)}, bf16[288,256]{1,0:T(8,128)(2,1)S(1)}, u32[]{:S(2)}, u32[]{:S(2)}) collective-permute-start(bf16[288,256]{1,0:T(8,128)(2,1)S(1)} %get-tuple-element.136), channel_id=1, source_target_pairs={{0,2},{1,3},{2,0},{3,1},{4,6},{5,7},{6,4},{7,5},{8,10},{9,11},{10,... | collective-permute-start | bytes 442376 | tf_op jit(solution)/shard_map/ppermute | solution.py:731
  17.0 1.6 %collective-permute-start.3 = (bf16[240,256]{1,0:T(8,128)(2,1)S(1)}, bf16[240,256]{1,0:T(8,128)(2,1)S(1)}, u32[]{:S(2)}, u32[]{:S(2)}) collective-permute-start(bf16[240,256]{1,0:T(8,128)(2,1)S(1)} %get-tuple-element.125.refs_6_), channel_id=1, source_target_pairs={{0,4},{4,0},{8,12},{12,8},{16,20},{20,16},{24,28},{28,24},{1,5},{5... | collective-permute-start | bytes 368648 | tf_op jit(solution)/shard_map/ppermute | solution.py:735
  20.1 0.7 shard_map.359
  20.9 2.2 %collective-permute-start.11 = (bf16[192,256]{1,0:T(8,128)(2,1)S(1)}, bf16[192,256]{1,0:T(8,128)(2,1)S(1)}, u32[]{:S(2)}, u32[]{:S(2)}) collective-permute-start(bf16[192,256]{1,0:T(8,128)(2,1)S(1)} %get-tuple-element.133.refs_5_.refs_15_), channel_id=1, source_target_pairs={{0,24},{4,28},{8,16},{12,20},{16,8},{20,12},{24,0},{28,4},{1,25},{... | collective-permute-start | bytes 294920 | tf_op jit(solution)/shard_map/ppermute | solution.py:735
  23.7 1.1 %collective-permute-start.6 = (bf16[192,256]{1,0:T(8,128)(2,1)S(1)}, bf16[192,256]{1,0:T(8,128)(2,1)S(1)}, u32[]{:S(2)}, u32[]{:S(2)}) collective-permute-start(bf16[192,256]{1,0:T(8,128)(2,1)S(1)} %get-tuple-element.133.refs_5_.refs_15_), channel_id=1, source_target_pairs={{0,4},{4,0},{8,12},{12,8},{16,20},{20,16},{24,28},{28,24},{1,5},{5... | collective-permute-start | bytes 294920 | tf_op jit(solution)/shard_map/ppermute | solution.py:735
  24.9 1.0 %collective-permute-done.11.refs_11_.refs_21_ = bf16[192,256]{1,0:T(8,128)(2,1)S(1)} collective-permute-done((bf16[192,256]{1,0:T(8,128)(2,1)S(1)}, bf16[192,256]{1,0:T(8,128)(2,1)S(1)}, u32[]{:S(2)}, u32[]{:S(2)}) %collective-permute-start.11) | collective-permute-done | bytes 98336 | tf_op jit(solution)/shard_map/ppermute | solution.py:735
  26.4 2.1 %collective-permute-done.9.refs_9_.refs_19_ = bf16[192,256]{1,0:T(8,128)(2,1)S(1)} collective-permute-done((bf16[192,256]{1,0:T(8,128)(2,1)S(1)}, bf16[192,256]{1,0:T(8,128)(2,1)S(1)}, u32[]{:S(2)}, u32[]{:S(2)}) %collective-permute-start.9) | collective-permute-done | bytes 98336 | tf_op jit(solution)/shard_map/ppermute | solution.py:735
  30.6 3.8 %shard_map.360 = (bf16[384,256]{1,0:T(8,128)(2,1)S(1)}, bf16[384,256]{1,0:T(8,128)(2,1)S(1)}, bf16[768,512]{1,0:T(8,128)(2,1)S(1)}, f32[256,384]{1,0:T(8,128)S(1...) custom-call(bf16[768,256]{1,0:T(8,128)(2,1)S(1)} %get-tuple-element.129.refs_0_, ...), custom_call_target="tpu_custom_call" | custom-call | tf_op jit(solution)/shard_map/pallas_call | solution.py:895
  35.5 3.8 %shard_map.361 = (bf16[384,256]{1,0:T(8,128)(2,1)S(1)}, bf16[384,256]{1,0:T(8,128)(2,1)S(1)}, bf16[768,512]{1,0:T(8,128)(2,1)S(1)}, f32[256,384]{1,0:T(8,128)S(1...) custom-call(bf16[768,256]{1,0:T(8,128)(2,1)S(1)} %get-tuple-element.129.refs_0_, ...), custom_call_target="tpu_custom_call" | custom-call | tf_op jit(solution)/shard_map/pallas_call | solution.py:895
  39.4 4.4 %shard_map.364 = (f32[2,1,2,192,256]{4,3,2,1,0:T(8,128)}, f32[768,256]{1,0:T(8,128)S(1)}, bf16[768,256]{1,0:T(8,128)(2,1)S(1)}, bf16[4,256,256]{2,1,0:T(8,128)(2...) custom-call(bf16[2,1,2,192,256]{4,3,2,1,0:T(8,128)(2,1)S(1)} %copy-done.1, ...), custom_call_target="tpu_custom_call" | custom-call | tf_op jit(solution)/shard_map/pallas_call | solution.py:918
  43.9 4.3 %shard_map.365 = (bf16[4,96,256]{2,1,0:T(8,128)(2,1)S(1)}, bf16[4,96,256]{2,1,0:T(8,128)(2,1)S(1)}, bf16[4,768,768]{2,1,0:T(8,128)(2,1)S(1)}, bf16[768,256]{1,0:...) custom-call(bf16[768,256]{1,0:T(8,128)(2,1)S(1)} %get-tuple-element.146.refs_0_, ...), custom_call_target="tpu_custom_call" | custom-call | tf_op jit(solution)/shard_map/pallas_call | solution.py:960
  48.3 1.3 %collective-permute-start.23 = (bf16[4,64,256]{2,1,0:T(8,128)(2,1)S(1)}, bf16[4,64,256]{2,1,0:T(8,128)(2,1)S(1)}, u32[]{:S(2)}, u32[]{:S(2)}) collective-permute-start(bf16[4,64,256]{2,1,0:T(8,128)(2,1)S(1)} %get-tuple-element.173), channel_id=1, source_target_pairs={{0,8},{4,12},{8,0},{12,4},{16,24},{20,28},{24,16},{28,20},{1,9},{5... | collective-permute-start | bytes 393224 | tf_op jit(solution)/shard_map/ppermute | solution.py:735
  49.6 0.7 collective-permute-start.24
  51.1 1.2 %collective-permute-start.21 = (bf16[4,96,256]{2,1,0:T(8,128)(2,1)S(1)}, bf16[4,96,256]{2,1,0:T(8,128)(2,1)S(1)}, u32[]{:S(2)}, u32[]{:S(2)}) collective-permute-start(bf16[4,96,256]{2,1,0:T(8,128)(2,1)S(1)} %get-tuple-element.171), channel_id=1, source_target_pairs={{0,4},{4,0},{8,12},{12,8},{16,20},{20,16},{24,28},{28,24},{1,5},{5... | collective-permute-start | bytes 589832 | tf_op jit(solution)/shard_map/ppermute | solution.py:735
  52.3 4.3 %shard_map.367 = (bf16[4,96,256]{2,1,0:T(8,128)(2,1)S(1)}, bf16[4,96,256]{2,1,0:T(8,128)(2,1)S(1)}, bf16[4,768,768]{2,1,0:T(8,128)(2,1)S(1)}, bf16[768,256]{1,0:...) custom-call(bf16[768,256]{1,0:T(8,128)(2,1)S(1)} %get-tuple-element.146.refs_0_, ...), custom_call_target="tpu_custom_call" | custom-call | tf_op jit(solution)/shard_map/pallas_call | solution.py:960
  56.6 2.6 %shard_map.368 = (bf16[4,128,256]{2,1,0:T(8,128)(2,1)S(1)}, bf16[4,128,256]{2,1,0:T(8,128)(2,1)S(1)}, f32[768,256]{1,0:T(8,128)S(1)}, f32[16,256]{1,0:T(8,128)S(1)}) custom-call(bf16[768,256]{1,0:T(8,128)(2,1)S(1)} %get-tuple-element.129.refs_0_, bf16[256,256]{1,0:T(8,128)(2,1)S(1)} %get-tuple-element.131.refs_3_.refs_1_, ...), custom_call_target="tpu_custom_call" | custom-call | tf_op jit(solution)/shard_map/pallas_call | solution.py:975
  59.9 1.3 %collective-permute-start.26 = (bf16[192,256]{1,0:T(8,128)(2,1)S(1)}, bf16[192,256]{1,0:T(8,128)(2,1)S(1)}, u32[]{:S(2)}, u32[]{:S(2)}) collective-permute-start(bf16[192,256]{1,0:T(8,128)(2,1)S(1)} %get-tuple-element.178), channel_id=1, source_target_pairs={{0,8},{4,12},{8,0},{12,4},{16,24},{20,28},{24,16},{28,20},{1,9},{5... | collective-permute-start | bytes 294920 | tf_op jit(solution)/shard_map/ppermute | solution.py:735
  61.2 0.7 collective-permute-start.27
  61.9 0.7 collective-permute-start.28
  62.9 1.8 %collective-permute-start.30 = (bf16[192,256]{1,0:T(8,128)(2,1)S(1)}, bf16[192,256]{1,0:T(8,128)(2,1)S(1)}, u32[]{:S(2)}, u32[]{:S(2)}) collective-permute-start(bf16[192,256]{1,0:T(8,128)(2,1)S(1)} %get-tuple-element.189), channel_id=1, source_target_pairs={{0,2},{1,3},{2,0},{3,1},{4,6},{5,7},{6,4},{7,5},{8,10},{9,11},{10,... | collective-permute-start | bytes 294920 | tf_op jit(solution)/shard_map/ppermute | solution.py:727
  65.3 1.8 %collective-permute-done.28.refs_3_ = bf16[192,256]{1,0:T(8,128)(2,1)S(1)} collective-permute-done((bf16[192,256]{1,0:T(8,128)(2,1)S(1)}, bf16[192,256]{1,0:T(8,128)(2,1)S(1)}, u32[]{:S(2)}, u32[]{:S(2)}) %collective-permute-start.28) | collective-permute-done | bytes 98336 | tf_op jit(solution)/shard_map/ppermute | solution.py:735
  67.4 1.5 %collective-permute-start.36 = (bf16[96,256]{1,0:T(8,128)(2,1)S(1)}, bf16[96,256]{1,0:T(8,128)(2,1)S(1)}, u32[]{:S(2)}, u32[]{:S(2)}) collective-permute-start(bf16[96,256]{1,0:T(8,128)(2,1)S(1)} %get-tuple-element.182.refs_0_.refs_2_), channel_id=1, source_target_pairs={{0,4},{4,0},{8,12},{12,8},{16,20},{20,16},{24,28},{28,24},{1,5},{5... | collective-permute-start | bytes 147464 | tf_op jit(solution)/shard_map/ppermute | solution.py:735
  69.0 1.1 %collective-permute-start.32 = (bf16[192,256]{1,0:T(8,128)(2,1)S(1)}, bf16[192,256]{1,0:T(8,128)(2,1)S(1)}, u32[]{:S(2)}, u32[]{:S(2)}) collective-permute-start(bf16[192,256]{1,0:T(8,128)(2,1)S(1)} %get-tuple-element.191), channel_id=1, source_target_pairs={{0,1},{1,2},{2,3},{3,0},{4,5},{5,6},{6,7},{7,4},{8,9},{9,10},{10,1... | collective-permute-start | bytes 294920 | tf_op jit(solution)/shard_map/ppermute | solution.py:727
  70.9 1.0 %collective-permute-start.38 = (bf16[144,256]{1,0:T(8,128)(2,1)S(1)}, bf16[144,256]{1,0:T(8,128)(2,1)S(1)}, u32[]{:S(2)}, u32[]{:S(2)}) collective-permute-start(bf16[144,256]{1,0:T(8,128)(2,1)S(1)} %get-tuple-element.195), channel_id=1, source_target_pairs={{0,1},{1,2},{2,3},{3,0},{4,5},{5,6},{6,7},{7,4},{8,9},{9,10},{10,1... | collective-permute-start | bytes 221192 | tf_op jit(solution)/shard_map/ppermute | solution.py:727
  72.0 1.5 %collective-permute-start.39 = (bf16[144,256]{1,0:T(8,128)(2,1)S(1)}, bf16[144,256]{1,0:T(8,128)(2,1)S(1)}, u32[]{:S(2)}, u32[]{:S(2)}) collective-permute-start(bf16[144,256]{1,0:T(8,128)(2,1)S(1)} %get-tuple-element.196), channel_id=1, source_target_pairs={{0,2},{1,3},{2,0},{3,1},{4,6},{5,7},{6,4},{7,5},{8,10},{9,11},{10,... | collective-permute-start | bytes 221192 | tf_op jit(solution)/shard_map/ppermute | solution.py:727
  74.1 1.3 %collective-permute-start.35 = (bf16[192,256]{1,0:T(8,128)(2,1)S(1)}, bf16[192,256]{1,0:T(8,128)(2,1)S(1)}, u32[]{:S(2)}, u32[]{:S(2)}) collective-permute-start(bf16[192,256]{1,0:T(8,128)(2,1)S(1)} %shard_map.375.refs_0_), channel_id=1, source_target_pairs={{0,24},{4,28},{8,16},{12,20},{16,8},{20,12},{24,0},{28,4},{1,25},{... | collective-permute-start | bytes 294920 | tf_op jit(solution)/shard_map/ppermute | solution.py:735
  75.3 0.9 collective-permute-start.34
  76.2 2.2 %collective-permute-start.33 = (bf16[192,256]{1,0:T(8,128)(2,1)S(1)}, bf16[192,256]{1,0:T(8,128)(2,1)S(1)}, u32[]{:S(2)}, u32[]{:S(2)}) collective-permute-start(bf16[192,256]{1,0:T(8,128)(2,1)S(1)} %shard_map.375.refs_0_), channel_id=1, source_target_pairs={{0,8},{4,12},{8,0},{12,4},{16,24},{20,28},{24,16},{28,20},{1,9},{5... | collective-permute-start | bytes 294920 | tf_op jit(solution)/shard_map/ppermute | solution.py:735
  78.4 1.3 %collective-permute-done.39.refs_2_ = bf16[144,256]{1,0:T(8,128)(2,1)S(1)} collective-permute-done((bf16[144,256]{1,0:T(8,128)(2,1)S(1)}, bf16[144,256]{1,0:T(8,128)(2,1)S(1)}, u32[]{:S(2)}, u32[]{:S(2)}) %collective-permute-start.39) | collective-permute-done | bytes 73760 | tf_op jit(solution)/shard_map/ppermute | solution.py:727
  79.7 1.4 %collective-permute-done.40.refs_3_ = bf16[144,256]{1,0:T(8,128)(2,1)S(1)} collective-permute-done((bf16[144,256]{1,0:T(8,128)(2,1)S(1)}, bf16[144,256]{1,0:T(8,128)(2,1)S(1)}, u32[]{:S(2)}, u32[]{:S(2)}) %collective-permute-start.40) | collective-permute-done | bytes 73760 | tf_op jit(solution)/shard_map/ppermute | solution.py:727
  81.2 1.5 %collective-permute-start.44 = (bf16[144,256]{1,0:T(8,128)(2,1)S(1)}, bf16[144,256]{1,0:T(8,128)(2,1)S(1)}, u32[]{:S(2)}, u32[]{:S(2)}) collective-permute-start(bf16[144,256]{1,0:T(8,128)(2,1)S(1)} %shard_map.377.refs_4_.refs_0_), channel_id=1, source_target_pairs={{0,24},{4,28},{8,16},{12,20},{16,8},{20,12},{24,0},{28,4},{1,25},{... | collective-permute-start | bytes 221192 | tf_op jit(solution)/shard_map/ppermute | solution.py:735
  83.9 1.4 %collective-permute-start.41 = (bf16[384,256]{1,0:T(8,128)(2,1)S(1)}, bf16[384,256]{1,0:T(8,128)(2,1)S(1)}, u32[]{:S(2)}, u32[]{:S(2)}) collective-permute-start(bf16[384,256]{1,0:T(8,128)(2,1)S(1)} %shard_map.378._.mine), channel_id=1, source_target_pairs={{0,4},{4,0},{8,12},{12,8},{16,20},{20,16},{24,28},{28,24},{1,5},{5... | collective-permute-start | bytes 589832 | tf_op jit(solution)/shard_map/ppermute | solution.py:735
  85.3 1.2 %shard_map.379 = (f32[2,1,2,192,256]{4,3,2,1,0:T(8,128)}, f32[8,128]{1,0:T(8,128)S(1)}) custom-call(f32[768,256]{1,0:T(8,128)S(1)} %get-tuple-element.143.refs_2_.middle, f32[768,256]{1,0:T(8,128)S(1)} %get-tuple-element.184.grad_normed, f32[768,256]{1,0:T(8,128)S(1)} %get-tuple-element.120.refs_0_.normal_ref, f32[768,128]{1,0:T(8,128)S(1)} %get-tuple-element.185.rstd_ref, ...), custom_call_target="tpu_custom_call" | custom-call | tf_op jit(solution)/shard_map/pallas_call | solution.py:1043
  87.4 1.5 %collective-permute-start.45 = (bf16[144,256]{1,0:T(8,128)(2,1)S(1)}, bf16[144,256]{1,0:T(8,128)(2,1)S(1)}, u32[]{:S(2)}, u32[]{:S(2)}) collective-permute-start(bf16[144,256]{1,0:T(8,128)(2,1)S(1)} %shard_map.380.mine_b), channel_id=1, source_target_pairs={{0,4},{4,0},{8,12},{12,8},{16,20},{20,16},{24,28},{28,24},{1,5},{5... | collective-permute-start | bytes 221192 | tf_op jit(solution)/shard_map/ppermute | solution.py:735
  88.9 0.9 %collective-permute-done.45.refs_0_ = bf16[144,256]{1,0:T(8,128)(2,1)S(1)} collective-permute-done((bf16[144,256]{1,0:T(8,128)(2,1)S(1)}, bf16[144,256]{1,0:T(8,128)(2,1)S(1)}, u32[]{:S(2)}, u32[]{:S(2)}) %collective-permute-start.45) | collective-permute-done | bytes 73760 | tf_op jit(solution)/shard_map/ppermute | solution.py:735
  89.8 1.0 %shard_map.382 = (f32[64,256]{1,0:T(8,128)}, f32[64,512]{1,0:T(8,128)}, f32[64,256]{1,0:T(8,128)}, f32[64,1024]{1,0:T(8,128)}, f32[256,256]{1,0:T(8,128)}, /*ind...) custom-call(bf16[384,256]{1,0:T(8,128)(2,1)S(1)} %shard_map.378._.mi, ...), custom_call_target="tpu_custom_call" | custom-call | tf_op jit(solution)/shard_map/pallas_call | solution.py:1055
  (99 shorter events, 13.0 us)
Async XLA Ops:
  2.5 14.5 %collective-permute-start.2 = (bf16[240,256]{1,0:T(8,128)(2,1)}, bf16[240,256]{1,0:T(8,128)(2,1)S(1)}, u32[]{:S(2)}, u32[]{:S(2)}) collective-permute-start(bf16[240,256]{1,0:T(8,128)(2,1)} %shard_map.356.packed), channel_id=1, source_target_pairs={{0,3},{1,0},{2,1},{3,2},{4,7},{5,4},{6,5},{7,6},{8,11},{9,8},{10,9... | collective-permute-start | bytes 368648 | tf_op jit(solution)/shard_map/ppermute | solution.py:727
  2.5 14.5 %collective-permute-start.1 = (bf16[240,256]{1,0:T(8,128)(2,1)}, bf16[240,256]{1,0:T(8,128)(2,1)S(1)}, u32[]{:S(2)}, u32[]{:S(2)}) collective-permute-start(bf16[240,256]{1,0:T(8,128)(2,1)} %shard_map.356.packed), channel_id=1, source_target_pairs={{0,2},{1,3},{2,0},{3,1},{4,6},{5,7},{6,4},{7,5},{8,10},{9,11},{10,... | collective-permute-start | bytes 368648 | tf_op jit(solution)/shard_map/ppermute | solution.py:727
  5.0 12.0 %collective-permute-start = (bf16[240,256]{1,0:T(8,128)(2,1)}, bf16[240,256]{1,0:T(8,128)(2,1)S(1)}, u32[]{:S(2)}, u32[]{:S(2)}) collective-permute-start(bf16[240,256]{1,0:T(8,128)(2,1)} %shard_map.356.packed), channel_id=1, source_target_pairs={{0,1},{1,2},{2,3},{3,0},{4,5},{5,6},{6,7},{7,4},{8,9},{9,10},{10,1... | collective-permute-start | bytes 368648 | tf_op jit(solution)/shard_map/ppermute | solution.py:727
  16.0 7.7 %collective-permute-start.14 = (bf16[288,256]{1,0:T(8,128)(2,1)S(1)}, bf16[288,256]{1,0:T(8,128)(2,1)S(1)}, u32[]{:S(2)}, u32[]{:S(2)}) collective-permute-start(bf16[288,256]{1,0:T(8,128)(2,1)S(1)} %get-tuple-element.136), channel_id=1, source_target_pairs={{0,2},{1,3},{2,0},{3,1},{4,6},{5,7},{6,4},{7,5},{8,10},{9,11},{10,... | collective-permute-start | bytes 442376 | tf_op jit(solution)/shard_map/ppermute | solution.py:731
  17.0 2.6 %collective-permute-start.3 = (bf16[240,256]{1,0:T(8,128)(2,1)S(1)}, bf16[240,256]{1,0:T(8,128)(2,1)S(1)}, u32[]{:S(2)}, u32[]{:S(2)}) collective-permute-start(bf16[240,256]{1,0:T(8,128)(2,1)S(1)} %get-tuple-element.125.refs_6_), channel_id=1, source_target_pairs={{0,4},{4,0},{8,12},{12,8},{16,20},{20,16},{24,28},{28,24},{1,5},{5... | collective-permute-start | bytes 368648 | tf_op jit(solution)/shard_map/ppermute | solution.py:735
  18.6 1.3 %collective-permute-start.4 = (bf16[240,256]{1,0:T(8,128)(2,1)S(1)}, bf16[240,256]{1,0:T(8,128)(2,1)S(1)}, u32[]{:S(2)}, u32[]{:S(2)}) collective-permute-start(bf16[240,256]{1,0:T(8,128)(2,1)S(1)} %get-tuple-element.126.refs_7_), channel_id=1, source_target_pairs={{0,4},{4,0},{8,12},{12,8},{16,20},{20,16},{24,28},{28,24},{1,5},{5... | collective-permute-start | bytes 368648 | tf_op jit(solution)/shard_map/ppermute | solution.py:735
  18.7 1.4 %collective-permute-start.5 = (bf16[240,256]{1,0:T(8,128)(2,1)S(1)}, bf16[240,256]{1,0:T(8,128)(2,1)S(1)}, u32[]{:S(2)}, u32[]{:S(2)}) collective-permute-start(bf16[240,256]{1,0:T(8,128)(2,1)S(1)} %get-tuple-element.127.refs_8_), channel_id=1, source_target_pairs={{0,4},{4,0},{8,12},{12,8},{16,20},{20,16},{24,28},{28,24},{1,5},{5... | collective-permute-start | bytes 368648 | tf_op jit(solution)/shard_map/ppermute | solution.py:735
  19.1 15.3 %collective-permute-start.13 = (bf16[288,256]{1,0:T(8,128)(2,1)S(1)}, bf16[288,256]{1,0:T(8,128)(2,1)S(1)}, u32[]{:S(2)}, u32[]{:S(2)}) collective-permute-start(bf16[288,256]{1,0:T(8,128)(2,1)S(1)} %get-tuple-element.136), channel_id=1, source_target_pairs={{0,1},{1,0},{2,3},{3,2},{4,5},{5,4},{6,7},{7,6},{8,9},{9,8},{10,11... | collective-permute-start | bytes 442376 | tf_op jit(solution)/shard_map/ppermute | solution.py:731
  20.9 5.0 %collective-permute-start.11 = (bf16[192,256]{1,0:T(8,128)(2,1)S(1)}, bf16[192,256]{1,0:T(8,128)(2,1)S(1)}, u32[]{:S(2)}, u32[]{:S(2)}) collective-permute-start(bf16[192,256]{1,0:T(8,128)(2,1)S(1)} %get-tuple-element.133.refs_5_.refs_15_), channel_id=1, source_target_pairs={{0,24},{4,28},{8,16},{12,20},{16,8},{20,12},{24,0},{28,4},{1,25},{... | collective-permute-start | bytes 294920 | tf_op jit(solution)/shard_map/ppermute | solution.py:735
  23.1 5.4 %collective-permute-start.9 = (bf16[192,256]{1,0:T(8,128)(2,1)S(1)}, bf16[192,256]{1,0:T(8,128)(2,1)S(1)}, u32[]{:S(2)}, u32[]{:S(2)}) collective-permute-start(bf16[192,256]{1,0:T(8,128)(2,1)S(1)} %get-tuple-element.133.refs_5_.refs_15_), channel_id=1, source_target_pairs={{0,16},{4,20},{8,24},{12,28},{16,0},{20,4},{24,8},{28,12},{1,17},{... | collective-permute-start | bytes 294920 | tf_op jit(solution)/shard_map/ppermute | solution.py:735
  23.3 5.8 %collective-permute-start.7 = (bf16[192,256]{1,0:T(8,128)(2,1)S(1)}, bf16[192,256]{1,0:T(8,128)(2,1)S(1)}, u32[]{:S(2)}, u32[]{:S(2)}) collective-permute-start(bf16[192,256]{1,0:T(8,128)(2,1)S(1)} %get-tuple-element.133.refs_5_.refs_15_), channel_id=1, source_target_pairs={{0,8},{4,12},{8,0},{12,4},{16,24},{20,28},{24,16},{28,20},{1,9},{5... | collective-permute-start | bytes 294920 | tf_op jit(solution)/shard_map/ppermute | solution.py:735
  23.7 5.5 %collective-permute-start.6 = (bf16[192,256]{1,0:T(8,128)(2,1)S(1)}, bf16[192,256]{1,0:T(8,128)(2,1)S(1)}, u32[]{:S(2)}, u32[]{:S(2)}) collective-permute-start(bf16[192,256]{1,0:T(8,128)(2,1)S(1)} %get-tuple-element.133.refs_5_.refs_15_), channel_id=1, source_target_pairs={{0,4},{4,0},{8,12},{12,8},{16,20},{20,16},{24,28},{28,24},{1,5},{5... | collective-permute-start | bytes 294920 | tf_op jit(solution)/shard_map/ppermute | solution.py:735
  24.9 14.5 %copy-start.1 = (bf16[2,1,2,192,256]{4,3,2,1,0:T(8,128)(2,1)S(1)}, bf16[2,1,2,192,256]{4,3,2,1,0:T(8,128)(2,1)}, u32[]{:S(2)}) copy-start(bf16[2,1,2,192,256]{4,3,2,1,0:T(8,128)(2,1)} %refs_0_.3) | copy-start | bytes 1179652
  24.9 14.5 %copy-start.2 = (f32[2,1,2,192,256]{4,3,2,1,0:T(8,128)S(1)}, f32[2,1,2,192,256]{4,3,2,1,0:T(8,128)}, u32[]{:S(2)}) copy-start(f32[2,1,2,192,256]{4,3,2,1,0:T(8,128)} %refs_1_.3) | copy-start | bytes 2359300
  25.9 8.6 %collective-permute-start.15 = (bf16[288,256]{1,0:T(8,128)(2,1)S(1)}, bf16[288,256]{1,0:T(8,128)(2,1)S(1)}, u32[]{:S(2)}, u32[]{:S(2)}) collective-permute-start(bf16[288,256]{1,0:T(8,128)(2,1)S(1)} %shard_map.362), channel_id=1, source_target_pairs={{0,1},{1,0},{2,3},{3,2},{4,5},{5,4},{6,7},{7,6},{8,9},{9,8},{10,11... | collective-permute-start | bytes 442376 | tf_op jit(solution)/shard_map/ppermute | solution.py:731
  28.5 1.6 %collective-permute-start.12 = (bf16[192,256]{1,0:T(8,128)(2,1)S(1)}, bf16[192,256]{1,0:T(8,128)(2,1)S(1)}, u32[]{:S(2)}, u32[]{:S(2)}) collective-permute-start(bf16[192,256]{1,0:T(8,128)(2,1)S(1)} %collective-permute-done.11.refs_11_.refs_21_), channel_id=1, source_target_pairs={{0,4},{4,0},{8,12},{12,8},{16,20},{20,16},{24,28},{28,24},{1,5},{5... | collective-permute-start | bytes 294920 | tf_op jit(solution)/shard_map/ppermute | solution.py:735
  29.1 1.3 %collective-permute-start.10 = (bf16[192,256]{1,0:T(8,128)(2,1)S(1)}, bf16[192,256]{1,0:T(8,128)(2,1)S(1)}, u32[]{:S(2)}, u32[]{:S(2)}) collective-permute-start(bf16[192,256]{1,0:T(8,128)(2,1)S(1)} %collective-permute-done.9.refs_9_.refs_19_), channel_id=1, source_target_pairs={{0,4},{4,0},{8,12},{12,8},{16,20},{20,16},{24,28},{28,24},{1,5},{5... | collective-permute-start | bytes 294920 | tf_op jit(solution)/shard_map/ppermute | solution.py:735
  29.2 1.4 %collective-permute-start.8 = (bf16[192,256]{1,0:T(8,128)(2,1)S(1)}, bf16[192,256]{1,0:T(8,128)(2,1)S(1)}, u32[]{:S(2)}, u32[]{:S(2)}) collective-permute-start(bf16[192,256]{1,0:T(8,128)(2,1)S(1)} %collective-permute-done.7.refs_7_.refs_17_), channel_id=1, source_target_pairs={{0,4},{4,0},{8,12},{12,8},{16,20},{20,16},{24,28},{28,24},{1,5},{5... | collective-permute-start | bytes 294920 | tf_op jit(solution)/shard_map/ppermute | solution.py:735
  30.1 9.2 %collective-permute-start.19 = (bf16[4,192,128]{2,1,0:T(8,128)(2,1)S(1)}, bf16[4,192,128]{2,1,0:T(8,128)(2,1)S(1)}, u32[]{:S(2)}, u32[]{:S(2)}) collective-permute-start(bf16[4,192,128]{2,1,0:T(8,128)(2,1)S(1)} %get-tuple-element.141), channel_id=1, source_target_pairs={{0,4},{4,0},{8,12},{12,8},{16,20},{20,16},{24,28},{28,24},{1,5},{5... | collective-permute-start | bytes 589832 | tf_op jit(solution)/shard_map/ppermute | solution.py:735
  34.5 4.8 %collective-permute-start.16 = (bf16[288,256]{1,0:T(8,128)(2,1)S(1)}, bf16[288,256]{1,0:T(8,128)(2,1)S(1)}, u32[]{:S(2)}, u32[]{:S(2)}) collective-permute-start(bf16[288,256]{1,0:T(8,128)(2,1)S(1)} %get-tuple-element.138.refs_9_), channel_id=1, source_target_pairs={{0,4},{4,0},{8,12},{12,8},{16,20},{20,16},{24,28},{28,24},{1,5},{5... | collective-permute-start | bytes 442376 | tf_op jit(solution)/shard_map/ppermute | solution.py:735
  34.9 4.4 %collective-permute-start.17 = (bf16[288,256]{1,0:T(8,128)(2,1)S(1)}, bf16[288,256]{1,0:T(8,128)(2,1)S(1)}, u32[]{:S(2)}, u32[]{:S(2)}) collective-permute-start(bf16[288,256]{1,0:T(8,128)(2,1)S(1)} %get-tuple-element.139.refs_10_), channel_id=1, source_target_pairs={{0,4},{4,0},{8,12},{12,8},{16,20},{20,16},{24,28},{28,24},{1,5},{5... | collective-permute-start | bytes 442376 | tf_op jit(solution)/shard_map/ppermute | solution.py:735
  35.1 4.2 %collective-permute-start.18 = (bf16[288,256]{1,0:T(8,128)(2,1)S(1)}, bf16[288,256]{1,0:T(8,128)(2,1)S(1)}, u32[]{:S(2)}, u32[]{:S(2)}) collective-permute-start(bf16[288,256]{1,0:T(8,128)(2,1)S(1)} %get-tuple-element.140.refs_11_), channel_id=1, source_target_pairs={{0,4},{4,0},{8,12},{12,8},{16,20},{20,16},{24,28},{28,24},{1,5},{5... | collective-permute-start | bytes 442376 | tf_op jit(solution)/shard_map/ppermute | solution.py:735
  43.8 4.4 %collective-permute-start.20 = (bf16[4,256,256]{2,1,0:T(8,128)(2,1)S(1)}, bf16[4,256,256]{2,1,0:T(8,128)(2,1)S(1)}, u32[]{:S(2)}, u32[]{:S(2)}) collective-permute-start(bf16[4,256,256]{2,1,0:T(8,128)(2,1)S(1)} %get-tuple-element.156), channel_id=1, source_target_pairs={{0,4},{4,0},{8,12},{12,8},{16,20},{20,16},{24,28},{28,24},{1,5},{5... | collective-permute-start | bytes 1572872 | tf_op jit(solution)/shard_map/ppermute | solution.py:735
  48.3 10.8 %collective-permute-start.23 = (bf16[4,64,256]{2,1,0:T(8,128)(2,1)S(1)}, bf16[4,64,256]{2,1,0:T(8,128)(2,1)S(1)}, u32[]{:S(2)}, u32[]{:S(2)}) collective-permute-start(bf16[4,64,256]{2,1,0:T(8,128)(2,1)S(1)} %get-tuple-element.173), channel_id=1, source_target_pairs={{0,8},{4,12},{8,0},{12,4},{16,24},{20,28},{24,16},{28,20},{1,9},{5... | collective-permute-start | bytes 393224 | tf_op jit(solution)/shard_map/ppermute | solution.py:735
  49.6 10.1 %collective-permute-start.24 = (bf16[4,64,256]{2,1,0:T(8,128)(2,1)S(1)}, bf16[4,64,256]{2,1,0:T(8,128)(2,1)S(1)}, u32[]{:S(2)}, u32[]{:S(2)}) collective-permute-start(bf16[4,64,256]{2,1,0:T(8,128)(2,1)S(1)} %get-tuple-element.174), channel_id=1, source_target_pairs={{0,16},{4,20},{8,24},{12,28},{16,0},{20,4},{24,8},{28,12},{1,17},{... | collective-permute-start | bytes 393224 | tf_op jit(solution)/shard_map/ppermute | solution.py:735
  50.4 9.4 %collective-permute-start.25 = (bf16[4,64,256]{2,1,0:T(8,128)(2,1)S(1)}, bf16[4,64,256]{2,1,0:T(8,128)(2,1)S(1)}, u32[]{:S(2)}, u32[]{:S(2)}) collective-permute-start(bf16[4,64,256]{2,1,0:T(8,128)(2,1)S(1)} %get-tuple-element.175), channel_id=1, source_target_pairs={{0,24},{4,28},{8,16},{12,20},{16,8},{20,12},{24,0},{28,4},{1,25},{... | collective-permute-start | bytes 393224 | tf_op jit(solution)/shard_map/ppermute | solution.py:735
  51.1 8.7 %collective-permute-start.21 = (bf16[4,96,256]{2,1,0:T(8,128)(2,1)S(1)}, bf16[4,96,256]{2,1,0:T(8,128)(2,1)S(1)}, u32[]{:S(2)}, u32[]{:S(2)}) collective-permute-start(bf16[4,96,256]{2,1,0:T(8,128)(2,1)S(1)} %get-tuple-element.171), channel_id=1, source_target_pairs={{0,4},{4,0},{8,12},{12,8},{16,20},{20,16},{24,28},{28,24},{1,5},{5... | collective-permute-start | bytes 589832 | tf_op jit(solution)/shard_map/ppermute | solution.py:735
  56.5 3.3 %collective-permute-start.22 = (bf16[4,96,256]{2,1,0:T(8,128)(2,1)S(1)}, bf16[4,96,256]{2,1,0:T(8,128)(2,1)S(1)}, u32[]{:S(2)}, u32[]{:S(2)}) collective-permute-start(bf16[4,96,256]{2,1,0:T(8,128)(2,1)S(1)} %get-tuple-element.172), channel_id=1, source_target_pairs={{0,4},{4,0},{8,12},{12,8},{16,20},{20,16},{24,28},{28,24},{1,5},{5... | collective-permute-start | bytes 589832 | tf_op jit(solution)/shard_map/ppermute | solution.py:735
  59.2 3.5 %collective-permute-start.29 = (bf16[4,128,256]{2,1,0:T(8,128)(2,1)S(1)}, bf16[4,128,256]{2,1,0:T(8,128)(2,1)S(1)}, u32[]{:S(2)}, u32[]{:S(2)}) collective-permute-start(bf16[4,128,256]{2,1,0:T(8,128)(2,1)S(1)} %get-tuple-element.187), channel_id=1, source_target_pairs={{0,4},{4,0},{8,12},{12,8},{16,20},{20,16},{24,28},{28,24},{1,5},{5... | collective-permute-start | bytes 786440 | tf_op jit(solution)/shard_map/ppermute | solution.py:735
  59.9 5.3 %collective-permute-start.26 = (bf16[192,256]{1,0:T(8,128)(2,1)S(1)}, bf16[192,256]{1,0:T(8,128)(2,1)S(1)}, u32[]{:S(2)}, u32[]{:S(2)}) collective-permute-start(bf16[192,256]{1,0:T(8,128)(2,1)S(1)} %get-tuple-element.178), channel_id=1, source_target_pairs={{0,8},{4,12},{8,0},{12,4},{16,24},{20,28},{24,16},{28,20},{1,9},{5... | collective-permute-start | bytes 294920 | tf_op jit(solution)/shard_map/ppermute | solution.py:735
  61.2 4.1 %collective-permute-start.27 = (bf16[192,256]{1,0:T(8,128)(2,1)S(1)}, bf16[192,256]{1,0:T(8,128)(2,1)S(1)}, u32[]{:S(2)}, u32[]{:S(2)}) collective-permute-start(bf16[192,256]{1,0:T(8,128)(2,1)S(1)} %get-tuple-element.179), channel_id=1, source_target_pairs={{0,16},{4,20},{8,24},{12,28},{16,0},{20,4},{24,8},{28,12},{1,17},{... | collective-permute-start | bytes 294920 | tf_op jit(solution)/shard_map/ppermute | solution.py:735
  61.9 5.1 %collective-permute-start.28 = (bf16[192,256]{1,0:T(8,128)(2,1)S(1)}, bf16[192,256]{1,0:T(8,128)(2,1)S(1)}, u32[]{:S(2)}, u32[]{:S(2)}) collective-permute-start(bf16[192,256]{1,0:T(8,128)(2,1)S(1)} %get-tuple-element.180), channel_id=1, source_target_pairs={{0,24},{4,28},{8,16},{12,20},{16,8},{20,12},{24,0},{28,4},{1,25},{... | collective-permute-start | bytes 294920 | tf_op jit(solution)/shard_map/ppermute | solution.py:735
  62.9 10.5 %collective-permute-start.30 = (bf16[192,256]{1,0:T(8,128)(2,1)S(1)}, bf16[192,256]{1,0:T(8,128)(2,1)S(1)}, u32[]{:S(2)}, u32[]{:S(2)}) collective-permute-start(bf16[192,256]{1,0:T(8,128)(2,1)S(1)} %get-tuple-element.189), channel_id=1, source_target_pairs={{0,2},{1,3},{2,0},{3,1},{4,6},{5,7},{6,4},{7,5},{8,10},{9,11},{10,... | collective-permute-start | bytes 294920 | tf_op jit(solution)/shard_map/ppermute | solution.py:727
  64.8 9.2 %collective-permute-start.31 = (bf16[192,256]{1,0:T(8,128)(2,1)S(1)}, bf16[192,256]{1,0:T(8,128)(2,1)S(1)}, u32[]{:S(2)}, u32[]{:S(2)}) collective-permute-start(bf16[192,256]{1,0:T(8,128)(2,1)S(1)} %get-tuple-element.190), channel_id=1, source_target_pairs={{0,3},{1,0},{2,1},{3,2},{4,7},{5,4},{6,5},{7,6},{8,11},{9,8},{10,9... | collective-permute-start | bytes 294920 | tf_op jit(solution)/shard_map/ppermute | solution.py:727
  67.4 3.2 %collective-permute-start.36 = (bf16[96,256]{1,0:T(8,128)(2,1)S(1)}, bf16[96,256]{1,0:T(8,128)(2,1)S(1)}, u32[]{:S(2)}, u32[]{:S(2)}) collective-permute-start(bf16[96,256]{1,0:T(8,128)(2,1)S(1)} %get-tuple-element.182.refs_0_.refs_2_), channel_id=1, source_target_pairs={{0,4},{4,0},{8,12},{12,8},{16,20},{20,16},{24,28},{28,24},{1,5},{5... | collective-permute-start | bytes 147464 | tf_op jit(solution)/shard_map/ppermute | solution.py:735
  68.9 1.7 %collective-permute-start.37 = (bf16[96,256]{1,0:T(8,128)(2,1)S(1)}, bf16[96,256]{1,0:T(8,128)(2,1)S(1)}, u32[]{:S(2)}, u32[]{:S(2)}) collective-permute-start(bf16[96,256]{1,0:T(8,128)(2,1)S(1)} %get-tuple-element.183.refs_1_.refs_3_), channel_id=1, source_target_pairs={{0,4},{4,0},{8,12},{12,8},{16,20},{20,16},{24,28},{28,24},{1,5},{5... | collective-permute-start | bytes 147464 | tf_op jit(solution)/shard_map/ppermute | solution.py:735
  69.0 5.0 %collective-permute-start.32 = (bf16[192,256]{1,0:T(8,128)(2,1)S(1)}, bf16[192,256]{1,0:T(8,128)(2,1)S(1)}, u32[]{:S(2)}, u32[]{:S(2)}) collective-permute-start(bf16[192,256]{1,0:T(8,128)(2,1)S(1)} %get-tuple-element.191), channel_id=1, source_target_pairs={{0,1},{1,2},{2,3},{3,0},{4,5},{5,6},{6,7},{7,4},{8,9},{9,10},{10,1... | collective-permute-start | bytes 294920 | tf_op jit(solution)/shard_map/ppermute | solution.py:727
  70.9 5.3 %collective-permute-start.38 = (bf16[144,256]{1,0:T(8,128)(2,1)S(1)}, bf16[144,256]{1,0:T(8,128)(2,1)S(1)}, u32[]{:S(2)}, u32[]{:S(2)}) collective-permute-start(bf16[144,256]{1,0:T(8,128)(2,1)S(1)} %get-tuple-element.195), channel_id=1, source_target_pairs={{0,1},{1,2},{2,3},{3,0},{4,5},{5,6},{6,7},{7,4},{8,9},{9,10},{10,1... | collective-permute-start | bytes 221192 | tf_op jit(solution)/shard_map/ppermute | solution.py:727
  72.0 7.7 %collective-permute-start.39 = (bf16[144,256]{1,0:T(8,128)(2,1)S(1)}, bf16[144,256]{1,0:T(8,128)(2,1)S(1)}, u32[]{:S(2)}, u32[]{:S(2)}) collective-permute-start(bf16[144,256]{1,0:T(8,128)(2,1)S(1)} %get-tuple-element.196), channel_id=1, source_target_pairs={{0,2},{1,3},{2,0},{3,1},{4,6},{5,7},{6,4},{7,5},{8,10},{9,11},{10,... | collective-permute-start | bytes 221192 | tf_op jit(solution)/shard_map/ppermute | solution.py:727
  73.5 7.6 %collective-permute-start.40 = (bf16[144,256]{1,0:T(8,128)(2,1)S(1)}, bf16[144,256]{1,0:T(8,128)(2,1)S(1)}, u32[]{:S(2)}, u32[]{:S(2)}) collective-permute-start(bf16[144,256]{1,0:T(8,128)(2,1)S(1)} %get-tuple-element.197), channel_id=1, source_target_pairs={{0,3},{1,0},{2,1},{3,2},{4,7},{5,4},{6,5},{7,6},{8,11},{9,8},{10,9... | collective-permute-start | bytes 221192 | tf_op jit(solution)/shard_map/ppermute | solution.py:727
  74.1 9.3 %collective-permute-start.35 = (bf16[192,256]{1,0:T(8,128)(2,1)S(1)}, bf16[192,256]{1,0:T(8,128)(2,1)S(1)}, u32[]{:S(2)}, u32[]{:S(2)}) collective-permute-start(bf16[192,256]{1,0:T(8,128)(2,1)S(1)} %shard_map.375.refs_0_), channel_id=1, source_target_pairs={{0,24},{4,28},{8,16},{12,20},{16,8},{20,12},{24,0},{28,4},{1,25},{... | collective-permute-start | bytes 294920 | tf_op jit(solution)/shard_map/ppermute | solution.py:735
  75.3 8.5 %collective-permute-start.34 = (bf16[192,256]{1,0:T(8,128)(2,1)S(1)}, bf16[192,256]{1,0:T(8,128)(2,1)S(1)}, u32[]{:S(2)}, u32[]{:S(2)}) collective-permute-start(bf16[192,256]{1,0:T(8,128)(2,1)S(1)} %shard_map.375.refs_0_), channel_id=1, source_target_pairs={{0,16},{4,20},{8,24},{12,28},{16,0},{20,4},{24,8},{28,12},{1,17},{... | collective-permute-start | bytes 294920 | tf_op jit(solution)/shard_map/ppermute | solution.py:735
  76.2 7.7 %collective-permute-start.33 = (bf16[192,256]{1,0:T(8,128)(2,1)S(1)}, bf16[192,256]{1,0:T(8,128)(2,1)S(1)}, u32[]{:S(2)}, u32[]{:S(2)}) collective-permute-start(bf16[192,256]{1,0:T(8,128)(2,1)S(1)} %shard_map.375.refs_0_), channel_id=1, source_target_pairs={{0,8},{4,12},{8,0},{12,4},{16,24},{20,28},{24,16},{28,20},{1,9},{5... | collective-permute-start | bytes 294920 | tf_op jit(solution)/shard_map/ppermute | solution.py:735
  81.2 5.4 %collective-permute-start.44 = (bf16[144,256]{1,0:T(8,128)(2,1)S(1)}, bf16[144,256]{1,0:T(8,128)(2,1)S(1)}, u32[]{:S(2)}, u32[]{:S(2)}) collective-permute-start(bf16[144,256]{1,0:T(8,128)(2,1)S(1)} %shard_map.377.refs_4_.refs_0_), channel_id=1, source_target_pairs={{0,24},{4,28},{8,16},{12,20},{16,8},{20,12},{24,0},{28,4},{1,25},{... | collective-permute-start | bytes 221192 | tf_op jit(solution)/shard_map/ppermute | solution.py:735
  82.7 4.0 %collective-permute-start.43 = (bf16[144,256]{1,0:T(8,128)(2,1)S(1)}, bf16[144,256]{1,0:T(8,128)(2,1)S(1)}, u32[]{:S(2)}, u32[]{:S(2)}) collective-permute-start(bf16[144,256]{1,0:T(8,128)(2,1)S(1)} %shard_map.377.refs_4_.refs_0_), channel_id=1, source_target_pairs={{0,16},{4,20},{8,24},{12,28},{16,0},{20,4},{24,8},{28,12},{1,17},{... | collective-permute-start | bytes 221192 | tf_op jit(solution)/shard_map/ppermute | solution.py:735
  83.3 4.1 %collective-permute-start.42 = (bf16[144,256]{1,0:T(8,128)(2,1)S(1)}, bf16[144,256]{1,0:T(8,128)(2,1)S(1)}, u32[]{:S(2)}, u32[]{:S(2)}) collective-permute-start(bf16[144,256]{1,0:T(8,128)(2,1)S(1)} %shard_map.377.refs_4_.refs_0_), channel_id=1, source_target_pairs={{0,8},{4,12},{8,0},{12,4},{16,24},{20,28},{24,16},{28,20},{1,9},{5... | collective-permute-start | bytes 221192 | tf_op jit(solution)/shard_map/ppermute | solution.py:735
  83.9 5.9 %collective-permute-start.41 = (bf16[384,256]{1,0:T(8,128)(2,1)S(1)}, bf16[384,256]{1,0:T(8,128)(2,1)S(1)}, u32[]{:S(2)}, u32[]{:S(2)}) collective-permute-start(bf16[384,256]{1,0:T(8,128)(2,1)S(1)} %shard_map.378._.mine), channel_id=1, source_target_pairs={{0,4},{4,0},{8,12},{12,8},{16,20},{20,16},{24,28},{28,24},{1,5},{5... | collective-permute-start | bytes 589832 | tf_op jit(solution)/shard_map/ppermute | solution.py:735
  87.4 2.4 %collective-permute-start.45 = (bf16[144,256]{1,0:T(8,128)(2,1)S(1)}, bf16[144,256]{1,0:T(8,128)(2,1)S(1)}, u32[]{:S(2)}, u32[]{:S(2)}) collective-permute-start(bf16[144,256]{1,0:T(8,128)(2,1)S(1)} %shard_map.380.mine_b), channel_id=1, source_target_pairs={{0,4},{4,0},{8,12},{12,8},{16,20},{20,16},{24,28},{28,24},{1,5},{5... | collective-permute-start | bytes 221192 | tf_op jit(solution)/shard_map/ppermute | solution.py:735
  (12 other events, 51.1 us)

commit v7 on v6

--- a/solution.py
+++ b/solution.py
@@ -195,7 +195,7 @@
         normed_ref[rows] = low
         masked = low.astype(f32) * mask_ref[rows]
         for part in range(dim // 128):
-            wide[part] = masked[:, part * 128 : (part + 1) * 128]
+            wide[part, :tok] = masked[:, part * 128 : (part + 1) * 128]
         for row in range(row_dev // 2):
             start = batch * key_dev + row * half_cols
             for offset in range(4):
@@ -617,7 +617,7 @@
                         row * half_cols : (row + 1) * half_cols, part * 128 : (part + 1) * 128
                     ]
         rows = slice(batch * tok, (batch + 1) * tok)
-        spread = jnp.concatenate([wide[part] for part in range(dim // 128)], axis=1)
+        spread = jnp.concatenate([wide[part, :tok] for part in range(dim // 128)], axis=1)
         grad_normed = gnormed[rows] + spread * mask_ref[rows]
         grad_ref[rows] = grad_normed
         gain_first = gain_first + jnp.sum(grad_normed * normal_ref[rows], axis=0, keepdims=True)
@@ -878,7 +878,7 @@
             shape(dim, 2 * dim),
             shape(VECS, dim, dtype=f32),
         ],
-        scratch=[pltpu.VMEM((batches * key_dev, 4 * dim), bf16), pltpu.VMEM((dim // 128, tok, 128), f32)],
+        scratch=[pltpu.VMEM((batches * key_dev, 4 * dim), bf16), pltpu.VMEM((dim // 128, tok + 8, 128), f32)],
     )(normal_first, mask, own_r, own_q, own_kv, own_vec, *mine_first, *other_first)
     across = swap(second_half, n_fs, 2)
     passed = call(functools.partial(relay_kernel, 1), [shape(dim + shard // 2, dim)], micros=15)(across, own_vec)
@@ -1011,7 +1011,7 @@
     grad_normed, vectors = call(
         functools.partial(normed_kernel, (batches, row_dev, cols, dim)),
         [shape(batches * tok, dim, dtype=f32), shape(VECS, dim)],
-        scratch=[pltpu.VMEM((dim // 128, tok, 128), f32)],
+        scratch=[pltpu.VMEM((dim // 128, tok + 8, 128), f32)],
     )(gnormed, mask, whole_reduce, normal_first, gvec_a, gvec_b, gvec_c, *grad_reduced)
     chunks_b = call(functools.partial(weight_kernel, batches), [shape(half + VECS, dim)] * n_fs)(
         patch_cols, patch_other, *grad_reduced, *grad_other, vectors

time: 92.1 us -> 92.1 us (level)
  no operation moved by 1% of the time
where the time goes in v7:
time: 92.1 us; the launch traced here: 91 us
  starting transfers between devices  40.1 us (44%)
  Pallas kernels  31.2 us (34%)
  waiting for transfers between devices  10.9 us (12%)
  local copies, waits for them, and re-layouts  7.67 us (8%)
  between operations  1.21 us (1%)
    ppermute x34, starting transfers between devices, flip(): return lax.ppermute(value, 'sp', [(i, i ^ bits) for i in range(n)])  27.3 us
    ppermute x9, starting transfers between devices, rotate(): return lax.ppermute(value, 'fs', [(i, (i + step) % n) for i in range(n)])  11.1 us
    pallas_call x2, Pallas kernels, on_device(): call(functools.partial(backward_kernel, (n_sp, batch, tok, key_dev, keys,...  8.51 us
    ppermute x34, waiting for transfers between devices, flip(): return lax.ppermute(value, 'sp', [(i, i ^ bits) for i in range(n)])  8 us
    pallas_call x2, Pallas kernels, on_device(): call(functools.partial(forward_kernel, (batch, tok, key_dev, keys, block,...  7.7 us
    unnamed x28, local copies, waits for them, and re-layouts  7.67 us
    pallas_call x1, Pallas kernels, on_device(): call(functools.partial(mlp_kernel, (n_fs, batches, row_dev, cols, dim, hi...  4.38 us
    ppermute x9, waiting for transfers between devices, rotate(): return lax.ppermute(value, 'fs', [(i, (i + step) % n) for i in range(n)])  2.72 us
  transfers between devices with their start and end apart: 46, of which 14 were waited for; matrix products, arithmetic and copies ran while one was open for 0% of the time, Pallas kernels for 26%

profile of v7, /device:TPU:9, one launch (start us, length us, event | category | flops | bytes accessed | tf_op | source)
XLA Modules:
  0.0 91.0 jit_solution(2473453075320667946)
XLA Ops:
  0.7 1.8 %shard_map.356.packed = bf16[240,256]{1,0:T(8,128)(2,1)} custom-call(bf16[64]{0:T(256)(128)(2,1)} %refs_0_.2, bf16[64]{0:T(256)(128)(2,1)} %refs_1_.2, bf16[64]{0:T(256)(128)(2,1)} %refs_2_.1, bf16[64]{0:T(256)(128)(2,1)} %refs_3_.1, bf16[64]{0:T(256)(128)(2,1)} %refs_4_.1, bf16[64]{0:T(256)(128)(2,1)} %refs_5_.1, bf16[64]{0:T(256)(128)(2,1)} %refs_6_.2, ...), custom_call_target="tpu_custom_call" | custom-call | tf_op jit(solution)/shard_map/pallas_call | solution.py:829
  2.5 2.5 %collective-permute-start.1 = (bf16[240,256]{1,0:T(8,128)(2,1)}, bf16[240,256]{1,0:T(8,128)(2,1)S(1)}, u32[]{:S(2)}, u32[]{:S(2)}) collective-permute-start(bf16[240,256]{1,0:T(8,128)(2,1)} %shard_map.356.packed), channel_id=1, source_target_pairs={{0,2},{1,3},{2,0},{3,1},{4,6},{5,7},{6,4},{7,5},{8,10},{9,11},{10,... | collective-permute-start | bytes 368648 | tf_op jit(solution)/shard_map/ppermute | solution.py:727
  5.0 2.2 %collective-permute-start = (bf16[240,256]{1,0:T(8,128)(2,1)}, bf16[240,256]{1,0:T(8,128)(2,1)S(1)}, u32[]{:S(2)}, u32[]{:S(2)}) collective-permute-start(bf16[240,256]{1,0:T(8,128)(2,1)} %shard_map.356.packed), channel_id=1, source_target_pairs={{0,1},{1,2},{2,3},{3,0},{4,5},{5,6},{6,7},{7,4},{8,9},{9,10},{10,1... | collective-permute-start | bytes 368648 | tf_op jit(solution)/shard_map/ppermute | solution.py:727
  7.2 1.0 %copy-done = bf16[2,1,2,192,256]{4,3,2,1,0:T(8,128)(2,1)S(1)} copy-done((bf16[2,1,2,192,256]{4,3,2,1,0:T(8,128)(2,1)S(1)}, bf16[2,1,2,192,256]{4,3,2,1,0:T(8,128)(2,1)}, u32[]{:S(2)}) %copy-start) | copy-done | bytes 393240
  8.1 0.9 copy-done.3
  9.1 0.9 copy-done.5
  10.0 0.9 copy-done.7
  10.9 0.9 copy-done.8
  11.8 0.8 copy-done.9
  12.6 0.8 copy-done.10
  13.4 0.8 copy-done.12
  14.8 1.2 %shard_map.357 = (f32[768,256]{1,0:T(8,128)S(1)}, f32[768,128]{1,0:T(8,128)S(1)}, f32[768,256]{1,0:T(8,128)S(1)}, bf16[2,768,256]{2,1,0:T(8,128)(2,1)S(1)}, bf16...) custom-call(s32[2,1,2]{2,1,0:T(1,128)S(1)} %copy-done.13, ...), custom_call_target="tpu_custom_call" | custom-call | tf_op jit(solution)/shard_map/pallas_call | solution.py:837
  16.0 1.0 %collective-permute-start.14 = (bf16[288,256]{1,0:T(8,128)(2,1)S(1)}, bf16[288,256]{1,0:T(8,128)(2,1)S(1)}, u32[]{:S(2)}, u32[]{:S(2)}) collective-permute-start(bf16[288,256]{1,0:T(8,128)(2,1)S(1)} %get-tuple-element.136), channel_id=1, source_target_pairs={{0,2},{1,3},{2,0},{3,1},{4,6},{5,7},{6,4},{7,5},{8,10},{9,11},{10,... | collective-permute-start | bytes 442376 | tf_op jit(solution)/shard_map/ppermute | solution.py:731
  17.0 1.6 %collective-permute-start.3 = (bf16[240,256]{1,0:T(8,128)(2,1)S(1)}, bf16[240,256]{1,0:T(8,128)(2,1)S(1)}, u32[]{:S(2)}, u32[]{:S(2)}) collective-permute-start(bf16[240,256]{1,0:T(8,128)(2,1)S(1)} %get-tuple-element.125.refs_6_), channel_id=1, source_target_pairs={{0,4},{4,0},{8,12},{12,8},{16,20},{20,16},{24,28},{28,24},{1,5},{5... | collective-permute-start | bytes 368648 | tf_op jit(solution)/shard_map/ppermute | solution.py:735
  20.1 0.7 shard_map.359
  20.9 2.2 %collective-permute-start.11 = (bf16[192,256]{1,0:T(8,128)(2,1)S(1)}, bf16[192,256]{1,0:T(8,128)(2,1)S(1)}, u32[]{:S(2)}, u32[]{:S(2)}) collective-permute-start(bf16[192,256]{1,0:T(8,128)(2,1)S(1)} %get-tuple-element.133.refs_5_.refs_15_), channel_id=1, source_target_pairs={{0,24},{4,28},{8,16},{12,20},{16,8},{20,12},{24,0},{28,4},{1,25},{... | collective-permute-start | bytes 294920 | tf_op jit(solution)/shard_map/ppermute | solution.py:735
  23.7 1.1 %collective-permute-start.6 = (bf16[192,256]{1,0:T(8,128)(2,1)S(1)}, bf16[192,256]{1,0:T(8,128)(2,1)S(1)}, u32[]{:S(2)}, u32[]{:S(2)}) collective-permute-start(bf16[192,256]{1,0:T(8,128)(2,1)S(1)} %get-tuple-element.133.refs_5_.refs_15_), channel_id=1, source_target_pairs={{0,4},{4,0},{8,12},{12,8},{16,20},{20,16},{24,28},{28,24},{1,5},{5... | collective-permute-start | bytes 294920 | tf_op jit(solution)/shard_map/ppermute | solution.py:735
  24.9 1.0 %collective-permute-done.11.refs_11_.refs_21_ = bf16[192,256]{1,0:T(8,128)(2,1)S(1)} collective-permute-done((bf16[192,256]{1,0:T(8,128)(2,1)S(1)}, bf16[192,256]{1,0:T(8,128)(2,1)S(1)}, u32[]{:S(2)}, u32[]{:S(2)}) %collective-permute-start.11) | collective-permute-done | bytes 98336 | tf_op jit(solution)/shard_map/ppermute | solution.py:735
  26.4 2.1 %collective-permute-done.9.refs_9_.refs_19_ = bf16[192,256]{1,0:T(8,128)(2,1)S(1)} collective-permute-done((bf16[192,256]{1,0:T(8,128)(2,1)S(1)}, bf16[192,256]{1,0:T(8,128)(2,1)S(1)}, u32[]{:S(2)}, u32[]{:S(2)}) %collective-permute-start.9) | collective-permute-done | bytes 98336 | tf_op jit(solution)/shard_map/ppermute | solution.py:735
  30.6 3.8 %shard_map.360 = (bf16[384,256]{1,0:T(8,128)(2,1)S(1)}, bf16[384,256]{1,0:T(8,128)(2,1)S(1)}, bf16[768,512]{1,0:T(8,128)(2,1)S(1)}, f32[256,384]{1,0:T(8,128)S(1...) custom-call(bf16[768,256]{1,0:T(8,128)(2,1)S(1)} %get-tuple-element.129.refs_0_, ...), custom_call_target="tpu_custom_call" | custom-call | tf_op jit(solution)/shard_map/pallas_call | solution.py:895
  35.5 3.8 %shard_map.361 = (bf16[384,256]{1,0:T(8,128)(2,1)S(1)}, bf16[384,256]{1,0:T(8,128)(2,1)S(1)}, bf16[768,512]{1,0:T(8,128)(2,1)S(1)}, f32[256,384]{1,0:T(8,128)S(1...) custom-call(bf16[768,256]{1,0:T(8,128)(2,1)S(1)} %get-tuple-element.129.refs_0_, ...), custom_call_target="tpu_custom_call" | custom-call | tf_op jit(solution)/shard_map/pallas_call | solution.py:895
  39.4 4.4 %shard_map.364 = (f32[2,1,2,192,256]{4,3,2,1,0:T(8,128)}, f32[768,256]{1,0:T(8,128)S(1)}, bf16[768,256]{1,0:T(8,128)(2,1)S(1)}, bf16[4,256,256]{2,1,0:T(8,128)(2...) custom-call(bf16[2,1,2,192,256]{4,3,2,1,0:T(8,128)(2,1)S(1)} %copy-done.1, ...), custom_call_target="tpu_custom_call" | custom-call | tf_op jit(solution)/shard_map/pallas_call | solution.py:918
  43.9 4.3 %shard_map.365 = (bf16[4,96,256]{2,1,0:T(8,128)(2,1)S(1)}, bf16[4,96,256]{2,1,0:T(8,128)(2,1)S(1)}, bf16[4,768,768]{2,1,0:T(8,128)(2,1)S(1)}, bf16[768,256]{1,0:...) custom-call(bf16[768,256]{1,0:T(8,128)(2,1)S(1)} %get-tuple-element.146.refs_0_, ...), custom_call_target="tpu_custom_call" | custom-call | tf_op jit(solution)/shard_map/pallas_call | solution.py:960
  48.3 1.3 %collective-permute-start.23 = (bf16[4,64,256]{2,1,0:T(8,128)(2,1)S(1)}, bf16[4,64,256]{2,1,0:T(8,128)(2,1)S(1)}, u32[]{:S(2)}, u32[]{:S(2)}) collective-permute-start(bf16[4,64,256]{2,1,0:T(8,128)(2,1)S(1)} %get-tuple-element.173), channel_id=1, source_target_pairs={{0,8},{4,12},{8,0},{12,4},{16,24},{20,28},{24,16},{28,20},{1,9},{5... | collective-permute-start | bytes 393224 | tf_op jit(solution)/shard_map/ppermute | solution.py:735
  49.6 0.7 collective-permute-start.24
  50.4 0.7 collective-permute-start.25
  51.1 1.2 %collective-permute-start.21 = (bf16[4,96,256]{2,1,0:T(8,128)(2,1)S(1)}, bf16[4,96,256]{2,1,0:T(8,128)(2,1)S(1)}, u32[]{:S(2)}, u32[]{:S(2)}) collective-permute-start(bf16[4,96,256]{2,1,0:T(8,128)(2,1)S(1)} %get-tuple-element.171), channel_id=1, source_target_pairs={{0,4},{4,0},{8,12},{12,8},{16,20},{20,16},{24,28},{28,24},{1,5},{5... | collective-permute-start | bytes 589832 | tf_op jit(solution)/shard_map/ppermute | solution.py:735
  52.3 4.3 %shard_map.367 = (bf16[4,96,256]{2,1,0:T(8,128)(2,1)S(1)}, bf16[4,96,256]{2,1,0:T(8,128)(2,1)S(1)}, bf16[4,768,768]{2,1,0:T(8,128)(2,1)S(1)}, bf16[768,256]{1,0:...) custom-call(bf16[768,256]{1,0:T(8,128)(2,1)S(1)} %get-tuple-element.146.refs_0_, ...), custom_call_target="tpu_custom_call" | custom-call | tf_op jit(solution)/shard_map/pallas_call | solution.py:960
  56.6 2.6 %shard_map.368 = (bf16[4,128,256]{2,1,0:T(8,128)(2,1)S(1)}, bf16[4,128,256]{2,1,0:T(8,128)(2,1)S(1)}, f32[768,256]{1,0:T(8,128)S(1)}, f32[16,256]{1,0:T(8,128)S(1)}) custom-call(bf16[768,256]{1,0:T(8,128)(2,1)S(1)} %get-tuple-element.129.refs_0_, bf16[256,256]{1,0:T(8,128)(2,1)S(1)} %get-tuple-element.131.refs_3_.refs_1_, ...), custom_call_target="tpu_custom_call" | custom-call | tf_op jit(solution)/shard_map/pallas_call | solution.py:975
  59.9 1.3 %collective-permute-start.26 = (bf16[192,256]{1,0:T(8,128)(2,1)S(1)}, bf16[192,256]{1,0:T(8,128)(2,1)S(1)}, u32[]{:S(2)}, u32[]{:S(2)}) collective-permute-start(bf16[192,256]{1,0:T(8,128)(2,1)S(1)} %get-tuple-element.178), channel_id=1, source_target_pairs={{0,8},{4,12},{8,0},{12,4},{16,24},{20,28},{24,16},{28,20},{1,9},{5... | collective-permute-start | bytes 294920 | tf_op jit(solution)/shard_map/ppermute | solution.py:735
  61.2 0.7 collective-permute-start.27
  62.9 1.8 %collective-permute-start.30 = (bf16[192,256]{1,0:T(8,128)(2,1)S(1)}, bf16[192,256]{1,0:T(8,128)(2,1)S(1)}, u32[]{:S(2)}, u32[]{:S(2)}) collective-permute-start(bf16[192,256]{1,0:T(8,128)(2,1)S(1)} %get-tuple-element.189), channel_id=1, source_target_pairs={{0,2},{1,3},{2,0},{3,1},{4,6},{5,7},{6,4},{7,5},{8,10},{9,11},{10,... | collective-permute-start | bytes 294920 | tf_op jit(solution)/shard_map/ppermute | solution.py:727
  65.3 1.8 %collective-permute-done.28.refs_3_ = bf16[192,256]{1,0:T(8,128)(2,1)S(1)} collective-permute-done((bf16[192,256]{1,0:T(8,128)(2,1)S(1)}, bf16[192,256]{1,0:T(8,128)(2,1)S(1)}, u32[]{:S(2)}, u32[]{:S(2)}) %collective-permute-start.28) | collective-permute-done | bytes 98336 | tf_op jit(solution)/shard_map/ppermute | solution.py:735
  67.4 1.5 %collective-permute-start.36 = (bf16[96,256]{1,0:T(8,128)(2,1)S(1)}, bf16[96,256]{1,0:T(8,128)(2,1)S(1)}, u32[]{:S(2)}, u32[]{:S(2)}) collective-permute-start(bf16[96,256]{1,0:T(8,128)(2,1)S(1)} %get-tuple-element.182.refs_0_.refs_2_), channel_id=1, source_target_pairs={{0,4},{4,0},{8,12},{12,8},{16,20},{20,16},{24,28},{28,24},{1,5},{5... | collective-permute-start | bytes 147464 | tf_op jit(solution)/shard_map/ppermute | solution.py:735
  69.0 1.1 %collective-permute-start.32 = (bf16[192,256]{1,0:T(8,128)(2,1)S(1)}, bf16[192,256]{1,0:T(8,128)(2,1)S(1)}, u32[]{:S(2)}, u32[]{:S(2)}) collective-permute-start(bf16[192,256]{1,0:T(8,128)(2,1)S(1)} %get-tuple-element.191), channel_id=1, source_target_pairs={{0,1},{1,2},{2,3},{3,0},{4,5},{5,6},{6,7},{7,4},{8,9},{9,10},{10,1... | collective-permute-start | bytes 294920 | tf_op jit(solution)/shard_map/ppermute | solution.py:727
  70.9 1.0 %collective-permute-start.38 = (bf16[144,256]{1,0:T(8,128)(2,1)S(1)}, bf16[144,256]{1,0:T(8,128)(2,1)S(1)}, u32[]{:S(2)}, u32[]{:S(2)}) collective-permute-start(bf16[144,256]{1,0:T(8,128)(2,1)S(1)} %get-tuple-element.195), channel_id=1, source_target_pairs={{0,1},{1,2},{2,3},{3,0},{4,5},{5,6},{6,7},{7,4},{8,9},{9,10},{10,1... | collective-permute-start | bytes 221192 | tf_op jit(solution)/shard_map/ppermute | solution.py:727
  72.0 1.5 %collective-permute-start.39 = (bf16[144,256]{1,0:T(8,128)(2,1)S(1)}, bf16[144,256]{1,0:T(8,128)(2,1)S(1)}, u32[]{:S(2)}, u32[]{:S(2)}) collective-permute-start(bf16[144,256]{1,0:T(8,128)(2,1)S(1)} %get-tuple-element.196), channel_id=1, source_target_pairs={{0,2},{1,3},{2,0},{3,1},{4,6},{5,7},{6,4},{7,5},{8,10},{9,11},{10,... | collective-permute-start | bytes 221192 | tf_op jit(solution)/shard_map/ppermute | solution.py:727
  74.1 1.3 %collective-permute-start.35 = (bf16[192,256]{1,0:T(8,128)(2,1)S(1)}, bf16[192,256]{1,0:T(8,128)(2,1)S(1)}, u32[]{:S(2)}, u32[]{:S(2)}) collective-permute-start(bf16[192,256]{1,0:T(8,128)(2,1)S(1)} %shard_map.375.refs_0_), channel_id=1, source_target_pairs={{0,24},{4,28},{8,16},{12,20},{16,8},{20,12},{24,0},{28,4},{1,25},{... | collective-permute-start | bytes 294920 | tf_op jit(solution)/shard_map/ppermute | solution.py:735
  75.3 0.9 collective-permute-start.34
  76.2 2.2 %collective-permute-start.33 = (bf16[192,256]{1,0:T(8,128)(2,1)S(1)}, bf16[192,256]{1,0:T(8,128)(2,1)S(1)}, u32[]{:S(2)}, u32[]{:S(2)}) collective-permute-start(bf16[192,256]{1,0:T(8,128)(2,1)S(1)} %shard_map.375.refs_0_), channel_id=1, source_target_pairs={{0,8},{4,12},{8,0},{12,4},{16,24},{20,28},{24,16},{28,20},{1,9},{5... | collective-permute-start | bytes 294920 | tf_op jit(solution)/shard_map/ppermute | solution.py:735
  78.4 1.3 %collective-permute-done.39.refs_2_ = bf16[144,256]{1,0:T(8,128)(2,1)S(1)} collective-permute-done((bf16[144,256]{1,0:T(8,128)(2,1)S(1)}, bf16[144,256]{1,0:T(8,128)(2,1)S(1)}, u32[]{:S(2)}, u32[]{:S(2)}) %collective-permute-start.39) | collective-permute-done | bytes 73760 | tf_op jit(solution)/shard_map/ppermute | solution.py:727
  79.7 1.4 %collective-permute-done.40.refs_3_ = bf16[144,256]{1,0:T(8,128)(2,1)S(1)} collective-permute-done((bf16[144,256]{1,0:T(8,128)(2,1)S(1)}, bf16[144,256]{1,0:T(8,128)(2,1)S(1)}, u32[]{:S(2)}, u32[]{:S(2)}) %collective-permute-start.40) | collective-permute-done | bytes 73760 | tf_op jit(solution)/shard_map/ppermute | solution.py:727
  81.2 1.5 %collective-permute-start.44 = (bf16[144,256]{1,0:T(8,128)(2,1)S(1)}, bf16[144,256]{1,0:T(8,128)(2,1)S(1)}, u32[]{:S(2)}, u32[]{:S(2)}) collective-permute-start(bf16[144,256]{1,0:T(8,128)(2,1)S(1)} %shard_map.377.refs_4_.refs_0_), channel_id=1, source_target_pairs={{0,24},{4,28},{8,16},{12,20},{16,8},{20,12},{24,0},{28,4},{1,25},{... | collective-permute-start | bytes 221192 | tf_op jit(solution)/shard_map/ppermute | solution.py:735
  83.9 1.4 %collective-permute-start.41 = (bf16[384,256]{1,0:T(8,128)(2,1)S(1)}, bf16[384,256]{1,0:T(8,128)(2,1)S(1)}, u32[]{:S(2)}, u32[]{:S(2)}) collective-permute-start(bf16[384,256]{1,0:T(8,128)(2,1)S(1)} %shard_map.378._.mine), channel_id=1, source_target_pairs={{0,4},{4,0},{8,12},{12,8},{16,20},{20,16},{24,28},{28,24},{1,5},{5... | collective-permute-start | bytes 589832 | tf_op jit(solution)/shard_map/ppermute | solution.py:735
  85.3 1.2 %shard_map.379 = (f32[2,1,2,192,256]{4,3,2,1,0:T(8,128)}, f32[8,128]{1,0:T(8,128)S(1)}) custom-call(f32[768,256]{1,0:T(8,128)S(1)} %get-tuple-element.143.refs_2_.middle, f32[768,256]{1,0:T(8,128)S(1)} %get-tuple-element.184.grad_normed, f32[768,256]{1,0:T(8,128)S(1)} %get-tuple-element.120.refs_0_.normal_ref, f32[768,128]{1,0:T(8,128)S(1)} %get-tuple-element.185.rstd_ref, ...), custom_call_target="tpu_custom_call" | custom-call | tf_op jit(solution)/shard_map/pallas_call | solution.py:1043
  87.4 1.5 %collective-permute-start.45 = (bf16[144,256]{1,0:T(8,128)(2,1)S(1)}, bf16[144,256]{1,0:T(8,128)(2,1)S(1)}, u32[]{:S(2)}, u32[]{:S(2)}) collective-permute-start(bf16[144,256]{1,0:T(8,128)(2,1)S(1)} %shard_map.380.mine_b), channel_id=1, source_target_pairs={{0,4},{4,0},{8,12},{12,8},{16,20},{20,16},{24,28},{28,24},{1,5},{5... | collective-permute-start | bytes 221192 | tf_op jit(solution)/shard_map/ppermute | solution.py:735
  88.9 0.9 %collective-permute-done.45.refs_0_ = bf16[144,256]{1,0:T(8,128)(2,1)S(1)} collective-permute-done((bf16[144,256]{1,0:T(8,128)(2,1)S(1)}, bf16[144,256]{1,0:T(8,128)(2,1)S(1)}, u32[]{:S(2)}, u32[]{:S(2)}) %collective-permute-start.45) | collective-permute-done | bytes 73760 | tf_op jit(solution)/shard_map/ppermute | solution.py:735
  89.8 1.0 %shard_map.382 = (f32[64,256]{1,0:T(8,128)}, f32[64,512]{1,0:T(8,128)}, f32[64,256]{1,0:T(8,128)}, f32[64,1024]{1,0:T(8,128)}, f32[256,256]{1,0:T(8,128)}, /*ind...) custom-call(bf16[384,256]{1,0:T(8,128)(2,1)S(1)} %shard_map.378._.mi, ...), custom_call_target="tpu_custom_call" | custom-call | tf_op jit(solution)/shard_map/pallas_call | solution.py:1055
  (99 shorter events, 13.0 us)
Async XLA Ops:
  2.5 14.5 %collective-permute-start.2 = (bf16[240,256]{1,0:T(8,128)(2,1)}, bf16[240,256]{1,0:T(8,128)(2,1)S(1)}, u32[]{:S(2)}, u32[]{:S(2)}) collective-permute-start(bf16[240,256]{1,0:T(8,128)(2,1)} %shard_map.356.packed), channel_id=1, source_target_pairs={{0,3},{1,0},{2,1},{3,2},{4,7},{5,4},{6,5},{7,6},{8,11},{9,8},{10,9... | collective-permute-start | bytes 368648 | tf_op jit(solution)/shard_map/ppermute | solution.py:727
  2.5 14.5 %collective-permute-start.1 = (bf16[240,256]{1,0:T(8,128)(2,1)}, bf16[240,256]{1,0:T(8,128)(2,1)S(1)}, u32[]{:S(2)}, u32[]{:S(2)}) collective-permute-start(bf16[240,256]{1,0:T(8,128)(2,1)} %shard_map.356.packed), channel_id=1, source_target_pairs={{0,2},{1,3},{2,0},{3,1},{4,6},{5,7},{6,4},{7,5},{8,10},{9,11},{10,... | collective-permute-start | bytes 368648 | tf_op jit(solution)/shard_map/ppermute | solution.py:727
  5.0 12.0 %collective-permute-start = (bf16[240,256]{1,0:T(8,128)(2,1)}, bf16[240,256]{1,0:T(8,128)(2,1)S(1)}, u32[]{:S(2)}, u32[]{:S(2)}) collective-permute-start(bf16[240,256]{1,0:T(8,128)(2,1)} %shard_map.356.packed), channel_id=1, source_target_pairs={{0,1},{1,2},{2,3},{3,0},{4,5},{5,6},{6,7},{7,4},{8,9},{9,10},{10,1... | collective-permute-start | bytes 368648 | tf_op jit(solution)/shard_map/ppermute | solution.py:727
  16.0 7.7 %collective-permute-start.14 = (bf16[288,256]{1,0:T(8,128)(2,1)S(1)}, bf16[288,256]{1,0:T(8,128)(2,1)S(1)}, u32[]{:S(2)}, u32[]{:S(2)}) collective-permute-start(bf16[288,256]{1,0:T(8,128)(2,1)S(1)} %get-tuple-element.136), channel_id=1, source_target_pairs={{0,2},{1,3},{2,0},{3,1},{4,6},{5,7},{6,4},{7,5},{8,10},{9,11},{10,... | collective-permute-start | bytes 442376 | tf_op jit(solution)/shard_map/ppermute | solution.py:731
  17.0 2.6 %collective-permute-start.3 = (bf16[240,256]{1,0:T(8,128)(2,1)S(1)}, bf16[240,256]{1,0:T(8,128)(2,1)S(1)}, u32[]{:S(2)}, u32[]{:S(2)}) collective-permute-start(bf16[240,256]{1,0:T(8,128)(2,1)S(1)} %get-tuple-element.125.refs_6_), channel_id=1, source_target_pairs={{0,4},{4,0},{8,12},{12,8},{16,20},{20,16},{24,28},{28,24},{1,5},{5... | collective-permute-start | bytes 368648 | tf_op jit(solution)/shard_map/ppermute | solution.py:735
  18.6 1.3 %collective-permute-start.4 = (bf16[240,256]{1,0:T(8,128)(2,1)S(1)}, bf16[240,256]{1,0:T(8,128)(2,1)S(1)}, u32[]{:S(2)}, u32[]{:S(2)}) collective-permute-start(bf16[240,256]{1,0:T(8,128)(2,1)S(1)} %get-tuple-element.126.refs_7_), channel_id=1, source_target_pairs={{0,4},{4,0},{8,12},{12,8},{16,20},{20,16},{24,28},{28,24},{1,5},{5... | collective-permute-start | bytes 368648 | tf_op jit(solution)/shard_map/ppermute | solution.py:735
  18.7 1.4 %collective-permute-start.5 = (bf16[240,256]{1,0:T(8,128)(2,1)S(1)}, bf16[240,256]{1,0:T(8,128)(2,1)S(1)}, u32[]{:S(2)}, u32[]{:S(2)}) collective-permute-start(bf16[240,256]{1,0:T(8,128)(2,1)S(1)} %get-tuple-element.127.refs_8_), channel_id=1, source_target_pairs={{0,4},{4,0},{8,12},{12,8},{16,20},{20,16},{24,28},{28,24},{1,5},{5... | collective-permute-start | bytes 368648 | tf_op jit(solution)/shard_map/ppermute | solution.py:735
  19.1 15.3 %collective-permute-start.13 = (bf16[288,256]{1,0:T(8,128)(2,1)S(1)}, bf16[288,256]{1,0:T(8,128)(2,1)S(1)}, u32[]{:S(2)}, u32[]{:S(2)}) collective-permute-start(bf16[288,256]{1,0:T(8,128)(2,1)S(1)} %get-tuple-element.136), channel_id=1, source_target_pairs={{0,1},{1,0},{2,3},{3,2},{4,5},{5,4},{6,7},{7,6},{8,9},{9,8},{10,11... | collective-permute-start | bytes 442376 | tf_op jit(solution)/shard_map/ppermute | solution.py:731
  20.9 5.0 %collective-permute-start.11 = (bf16[192,256]{1,0:T(8,128)(2,1)S(1)}, bf16[192,256]{1,0:T(8,128)(2,1)S(1)}, u32[]{:S(2)}, u32[]{:S(2)}) collective-permute-start(bf16[192,256]{1,0:T(8,128)(2,1)S(1)} %get-tuple-element.133.refs_5_.refs_15_), channel_id=1, source_target_pairs={{0,24},{4,28},{8,16},{12,20},{16,8},{20,12},{24,0},{28,4},{1,25},{... | collective-permute-start | bytes 294920 | tf_op jit(solution)/shard_map/ppermute | solution.py:735
  23.1 5.4 %collective-permute-start.9 = (bf16[192,256]{1,0:T(8,128)(2,1)S(1)}, bf16[192,256]{1,0:T(8,128)(2,1)S(1)}, u32[]{:S(2)}, u32[]{:S(2)}) collective-permute-start(bf16[192,256]{1,0:T(8,128)(2,1)S(1)} %get-tuple-element.133.refs_5_.refs_15_), channel_id=1, source_target_pairs={{0,16},{4,20},{8,24},{12,28},{16,0},{20,4},{24,8},{28,12},{1,17},{... | collective-permute-start | bytes 294920 | tf_op jit(solution)/shard_map/ppermute | solution.py:735
  23.3 5.8 %collective-permute-start.7 = (bf16[192,256]{1,0:T(8,128)(2,1)S(1)}, bf16[192,256]{1,0:T(8,128)(2,1)S(1)}, u32[]{:S(2)}, u32[]{:S(2)}) collective-permute-start(bf16[192,256]{1,0:T(8,128)(2,1)S(1)} %get-tuple-element.133.refs_5_.refs_15_), channel_id=1, source_target_pairs={{0,8},{4,12},{8,0},{12,4},{16,24},{20,28},{24,16},{28,20},{1,9},{5... | collective-permute-start | bytes 294920 | tf_op jit(solution)/shard_map/ppermute | solution.py:735
  23.7 5.5 %collective-permute-start.6 = (bf16[192,256]{1,0:T(8,128)(2,1)S(1)}, bf16[192,256]{1,0:T(8,128)(2,1)S(1)}, u32[]{:S(2)}, u32[]{:S(2)}) collective-permute-start(bf16[192,256]{1,0:T(8,128)(2,1)S(1)} %get-tuple-element.133.refs_5_.refs_15_), channel_id=1, source_target_pairs={{0,4},{4,0},{8,12},{12,8},{16,20},{20,16},{24,28},{28,24},{1,5},{5... | collective-permute-start | bytes 294920 | tf_op jit(solution)/shard_map/ppermute | solution.py:735
  24.9 14.5 %copy-start.1 = (bf16[2,1,2,192,256]{4,3,2,1,0:T(8,128)(2,1)S(1)}, bf16[2,1,2,192,256]{4,3,2,1,0:T(8,128)(2,1)}, u32[]{:S(2)}) copy-start(bf16[2,1,2,192,256]{4,3,2,1,0:T(8,128)(2,1)} %refs_0_.3) | copy-start | bytes 1179652
  24.9 14.5 %copy-start.2 = (f32[2,1,2,192,256]{4,3,2,1,0:T(8,128)S(1)}, f32[2,1,2,192,256]{4,3,2,1,0:T(8,128)}, u32[]{:S(2)}) copy-start(f32[2,1,2,192,256]{4,3,2,1,0:T(8,128)} %refs_1_.3) | copy-start | bytes 2359300
  25.9 8.6 %collective-permute-start.15 = (bf16[288,256]{1,0:T(8,128)(2,1)S(1)}, bf16[288,256]{1,0:T(8,128)(2,1)S(1)}, u32[]{:S(2)}, u32[]{:S(2)}) collective-permute-start(bf16[288,256]{1,0:T(8,128)(2,1)S(1)} %shard_map.362), channel_id=1, source_target_pairs={{0,1},{1,0},{2,3},{3,2},{4,5},{5,4},{6,7},{7,6},{8,9},{9,8},{10,11... | collective-permute-start | bytes 442376 | tf_op jit(solution)/shard_map/ppermute | solution.py:731
  28.5 1.6 %collective-permute-start.12 = (bf16[192,256]{1,0:T(8,128)(2,1)S(1)}, bf16[192,256]{1,0:T(8,128)(2,1)S(1)}, u32[]{:S(2)}, u32[]{:S(2)}) collective-permute-start(bf16[192,256]{1,0:T(8,128)(2,1)S(1)} %collective-permute-done.11.refs_11_.refs_21_), channel_id=1, source_target_pairs={{0,4},{4,0},{8,12},{12,8},{16,20},{20,16},{24,28},{28,24},{1,5},{5... | collective-permute-start | bytes 294920 | tf_op jit(solution)/shard_map/ppermute | solution.py:735
  29.1 1.3 %collective-permute-start.10 = (bf16[192,256]{1,0:T(8,128)(2,1)S(1)}, bf16[192,256]{1,0:T(8,128)(2,1)S(1)}, u32[]{:S(2)}, u32[]{:S(2)}) collective-permute-start(bf16[192,256]{1,0:T(8,128)(2,1)S(1)} %collective-permute-done.9.refs_9_.refs_19_), channel_id=1, source_target_pairs={{0,4},{4,0},{8,12},{12,8},{16,20},{20,16},{24,28},{28,24},{1,5},{5... | collective-permute-start | bytes 294920 | tf_op jit(solution)/shard_map/ppermute | solution.py:735
  29.2 1.4 %collective-permute-start.8 = (bf16[192,256]{1,0:T(8,128)(2,1)S(1)}, bf16[192,256]{1,0:T(8,128)(2,1)S(1)}, u32[]{:S(2)}, u32[]{:S(2)}) collective-permute-start(bf16[192,256]{1,0:T(8,128)(2,1)S(1)} %collective-permute-done.7.refs_7_.refs_17_), channel_id=1, source_target_pairs={{0,4},{4,0},{8,12},{12,8},{16,20},{20,16},{24,28},{28,24},{1,5},{5... | collective-permute-start | bytes 294920 | tf_op jit(solution)/shard_map/ppermute | solution.py:735
  30.1 9.2 %collective-permute-start.19 = (bf16[4,192,128]{2,1,0:T(8,128)(2,1)S(1)}, bf16[4,192,128]{2,1,0:T(8,128)(2,1)S(1)}, u32[]{:S(2)}, u32[]{:S(2)}) collective-permute-start(bf16[4,192,128]{2,1,0:T(8,128)(2,1)S(1)} %get-tuple-element.141), channel_id=1, source_target_pairs={{0,4},{4,0},{8,12},{12,8},{16,20},{20,16},{24,28},{28,24},{1,5},{5... | collective-permute-start | bytes 589832 | tf_op jit(solution)/shard_map/ppermute | solution.py:735
  34.5 4.8 %collective-permute-start.16 = (bf16[288,256]{1,0:T(8,128)(2,1)S(1)}, bf16[288,256]{1,0:T(8,128)(2,1)S(1)}, u32[]{:S(2)}, u32[]{:S(2)}) collective-permute-start(bf16[288,256]{1,0:T(8,128)(2,1)S(1)} %get-tuple-element.138.refs_9_), channel_id=1, source_target_pairs={{0,4},{4,0},{8,12},{12,8},{16,20},{20,16},{24,28},{28,24},{1,5},{5... | collective-permute-start | bytes 442376 | tf_op jit(solution)/shard_map/ppermute | solution.py:735
  34.9 4.4 %collective-permute-start.17 = (bf16[288,256]{1,0:T(8,128)(2,1)S(1)}, bf16[288,256]{1,0:T(8,128)(2,1)S(1)}, u32[]{:S(2)}, u32[]{:S(2)}) collective-permute-start(bf16[288,256]{1,0:T(8,128)(2,1)S(1)} %get-tuple-element.139.refs_10_), channel_id=1, source_target_pairs={{0,4},{4,0},{8,12},{12,8},{16,20},{20,16},{24,28},{28,24},{1,5},{5... | collective-permute-start | bytes 442376 | tf_op jit(solution)/shard_map/ppermute | solution.py:735
  35.1 4.2 %collective-permute-start.18 = (bf16[288,256]{1,0:T(8,128)(2,1)S(1)}, bf16[288,256]{1,0:T(8,128)(2,1)S(1)}, u32[]{:S(2)}, u32[]{:S(2)}) collective-permute-start(bf16[288,256]{1,0:T(8,128)(2,1)S(1)} %get-tuple-element.140.refs_11_), channel_id=1, source_target_pairs={{0,4},{4,0},{8,12},{12,8},{16,20},{20,16},{24,28},{28,24},{1,5},{5... | collective-permute-start | bytes 442376 | tf_op jit(solution)/shard_map/ppermute | solution.py:735
  43.8 4.4 %collective-permute-start.20 = (bf16[4,256,256]{2,1,0:T(8,128)(2,1)S(1)}, bf16[4,256,256]{2,1,0:T(8,128)(2,1)S(1)}, u32[]{:S(2)}, u32[]{:S(2)}) collective-permute-start(bf16[4,256,256]{2,1,0:T(8,128)(2,1)S(1)} %get-tuple-element.156), channel_id=1, source_target_pairs={{0,4},{4,0},{8,12},{12,8},{16,20},{20,16},{24,28},{28,24},{1,5},{5... | collective-permute-start | bytes 1572872 | tf_op jit(solution)/shard_map/ppermute | solution.py:735
  48.3 10.8 %collective-permute-start.23 = (bf16[4,64,256]{2,1,0:T(8,128)(2,1)S(1)}, bf16[4,64,256]{2,1,0:T(8,128)(2,1)S(1)}, u32[]{:S(2)}, u32[]{:S(2)}) collective-permute-start(bf16[4,64,256]{2,1,0:T(8,128)(2,1)S(1)} %get-tuple-element.173), channel_id=1, source_target_pairs={{0,8},{4,12},{8,0},{12,4},{16,24},{20,28},{24,16},{28,20},{1,9},{5... | collective-permute-start | bytes 393224 | tf_op jit(solution)/shard_map/ppermute | solution.py:735
  49.6 10.1 %collective-permute-start.24 = (bf16[4,64,256]{2,1,0:T(8,128)(2,1)S(1)}, bf16[4,64,256]{2,1,0:T(8,128)(2,1)S(1)}, u32[]{:S(2)}, u32[]{:S(2)}) collective-permute-start(bf16[4,64,256]{2,1,0:T(8,128)(2,1)S(1)} %get-tuple-element.174), channel_id=1, source_target_pairs={{0,16},{4,20},{8,24},{12,28},{16,0},{20,4},{24,8},{28,12},{1,17},{... | collective-permute-start | bytes 393224 | tf_op jit(solution)/shard_map/ppermute | solution.py:735
  50.4 9.4 %collective-permute-start.25 = (bf16[4,64,256]{2,1,0:T(8,128)(2,1)S(1)}, bf16[4,64,256]{2,1,0:T(8,128)(2,1)S(1)}, u32[]{:S(2)}, u32[]{:S(2)}) collective-permute-start(bf16[4,64,256]{2,1,0:T(8,128)(2,1)S(1)} %get-tuple-element.175), channel_id=1, source_target_pairs={{0,24},{4,28},{8,16},{12,20},{16,8},{20,12},{24,0},{28,4},{1,25},{... | collective-permute-start | bytes 393224 | tf_op jit(solution)/shard_map/ppermute | solution.py:735
  51.1 8.7 %collective-permute-start.21 = (bf16[4,96,256]{2,1,0:T(8,128)(2,1)S(1)}, bf16[4,96,256]{2,1,0:T(8,128)(2,1)S(1)}, u32[]{:S(2)}, u32[]{:S(2)}) collective-permute-start(bf16[4,96,256]{2,1,0:T(8,128)(2,1)S(1)} %get-tuple-element.171), channel_id=1, source_target_pairs={{0,4},{4,0},{8,12},{12,8},{16,20},{20,16},{24,28},{28,24},{1,5},{5... | collective-permute-start | bytes 589832 | tf_op jit(solution)/shard_map/ppermute | solution.py:735
  56.5 3.3 %collective-permute-start.22 = (bf16[4,96,256]{2,1,0:T(8,128)(2,1)S(1)}, bf16[4,96,256]{2,1,0:T(8,128)(2,1)S(1)}, u32[]{:S(2)}, u32[]{:S(2)}) collective-permute-start(bf16[4,96,256]{2,1,0:T(8,128)(2,1)S(1)} %get-tuple-element.172), channel_id=1, source_target_pairs={{0,4},{4,0},{8,12},{12,8},{16,20},{20,16},{24,28},{28,24},{1,5},{5... | collective-permute-start | bytes 589832 | tf_op jit(solution)/shard_map/ppermute | solution.py:735
  59.2 3.5 %collective-permute-start.29 = (bf16[4,128,256]{2,1,0:T(8,128)(2,1)S(1)}, bf16[4,128,256]{2,1,0:T(8,128)(2,1)S(1)}, u32[]{:S(2)}, u32[]{:S(2)}) collective-permute-start(bf16[4,128,256]{2,1,0:T(8,128)(2,1)S(1)} %get-tuple-element.187), channel_id=1, source_target_pairs={{0,4},{4,0},{8,12},{12,8},{16,20},{20,16},{24,28},{28,24},{1,5},{5... | collective-permute-start | bytes 786440 | tf_op jit(solution)/shard_map/ppermute | solution.py:735
  59.9 5.3 %collective-permute-start.26 = (bf16[192,256]{1,0:T(8,128)(2,1)S(1)}, bf16[192,256]{1,0:T(8,128)(2,1)S(1)}, u32[]{:S(2)}, u32[]{:S(2)}) collective-permute-start(bf16[192,256]{1,0:T(8,128)(2,1)S(1)} %get-tuple-element.178), channel_id=1, source_target_pairs={{0,8},{4,12},{8,0},{12,4},{16,24},{20,28},{24,16},{28,20},{1,9},{5... | collective-permute-start | bytes 294920 | tf_op jit(solution)/shard_map/ppermute | solution.py:735
  61.2 4.1 %collective-permute-start.27 = (bf16[192,256]{1,0:T(8,128)(2,1)S(1)}, bf16[192,256]{1,0:T(8,128)(2,1)S(1)}, u32[]{:S(2)}, u32[]{:S(2)}) collective-permute-start(bf16[192,256]{1,0:T(8,128)(2,1)S(1)} %get-tuple-element.179), channel_id=1, source_target_pairs={{0,16},{4,20},{8,24},{12,28},{16,0},{20,4},{24,8},{28,12},{1,17},{... | collective-permute-start | bytes 294920 | tf_op jit(solution)/shard_map/ppermute | solution.py:735
  61.9 5.1 %collective-permute-start.28 = (bf16[192,256]{1,0:T(8,128)(2,1)S(1)}, bf16[192,256]{1,0:T(8,128)(2,1)S(1)}, u32[]{:S(2)}, u32[]{:S(2)}) collective-permute-start(bf16[192,256]{1,0:T(8,128)(2,1)S(1)} %get-tuple-element.180), channel_id=1, source_target_pairs={{0,24},{4,28},{8,16},{12,20},{16,8},{20,12},{24,0},{28,4},{1,25},{... | collective-permute-start | bytes 294920 | tf_op jit(solution)/shard_map/ppermute | solution.py:735
  62.9 10.5 %collective-permute-start.30 = (bf16[192,256]{1,0:T(8,128)(2,1)S(1)}, bf16[192,256]{1,0:T(8,128)(2,1)S(1)}, u32[]{:S(2)}, u32[]{:S(2)}) collective-permute-start(bf16[192,256]{1,0:T(8,128)(2,1)S(1)} %get-tuple-element.189), channel_id=1, source_target_pairs={{0,2},{1,3},{2,0},{3,1},{4,6},{5,7},{6,4},{7,5},{8,10},{9,11},{10,... | collective-permute-start | bytes 294920 | tf_op jit(solution)/shard_map/ppermute | solution.py:727
  64.7 9.2 %collective-permute-start.31 = (bf16[192,256]{1,0:T(8,128)(2,1)S(1)}, bf16[192,256]{1,0:T(8,128)(2,1)S(1)}, u32[]{:S(2)}, u32[]{:S(2)}) collective-permute-start(bf16[192,256]{1,0:T(8,128)(2,1)S(1)} %get-tuple-element.190), channel_id=1, source_target_pairs={{0,3},{1,0},{2,1},{3,2},{4,7},{5,4},{6,5},{7,6},{8,11},{9,8},{10,9... | collective-permute-start | bytes 294920 | tf_op jit(solution)/shard_map/ppermute | solution.py:727
  67.4 3.2 %collective-permute-start.36 = (bf16[96,256]{1,0:T(8,128)(2,1)S(1)}, bf16[96,256]{1,0:T(8,128)(2,1)S(1)}, u32[]{:S(2)}, u32[]{:S(2)}) collective-permute-start(bf16[96,256]{1,0:T(8,128)(2,1)S(1)} %get-tuple-element.182.refs_0_.refs_2_), channel_id=1, source_target_pairs={{0,4},{4,0},{8,12},{12,8},{16,20},{20,16},{24,28},{28,24},{1,5},{5... | collective-permute-start | bytes 147464 | tf_op jit(solution)/shard_map/ppermute | solution.py:735
  68.9 1.7 %collective-permute-start.37 = (bf16[96,256]{1,0:T(8,128)(2,1)S(1)}, bf16[96,256]{1,0:T(8,128)(2,1)S(1)}, u32[]{:S(2)}, u32[]{:S(2)}) collective-permute-start(bf16[96,256]{1,0:T(8,128)(2,1)S(1)} %get-tuple-element.183.refs_1_.refs_3_), channel_id=1, source_target_pairs={{0,4},{4,0},{8,12},{12,8},{16,20},{20,16},{24,28},{28,24},{1,5},{5... | collective-permute-start | bytes 147464 | tf_op jit(solution)/shard_map/ppermute | solution.py:735
  69.0 5.0 %collective-permute-start.32 = (bf16[192,256]{1,0:T(8,128)(2,1)S(1)}, bf16[192,256]{1,0:T(8,128)(2,1)S(1)}, u32[]{:S(2)}, u32[]{:S(2)}) collective-permute-start(bf16[192,256]{1,0:T(8,128)(2,1)S(1)} %get-tuple-element.191), channel_id=1, source_target_pairs={{0,1},{1,2},{2,3},{3,0},{4,5},{5,6},{6,7},{7,4},{8,9},{9,10},{10,1... | collective-permute-start | bytes 294920 | tf_op jit(solution)/shard_map/ppermute | solution.py:727
  70.9 5.3 %collective-permute-start.38 = (bf16[144,256]{1,0:T(8,128)(2,1)S(1)}, bf16[144,256]{1,0:T(8,128)(2,1)S(1)}, u32[]{:S(2)}, u32[]{:S(2)}) collective-permute-start(bf16[144,256]{1,0:T(8,128)(2,1)S(1)} %get-tuple-element.195), channel_id=1, source_target_pairs={{0,1},{1,2},{2,3},{3,0},{4,5},{5,6},{6,7},{7,4},{8,9},{9,10},{10,1... | collective-permute-start | bytes 221192 | tf_op jit(solution)/shard_map/ppermute | solution.py:727
  72.0 7.7 %collective-permute-start.39 = (bf16[144,256]{1,0:T(8,128)(2,1)S(1)}, bf16[144,256]{1,0:T(8,128)(2,1)S(1)}, u32[]{:S(2)}, u32[]{:S(2)}) collective-permute-start(bf16[144,256]{1,0:T(8,128)(2,1)S(1)} %get-tuple-element.196), channel_id=1, source_target_pairs={{0,2},{1,3},{2,0},{3,1},{4,6},{5,7},{6,4},{7,5},{8,10},{9,11},{10,... | collective-permute-start | bytes 221192 | tf_op jit(solution)/shard_map/ppermute | solution.py:727
  73.5 7.6 %collective-permute-start.40 = (bf16[144,256]{1,0:T(8,128)(2,1)S(1)}, bf16[144,256]{1,0:T(8,128)(2,1)S(1)}, u32[]{:S(2)}, u32[]{:S(2)}) collective-permute-start(bf16[144,256]{1,0:T(8,128)(2,1)S(1)} %get-tuple-element.197), channel_id=1, source_target_pairs={{0,3},{1,0},{2,1},{3,2},{4,7},{5,4},{6,5},{7,6},{8,11},{9,8},{10,9... | collective-permute-start | bytes 221192 | tf_op jit(solution)/shard_map/ppermute | solution.py:727
  74.1 9.3 %collective-permute-start.35 = (bf16[192,256]{1,0:T(8,128)(2,1)S(1)}, bf16[192,256]{1,0:T(8,128)(2,1)S(1)}, u32[]{:S(2)}, u32[]{:S(2)}) collective-permute-start(bf16[192,256]{1,0:T(8,128)(2,1)S(1)} %shard_map.375.refs_0_), channel_id=1, source_target_pairs={{0,24},{4,28},{8,16},{12,20},{16,8},{20,12},{24,0},{28,4},{1,25},{... | collective-permute-start | bytes 294920 | tf_op jit(solution)/shard_map/ppermute | solution.py:735
  75.3 8.5 %collective-permute-start.34 = (bf16[192,256]{1,0:T(8,128)(2,1)S(1)}, bf16[192,256]{1,0:T(8,128)(2,1)S(1)}, u32[]{:S(2)}, u32[]{:S(2)}) collective-permute-start(bf16[192,256]{1,0:T(8,128)(2,1)S(1)} %shard_map.375.refs_0_), channel_id=1, source_target_pairs={{0,16},{4,20},{8,24},{12,28},{16,0},{20,4},{24,8},{28,12},{1,17},{... | collective-permute-start | bytes 294920 | tf_op jit(solution)/shard_map/ppermute | solution.py:735
  76.2 7.7 %collective-permute-start.33 = (bf16[192,256]{1,0:T(8,128)(2,1)S(1)}, bf16[192,256]{1,0:T(8,128)(2,1)S(1)}, u32[]{:S(2)}, u32[]{:S(2)}) collective-permute-start(bf16[192,256]{1,0:T(8,128)(2,1)S(1)} %shard_map.375.refs_0_), channel_id=1, source_target_pairs={{0,8},{4,12},{8,0},{12,4},{16,24},{20,28},{24,16},{28,20},{1,9},{5... | collective-permute-start | bytes 294920 | tf_op jit(solution)/shard_map/ppermute | solution.py:735
  81.2 5.4 %collective-permute-start.44 = (bf16[144,256]{1,0:T(8,128)(2,1)S(1)}, bf16[144,256]{1,0:T(8,128)(2,1)S(1)}, u32[]{:S(2)}, u32[]{:S(2)}) collective-permute-start(bf16[144,256]{1,0:T(8,128)(2,1)S(1)} %shard_map.377.refs_4_.refs_0_), channel_id=1, source_target_pairs={{0,24},{4,28},{8,16},{12,20},{16,8},{20,12},{24,0},{28,4},{1,25},{... | collective-permute-start | bytes 221192 | tf_op jit(solution)/shard_map/ppermute | solution.py:735
  82.7 4.0 %collective-permute-start.43 = (bf16[144,256]{1,0:T(8,128)(2,1)S(1)}, bf16[144,256]{1,0:T(8,128)(2,1)S(1)}, u32[]{:S(2)}, u32[]{:S(2)}) collective-permute-start(bf16[144,256]{1,0:T(8,128)(2,1)S(1)} %shard_map.377.refs_4_.refs_0_), channel_id=1, source_target_pairs={{0,16},{4,20},{8,24},{12,28},{16,0},{20,4},{24,8},{28,12},{1,17},{... | collective-permute-start | bytes 221192 | tf_op jit(solution)/shard_map/ppermute | solution.py:735
  83.3 4.1 %collective-permute-start.42 = (bf16[144,256]{1,0:T(8,128)(2,1)S(1)}, bf16[144,256]{1,0:T(8,128)(2,1)S(1)}, u32[]{:S(2)}, u32[]{:S(2)}) collective-permute-start(bf16[144,256]{1,0:T(8,128)(2,1)S(1)} %shard_map.377.refs_4_.refs_0_), channel_id=1, source_target_pairs={{0,8},{4,12},{8,0},{12,4},{16,24},{20,28},{24,16},{28,20},{1,9},{5... | collective-permute-start | bytes 221192 | tf_op jit(solution)/shard_map/ppermute | solution.py:735
  83.9 5.9 %collective-permute-start.41 = (bf16[384,256]{1,0:T(8,128)(2,1)S(1)}, bf16[384,256]{1,0:T(8,128)(2,1)S(1)}, u32[]{:S(2)}, u32[]{:S(2)}) collective-permute-start(bf16[384,256]{1,0:T(8,128)(2,1)S(1)} %shard_map.378._.mine), channel_id=1, source_target_pairs={{0,4},{4,0},{8,12},{12,8},{16,20},{20,16},{24,28},{28,24},{1,5},{5... | collective-permute-start | bytes 589832 | tf_op jit(solution)/shard_map/ppermute | solution.py:735
  87.4 2.4 %collective-permute-start.45 = (bf16[144,256]{1,0:T(8,128)(2,1)S(1)}, bf16[144,256]{1,0:T(8,128)(2,1)S(1)}, u32[]{:S(2)}, u32[]{:S(2)}) collective-permute-start(bf16[144,256]{1,0:T(8,128)(2,1)S(1)} %shard_map.380.mine_b), channel_id=1, source_target_pairs={{0,4},{4,0},{8,12},{12,8},{16,20},{20,16},{24,28},{28,24},{1,5},{5... | collective-permute-start | bytes 221192 | tf_op jit(solution)/shard_map/ppermute | solution.py:735
  (12 other events, 51.1 us)

commit v8 on v7

--- a/solution.py
+++ b/solution.py
@@ -115,19 +115,17 @@
     return pl.ds(pl.multiple_of(place * rows, rows), rows)
 
 
-def begin_kernel(dims, sizes, tokens, reduce_w, query_w, keyval_w, hidden_w, return_w, output_w, packed, *outs):
+def begin_kernel(dims, sizes, tokens, hidden_w, return_w, output_w, packed, *refs):
+    outs = refs[2:]
     n_sp, batches, row_dev, cols, dim = dims
-    normal_ref, rstd_ref, mask_ref, bias_ref, own_r, own_q, own_kv, own_vec, second = outs
+    normal_ref, rstd_ref, mask_ref, bias_ref, own_half, begun_ref, second = outs
     tok = row_dev * cols
     half_cols = cols // 2
     rows_dev = row_dev // 2
-    half = dim // 2
     shard = hidden_w.shape[0]
     sp = lax.axis_index("sp")
-    own_r[...] = reduce_w[...]
-    own_q[...] = query_w[...]
-    own_kv[...] = keyval_w[...]
-    own_vec[...] = packed[half : half + VECS].astype(f32)
+    own_half[...] = packed[...]
+    begun_ref[...] = jnp.zeros_like(begun_ref)
 
     @pl.when(sp % 2 == 0)
     def _():
@@ -163,8 +161,7 @@
 
 def reduce_kernel(dims, *refs):
     n_fs, batches, row_dev, cols, dim = dims
-    ins, mine, other, outs = take(refs, 6, n_fs - 1, n_fs - 1)
-    normal_in, mask_ref, own_w, own_q, own_kv, own_vec = ins
+    (normal_in, mask_ref), mine, other, outs = take(refs, 2, n_fs, n_fs)
     normed_ref, cols_ref, send_ref, reduced_ref, key_ref, weight_ref, wq, wkv, vec_ref, patch_ref, wide = outs
     half = dim // 2
     shard = dim // n_fs
@@ -173,13 +170,9 @@
     half_cols = cols // 2
     key_dev = tok // 4
     fs = lax.axis_index("fs")
-    weight_ref[fs] = own_w[...]
-    here = shard_rows(fs, shard)
-    wq[here, :] = own_q[...]
-    wkv[here, :] = own_kv[...]
-    vec = own_vec[...]
-    for step in range(1, n_fs):
-        low, high = both_halves(mine[step - 1], other[step - 1])
+    vec = jnp.zeros((VECS, dim), f32)
+    for step in range(n_fs):
+        low, high = both_halves(mine[step], other[step])
         place = lax.rem(fs + n_fs - step, n_fs)
         weight_ref[place, :half] = low[:half]
         weight_ref[place, half:] = high[:half]
@@ -832,7 +825,7 @@
         scratch=[pltpu.VMEM((VECS, dim), f32)],
         limit=WHOLE_VMEM,
     )(*smalls, hidden_bias, reduce_weight, query_weight, keyval_weight)
-    mine_first = to_owners([first_half] * n_fs, n_fs)[1:]
+    arrived_first = to_owners([first_half] * n_fs, n_fs)[1:]
 
     begun = call(
         functools.partial(begin_kernel, (n_sp, batches, row_dev, cols, dim)),
@@ -841,28 +834,25 @@
             shape(batches * tok, 128, dtype=f32),
             shape(batches * tok, dim, dtype=f32),
             shape(batches, keys, dim),
-            shape(dim, dim),
-            shape(shard, dim),
-            shape(shard, 2 * dim),
-            shape(VECS, dim, dtype=f32),
+            shape(*first_half.shape),
+            shape(8, 128, dtype=f32),
             shape(dim + shard // 2, dim),
         ],
-        in_specs=[smem] + [vmem] * 8,
+        in_specs=[smem] + [vmem] * 7,
         limit=SMALL_VMEM if single else WHOLE_VMEM,
     )(
         image_sizes,
         tokens,
-        reduce_weight,
-        query_weight,
-        keyval_weight,
         hidden_weight,
         return_weight,
         output_weight,
         first_half,
-    )
-    normal_first, rstd_first, mask, bias, own_r, own_q, own_kv, own_vec, second_half = begun
-    mine_first = call(functools.partial(relay_kernel, n_fs - 1), [shape(*first_half.shape)] * (n_fs - 1))(
-        *mine_first, own_vec
+        reduce_weight,
+        keyval_weight,
+    )
+    normal_first, rstd_first, mask, bias, own_half, done, second_half = begun
+    mine_first = call(functools.partial(relay_kernel, n_fs), [shape(*first_half.shape)] * n_fs)(
+        own_half, *arrived_first, done
     )
     other_first = [flip(piece, n_sp, 1) for piece in mine_first]
     normed, patch_cols, patch_send, reduced, key_low, whole_reduce, wq, wkv, vec = call(
@@ -879,9 +869,9 @@
             shape(VECS, dim, dtype=f32),
         ],
         scratch=[pltpu.VMEM((batches * key_dev, 4 * dim), bf16), pltpu.VMEM((dim // 128, tok + 8, 128), f32)],
-    )(normal_first, mask, own_r, own_q, own_kv, own_vec, *mine_first, *other_first)
+    )(normal_first, mask, *mine_first, *other_first)
     across = swap(second_half, n_fs, 2)
-    passed = call(functools.partial(relay_kernel, 1), [shape(dim + shard // 2, dim)], micros=15)(across, own_vec)
+    passed = call(functools.partial(relay_kernel, 1), [shape(dim + shard // 2, dim)], micros=15)(across, done)
     mine_second = [swap(second_half, n_fs, 1), across, swap(passed[0], n_fs, 1)]
 
     if split:

time: 92.1 us -> 91.4 us (level)
  waiting for transfers between devices: 10.9 us -> 13.7 us
  starting transfers between devices: 40.1 us -> 37.6 us
    ppermute x34 -> x35, starting transfers between devices: 27.3 us -> 25 us  [flip(): return lax.ppermute(value, 'sp', [(i, i ^ bits) for i in range(n)])]
    ppermute x9, waiting for transfers between devices: 2.72 us -> 4.36 us  [rotate(): return lax.ppermute(value, 'fs', [(i, (i + step) % n) for i in range(n)])]
    ppermute x34 -> x35, waiting for transfers between devices: 8 us -> 9.3 us  [flip(): return lax.ppermute(value, 'sp', [(i, i ^ bits) for i in range(n)])]
    unnamed x28 -> x26, local copies, waits for them, and re-layouts: 7.67 us -> 6.91 us
  transfers between devices with their start and end apart: 46 -> 47, of which waited for: 14 -> 14; matrix products, arithmetic and copies ran while one was open for 0% -> 0% of each run, Pallas kernels for 26% -> 26%
where the time goes in v8:
time: 91.4 us; the launch traced here: 90.4 us
  starting transfers between devices  37.6 us (41%)
  Pallas kernels  30.9 us (34%)
  waiting for transfers between devices  13.7 us (15%)
  local copies, waits for them, and re-layouts  6.91 us (8%)
  between operations  1.21 us (1%)
    ppermute x35, starting transfers between devices, flip(): return lax.ppermute(value, 'sp', [(i, i ^ bits) for i in range(n)])  25 us
    ppermute x9, starting transfers between devices, rotate(): return lax.ppermute(value, 'fs', [(i, (i + step) % n) for i in range(n)])  11.4 us
    ppermute x35, waiting for transfers between devices, flip(): return lax.ppermute(value, 'sp', [(i, i ^ bits) for i in range(n)])  9.3 us
    pallas_call x2, Pallas kernels, on_device(): call(functools.partial(backward_kernel, (n_sp, batch, tok, key_dev, keys,...  8.51 us
    pallas_call x2, Pallas kernels, on_device(): call(functools.partial(forward_kernel, (batch, tok, key_dev, keys, block,...  7.69 us
    unnamed x26, local copies, waits for them, and re-layouts  6.91 us
    pallas_call x1, Pallas kernels, on_device(): call(functools.partial(mlp_kernel, (n_fs, batches, row_dev, cols, dim, hi...  4.38 us
    ppermute x9, waiting for transfers between devices, rotate(): return lax.ppermute(value, 'fs', [(i, (i + step) % n) for i in range(n)])  4.36 us
  transfers between devices with their start and end apart: 47, of which 14 were waited for; matrix products, arithmetic and copies ran while one was open for 0% of the time, Pallas kernels for 26%

profile of v8, /device:TPU:9, one launch (start us, length us, event | category | flops | bytes accessed | tf_op | source)
XLA Modules:
  0.0 90.4 jit_solution(9461415221653986965)
XLA Ops:
  0.7 1.8 %shard_map.356.packed = bf16[240,256]{1,0:T(8,128)(2,1)} custom-call(bf16[64]{0:T(256)(128)(2,1)} %refs_0_.3, bf16[64]{0:T(256)(128)(2,1)} %refs_1_.3, bf16[64]{0:T(256)(128)(2,1)} %refs_2_.1, bf16[64]{0:T(256)(128)(2,1)} %refs_3_.1, bf16[64]{0:T(256)(128)(2,1)} %refs_4_.1, bf16[64]{0:T(256)(128)(2,1)} %refs_5_.1, bf16[64]{0:T(256)(128)(2,1)} %refs_6_.2, ...), custom_call_target="tpu_custom_call" | custom-call | tf_op jit(solution)/shard_map/pallas_call | solution.py:822
  2.5 2.5 %collective-permute-start.1 = (bf16[240,256]{1,0:T(8,128)(2,1)}, bf16[240,256]{1,0:T(8,128)(2,1)S(1)}, u32[]{:S(2)}, u32[]{:S(2)}) collective-permute-start(bf16[240,256]{1,0:T(8,128)(2,1)} %shard_map.356.packed), channel_id=1, source_target_pairs={{0,2},{1,3},{2,0},{3,1},{4,6},{5,7},{6,4},{7,5},{8,10},{9,11},{10,... | collective-permute-start | bytes 368648 | tf_op jit(solution)/shard_map/ppermute | solution.py:720
  5.0 2.2 %collective-permute-start = (bf16[240,256]{1,0:T(8,128)(2,1)}, bf16[240,256]{1,0:T(8,128)(2,1)S(1)}, u32[]{:S(2)}, u32[]{:S(2)}) collective-permute-start(bf16[240,256]{1,0:T(8,128)(2,1)} %shard_map.356.packed), channel_id=1, source_target_pairs={{0,1},{1,2},{2,3},{3,0},{4,5},{5,6},{6,7},{7,4},{8,9},{9,10},{10,1... | collective-permute-start | bytes 368648 | tf_op jit(solution)/shard_map/ppermute | solution.py:720
  7.2 1.0 %copy-done = bf16[2,1,2,192,256]{4,3,2,1,0:T(8,128)(2,1)S(1)} copy-done((bf16[2,1,2,192,256]{4,3,2,1,0:T(8,128)(2,1)S(1)}, bf16[2,1,2,192,256]{4,3,2,1,0:T(8,128)(2,1)}, u32[]{:S(2)}) %copy-start) | copy-done | bytes 393240
  8.1 0.9 copy-done.3
  9.1 0.9 copy-done.5
  10.0 0.9 copy-done.7
  10.9 0.9 copy-done.8
  11.8 0.8 copy-done.9
  12.6 0.8 copy-done.10
  13.4 0.7 copy-done.12
  14.0 1.2 %shard_map.357 = (f32[768,256]{1,0:T(8,128)S(1)}, f32[768,128]{1,0:T(8,128)S(1)}, f32[768,256]{1,0:T(8,128)S(1)}, bf16[2,768,256]{2,1,0:T(8,128)(2,1)S(1)}, bf16...) custom-call(s32[2,1,2]{2,1,0:T(1,128)S(1)} %copy-done.12, ...), custom_call_target="tpu_custom_call" | custom-call | tf_op jit(solution)/shard_map/pallas_call | solution.py:830
  15.2 1.0 %collective-permute-start.15 = (bf16[288,256]{1,0:T(8,128)(2,1)S(1)}, bf16[288,256]{1,0:T(8,128)(2,1)S(1)}, u32[]{:S(2)}, u32[]{:S(2)}) collective-permute-start(bf16[288,256]{1,0:T(8,128)(2,1)S(1)} %get-tuple-element.134), channel_id=1, source_target_pairs={{0,2},{1,3},{2,0},{3,1},{4,6},{5,7},{6,4},{7,5},{8,10},{9,11},{10,... | collective-permute-start | bytes 442376 | tf_op jit(solution)/shard_map/ppermute | solution.py:724
  16.3 1.6 %collective-permute-start.3 = (bf16[240,256]{1,0:T(8,128)(2,1)S(1)}, bf16[240,256]{1,0:T(8,128)(2,1)S(1)}, u32[]{:S(2)}, u32[]{:S(2)}) collective-permute-start(bf16[240,256]{1,0:T(8,128)(2,1)S(1)} %get-tuple-element.122.refs_2_), channel_id=1, source_target_pairs={{0,4},{4,0},{8,12},{12,8},{16,20},{20,16},{24,28},{28,24},{1,5},{5... | collective-permute-start | bytes 368648 | tf_op jit(solution)/shard_map/ppermute | solution.py:728
  19.7 0.7 shard_map.359
  20.4 2.2 %collective-permute-start.12 = (bf16[192,256]{1,0:T(8,128)(2,1)S(1)}, bf16[192,256]{1,0:T(8,128)(2,1)S(1)}, u32[]{:S(2)}, u32[]{:S(2)}) collective-permute-start(bf16[192,256]{1,0:T(8,128)(2,1)S(1)} %get-tuple-element.131.refs_5_.refs_15_), channel_id=1, source_target_pairs={{0,24},{4,28},{8,16},{12,20},{16,8},{20,12},{24,0},{28,4},{1,25},{... | collective-permute-start | bytes 294920 | tf_op jit(solution)/shard_map/ppermute | solution.py:728
  23.2 1.0 %collective-permute-start.7 = (bf16[192,256]{1,0:T(8,128)(2,1)S(1)}, bf16[192,256]{1,0:T(8,128)(2,1)S(1)}, u32[]{:S(2)}, u32[]{:S(2)}) collective-permute-start(bf16[192,256]{1,0:T(8,128)(2,1)S(1)} %get-tuple-element.131.refs_5_.refs_15_), channel_id=1, source_target_pairs={{0,4},{4,0},{8,12},{12,8},{16,20},{20,16},{24,28},{28,24},{1,5},{5... | collective-permute-start | bytes 294920 | tf_op jit(solution)/shard_map/ppermute | solution.py:728
  24.2 1.4 %collective-permute-done.12.refs_11_.refs_21_ = bf16[192,256]{1,0:T(8,128)(2,1)S(1)} collective-permute-done((bf16[192,256]{1,0:T(8,128)(2,1)S(1)}, bf16[192,256]{1,0:T(8,128)(2,1)S(1)}, u32[]{:S(2)}, u32[]{:S(2)}) %collective-permute-start.12) | collective-permute-done | bytes 98336 | tf_op jit(solution)/shard_map/ppermute | solution.py:728
  25.6 2.6 %collective-permute-done.10.refs_9_.refs_19_ = bf16[192,256]{1,0:T(8,128)(2,1)S(1)} collective-permute-done((bf16[192,256]{1,0:T(8,128)(2,1)S(1)}, bf16[192,256]{1,0:T(8,128)(2,1)S(1)}, u32[]{:S(2)}, u32[]{:S(2)}) %collective-permute-start.10) | collective-permute-done | bytes 98336 | tf_op jit(solution)/shard_map/ppermute | solution.py:728
  30.2 3.8 %shard_map.360 = (bf16[384,256]{1,0:T(8,128)(2,1)S(1)}, bf16[384,256]{1,0:T(8,128)(2,1)S(1)}, bf16[768,512]{1,0:T(8,128)(2,1)S(1)}, f32[256,384]{1,0:T(8,128)S(1...) custom-call(bf16[768,256]{1,0:T(8,128)(2,1)S(1)} %get-tuple-element.127.refs_0_, ...), custom_call_target="tpu_custom_call" | custom-call | tf_op jit(solution)/shard_map/pallas_call | solution.py:885
  35.0 3.8 %shard_map.361 = (bf16[384,256]{1,0:T(8,128)(2,1)S(1)}, bf16[384,256]{1,0:T(8,128)(2,1)S(1)}, bf16[768,512]{1,0:T(8,128)(2,1)S(1)}, f32[256,384]{1,0:T(8,128)S(1...) custom-call(bf16[768,256]{1,0:T(8,128)(2,1)S(1)} %get-tuple-element.127.refs_0_, ...), custom_call_target="tpu_custom_call" | custom-call | tf_op jit(solution)/shard_map/pallas_call | solution.py:885
  39.0 4.4 %shard_map.364 = (f32[2,1,2,192,256]{4,3,2,1,0:T(8,128)}, f32[768,256]{1,0:T(8,128)S(1)}, bf16[768,256]{1,0:T(8,128)(2,1)S(1)}, bf16[4,256,256]{2,1,0:T(8,128)(2...) custom-call(bf16[2,1,2,192,256]{4,3,2,1,0:T(8,128)(2,1)S(1)} %copy-done.1, ...), custom_call_target="tpu_custom_call" | custom-call | tf_op jit(solution)/shard_map/pallas_call | solution.py:908
  43.5 4.3 %shard_map.365 = (bf16[4,96,256]{2,1,0:T(8,128)(2,1)S(1)}, bf16[4,96,256]{2,1,0:T(8,128)(2,1)S(1)}, bf16[4,768,768]{2,1,0:T(8,128)(2,1)S(1)}, bf16[768,256]{1,0:...) custom-call(bf16[768,256]{1,0:T(8,128)(2,1)S(1)} %get-tuple-element.144.refs_0_, ...), custom_call_target="tpu_custom_call" | custom-call | tf_op jit(solution)/shard_map/pallas_call | solution.py:950
  47.9 1.3 %collective-permute-start.24 = (bf16[4,64,256]{2,1,0:T(8,128)(2,1)S(1)}, bf16[4,64,256]{2,1,0:T(8,128)(2,1)S(1)}, u32[]{:S(2)}, u32[]{:S(2)}) collective-permute-start(bf16[4,64,256]{2,1,0:T(8,128)(2,1)S(1)} %get-tuple-element.171), channel_id=1, source_target_pairs={{0,8},{4,12},{8,0},{12,4},{16,24},{20,28},{24,16},{28,20},{1,9},{5... | collective-permute-start | bytes 393224 | tf_op jit(solution)/shard_map/ppermute | solution.py:728
  49.2 1.1 %collective-permute-start.25 = (bf16[4,64,256]{2,1,0:T(8,128)(2,1)S(1)}, bf16[4,64,256]{2,1,0:T(8,128)(2,1)S(1)}, u32[]{:S(2)}, u32[]{:S(2)}) collective-permute-start(bf16[4,64,256]{2,1,0:T(8,128)(2,1)S(1)} %get-tuple-element.172), channel_id=1, source_target_pairs={{0,16},{4,20},{8,24},{12,28},{16,0},{20,4},{24,8},{28,12},{1,17},{... | collective-permute-start | bytes 393224 | tf_op jit(solution)/shard_map/ppermute | solution.py:728
  50.6 1.2 %collective-permute-start.22 = (bf16[4,96,256]{2,1,0:T(8,128)(2,1)S(1)}, bf16[4,96,256]{2,1,0:T(8,128)(2,1)S(1)}, u32[]{:S(2)}, u32[]{:S(2)}) collective-permute-start(bf16[4,96,256]{2,1,0:T(8,128)(2,1)S(1)} %get-tuple-element.169), channel_id=1, source_target_pairs={{0,4},{4,0},{8,12},{12,8},{16,20},{20,16},{24,28},{28,24},{1,5},{5... | collective-permute-start | bytes 589832 | tf_op jit(solution)/shard_map/ppermute | solution.py:728
  51.8 4.3 %shard_map.367 = (bf16[4,96,256]{2,1,0:T(8,128)(2,1)S(1)}, bf16[4,96,256]{2,1,0:T(8,128)(2,1)S(1)}, bf16[4,768,768]{2,1,0:T(8,128)(2,1)S(1)}, bf16[768,256]{1,0:...) custom-call(bf16[768,256]{1,0:T(8,128)(2,1)S(1)} %get-tuple-element.144.refs_0_, ...), custom_call_target="tpu_custom_call" | custom-call | tf_op jit(solution)/shard_map/pallas_call | solution.py:950
  56.2 2.6 %shard_map.368 = (bf16[4,128,256]{2,1,0:T(8,128)(2,1)S(1)}, bf16[4,128,256]{2,1,0:T(8,128)(2,1)S(1)}, f32[768,256]{1,0:T(8,128)S(1)}, f32[16,256]{1,0:T(8,128)S(1)}) custom-call(bf16[768,256]{1,0:T(8,128)(2,1)S(1)} %get-tuple-element.127.refs_0_, bf16[256,256]{1,0:T(8,128)(2,1)S(1)} %get-tuple-element.129.refs_3_.refs_1_, ...), custom_call_target="tpu_custom_call" | custom-call | tf_op jit(solution)/shard_map/pallas_call | solution.py:965
  59.5 1.3 %collective-permute-start.27 = (bf16[192,256]{1,0:T(8,128)(2,1)S(1)}, bf16[192,256]{1,0:T(8,128)(2,1)S(1)}, u32[]{:S(2)}, u32[]{:S(2)}) collective-permute-start(bf16[192,256]{1,0:T(8,128)(2,1)S(1)} %get-tuple-element.176), channel_id=1, source_target_pairs={{0,8},{4,12},{8,0},{12,4},{16,24},{20,28},{24,16},{28,20},{1,9},{5... | collective-permute-start | bytes 294920 | tf_op jit(solution)/shard_map/ppermute | solution.py:728
  60.8 1.1 %collective-permute-start.28 = (bf16[192,256]{1,0:T(8,128)(2,1)S(1)}, bf16[192,256]{1,0:T(8,128)(2,1)S(1)}, u32[]{:S(2)}, u32[]{:S(2)}) collective-permute-start(bf16[192,256]{1,0:T(8,128)(2,1)S(1)} %get-tuple-element.177), channel_id=1, source_target_pairs={{0,16},{4,20},{8,24},{12,28},{16,0},{20,4},{24,8},{28,12},{1,17},{... | collective-permute-start | bytes 294920 | tf_op jit(solution)/shard_map/ppermute | solution.py:728
  62.3 1.8 %collective-permute-start.31 = (bf16[192,256]{1,0:T(8,128)(2,1)S(1)}, bf16[192,256]{1,0:T(8,128)(2,1)S(1)}, u32[]{:S(2)}, u32[]{:S(2)}) collective-permute-start(bf16[192,256]{1,0:T(8,128)(2,1)S(1)} %get-tuple-element.187), channel_id=1, source_target_pairs={{0,2},{1,3},{2,0},{3,1},{4,6},{5,7},{6,4},{7,5},{8,10},{9,11},{10,... | collective-permute-start | bytes 294920 | tf_op jit(solution)/shard_map/ppermute | solution.py:720
  64.9 1.5 %collective-permute-done.29.refs_3_ = bf16[192,256]{1,0:T(8,128)(2,1)S(1)} collective-permute-done((bf16[192,256]{1,0:T(8,128)(2,1)S(1)}, bf16[192,256]{1,0:T(8,128)(2,1)S(1)}, u32[]{:S(2)}, u32[]{:S(2)}) %collective-permute-start.29) | collective-permute-done | bytes 98336 | tf_op jit(solution)/shard_map/ppermute | solution.py:728
  66.7 1.8 %collective-permute-start.37 = (bf16[96,256]{1,0:T(8,128)(2,1)S(1)}, bf16[96,256]{1,0:T(8,128)(2,1)S(1)}, u32[]{:S(2)}, u32[]{:S(2)}) collective-permute-start(bf16[96,256]{1,0:T(8,128)(2,1)S(1)} %get-tuple-element.180.refs_0_.refs_2_), channel_id=1, source_target_pairs={{0,4},{4,0},{8,12},{12,8},{16,20},{20,16},{24,28},{28,24},{1,5},{5... | collective-permute-start | bytes 147464 | tf_op jit(solution)/shard_map/ppermute | solution.py:728
  68.6 1.2 %collective-permute-start.33 = (bf16[192,256]{1,0:T(8,128)(2,1)S(1)}, bf16[192,256]{1,0:T(8,128)(2,1)S(1)}, u32[]{:S(2)}, u32[]{:S(2)}) collective-permute-start(bf16[192,256]{1,0:T(8,128)(2,1)S(1)} %get-tuple-element.189), channel_id=1, source_target_pairs={{0,1},{1,2},{2,3},{3,0},{4,5},{5,6},{6,7},{7,4},{8,9},{9,10},{10,1... | collective-permute-start | bytes 294920 | tf_op jit(solution)/shard_map/ppermute | solution.py:720
  70.6 0.9 collective-permute-start.39
  71.5 1.5 %collective-permute-start.40 = (bf16[144,256]{1,0:T(8,128)(2,1)S(1)}, bf16[144,256]{1,0:T(8,128)(2,1)S(1)}, u32[]{:S(2)}, u32[]{:S(2)}) collective-permute-start(bf16[144,256]{1,0:T(8,128)(2,1)S(1)} %get-tuple-element.194), channel_id=1, source_target_pairs={{0,2},{1,3},{2,0},{3,1},{4,6},{5,7},{6,4},{7,5},{8,10},{9,11},{10,... | collective-permute-start | bytes 221192 | tf_op jit(solution)/shard_map/ppermute | solution.py:720
  73.8 1.3 %collective-permute-start.36 = (bf16[192,256]{1,0:T(8,128)(2,1)S(1)}, bf16[192,256]{1,0:T(8,128)(2,1)S(1)}, u32[]{:S(2)}, u32[]{:S(2)}) collective-permute-start(bf16[192,256]{1,0:T(8,128)(2,1)S(1)} %shard_map.375.refs_0_), channel_id=1, source_target_pairs={{0,24},{4,28},{8,16},{12,20},{16,8},{20,12},{24,0},{28,4},{1,25},{... | collective-permute-start | bytes 294920 | tf_op jit(solution)/shard_map/ppermute | solution.py:728
  75.6 0.9 collective-permute-start.34
  76.5 2.4 %collective-permute-done.40.refs_2_ = bf16[144,256]{1,0:T(8,128)(2,1)S(1)} collective-permute-done((bf16[144,256]{1,0:T(8,128)(2,1)S(1)}, bf16[144,256]{1,0:T(8,128)(2,1)S(1)}, u32[]{:S(2)}, u32[]{:S(2)}) %collective-permute-start.40) | collective-permute-done | bytes 73760 | tf_op jit(solution)/shard_map/ppermute | solution.py:720
  78.8 2.0 %collective-permute-done.41.refs_3_ = bf16[144,256]{1,0:T(8,128)(2,1)S(1)} collective-permute-done((bf16[144,256]{1,0:T(8,128)(2,1)S(1)}, bf16[144,256]{1,0:T(8,128)(2,1)S(1)}, u32[]{:S(2)}, u32[]{:S(2)}) %collective-permute-start.41) | collective-permute-done | bytes 73760 | tf_op jit(solution)/shard_map/ppermute | solution.py:720
  80.9 1.3 %collective-permute-start.45 = (bf16[144,256]{1,0:T(8,128)(2,1)S(1)}, bf16[144,256]{1,0:T(8,128)(2,1)S(1)}, u32[]{:S(2)}, u32[]{:S(2)}) collective-permute-start(bf16[144,256]{1,0:T(8,128)(2,1)S(1)} %shard_map.377.refs_4_.refs_0_), channel_id=1, source_target_pairs={{0,24},{4,28},{8,16},{12,20},{16,8},{20,12},{24,0},{28,4},{1,25},{... | collective-permute-start | bytes 221192 | tf_op jit(solution)/shard_map/ppermute | solution.py:728
  82.7 0.9 collective-permute-start.43
  83.7 1.4 %collective-permute-start.42 = (bf16[384,256]{1,0:T(8,128)(2,1)S(1)}, bf16[384,256]{1,0:T(8,128)(2,1)S(1)}, u32[]{:S(2)}, u32[]{:S(2)}) collective-permute-start(bf16[384,256]{1,0:T(8,128)(2,1)S(1)} %shard_map.378._.mine), channel_id=1, source_target_pairs={{0,4},{4,0},{8,12},{12,8},{16,20},{20,16},{24,28},{28,24},{1,5},{5... | collective-permute-start | bytes 589832 | tf_op jit(solution)/shard_map/ppermute | solution.py:728
  85.1 1.2 %shard_map.379 = (f32[2,1,2,192,256]{4,3,2,1,0:T(8,128)}, f32[8,128]{1,0:T(8,128)S(1)}) custom-call(f32[768,256]{1,0:T(8,128)S(1)} %get-tuple-element.141.refs_2_.middle, f32[768,256]{1,0:T(8,128)S(1)} %get-tuple-element.182.grad_normed, f32[768,256]{1,0:T(8,128)S(1)} %get-tuple-element.119.refs_0_.normal_ref, f32[768,128]{1,0:T(8,128)S(1)} %get-tuple-element.183.rstd_ref, ...), custom_call_target="tpu_custom_call" | custom-call | tf_op jit(solution)/shard_map/pallas_call | solution.py:1033
  86.3 1.2 %collective-permute-done.44.refs_2_ = bf16[144,256]{1,0:T(8,128)(2,1)S(1)} collective-permute-done((bf16[144,256]{1,0:T(8,128)(2,1)S(1)}, bf16[144,256]{1,0:T(8,128)(2,1)S(1)}, u32[]{:S(2)}, u32[]{:S(2)}) %collective-permute-start.44) | collective-permute-done | bytes 73760 | tf_op jit(solution)/shard_map/ppermute | solution.py:728
  87.5 0.7 collective-permute-start.46
  88.2 0.9 %collective-permute-done.46.refs_0_ = bf16[144,256]{1,0:T(8,128)(2,1)S(1)} collective-permute-done((bf16[144,256]{1,0:T(8,128)(2,1)S(1)}, bf16[144,256]{1,0:T(8,128)(2,1)S(1)}, u32[]{:S(2)}, u32[]{:S(2)}) %collective-permute-start.46) | collective-permute-done | bytes 73760 | tf_op jit(solution)/shard_map/ppermute | solution.py:728
  89.2 1.0 %shard_map.382 = (f32[64,256]{1,0:T(8,128)}, f32[64,512]{1,0:T(8,128)}, f32[64,256]{1,0:T(8,128)}, f32[64,1024]{1,0:T(8,128)}, f32[256,256]{1,0:T(8,128)}, /*ind...) custom-call(bf16[384,256]{1,0:T(8,128)(2,1)S(1)} %shard_map.378._.mi, ...), custom_call_target="tpu_custom_call" | custom-call | tf_op jit(solution)/shard_map/pallas_call | solution.py:1045
  (99 shorter events, 11.1 us)
Async XLA Ops:
  2.5 13.7 %collective-permute-start.2 = (bf16[240,256]{1,0:T(8,128)(2,1)}, bf16[240,256]{1,0:T(8,128)(2,1)S(1)}, u32[]{:S(2)}, u32[]{:S(2)}) collective-permute-start(bf16[240,256]{1,0:T(8,128)(2,1)} %shard_map.356.packed), channel_id=1, source_target_pairs={{0,3},{1,0},{2,1},{3,2},{4,7},{5,4},{6,5},{7,6},{8,11},{9,8},{10,9... | collective-permute-start | bytes 368648 | tf_op jit(solution)/shard_map/ppermute | solution.py:720
  2.5 13.7 %collective-permute-start.1 = (bf16[240,256]{1,0:T(8,128)(2,1)}, bf16[240,256]{1,0:T(8,128)(2,1)S(1)}, u32[]{:S(2)}, u32[]{:S(2)}) collective-permute-start(bf16[240,256]{1,0:T(8,128)(2,1)} %shard_map.356.packed), channel_id=1, source_target_pairs={{0,2},{1,3},{2,0},{3,1},{4,6},{5,7},{6,4},{7,5},{8,10},{9,11},{10,... | collective-permute-start | bytes 368648 | tf_op jit(solution)/shard_map/ppermute | solution.py:720
  5.0 11.3 %collective-permute-start = (bf16[240,256]{1,0:T(8,128)(2,1)}, bf16[240,256]{1,0:T(8,128)(2,1)S(1)}, u32[]{:S(2)}, u32[]{:S(2)}) collective-permute-start(bf16[240,256]{1,0:T(8,128)(2,1)} %shard_map.356.packed), channel_id=1, source_target_pairs={{0,1},{1,2},{2,3},{3,0},{4,5},{5,6},{6,7},{7,4},{8,9},{9,10},{10,1... | collective-permute-start | bytes 368648 | tf_op jit(solution)/shard_map/ppermute | solution.py:720
  15.2 7.9 %collective-permute-start.15 = (bf16[288,256]{1,0:T(8,128)(2,1)S(1)}, bf16[288,256]{1,0:T(8,128)(2,1)S(1)}, u32[]{:S(2)}, u32[]{:S(2)}) collective-permute-start(bf16[288,256]{1,0:T(8,128)(2,1)S(1)} %get-tuple-element.134), channel_id=1, source_target_pairs={{0,2},{1,3},{2,0},{3,1},{4,6},{5,7},{6,4},{7,5},{8,10},{9,11},{10,... | collective-permute-start | bytes 442376 | tf_op jit(solution)/shard_map/ppermute | solution.py:724
  16.3 2.6 %collective-permute-start.3 = (bf16[240,256]{1,0:T(8,128)(2,1)S(1)}, bf16[240,256]{1,0:T(8,128)(2,1)S(1)}, u32[]{:S(2)}, u32[]{:S(2)}) collective-permute-start(bf16[240,256]{1,0:T(8,128)(2,1)S(1)} %get-tuple-element.122.refs_2_), channel_id=1, source_target_pairs={{0,4},{4,0},{8,12},{12,8},{16,20},{20,16},{24,28},{28,24},{1,5},{5... | collective-permute-start | bytes 368648 | tf_op jit(solution)/shard_map/ppermute | solution.py:728
  17.8 1.3 %collective-permute-start.4 = (bf16[240,256]{1,0:T(8,128)(2,1)S(1)}, bf16[240,256]{1,0:T(8,128)(2,1)S(1)}, u32[]{:S(2)}, u32[]{:S(2)}) collective-permute-start(bf16[240,256]{1,0:T(8,128)(2,1)S(1)} %get-tuple-element.123.refs_3_), channel_id=1, source_target_pairs={{0,4},{4,0},{8,12},{12,8},{16,20},{20,16},{24,28},{28,24},{1,5},{5... | collective-permute-start | bytes 368648 | tf_op jit(solution)/shard_map/ppermute | solution.py:728
  17.9 1.4 %collective-permute-start.5 = (bf16[240,256]{1,0:T(8,128)(2,1)S(1)}, bf16[240,256]{1,0:T(8,128)(2,1)S(1)}, u32[]{:S(2)}, u32[]{:S(2)}) collective-permute-start(bf16[240,256]{1,0:T(8,128)(2,1)S(1)} %get-tuple-element.124.refs_4_), channel_id=1, source_target_pairs={{0,4},{4,0},{8,12},{12,8},{16,20},{20,16},{24,28},{28,24},{1,5},{5... | collective-permute-start | bytes 368648 | tf_op jit(solution)/shard_map/ppermute | solution.py:728
  18.4 1.3 %collective-permute-start.6 = (bf16[240,256]{1,0:T(8,128)(2,1)S(1)}, bf16[240,256]{1,0:T(8,128)(2,1)S(1)}, u32[]{:S(2)}, u32[]{:S(2)}) collective-permute-start(bf16[240,256]{1,0:T(8,128)(2,1)S(1)} %get-tuple-element.125.refs_5_), channel_id=1, source_target_pairs={{0,4},{4,0},{8,12},{12,8},{16,20},{20,16},{24,28},{28,24},{1,5},{5... | collective-permute-start | bytes 368648 | tf_op jit(solution)/shard_map/ppermute | solution.py:728
  18.8 15.2 %collective-permute-start.14 = (bf16[288,256]{1,0:T(8,128)(2,1)S(1)}, bf16[288,256]{1,0:T(8,128)(2,1)S(1)}, u32[]{:S(2)}, u32[]{:S(2)}) collective-permute-start(bf16[288,256]{1,0:T(8,128)(2,1)S(1)} %get-tuple-element.134), channel_id=1, source_target_pairs={{0,1},{1,0},{2,3},{3,2},{4,5},{5,4},{6,7},{7,6},{8,9},{9,8},{10,11... | collective-permute-start | bytes 442376 | tf_op jit(solution)/shard_map/ppermute | solution.py:724
  20.4 5.2 %collective-permute-start.12 = (bf16[192,256]{1,0:T(8,128)(2,1)S(1)}, bf16[192,256]{1,0:T(8,128)(2,1)S(1)}, u32[]{:S(2)}, u32[]{:S(2)}) collective-permute-start(bf16[192,256]{1,0:T(8,128)(2,1)S(1)} %get-tuple-element.131.refs_5_.refs_15_), channel_id=1, source_target_pairs={{0,24},{4,28},{8,16},{12,20},{16,8},{20,12},{24,0},{28,4},{1,25},{... | collective-permute-start | bytes 294920 | tf_op jit(solution)/shard_map/ppermute | solution.py:728
  22.7 5.6 %collective-permute-start.10 = (bf16[192,256]{1,0:T(8,128)(2,1)S(1)}, bf16[192,256]{1,0:T(8,128)(2,1)S(1)}, u32[]{:S(2)}, u32[]{:S(2)}) collective-permute-start(bf16[192,256]{1,0:T(8,128)(2,1)S(1)} %get-tuple-element.131.refs_5_.refs_15_), channel_id=1, source_target_pairs={{0,16},{4,20},{8,24},{12,28},{16,0},{20,4},{24,8},{28,12},{1,17},{... | collective-permute-start | bytes 294920 | tf_op jit(solution)/shard_map/ppermute | solution.py:728
  22.9 5.8 %collective-permute-start.8 = (bf16[192,256]{1,0:T(8,128)(2,1)S(1)}, bf16[192,256]{1,0:T(8,128)(2,1)S(1)}, u32[]{:S(2)}, u32[]{:S(2)}) collective-permute-start(bf16[192,256]{1,0:T(8,128)(2,1)S(1)} %get-tuple-element.131.refs_5_.refs_15_), channel_id=1, source_target_pairs={{0,8},{4,12},{8,0},{12,4},{16,24},{20,28},{24,16},{28,20},{1,9},{5... | collective-permute-start | bytes 294920 | tf_op jit(solution)/shard_map/ppermute | solution.py:728
  23.2 5.6 %collective-permute-start.7 = (bf16[192,256]{1,0:T(8,128)(2,1)S(1)}, bf16[192,256]{1,0:T(8,128)(2,1)S(1)}, u32[]{:S(2)}, u32[]{:S(2)}) collective-permute-start(bf16[192,256]{1,0:T(8,128)(2,1)S(1)} %get-tuple-element.131.refs_5_.refs_15_), channel_id=1, source_target_pairs={{0,4},{4,0},{8,12},{12,8},{16,20},{20,16},{24,28},{28,24},{1,5},{5... | collective-permute-start | bytes 294920 | tf_op jit(solution)/shard_map/ppermute | solution.py:728
  24.2 14.7 %copy-start.1 = (bf16[2,1,2,192,256]{4,3,2,1,0:T(8,128)(2,1)S(1)}, bf16[2,1,2,192,256]{4,3,2,1,0:T(8,128)(2,1)}, u32[]{:S(2)}) copy-start(bf16[2,1,2,192,256]{4,3,2,1,0:T(8,128)(2,1)} %refs_0_.5) | copy-start | bytes 1179652
  25.6 8.4 %collective-permute-start.16 = (bf16[288,256]{1,0:T(8,128)(2,1)S(1)}, bf16[288,256]{1,0:T(8,128)(2,1)S(1)}, u32[]{:S(2)}, u32[]{:S(2)}) collective-permute-start(bf16[288,256]{1,0:T(8,128)(2,1)S(1)} %shard_map.362), channel_id=1, source_target_pairs={{0,1},{1,0},{2,3},{3,2},{4,5},{5,4},{6,7},{7,6},{8,9},{9,8},{10,11... | collective-permute-start | bytes 442376 | tf_op jit(solution)/shard_map/ppermute | solution.py:724
  28.2 1.4 %collective-permute-start.13 = (bf16[192,256]{1,0:T(8,128)(2,1)S(1)}, bf16[192,256]{1,0:T(8,128)(2,1)S(1)}, u32[]{:S(2)}, u32[]{:S(2)}) collective-permute-start(bf16[192,256]{1,0:T(8,128)(2,1)S(1)} %collective-permute-done.12.refs_11_.refs_21_), channel_id=1, source_target_pairs={{0,4},{4,0},{8,12},{12,8},{16,20},{20,16},{24,28},{28,24},{1,5},{5... | collective-permute-start | bytes 294920 | tf_op jit(solution)/shard_map/ppermute | solution.py:728
  28.7 1.3 %collective-permute-start.11 = (bf16[192,256]{1,0:T(8,128)(2,1)S(1)}, bf16[192,256]{1,0:T(8,128)(2,1)S(1)}, u32[]{:S(2)}, u32[]{:S(2)}) collective-permute-start(bf16[192,256]{1,0:T(8,128)(2,1)S(1)} %collective-permute-done.10.refs_9_.refs_19_), channel_id=1, source_target_pairs={{0,4},{4,0},{8,12},{12,8},{16,20},{20,16},{24,28},{28,24},{1,5},{5... | collective-permute-start | bytes 294920 | tf_op jit(solution)/shard_map/ppermute | solution.py:728
  28.8 1.4 %collective-permute-start.9 = (bf16[192,256]{1,0:T(8,128)(2,1)S(1)}, bf16[192,256]{1,0:T(8,128)(2,1)S(1)}, u32[]{:S(2)}, u32[]{:S(2)}) collective-permute-start(bf16[192,256]{1,0:T(8,128)(2,1)S(1)} %collective-permute-done.8.refs_7_.refs_17_), channel_id=1, source_target_pairs={{0,4},{4,0},{8,12},{12,8},{16,20},{20,16},{24,28},{28,24},{1,5},{5... | collective-permute-start | bytes 294920 | tf_op jit(solution)/shard_map/ppermute | solution.py:728
  29.7 9.2 %collective-permute-start.20 = (bf16[4,192,128]{2,1,0:T(8,128)(2,1)S(1)}, bf16[4,192,128]{2,1,0:T(8,128)(2,1)S(1)}, u32[]{:S(2)}, u32[]{:S(2)}) collective-permute-start(bf16[4,192,128]{2,1,0:T(8,128)(2,1)S(1)} %get-tuple-element.139), channel_id=1, source_target_pairs={{0,4},{4,0},{8,12},{12,8},{16,20},{20,16},{24,28},{28,24},{1,5},{5... | collective-permute-start | bytes 589832 | tf_op jit(solution)/shard_map/ppermute | solution.py:728
  34.1 4.8 %collective-permute-start.17 = (bf16[288,256]{1,0:T(8,128)(2,1)S(1)}, bf16[288,256]{1,0:T(8,128)(2,1)S(1)}, u32[]{:S(2)}, u32[]{:S(2)}) collective-permute-start(bf16[288,256]{1,0:T(8,128)(2,1)S(1)} %get-tuple-element.136.refs_9_), channel_id=1, source_target_pairs={{0,4},{4,0},{8,12},{12,8},{16,20},{20,16},{24,28},{28,24},{1,5},{5... | collective-permute-start | bytes 442376 | tf_op jit(solution)/shard_map/ppermute | solution.py:728
  34.5 4.4 %collective-permute-start.18 = (bf16[288,256]{1,0:T(8,128)(2,1)S(1)}, bf16[288,256]{1,0:T(8,128)(2,1)S(1)}, u32[]{:S(2)}, u32[]{:S(2)}) collective-permute-start(bf16[288,256]{1,0:T(8,128)(2,1)S(1)} %get-tuple-element.137.refs_10_), channel_id=1, source_target_pairs={{0,4},{4,0},{8,12},{12,8},{16,20},{20,16},{24,28},{28,24},{1,5},{5... | collective-permute-start | bytes 442376 | tf_op jit(solution)/shard_map/ppermute | solution.py:728
  34.7 4.2 %collective-permute-start.19 = (bf16[288,256]{1,0:T(8,128)(2,1)S(1)}, bf16[288,256]{1,0:T(8,128)(2,1)S(1)}, u32[]{:S(2)}, u32[]{:S(2)}) collective-permute-start(bf16[288,256]{1,0:T(8,128)(2,1)S(1)} %get-tuple-element.138.refs_11_), channel_id=1, source_target_pairs={{0,4},{4,0},{8,12},{12,8},{16,20},{20,16},{24,28},{28,24},{1,5},{5... | collective-permute-start | bytes 442376 | tf_op jit(solution)/shard_map/ppermute | solution.py:728
  43.4 4.4 %collective-permute-start.21 = (bf16[4,256,256]{2,1,0:T(8,128)(2,1)S(1)}, bf16[4,256,256]{2,1,0:T(8,128)(2,1)S(1)}, u32[]{:S(2)}, u32[]{:S(2)}) collective-permute-start(bf16[4,256,256]{2,1,0:T(8,128)(2,1)S(1)} %get-tuple-element.154), channel_id=1, source_target_pairs={{0,4},{4,0},{8,12},{12,8},{16,20},{20,16},{24,28},{28,24},{1,5},{5... | collective-permute-start | bytes 1572872 | tf_op jit(solution)/shard_map/ppermute | solution.py:728
  47.9 10.8 %collective-permute-start.24 = (bf16[4,64,256]{2,1,0:T(8,128)(2,1)S(1)}, bf16[4,64,256]{2,1,0:T(8,128)(2,1)S(1)}, u32[]{:S(2)}, u32[]{:S(2)}) collective-permute-start(bf16[4,64,256]{2,1,0:T(8,128)(2,1)S(1)} %get-tuple-element.171), channel_id=1, source_target_pairs={{0,8},{4,12},{8,0},{12,4},{16,24},{20,28},{24,16},{28,20},{1,9},{5... | collective-permute-start | bytes 393224 | tf_op jit(solution)/shard_map/ppermute | solution.py:728
  49.2 10.1 %collective-permute-start.25 = (bf16[4,64,256]{2,1,0:T(8,128)(2,1)S(1)}, bf16[4,64,256]{2,1,0:T(8,128)(2,1)S(1)}, u32[]{:S(2)}, u32[]{:S(2)}) collective-permute-start(bf16[4,64,256]{2,1,0:T(8,128)(2,1)S(1)} %get-tuple-element.172), channel_id=1, source_target_pairs={{0,16},{4,20},{8,24},{12,28},{16,0},{20,4},{24,8},{28,12},{1,17},{... | collective-permute-start | bytes 393224 | tf_op jit(solution)/shard_map/ppermute | solution.py:728
  50.4 9.0 %collective-permute-start.26 = (bf16[4,64,256]{2,1,0:T(8,128)(2,1)S(1)}, bf16[4,64,256]{2,1,0:T(8,128)(2,1)S(1)}, u32[]{:S(2)}, u32[]{:S(2)}) collective-permute-start(bf16[4,64,256]{2,1,0:T(8,128)(2,1)S(1)} %get-tuple-element.173), channel_id=1, source_target_pairs={{0,24},{4,28},{8,16},{12,20},{16,8},{20,12},{24,0},{28,4},{1,25},{... | collective-permute-start | bytes 393224 | tf_op jit(solution)/shard_map/ppermute | solution.py:728
  50.6 8.7 %collective-permute-start.22 = (bf16[4,96,256]{2,1,0:T(8,128)(2,1)S(1)}, bf16[4,96,256]{2,1,0:T(8,128)(2,1)S(1)}, u32[]{:S(2)}, u32[]{:S(2)}) collective-permute-start(bf16[4,96,256]{2,1,0:T(8,128)(2,1)S(1)} %get-tuple-element.169), channel_id=1, source_target_pairs={{0,4},{4,0},{8,12},{12,8},{16,20},{20,16},{24,28},{28,24},{1,5},{5... | collective-permute-start | bytes 589832 | tf_op jit(solution)/shard_map/ppermute | solution.py:728
  56.1 3.3 %collective-permute-start.23 = (bf16[4,96,256]{2,1,0:T(8,128)(2,1)S(1)}, bf16[4,96,256]{2,1,0:T(8,128)(2,1)S(1)}, u32[]{:S(2)}, u32[]{:S(2)}) collective-permute-start(bf16[4,96,256]{2,1,0:T(8,128)(2,1)S(1)} %get-tuple-element.170), channel_id=1, source_target_pairs={{0,4},{4,0},{8,12},{12,8},{16,20},{20,16},{24,28},{28,24},{1,5},{5... | collective-permute-start | bytes 589832 | tf_op jit(solution)/shard_map/ppermute | solution.py:728
  58.8 3.5 %collective-permute-start.30 = (bf16[4,128,256]{2,1,0:T(8,128)(2,1)S(1)}, bf16[4,128,256]{2,1,0:T(8,128)(2,1)S(1)}, u32[]{:S(2)}, u32[]{:S(2)}) collective-permute-start(bf16[4,128,256]{2,1,0:T(8,128)(2,1)S(1)} %get-tuple-element.185), channel_id=1, source_target_pairs={{0,4},{4,0},{8,12},{12,8},{16,20},{20,16},{24,28},{28,24},{1,5},{5... | collective-permute-start | bytes 786440 | tf_op jit(solution)/shard_map/ppermute | solution.py:728
  59.5 5.3 %collective-permute-start.27 = (bf16[192,256]{1,0:T(8,128)(2,1)S(1)}, bf16[192,256]{1,0:T(8,128)(2,1)S(1)}, u32[]{:S(2)}, u32[]{:S(2)}) collective-permute-start(bf16[192,256]{1,0:T(8,128)(2,1)S(1)} %get-tuple-element.176), channel_id=1, source_target_pairs={{0,8},{4,12},{8,0},{12,4},{16,24},{20,28},{24,16},{28,20},{1,9},{5... | collective-permute-start | bytes 294920 | tf_op jit(solution)/shard_map/ppermute | solution.py:728
  60.8 4.1 %collective-permute-start.28 = (bf16[192,256]{1,0:T(8,128)(2,1)S(1)}, bf16[192,256]{1,0:T(8,128)(2,1)S(1)}, u32[]{:S(2)}, u32[]{:S(2)}) collective-permute-start(bf16[192,256]{1,0:T(8,128)(2,1)S(1)} %get-tuple-element.177), channel_id=1, source_target_pairs={{0,16},{4,20},{8,24},{12,28},{16,0},{20,4},{24,8},{28,12},{1,17},{... | collective-permute-start | bytes 294920 | tf_op jit(solution)/shard_map/ppermute | solution.py:728
  61.9 4.4 %collective-permute-start.29 = (bf16[192,256]{1,0:T(8,128)(2,1)S(1)}, bf16[192,256]{1,0:T(8,128)(2,1)S(1)}, u32[]{:S(2)}, u32[]{:S(2)}) collective-permute-start(bf16[192,256]{1,0:T(8,128)(2,1)S(1)} %get-tuple-element.178), channel_id=1, source_target_pairs={{0,24},{4,28},{8,16},{12,20},{16,8},{20,12},{24,0},{28,4},{1,25},{... | collective-permute-start | bytes 294920 | tf_op jit(solution)/shard_map/ppermute | solution.py:728
  62.3 10.8 %collective-permute-start.31 = (bf16[192,256]{1,0:T(8,128)(2,1)S(1)}, bf16[192,256]{1,0:T(8,128)(2,1)S(1)}, u32[]{:S(2)}, u32[]{:S(2)}) collective-permute-start(bf16[192,256]{1,0:T(8,128)(2,1)S(1)} %get-tuple-element.187), channel_id=1, source_target_pairs={{0,2},{1,3},{2,0},{3,1},{4,6},{5,7},{6,4},{7,5},{8,10},{9,11},{10,... | collective-permute-start | bytes 294920 | tf_op jit(solution)/shard_map/ppermute | solution.py:720
  64.1 9.6 %collective-permute-start.32 = (bf16[192,256]{1,0:T(8,128)(2,1)S(1)}, bf16[192,256]{1,0:T(8,128)(2,1)S(1)}, u32[]{:S(2)}, u32[]{:S(2)}) collective-permute-start(bf16[192,256]{1,0:T(8,128)(2,1)S(1)} %get-tuple-element.188), channel_id=1, source_target_pairs={{0,3},{1,0},{2,1},{3,2},{4,7},{5,4},{6,5},{7,6},{8,11},{9,8},{10,9... | collective-permute-start | bytes 294920 | tf_op jit(solution)/shard_map/ppermute | solution.py:720
  66.7 3.6 %collective-permute-start.37 = (bf16[96,256]{1,0:T(8,128)(2,1)S(1)}, bf16[96,256]{1,0:T(8,128)(2,1)S(1)}, u32[]{:S(2)}, u32[]{:S(2)}) collective-permute-start(bf16[96,256]{1,0:T(8,128)(2,1)S(1)} %get-tuple-element.180.refs_0_.refs_2_), channel_id=1, source_target_pairs={{0,4},{4,0},{8,12},{12,8},{16,20},{20,16},{24,28},{28,24},{1,5},{5... | collective-permute-start | bytes 147464 | tf_op jit(solution)/shard_map/ppermute | solution.py:728
  68.5 1.8 %collective-permute-start.38 = (bf16[96,256]{1,0:T(8,128)(2,1)S(1)}, bf16[96,256]{1,0:T(8,128)(2,1)S(1)}, u32[]{:S(2)}, u32[]{:S(2)}) collective-permute-start(bf16[96,256]{1,0:T(8,128)(2,1)S(1)} %get-tuple-element.181.refs_1_.refs_3_), channel_id=1, source_target_pairs={{0,4},{4,0},{8,12},{12,8},{16,20},{20,16},{24,28},{28,24},{1,5},{5... | collective-permute-start | bytes 147464 | tf_op jit(solution)/shard_map/ppermute | solution.py:728
  68.6 5.2 %collective-permute-start.33 = (bf16[192,256]{1,0:T(8,128)(2,1)S(1)}, bf16[192,256]{1,0:T(8,128)(2,1)S(1)}, u32[]{:S(2)}, u32[]{:S(2)}) collective-permute-start(bf16[192,256]{1,0:T(8,128)(2,1)S(1)} %get-tuple-element.189), channel_id=1, source_target_pairs={{0,1},{1,2},{2,3},{3,0},{4,5},{5,6},{6,7},{7,4},{8,9},{9,10},{10,1... | collective-permute-start | bytes 294920 | tf_op jit(solution)/shard_map/ppermute | solution.py:720
  70.6 5.0 %collective-permute-start.39 = (bf16[144,256]{1,0:T(8,128)(2,1)S(1)}, bf16[144,256]{1,0:T(8,128)(2,1)S(1)}, u32[]{:S(2)}, u32[]{:S(2)}) collective-permute-start(bf16[144,256]{1,0:T(8,128)(2,1)S(1)} %get-tuple-element.193), channel_id=1, source_target_pairs={{0,1},{1,2},{2,3},{3,0},{4,5},{5,6},{6,7},{7,4},{8,9},{9,10},{10,1... | collective-permute-start | bytes 221192 | tf_op jit(solution)/shard_map/ppermute | solution.py:720
  71.5 7.3 %collective-permute-start.40 = (bf16[144,256]{1,0:T(8,128)(2,1)S(1)}, bf16[144,256]{1,0:T(8,128)(2,1)S(1)}, u32[]{:S(2)}, u32[]{:S(2)}) collective-permute-start(bf16[144,256]{1,0:T(8,128)(2,1)S(1)} %get-tuple-element.194), channel_id=1, source_target_pairs={{0,2},{1,3},{2,0},{3,1},{4,6},{5,7},{6,4},{7,5},{8,10},{9,11},{10,... | collective-permute-start | bytes 221192 | tf_op jit(solution)/shard_map/ppermute | solution.py:720
  73.1 7.8 %collective-permute-start.41 = (bf16[144,256]{1,0:T(8,128)(2,1)S(1)}, bf16[144,256]{1,0:T(8,128)(2,1)S(1)}, u32[]{:S(2)}, u32[]{:S(2)}) collective-permute-start(bf16[144,256]{1,0:T(8,128)(2,1)S(1)} %get-tuple-element.195), channel_id=1, source_target_pairs={{0,3},{1,0},{2,1},{3,2},{4,7},{5,4},{6,5},{7,6},{8,11},{9,8},{10,9... | collective-permute-start | bytes 221192 | tf_op jit(solution)/shard_map/ppermute | solution.py:720
  73.8 9.0 %collective-permute-start.36 = (bf16[192,256]{1,0:T(8,128)(2,1)S(1)}, bf16[192,256]{1,0:T(8,128)(2,1)S(1)}, u32[]{:S(2)}, u32[]{:S(2)}) collective-permute-start(bf16[192,256]{1,0:T(8,128)(2,1)S(1)} %shard_map.375.refs_0_), channel_id=1, source_target_pairs={{0,24},{4,28},{8,16},{12,20},{16,8},{20,12},{24,0},{28,4},{1,25},{... | collective-permute-start | bytes 294920 | tf_op jit(solution)/shard_map/ppermute | solution.py:728
  75.1 8.5 %collective-permute-start.35 = (bf16[192,256]{1,0:T(8,128)(2,1)S(1)}, bf16[192,256]{1,0:T(8,128)(2,1)S(1)}, u32[]{:S(2)}, u32[]{:S(2)}) collective-permute-start(bf16[192,256]{1,0:T(8,128)(2,1)S(1)} %shard_map.375.refs_0_), channel_id=1, source_target_pairs={{0,16},{4,20},{8,24},{12,28},{16,0},{20,4},{24,8},{28,12},{1,17},{... | collective-permute-start | bytes 294920 | tf_op jit(solution)/shard_map/ppermute | solution.py:728
  75.6 8.0 %collective-permute-start.34 = (bf16[192,256]{1,0:T(8,128)(2,1)S(1)}, bf16[192,256]{1,0:T(8,128)(2,1)S(1)}, u32[]{:S(2)}, u32[]{:S(2)}) collective-permute-start(bf16[192,256]{1,0:T(8,128)(2,1)S(1)} %shard_map.375.refs_0_), channel_id=1, source_target_pairs={{0,8},{4,12},{8,0},{12,4},{16,24},{20,28},{24,16},{28,20},{1,9},{5... | collective-permute-start | bytes 294920 | tf_op jit(solution)/shard_map/ppermute | solution.py:728
  80.9 5.4 %collective-permute-start.45 = (bf16[144,256]{1,0:T(8,128)(2,1)S(1)}, bf16[144,256]{1,0:T(8,128)(2,1)S(1)}, u32[]{:S(2)}, u32[]{:S(2)}) collective-permute-start(bf16[144,256]{1,0:T(8,128)(2,1)S(1)} %shard_map.377.refs_4_.refs_0_), channel_id=1, source_target_pairs={{0,24},{4,28},{8,16},{12,20},{16,8},{20,12},{24,0},{28,4},{1,25},{... | collective-permute-start | bytes 221192 | tf_op jit(solution)/shard_map/ppermute | solution.py:728
  82.2 5.3 %collective-permute-start.44 = (bf16[144,256]{1,0:T(8,128)(2,1)S(1)}, bf16[144,256]{1,0:T(8,128)(2,1)S(1)}, u32[]{:S(2)}, u32[]{:S(2)}) collective-permute-start(bf16[144,256]{1,0:T(8,128)(2,1)S(1)} %shard_map.377.refs_4_.refs_0_), channel_id=1, source_target_pairs={{0,16},{4,20},{8,24},{12,28},{16,0},{20,4},{24,8},{28,12},{1,17},{... | collective-permute-start | bytes 221192 | tf_op jit(solution)/shard_map/ppermute | solution.py:728
  82.7 4.8 %collective-permute-start.43 = (bf16[144,256]{1,0:T(8,128)(2,1)S(1)}, bf16[144,256]{1,0:T(8,128)(2,1)S(1)}, u32[]{:S(2)}, u32[]{:S(2)}) collective-permute-start(bf16[144,256]{1,0:T(8,128)(2,1)S(1)} %shard_map.377.refs_4_.refs_0_), channel_id=1, source_target_pairs={{0,8},{4,12},{8,0},{12,4},{16,24},{20,28},{24,16},{28,20},{1,9},{5... | collective-permute-start | bytes 221192 | tf_op jit(solution)/shard_map/ppermute | solution.py:728
  83.7 5.5 %collective-permute-start.42 = (bf16[384,256]{1,0:T(8,128)(2,1)S(1)}, bf16[384,256]{1,0:T(8,128)(2,1)S(1)}, u32[]{:S(2)}, u32[]{:S(2)}) collective-permute-start(bf16[384,256]{1,0:T(8,128)(2,1)S(1)} %shard_map.378._.mine), channel_id=1, source_target_pairs={{0,4},{4,0},{8,12},{12,8},{16,20},{20,16},{24,28},{28,24},{1,5},{5... | collective-permute-start | bytes 589832 | tf_op jit(solution)/shard_map/ppermute | solution.py:728
  87.5 1.6 %collective-permute-start.46 = (bf16[144,256]{1,0:T(8,128)(2,1)S(1)}, bf16[144,256]{1,0:T(8,128)(2,1)S(1)}, u32[]{:S(2)}, u32[]{:S(2)}) collective-permute-start(bf16[144,256]{1,0:T(8,128)(2,1)S(1)} %shard_map.380.mine_b), channel_id=1, source_target_pairs={{0,4},{4,0},{8,12},{12,8},{16,20},{20,16},{24,28},{28,24},{1,5},{5... | collective-permute-start | bytes 221192 | tf_op jit(solution)/shard_map/ppermute | solution.py:728
  (12 other events, 65.8 us)
